TPU v7x, 32 devices: a whole 2x2x4 slice. The times are simulated.
32 devices in a mesh: ctx: 16 (over z, x, core), head: 2 (over y).
Axes of the slice: x: 2, y: 2, z: 4, core: 2. Of those that a mesh axis runs over, the one named last changes fastest.
Arguments:
- queries: bfloat16 [3120, 768], P('ctx', 'head'), may hold values from -6 to 6
- keys: bfloat16 [3120, 768], P('ctx', 'head'), may hold values from -6 to 6
- values: bfloat16 [3120, 768], P('ctx', 'head'), may hold values from -6 to 6
- rates: float32 [3120, 6], P('ctx', 'head'), may hold values from 0.1 to 1
- frame_update: int32 [16], P('ctx'), may hold values 0 or 1
- fast_weights: float32 [3, 6, 512, 128], P(None, 'head', 'ctx'), may hold values from -2 to 2
- gain: float32 [768], P('head'), may hold values from 0.5 to 1.5
Outputs:
- block_out: bfloat16 [3120, 768], P('ctx', 'head')
- new_weights: float32 [3, 6, 512, 128], P(None, 'head', 'ctx')
All inputs are finite; a program needn't handle non-finite values. No bound on the sum of `frame_update` on one device may be relied on, other than what follows from the above.
Results may differ from a plain program's by a relative error of at most 0.0071.
Values may be sent and summed in bfloat16 or wider, within the bound.
No kernel may reach another device: no remote copies, remote signals or barrier semaphores. Data moves between devices by JAX's collectives and lax.ppermute only.
A program may use at most 64 MiB of HBM per device.

v0:
```python
import functools

import jax
import jax.numpy as jnp
import numpy as np
from jax import lax
from jax.experimental import pallas as pl
from jax.experimental.pallas import tpu as pltpu
from jax.sharding import Mesh, PartitionSpec as P

HD = 128
NS_STEPS = 5

epsilon = 1e-06
quintic_a = 3.4445
quintic_b = -4.775
quintic_c = 2.0315
highest = lax.Precision.HIGHEST
f32 = jnp.float32
bf16 = jnp.bfloat16
VMEM_LIMIT = 24 * 1024 * 1024
VMEM_MOST = 56 * 1024 * 1024


def dot(a, b, contract, precision=None):
    return lax.dot_general(
        a, b, ((contract[:1], contract[1:]), ((), ())),
        precision=precision, preferred_element_type=f32,
    )


def call(body, outs, scratch=(), in_specs=None, flops=1e8, **kw):
    given = {} if in_specs is None else {"in_specs": in_specs}
    return pl.pallas_call(
        body,
        out_shape=outs,
        **given,
        scratch_shapes=list(scratch),
        compiler_params=pltpu.CompilerParams(vmem_limit_bytes=VMEM_LIMIT),
        cost_estimate=pl.CostEstimate(flops=int(flops), bytes_accessed=1 << 20, transcendentals=0),
        **kw,
    )


smem = pl.BlockSpec(memory_space=pltpu.SMEM)
vmem = pl.BlockSpec(memory_space=pltpu.VMEM)


def sds(shape, dtype):
    return jax.ShapeDtypeStruct(shape, dtype)


def prep_body(heads, group, tokens, place, update, w_ref, k_ref, v_ref, q_ref, rate_ref, *outs):
    w_out, kv_out = outs[:2]
    token_outs = outs[2:]
    padded = kv_out.shape[0]
    slots = w_out.shape[0] // group
    for j in range(group):
        for m in range(3):
            low = w_ref[m, min(j, heads - 1)].astype(bf16)
            for z in range(slots):
                w_out[z * group + j, m] = low
    valid = lax.broadcasted_iota(jnp.int32, (padded, 1), 0) < tokens
    none = jnp.zeros((), bf16)
    keep = update[0].astype(f32)
    row = lax.broadcasted_iota(jnp.int32, (heads, HD), 0)
    for d in range(group):
        head = jnp.minimum(place[1] ^ d, heads - 1)
        cols = pl.ds(pl.multiple_of(head * HD, HD), HD)
        rate = dot(rate_ref[...], (row == head).astype(f32), (0, 0), highest)[:padded]
        target = ((rate * keep) * v_ref[:, cols].astype(f32)).astype(bf16)
        token_outs[d][:, :HD] = jnp.where(valid, k_ref[:, cols], none)
        token_outs[d][:, HD : 2 * HD] = jnp.where(valid, target, none)
        token_outs[d][:, 2 * HD :] = jnp.where(valid, q_ref[:, cols], none)
    kv_out[:, : heads * HD] = jnp.where(valid, k_ref[...], none)
    kv_out[:, heads * HD :] = jnp.where(valid, v_ref[...], none)


def grad_body(group, slots, place, *refs):
    token_refs, w_ref = refs[:group], refs[group]
    outs = refs[group + 1 : group + 1 + slots]
    k_all, t_all, grads = refs[group + 1 + slots :]
    padded = token_refs[0].shape[0]
    width = k_all.shape[0]
    for d in range(group):
        k_all[d * padded : (d + 1) * padded] = token_refs[d][:, :HD]
        t_all[d * padded : (d + 1) * padded] = token_refs[d][:, HD : 2 * HD]
    if width > group * padded:
        k_all[group * padded :] = jnp.zeros((width - group * padded, HD), bf16)
        t_all[group * padded :] = jnp.zeros((width - group * padded, HD), bf16)
    hidden = grads.shape[1]
    block = 128
    key, target = k_all[...], t_all[...]
    for start in range(0, hidden, block):
        rows = slice(start, start + block)
        w1, w3, w2 = (weight_rows(w_ref, m, start, block) for m in range(3))
        pre_one = dot(w1, key, (1, 1))
        pre_three = dot(w3, key, (1, 1))
        back = dot(w2, target, (1, 1))
        sig = jax.nn.sigmoid(pre_one)
        gate = pre_one * sig
        act = (gate * pre_three).astype(bf16)
        delta_one = (back * pre_three * sig * (1.0 + pre_one * (1.0 - sig))).astype(bf16)
        delta_three = (back * gate).astype(bf16)
        grads[0, rows] = dot(delta_one, key, (1, 0)).astype(bf16)
        grads[1, rows] = dot(delta_three, key, (1, 0)).astype(bf16)
        grads[2, rows] = dot(act, target, (1, 0)).astype(bf16)
    for d in range(slots):
        matrix = lax.rem((place[0] ^ d) - place[1] + group * slots, slots)
        chosen = grads[jnp.minimum(matrix, 2)]
        outs[d][...] = jnp.where(matrix < 3, chosen, jnp.zeros_like(chosen))


def weight_rows(w_ref, m, start, block):
    if len(w_ref.shape) == 3:
        return w_ref[m, start : start + block]
    rows = w_ref.shape[2]
    return w_ref[start // rows : (start + block) // rows, m].reshape(block, HD)


def apply_body(group, place, *refs):
    token_refs, w_ref, out = refs[:group], refs[group], refs[group + 1]
    hidden = w_ref.shape[1] if len(w_ref.shape) == 3 else w_ref.shape[0] * w_ref.shape[2]
    w1, w3, w2 = (weight_rows(w_ref, m, 0, hidden) for m in range(3))
    for d in range(group):
        query = token_refs[d][:, 2 * HD :]
        proj_one = dot(query, w1, (1, 1))
        proj_three = dot(query, w3, (1, 1))
        act = (proj_one * jax.nn.sigmoid(proj_one) * proj_three).astype(bf16)
        out[place[1] ^ d] = dot(act, w2, (1, 0)).astype(out.dtype)


def ortho_body(*refs):
    parts, out = refs[:-1], refs[-1]
    grads = parts[0][...].astype(f32)
    for part in parts[1:]:
        grads = grads + part[...].astype(f32)
    square = jnp.sum(jnp.sum(grads * grads, axis=0, keepdims=True), axis=1, keepdims=True)
    ortho = grads * lax.rsqrt(square + epsilon)
    gram = dot(ortho, ortho, (0, 0), highest)
    eye = (
        lax.broadcasted_iota(jnp.int32, (HD, HD), 0) == lax.broadcasted_iota(jnp.int32, (HD, HD), 1)
    ).astype(f32)
    total = None
    for step in range(NS_STEPS):
        square_gram = dot(gram, gram, (1, 0), highest)
        mix = quintic_a * eye + quintic_b * gram + quintic_c * square_gram
        if step < NS_STEPS - 1:
            gram = dot(dot(gram, mix, (1, 0), highest), mix, (1, 0), highest)
        total = mix if total is None else dot(total, mix, (1, 0), highest)
    out[...] = dot(ortho, total, (1, 0), highest).astype(out.dtype)


def finish_body(slots, group, w_ref, rows_ref, out):
    heads = w_ref.shape[1]
    for m in range(3):
        for h in range(heads):
            weights = w_ref[m, h]
            summed = weights + rows_ref[((m + h) % slots) * group + h].astype(f32)
            old = jnp.sqrt(jnp.sum(weights * weights, axis=1, keepdims=True))
            new = lax.rsqrt(jnp.sum(summed * summed, axis=1, keepdims=True) + epsilon)
            out[m, h] = summed * (old * new)


def attend_body(heads, tokens, place, q_ref, own_ref, back_ref, out):
    padded = own_ref.shape[0]
    span = heads * HD
    column = lax.broadcasted_iota(jnp.int32, (1, 2 * padded), 1)
    first = (place[0] == 0) & (place[1] == 0)
    stop = jnp.where(first, padded, padded + tokens)
    live = (column < tokens) | ((column >= padded) & (column < stop))
    for h in range(heads):
        cols = slice(h * HD, (h + 1) * HD)
        key = jnp.concatenate([own_ref[:, cols], back_ref[:, cols]], axis=0)
        vcols = slice(span + h * HD, span + (h + 1) * HD)
        value = jnp.concatenate([own_ref[:, vcols], back_ref[:, vcols]], axis=0)
        scores = dot(q_ref[:, cols], key, (1, 1)) * (HD ** (-0.5))
        scores = jnp.where(live, scores, -1e30)
        weights = jnp.exp(scores - jnp.max(scores, axis=1, keepdims=True))
        probs = (weights / jnp.sum(weights, axis=1, keepdims=True)).astype(bf16)
        out[:, cols] = dot(probs, value, (1, 0))


def assemble_body(heads, slots, out, squares):
    for h in range(heads):
        out[:, h * HD : (h + 1) * HD] = slots[h]
    fast = out[...].astype(f32)
    squares[...] = dot(jnp.ones((8, heads * HD), f32), fast * fast, (1, 1), highest)


def block_body(features, gain_ref, attended_ref, fast_ref, *refs):
    squares, out = refs[:-1], refs[-1]
    total = squares[0][...]
    for other in squares[1:]:
        total = total + other[...]
    pick = (lax.broadcasted_iota(jnp.int32, (8, HD), 0) == 0).astype(f32)
    spread = dot(total, pick, (0, 0), highest) * (1.0 / features)
    scale = lax.rsqrt(spread + epsilon)
    for h in range(fast_ref.shape[1] // HD):
        cols = slice(h * HD, (h + 1) * HD)
        out[:, cols] = (
            attended_ref[:, cols] + fast_ref[:, cols].astype(f32) * gain_ref[:, cols] * scale
        ).astype(bf16)


def on_device(queries, keys, values, rates, frame_update, fast_weights, gain):
    tokens = queries.shape[0]
    heads = queries.shape[1] // HD
    rows_local = fast_weights.shape[2]
    nz, group, nh = lax.axis_size("z"), lax.axis_size("grp"), lax.axis_size("head")
    count = nz * group
    hidden = count * rows_local
    place = jnp.stack([lax.axis_index("z"), lax.axis_index("grp")]).astype(jnp.int32)
    padded = -(-tokens // 16) * 16
    span = heads * HD

    def whole(*shape):
        return pl.BlockSpec(shape, lambda i: (0,) * len(shape))

    low_shape = (count, 3, rows_local, HD)
    prepared = pl.pallas_call(
        functools.partial(prep_body, heads, group, tokens),
        grid=(1,),
        out_shape=[sds(low_shape, bf16), sds((padded, 2 * span), bf16)]
        + [sds((padded, 3 * HD), bf16)] * group,
        in_specs=[smem, smem, whole(*fast_weights.shape)]
        + [whole(padded, span)] * 3
        + [whole(heads, -(-padded // 128) * 128)],
        out_specs=[whole(*low_shape), whole(padded, 2 * span)]
        + [whole(padded, 3 * HD)] * group,
        compiler_params=pltpu.CompilerParams(vmem_limit_bytes=VMEM_MOST),
    )(place, frame_update, fast_weights, keys, values, queries, rates.T)
    low, kv_own, token_slots = prepared[0], prepared[1], list(prepared[2:])

    weights = lax.all_to_all(low, ("z", "grp"), 0, 0, tiled=True)
    if rows_local % 16:
        weights = weights.transpose(1, 0, 2, 3).reshape(3, hidden, HD)
    for d in range(1, group):
        pairs = [(s, s ^ d) for s in range(group) if s ^ d < heads]
        token_slots[d] = lax.ppermute(token_slots[d], "grp", pairs)

    width = -(-group * padded // 128) * 128
    partials = list(
        call(
            functools.partial(grad_body, group, nz),
            [sds((hidden, HD), bf16)] * nz,
            scratch=[
                pltpu.VMEM((width, HD), bf16),
                pltpu.VMEM((width, HD), bf16),
                pltpu.VMEM((3, hidden, HD), bf16),
            ],
            in_specs=[smem] + [vmem] * (group + 1),
            flops=1e9,
        )(place, *token_slots, weights)
    )
    kv_own, weights, partials[0] = lax.optimization_barrier((kv_own, weights, partials[0]))
    for d in range(1, nz):
        pairs = []
        for z in range(nz):
            pairs += [
                (z * group + j, (z ^ d) * group + j)
                for j in range(heads)
                if ((z ^ d) - j) % nz < 3
            ]
        partials[d] = lax.ppermute(partials[d], ("z", "grp"), pairs)

    fast_slots = call(
        functools.partial(apply_body, group),
        sds((group, padded, HD), bf16),
        in_specs=[smem] + [vmem] * (group + 1),
        flops=5e8,
    )(place, *token_slots, weights)
    queries, fast_slots = lax.optimization_barrier((queries, fast_slots))
    fast_slots = lax.all_to_all(fast_slots, "grp", 0, 0, tiled=True)

    ring = [(i, i + 1) for i in range(count - 1)]
    kv_back = lax.ppermute(kv_own, ("z", "grp"), ring)
    attended = pl.pallas_call(
        functools.partial(attend_body, heads, tokens),
        grid=(1,),
        out_shape=sds((padded, span), f32),
        in_specs=[smem, whole(padded, span)] + [whole(padded, 2 * span)] * 2,
        out_specs=whole(padded, span),
        compiler_params=pltpu.CompilerParams(vmem_limit_bytes=VMEM_LIMIT),
    )(place, queries, kv_own, kv_back)
    attended, partials[0] = lax.optimization_barrier((attended, partials[0]))

    ortho = call(ortho_body, sds((hidden, HD), bf16), flops=1e9)(*partials)
    rows = lax.all_to_all(
        ortho.reshape(count, rows_local, HD), ("z", "grp"), 0, 0, tiled=True
    )
    new_weights = call(
        functools.partial(finish_body, nz, group), sds(fast_weights.shape, f32), flops=1e6
    )(fast_weights, rows)

    fast, squares = call(
        functools.partial(assemble_body, heads),
        [sds((padded, span), bf16), sds((8, padded), f32)],
        flops=1e7,
    )(fast_slots)
    all_squares = [squares] + [
        lax.ppermute(squares, "head", [(s, (s + d) % nh) for s in range(nh)]) for d in range(1, nh)
    ]
    block_out = pl.pallas_call(
        functools.partial(block_body, span * nh),
        grid=(1,),
        out_shape=sds((tokens, span), bf16),
        in_specs=[whole(1, span), whole(padded, span), whole(padded, span)]
        + [whole(8, padded)] * nh,
        out_specs=whole(padded, span),
        compiler_params=pltpu.CompilerParams(vmem_limit_bytes=VMEM_LIMIT),
    )(gain.reshape(1, span), attended, fast, *all_squares)
    return (block_out, new_weights)


def solution(mesh):
    group = 4
    nh = mesh.shape["head"]
    inner = Mesh(
        np.asarray(mesh.devices).reshape(mesh.shape["ctx"] // group, group, nh),
        ("z", "grp", "head"),
    )
    ctx = ("z", "grp")
    placed = (
        P(ctx, "head"),
        P(ctx, "head"),
        P(ctx, "head"),
        P(ctx, "head"),
        P(ctx),
        P(None, "head", ctx, None),
        P("head"),
    )
    return jax.shard_map(
        on_device,
        mesh=inner,
        in_specs=placed,
        out_specs=(P(ctx, "head"), P(None, "head", ctx, None)),
        check_vma=False,
    )
```

profile of v0, /device:TPU:0, one launch (start us, length us, event | category | flops | bytes accessed | tf_op | source)
XLA Modules:
  0.0 68.5 jit_solution(3923383288154629786)
XLA Ops:
  1.3 0.7 pad_add_fusion.place
  1.9 2.8 %shard_map.86 = (bf16[16,3,32,128]{3,2,1,0:T(8,128)(2,1)}, bf16[208,768]{1,0:T(8,128)(2,1)}, bf16[208,384]{1,0:T(8,128)(2,1)}, bf16[208,384]{1,0:T(8,128)(2,1)},...) custom-call(s32[2]{0:T(128)} %pad_add_fusion.place, s32[1]{0:T(128)S(6)} %copy.9.update, f32[3,3,32,128]{3,2,1,0:T(8,128)} %w_ref.3, ...), custom_call_target="tpu_custom_call" | custom-call | tf_op jit(solution)/shard_map/pallas_call | solution.py:221
  4.7 0.0 copy-start.8
  4.7 0.0 copy-start.7
  4.7 0.0 copy-start.6
  4.8 0.0 copy-start.4
  4.8 7.5 %all-to-all-start = ((bf16[16,3,32,128]{3,2,1,0:T(8,128)(2,1)}), bf16[16,3,32,128]{3,2,1,0:T(8,128)(2,1)S(1)}, u32[]{:S(2)}, u32[]{:S(2)}) async-start(bf16[16,3,32,128]{3,2,1,0:T(8,128)(2,1)} %get-tuple-element.26), calls=%async_computation | async-start | bytes 786432 | tf_op jit(solution)/shard_map/all_to_all | solution.py:235
  12.3 0.0 copy-done.8
  12.3 2.3 %collective-permute-start = (bf16[208,384]{1,0:T(8,128)(2,1)S(1)}, bf16[208,384]{1,0:T(8,128)(2,1)S(1)}, u32[]{:S(2)}, u32[]{:S(2)}) collective-permute-start(bf16[208,384]{1,0:T(8,128)(2,1)S(1)} %copy-done.8), channel_id=1, source_target_pairs={{0,2},{2,0},{6,4},{1,3},{3,1},{7,5},{8,10},{10,8},{14,12},{9,11},{... | collective-permute-start | bytes 479240 | tf_op jit(solution)/shard_map/ppermute | solution.py:240
  14.6 0.0 copy-done.7
  14.6 2.8 %collective-permute-start.1 = (bf16[208,384]{1,0:T(8,128)(2,1)S(1)}, bf16[208,384]{1,0:T(8,128)(2,1)S(1)}, u32[]{:S(2)}, u32[]{:S(2)}) collective-permute-start(bf16[208,384]{1,0:T(8,128)(2,1)S(1)} %copy-done.7), channel_id=1, source_target_pairs={{0,4},{4,0},{6,2},{1,5},{5,1},{7,3},{8,12},{12,8},{14,10},{9,13},{... | collective-permute-start | bytes 479240 | tf_op jit(solution)/shard_map/ppermute | solution.py:240
  17.4 0.0 copy-done.6
  17.4 0.0 copy-start.3
  17.5 1.3 %collective-permute-start.2 = (bf16[208,384]{1,0:T(8,128)(2,1)S(1)}, bf16[208,384]{1,0:T(8,128)(2,1)S(1)}, u32[]{:S(2)}, u32[]{:S(2)}) collective-permute-start(bf16[208,384]{1,0:T(8,128)(2,1)S(1)} %copy-done.6), channel_id=1, source_target_pairs={{2,4},{4,2},{6,0},{3,5},{5,3},{7,1},{10,12},{12,10},{14,8},{11,13}... | collective-permute-start | bytes 479240 | tf_op jit(solution)/shard_map/ppermute | solution.py:240
  18.8 0.0 collective-permute-done.refs_1_
  18.8 6.3 %collective-permute-done.1.refs_2_ = bf16[208,384]{1,0:T(8,128)(2,1)S(1)} collective-permute-done((bf16[208,384]{1,0:T(8,128)(2,1)S(1)}, bf16[208,384]{1,0:T(8,128)(2,1)S(1)}, u32[]{:S(2)}, u32[]{:S(2)}) %collective-permute-start.1) | collective-permute-done | bytes 159776 | tf_op jit(solution)/shard_map/ppermute | solution.py:240
  25.1 2.2 %collective-permute-done.2.refs_3_ = bf16[208,384]{1,0:T(8,128)(2,1)S(1)} collective-permute-done((bf16[208,384]{1,0:T(8,128)(2,1)S(1)}, bf16[208,384]{1,0:T(8,128)(2,1)S(1)}, u32[]{:S(2)}, u32[]{:S(2)}) %collective-permute-start.2) | collective-permute-done | bytes 159776 | tf_op jit(solution)/shard_map/ppermute | solution.py:240
  27.3 0.0 all-to-all-done.refs_4_
  27.3 0.0 copy-done.4
  27.3 0.0 copy-done.3
  27.3 0.0 copy-start.2
  27.3 3.1 %shard_map.87 = (bf16[512,128]{1,0:T(8,128)(2,1)S(1)}, bf16[512,128]{1,0:T(8,128)(2,1)S(1)}, bf16[512,128]{1,0:T(8,128)(2,1)S(1)}, bf16[512,128]{1,0:T(8,128)(2,1)S(1)}) custom-call(s32[2]{0:T(128)S(1)} %copy-done.3, bf16[208,384]{1,0:T(8,128)(2,1)S(1)} %copy-done.4, bf16[208,384]{1,0:T(8,128)(2,1)S(1)} %collective-permute-done.refs_1_, ...), custom_call_target="tpu_custom_call" | custom-call | flops 1000000000 | bytes 1048576 | tf_op jit(solution)/shard_map/pallas_call | solution.py:244
  30.4 0.0 copy-done.2
  30.4 2.4 %collective-permute-start.3 = (bf16[208,768]{1,0:T(8,128)(2,1)S(1)}, bf16[208,768]{1,0:T(8,128)(2,1)S(1)}, u32[]{:S(2)}, u32[]{:S(2)}) collective-permute-start(bf16[208,768]{1,0:T(8,128)(2,1)S(1)} %copy-done.2), channel_id=1, source_target_pairs={{0,2},{2,4},{4,6},{6,8},{8,10},{10,12},{12,14},{14,16},{16,18},{18... | collective-permute-start | bytes 958472 | tf_op jit(solution)/shard_map/ppermute | solution.py:277
  32.8 3.8 %collective-permute-start.5 = (bf16[512,128]{1,0:T(8,128)(2,1)S(1)}, bf16[512,128]{1,0:T(8,128)(2,1)S(1)}, u32[]{:S(2)}, u32[]{:S(2)}) collective-permute-start(bf16[512,128]{1,0:T(8,128)(2,1)S(1)} %get-tuple-element.37), channel_id=1, source_target_pairs={{0,8},{2,10},{8,0},{12,4},{18,26},{20,28},{24,16},{26,18},{28,20},... | collective-permute-start | bytes 393224 | tf_op jit(solution)/shard_map/ppermute | solution.py:265
  36.6 2.1 %collective-permute-start.6 = (bf16[512,128]{1,0:T(8,128)(2,1)S(1)}, bf16[512,128]{1,0:T(8,128)(2,1)S(1)}, u32[]{:S(2)}, u32[]{:S(2)}) collective-permute-start(bf16[512,128]{1,0:T(8,128)(2,1)S(1)} %get-tuple-element.38), channel_id=1, source_target_pairs={{0,16},{2,18},{4,20},{10,26},{12,28},{16,0},{20,4},{24,8},{26,10},... | collective-permute-start | bytes 393224 | tf_op jit(solution)/shard_map/ppermute | solution.py:265
  38.6 1.3 %collective-permute-start.7 = (bf16[512,128]{1,0:T(8,128)(2,1)S(1)}, bf16[512,128]{1,0:T(8,128)(2,1)S(1)}, u32[]{:S(2)}, u32[]{:S(2)}) collective-permute-start(bf16[512,128]{1,0:T(8,128)(2,1)S(1)} %get-tuple-element.39), channel_id=1, source_target_pairs={{2,26},{4,28},{8,16},{10,18},{12,20},{16,8},{18,10},{24,0},{28,4},... | collective-permute-start | bytes 393224 | tf_op jit(solution)/shard_map/ppermute | solution.py:265
  39.9 2.4 %shard_map.88 = bf16[4,208,128]{2,1,0:T(8,128)(2,1)} custom-call(s32[2]{0:T(128)S(1)} %copy-done.3, bf16[208,384]{1,0:T(8,128)(2,1)S(1)} %copy-done.4, bf16[208,384]{1,0:T(8,128)(2,1)S(1)} %collective-permute-done.refs_1_, bf16[208,384]{1,0:T(8,128)(2,1)S(1)} %collective-permute-done.1.refs_2_, bf16[208,384]{1,0:T(8,128)(2,1)S(1)} %collective-permute-done.2.refs_3_, ...), custom_call_target="tpu_custom_call" | custom-call | flops 500000000 | bytes 1048576 | tf_op jit(solution)/shard_map/pallas_call | solution.py:267
  42.3 3.6 %all-to-all-start.1 = ((bf16[4,208,128]{2,1,0:T(8,128)(2,1)}), bf16[4,208,128]{2,1,0:T(8,128)(2,1)S(1)}, u32[]{:S(2)}, u32[]{:S(2)}) async-start(bf16[4,208,128]{2,1,0:T(8,128)(2,1)} %shard_map.88), calls=%async_computation.1 | async-start | bytes 425984 | tf_op jit(solution)/shard_map/all_to_all | solution.py:274
  45.9 0.0 collective-permute-done.3.back_ref
  45.9 0.0 copy-done
  45.9 1.9 %shard_map.89.attended_ref = f32[208,384]{1,0:T(8,128)S(1)} custom-call(s32[2]{0:T(128)S(1)} %copy-done.3, bf16[195,384]{1,0:T(8,128)(2,1)S(1)} %copy-done, bf16[208,768]{1,0:T(8,128)(2,1)S(1)} %copy-done.2, bf16[208,768]{1,0:T(8,128)(2,1)S(1)} %collective-permute-done.3.back_ref), custom_call_target="tpu_custom_call" | custom-call | tf_op jit(solution)/shard_map/pallas_call | solution.py:278
  47.8 0.0 collective-permute-done.5.refs_1_
  47.8 1.2 %collective-permute-done.6.refs_2_ = bf16[512,128]{1,0:T(8,128)(2,1)S(1)} collective-permute-done((bf16[512,128]{1,0:T(8,128)(2,1)S(1)}, bf16[512,128]{1,0:T(8,128)(2,1)S(1)}, u32[]{:S(2)}, u32[]{:S(2)}) %collective-permute-start.6) | collective-permute-done | bytes 131104 | tf_op jit(solution)/shard_map/ppermute | solution.py:265
  49.0 0.0 collective-permute-done.7.refs_3_
  49.0 4.7 %shard_map.92 = bf16[512,128]{1,0:T(8,128)(2,1)} custom-call(bf16[512,128]{1,0:T(8,128)(2,1)S(1)} %get-tuple-element.36.refs_0_, bf16[512,128]{1,0:T(8,128)(2,1)S(1)} %collective-permute-done.5.refs_1_, bf16[512,128]{1,0:T(8,128)(2,1)S(1)} %collective-permute-done.6.refs_2_, bf16[512,128]{1,0:T(8,128)(2,1)S(1)} %collective-permute-done.7.refs_3_), custom_call_target="tpu_custom_call" | custom-call | flops 1000000000 | bytes 1048576 | tf_op jit(solution)/shard_map/pallas_call | solution.py:288
  53.7 0.0 all-to-all-done.1.slots
  53.7 6.0 %all-to-all-start.2 = ((bf16[16,32,128]{2,1,0:T(8,128)(2,1)}), bf16[16,32,128]{2,1,0:T(8,128)(2,1)S(1)}, u32[]{:S(2)}, u32[]{:S(2)}) async-start(bf16[16,32,128]{2,1,0:T(8,128)(2,1)} %bitcast.3), calls=%async_computation.2 | async-start | bytes 262144 | tf_op jit(solution)/shard_map/all_to_all | solution.py:289
  59.7 0.0 copy-start.5
  59.7 0.4 shard_map.90
  60.2 1.6 %collective-permute-start.4 = (f32[8,208]{1,0:T(8,128)S(1)}, f32[8,208]{1,0:T(8,128)S(1)}, u32[]{:S(2)}, u32[]{:S(2)}) collective-permute-start(f32[8,208]{1,0:T(8,128)S(1)} %get-tuple-element.35.refs_0_), channel_id=1, source_target_pairs={{0,1},{1,0},{2,3},{3,2},{4,5},{5,4},{6,7},{7,6},{8,9},{9,8},{10,11... | collective-permute-start | bytes 19976 | tf_op jit(solution)/shard_map/ppermute | solution.py:302
  61.7 0.0 copy-done.5
  61.7 2.1 %collective-permute-done.4.refs_1_ = f32[8,208]{1,0:T(8,128)S(1)} collective-permute-done((f32[8,208]{1,0:T(8,128)S(1)}, f32[8,208]{1,0:T(8,128)S(1)}, u32[]{:S(2)}, u32[]{:S(2)}) %collective-permute-start.4) | collective-permute-done | bytes 6688 | tf_op jit(solution)/shard_map/ppermute | solution.py:302
  63.8 0.0 copy-start.1
  63.8 1.0 %shard_map.91 = bf16[195,384]{1,0:T(8,128)(2,1)} custom-call(f32[1,384]{1,0:T(1,128)S(1)} %reshape.10.gain_ref, f32[208,384]{1,0:T(8,128)S(1)} %shard_map.89.attended_ref, bf16[208,384]{1,0:T(8,128)(2,1)S(1)} %get-tuple-element.34.fast_ref, f32[8,208]{1,0:T(8,128)S(1)} %get-tuple-element.35.refs_0_, f32[8,208]{1,0:T(8,128)S(1)} %collective-permute-done.4.refs_1_), custom_call_target="tpu_custom_call" | custom-call | tf_op jit(solution)/shard_map/pallas_call | solution.py:304
  64.8 2.8 %all-to-all-done.2.rows_ref = bf16[16,32,128]{2,1,0:T(8,128)(2,1)S(1)} async-done(((bf16[16,32,128]{2,1,0:T(8,128)(2,1)}), bf16[16,32,128]{2,1,0:T(8,128)(2,1)S(1)}, u32[]{:S(2)}, u32[]{:S(2)}) %all-to-all-start.2) | async-done | bytes 131104 | tf_op jit(solution)/shard_map/all_to_all | solution.py:289
  67.6 0.0 copy-done.1
  67.7 0.8 %shard_map.93 = f32[3,3,32,128]{3,2,1,0:T(8,128)} custom-call(f32[3,3,32,128]{3,2,1,0:T(8,128)S(1)} %copy-done.1, bf16[16,32,128]{2,1,0:T(8,128)(2,1)S(1)} %all-to-all-done.2.rows_ref), custom_call_target="tpu_custom_call" | custom-call | flops 1000000 | bytes 1048576 | tf_op jit(solution)/shard_map/pallas_call | solution.py:292
  (2 shorter events, 0.0 us)
Async XLA Ops:
  4.7 7.5 %copy-start.8 = (bf16[208,384]{1,0:T(8,128)(2,1)S(1)}, bf16[208,384]{1,0:T(8,128)(2,1)}, u32[]{:S(2)}) copy-start(bf16[208,384]{1,0:T(8,128)(2,1)} %get-tuple-element.22) | copy-start | bytes 479236
  4.7 9.9 %copy-start.7 = (bf16[208,384]{1,0:T(8,128)(2,1)S(1)}, bf16[208,384]{1,0:T(8,128)(2,1)}, u32[]{:S(2)}) copy-start(bf16[208,384]{1,0:T(8,128)(2,1)} %get-tuple-element.23) | copy-start | bytes 479236
  4.7 12.7 %copy-start.6 = (bf16[208,384]{1,0:T(8,128)(2,1)S(1)}, bf16[208,384]{1,0:T(8,128)(2,1)}, u32[]{:S(2)}) copy-start(bf16[208,384]{1,0:T(8,128)(2,1)} %get-tuple-element.24) | copy-start | bytes 479236
  4.8 22.5 %copy-start.4 = (bf16[208,384]{1,0:T(8,128)(2,1)S(1)}, bf16[208,384]{1,0:T(8,128)(2,1)}, u32[]{:S(2)}) copy-start(bf16[208,384]{1,0:T(8,128)(2,1)} %get-tuple-element.21.refs_0_) | copy-start | bytes 479236
  4.8 22.5 %all-to-all-start = ((bf16[16,3,32,128]{3,2,1,0:T(8,128)(2,1)}), bf16[16,3,32,128]{3,2,1,0:T(8,128)(2,1)S(1)}, u32[]{:S(2)}, u32[]{:S(2)}) async-start(bf16[16,3,32,128]{3,2,1,0:T(8,128)(2,1)} %get-tuple-element.26), calls=%async_computation | async-start | bytes 786432 | tf_op jit(solution)/shard_map/all_to_all | solution.py:235
  12.3 6.5 %collective-permute-start = (bf16[208,384]{1,0:T(8,128)(2,1)S(1)}, bf16[208,384]{1,0:T(8,128)(2,1)S(1)}, u32[]{:S(2)}, u32[]{:S(2)}) collective-permute-start(bf16[208,384]{1,0:T(8,128)(2,1)S(1)} %copy-done.8), channel_id=1, source_target_pairs={{0,2},{2,0},{6,4},{1,3},{3,1},{7,5},{8,10},{10,8},{14,12},{9,11},{... | collective-permute-start | bytes 479240 | tf_op jit(solution)/shard_map/ppermute | solution.py:240
  14.6 10.4 %collective-permute-start.1 = (bf16[208,384]{1,0:T(8,128)(2,1)S(1)}, bf16[208,384]{1,0:T(8,128)(2,1)S(1)}, u32[]{:S(2)}, u32[]{:S(2)}) collective-permute-start(bf16[208,384]{1,0:T(8,128)(2,1)S(1)} %copy-done.7), channel_id=1, source_target_pairs={{0,4},{4,0},{6,2},{1,5},{5,1},{7,3},{8,12},{12,8},{14,10},{9,13},{... | collective-permute-start | bytes 479240 | tf_op jit(solution)/shard_map/ppermute | solution.py:240
  17.4 9.8 %copy-start.3 = (s32[2]{0:T(128)S(1)}, s32[2]{0:T(128)}, u32[]{:S(2)}) copy-start(s32[2]{0:T(128)} %pad_add_fusion.place) | copy-start | bytes 28
  17.5 9.8 %collective-permute-start.2 = (bf16[208,384]{1,0:T(8,128)(2,1)S(1)}, bf16[208,384]{1,0:T(8,128)(2,1)S(1)}, u32[]{:S(2)}, u32[]{:S(2)}) collective-permute-start(bf16[208,384]{1,0:T(8,128)(2,1)S(1)} %copy-done.6), channel_id=1, source_target_pairs={{2,4},{4,2},{6,0},{3,5},{5,3},{7,1},{10,12},{12,10},{14,8},{11,13}... | collective-permute-start | bytes 479240 | tf_op jit(solution)/shard_map/ppermute | solution.py:240
  27.3 3.1 %copy-start.2 = (bf16[208,768]{1,0:T(8,128)(2,1)S(1)}, bf16[208,768]{1,0:T(8,128)(2,1)}, u32[]{:S(2)}) copy-start(bf16[208,768]{1,0:T(8,128)(2,1)} %get-tuple-element.30.own_ref) | copy-start | bytes 958468
  30.4 15.5 %collective-permute-start.3 = (bf16[208,768]{1,0:T(8,128)(2,1)S(1)}, bf16[208,768]{1,0:T(8,128)(2,1)S(1)}, u32[]{:S(2)}, u32[]{:S(2)}) collective-permute-start(bf16[208,768]{1,0:T(8,128)(2,1)S(1)} %copy-done.2), channel_id=1, source_target_pairs={{0,2},{2,4},{4,6},{6,8},{8,10},{10,12},{12,14},{14,16},{16,18},{18... | collective-permute-start | bytes 958472 | tf_op jit(solution)/shard_map/ppermute | solution.py:277
  32.8 15.0 %collective-permute-start.5 = (bf16[512,128]{1,0:T(8,128)(2,1)S(1)}, bf16[512,128]{1,0:T(8,128)(2,1)S(1)}, u32[]{:S(2)}, u32[]{:S(2)}) collective-permute-start(bf16[512,128]{1,0:T(8,128)(2,1)S(1)} %get-tuple-element.37), channel_id=1, source_target_pairs={{0,8},{2,10},{8,0},{12,4},{18,26},{20,28},{24,16},{26,18},{28,20},... | collective-permute-start | bytes 393224 | tf_op jit(solution)/shard_map/ppermute | solution.py:265
  36.6 12.4 %collective-permute-start.6 = (bf16[512,128]{1,0:T(8,128)(2,1)S(1)}, bf16[512,128]{1,0:T(8,128)(2,1)S(1)}, u32[]{:S(2)}, u32[]{:S(2)}) collective-permute-start(bf16[512,128]{1,0:T(8,128)(2,1)S(1)} %get-tuple-element.38), channel_id=1, source_target_pairs={{0,16},{2,18},{4,20},{10,26},{12,28},{16,0},{20,4},{24,8},{26,10},... | collective-permute-start | bytes 393224 | tf_op jit(solution)/shard_map/ppermute | solution.py:265
  38.6 10.3 %collective-permute-start.7 = (bf16[512,128]{1,0:T(8,128)(2,1)S(1)}, bf16[512,128]{1,0:T(8,128)(2,1)S(1)}, u32[]{:S(2)}, u32[]{:S(2)}) collective-permute-start(bf16[512,128]{1,0:T(8,128)(2,1)S(1)} %get-tuple-element.39), channel_id=1, source_target_pairs={{2,26},{4,28},{8,16},{10,18},{12,20},{16,8},{18,10},{24,0},{28,4},... | collective-permute-start | bytes 393224 | tf_op jit(solution)/shard_map/ppermute | solution.py:265
  42.3 3.6 %copy-start = (bf16[195,384]{1,0:T(8,128)(2,1)S(1)}, bf16[195,384]{1,0:T(8,128)(2,1)}, u32[]{:S(2)}) copy-start(bf16[195,384]{1,0:T(8,128)(2,1)} %q_ref.2) | copy-start | bytes 449284
  42.3 11.3 %all-to-all-start.1 = ((bf16[4,208,128]{2,1,0:T(8,128)(2,1)}), bf16[4,208,128]{2,1,0:T(8,128)(2,1)S(1)}, u32[]{:S(2)}, u32[]{:S(2)}) async-start(bf16[4,208,128]{2,1,0:T(8,128)(2,1)} %shard_map.88), calls=%async_computation.1 | async-start | bytes 425984 | tf_op jit(solution)/shard_map/all_to_all | solution.py:274
  53.7 14.0 %all-to-all-start.2 = ((bf16[16,32,128]{2,1,0:T(8,128)(2,1)}), bf16[16,32,128]{2,1,0:T(8,128)(2,1)S(1)}, u32[]{:S(2)}, u32[]{:S(2)}) async-start(bf16[16,32,128]{2,1,0:T(8,128)(2,1)} %bitcast.3), calls=%async_computation.2 | async-start | bytes 262144 | tf_op jit(solution)/shard_map/all_to_all | solution.py:289
  59.7 2.0 %copy-start.5 = (f32[384]{0:T(512)S(1)}, f32[384]{0:T(512)}, u32[]{:S(2)}) copy-start(f32[384]{0:T(512)} %param.13) | copy-start | bytes 4612
  60.2 3.7 %collective-permute-start.4 = (f32[8,208]{1,0:T(8,128)S(1)}, f32[8,208]{1,0:T(8,128)S(1)}, u32[]{:S(2)}, u32[]{:S(2)}) collective-permute-start(f32[8,208]{1,0:T(8,128)S(1)} %get-tuple-element.35.refs_0_), channel_id=1, source_target_pairs={{0,1},{1,0},{2,3},{3,2},{4,5},{5,4},{6,7},{7,6},{8,9},{9,8},{10,11... | collective-permute-start | bytes 19976 | tf_op jit(solution)/shard_map/ppermute | solution.py:302
  63.8 3.8 %copy-start.1 = (f32[3,3,32,128]{3,2,1,0:T(8,128)S(1)}, f32[3,3,32,128]{3,2,1,0:T(8,128)}, u32[]{:S(2)}) copy-start(f32[3,3,32,128]{3,2,1,0:T(8,128)} %w_ref.3) | copy-start | bytes 442372
where the time goes:
time: 69.1 us; the launch traced here: 68.5 us
  starting transfers between devices  34.6 us (50%)
  Pallas kernels  17.1 us (25%)
  waiting for transfers between devices  14.6 us (21%)
  between operations  1.46 us (2%)
    ppermute x3, waiting for transfers between devices, on_device(): token_slots[d] = lax.ppermute(token_slots[d], 'grp', pairs)  8.49 us
    all_to_all x1, starting transfers between devices, on_device(): weights = lax.all_to_all(low, ('z', 'grp'), 0, 0, tiled=True)  7.5 us
    ppermute x3, starting transfers between devices, on_device(): partials[d] = lax.ppermute(partials[d], ('z', 'grp'), pairs)  7.1 us
    ppermute x3, starting transfers between devices, on_device(): token_slots[d] = lax.ppermute(token_slots[d], 'grp', pairs)  6.41 us
    all_to_all x1, starting transfers between devices, on_device(): lax.all_to_all(ortho.reshape(count, rows_local, HD), ('z', 'grp'), 0, 0,...  6.05 us
    pallas_call x1, Pallas kernels, on_device(): call(ortho_body, sds((hidden, HD), bf16), flops=1000000000.0)(*partials)  4.68 us
    all_to_all x1, starting transfers between devices, on_device(): fast_slots = lax.all_to_all(fast_slots, 'grp', 0, 0, tiled=True)  3.57 us
    pallas_call x1, Pallas kernels, on_device(): call(functools.partial(grad_body, group, nz), [sds((hidden, HD), bf16)] *...  3.11 us
  transfers between devices with their start and end apart: 11, of which 5 were waited for; matrix products, arithmetic and copies ran while one was open for 0% of the time, Pallas kernels for 15%

commit v1 on v0

v1 whole, which is shorter than its diff:
```python
import functools

import jax
import jax.numpy as jnp
import numpy as np
from jax import lax
from jax.experimental import pallas as pl
from jax.experimental.pallas import tpu as pltpu
from jax.sharding import Mesh, PartitionSpec as P

HD = 128
NS_STEPS = 5

epsilon = 1e-06
quintic_a = 3.4445
quintic_b = -4.775
quintic_c = 2.0315
highest = lax.Precision.HIGHEST
f32 = jnp.float32
bf16 = jnp.bfloat16
VMEM_LIMIT = 24 * 1024 * 1024
VMEM_MOST = 56 * 1024 * 1024


def dot(a, b, contract, precision=None):
    return lax.dot_general(
        a, b, ((contract[:1], contract[1:]), ((), ())),
        precision=precision, preferred_element_type=f32,
    )


def call(body, outs, scratch=(), in_specs=None, flops=1e8, moved=1 << 20, **kw):
    given = {} if in_specs is None else {"in_specs": in_specs}
    return pl.pallas_call(
        body,
        out_shape=outs,
        **given,
        scratch_shapes=list(scratch),
        compiler_params=pltpu.CompilerParams(vmem_limit_bytes=VMEM_LIMIT),
        cost_estimate=pl.CostEstimate(flops=int(flops), bytes_accessed=moved, transcendentals=0),
        **kw,
    )


def sds(shape, dtype):
    return jax.ShapeDtypeStruct(shape, dtype)


def served(n):
    return [0] + list(range(n - 1, 0, -1))


def position():
    return lax.axis_index("z"), lax.axis_index("grp")


def sigmoid(x):
    return 0.5 * jnp.tanh(0.5 * x) + 0.5


def prep_body(heads, group, tokens, update, w_ref, k_ref, v_ref, q_ref, rate_ref, *outs):
    w_out, kv_out = outs[:2]
    token_outs = outs[2:]
    padded = kv_out.shape[0]
    slots = w_out.shape[0] // group
    for j in range(group):
        for m in range(3):
            low = w_ref[m, min(j, heads - 1)].astype(bf16)
            for z in range(slots):
                w_out[z * group + j, m] = low
    place = position()
    valid = lax.broadcasted_iota(jnp.int32, (padded, 1), 0) < tokens
    none = jnp.zeros((), bf16)
    keep = update[...].astype(f32)
    row = lax.broadcasted_iota(jnp.int32, (heads, HD), 0)
    for d in range(group):
        head = jnp.minimum(place[1] ^ d, heads - 1)
        cols = pl.ds(pl.multiple_of(head * HD, HD), HD)
        rate = dot(rate_ref[...], (row == head).astype(f32), (0, 0), highest)[:padded]
        target = ((rate * keep) * v_ref[:, cols].astype(f32)).astype(bf16)
        token_outs[d][:, :HD] = jnp.where(valid, k_ref[:, cols], none)
        token_outs[d][:, HD : 2 * HD] = jnp.where(valid, target, none)
        token_outs[d][:, 2 * HD :] = jnp.where(valid, q_ref[:, cols], none)
    kv_out[:, : heads * HD] = jnp.where(valid, k_ref[...], none)
    kv_out[:, heads * HD :] = jnp.where(valid, v_ref[...], none)


def gradients(token_refs, w_ref, k_all, t_all, staged, deltas):
    padded = token_refs[0].shape[0]
    width = k_all.shape[0]
    filled = len(token_refs) * padded
    for i, ref in enumerate(token_refs):
        k_all[i * padded : (i + 1) * padded] = ref[:, :HD]
        t_all[i * padded : (i + 1) * padded] = ref[:, HD : 2 * HD]
    if width > filled:
        k_all[filled:] = jnp.zeros((width - filled, HD), bf16)
        t_all[filled:] = jnp.zeros((width - filled, HD), bf16)
    hidden = deltas.shape[1]
    w1, w3, w2 = (weight_rows(w_ref, m, 0, hidden) for m in range(3))
    tall = 64
    for left in range(0, width, staged.shape[3]):
        right = min(left + staged.shape[3], width)
        cols, used = slice(left, right), slice(0, right - left)
        stage = staged.at[(left // staged.shape[3]) % staged.shape[0]]
        stage[0, :, used] = dot(w1, k_all[cols], (1, 1))
        stage[1, :, used] = dot(w3, k_all[cols], (1, 1))
        stage[2, :, used] = dot(w2, t_all[cols], (1, 1))
        for start in range(0, hidden, tall):
            rows = slice(start, start + tall)
            pre_one, pre_three, back = (stage[i, rows, used] for i in range(3))
            sig = sigmoid(pre_one)
            gate = pre_one * sig
            deltas[2, rows, cols] = (gate * pre_three).astype(bf16)
            deltas[1, rows, cols] = (back * gate).astype(bf16)
            deltas[0, rows, cols] = (
                (back * pre_three) * (sig * (1.0 + pre_one * (1.0 - sig)))
            ).astype(bf16)
    return (
        dot(deltas[0], k_all[...], (1, 0)),
        dot(deltas[1], k_all[...], (1, 0)),
        dot(deltas[2], t_all[...], (1, 0)),
    )


def gradient_scratch(slots, padded, hidden):
    width = -(-slots * padded // 128) * 128
    return [
        pltpu.VMEM((width, HD), bf16),
        pltpu.VMEM((width, HD), bf16),
        pltpu.VMEM((2, 3, hidden, 256), f32),
        pltpu.VMEM((3, hidden, width), bf16),
    ]


def apply_tokens(token_ref, w_ref, stage, act):
    hidden = act.shape[1]
    tall = 16
    w1, w3, w2 = (weight_rows(w_ref, m, 0, hidden) for m in range(3))
    query = token_ref[:, 2 * HD :]
    stage[0] = dot(query, w1, (1, 1))
    stage[1] = dot(query, w3, (1, 1))
    for start in range(0, query.shape[0], tall):
        rows = slice(start, start + tall)
        proj = stage[0, rows]
        act[rows] = (proj * sigmoid(proj) * stage[1, rows]).astype(bf16)
    return dot(act[...], w2, (1, 0)).astype(bf16)


def apply_scratch(padded, hidden):
    return [pltpu.VMEM((2, 2, padded, hidden), f32), pltpu.VMEM((2, padded, hidden), bf16)]


def early_body(count, *refs):
    token_refs, w_ref = refs[:count], refs[count]
    grads, fast = refs[count + 1 : count + 3]
    scratch, (staged, acts) = refs[count + 3 : -2], refs[-2:]
    for m, grad in enumerate(gradients(token_refs, w_ref, *scratch)):
        grads[m] = grad
    for i, ref in enumerate(token_refs):
        fast[i] = apply_tokens(ref, w_ref, staged.at[i % 2], acts.at[i % 2])


def late_body(group, slots, token_ref, w_ref, early, *refs):
    place = position()
    outs, sums, scratch = refs[:slots], refs[slots], refs[slots + 1 :]
    for m, grad in enumerate(gradients([token_ref], w_ref, *scratch)):
        sums[m] = (early[m] + grad).astype(bf16)
    for d in range(slots):
        matrix = lax.rem((place[0] ^ d) - place[1] + group * slots, slots)
        chosen = sums[jnp.minimum(matrix, 2)]
        outs[d][...] = jnp.where(matrix < 3, chosen, jnp.zeros_like(chosen))


def late_apply_body(early_slots, last, token_ref, w_ref, early, out, staged, acts):
    place = position()
    for i, d in enumerate(early_slots):
        out[place[1] ^ d] = early[i]
    out[place[1] ^ last] = apply_tokens(token_ref, w_ref, staged.at[0], acts.at[0])


def weight_rows(w_ref, m, start, block):
    if len(w_ref.shape) == 3:
        return w_ref[m, start : start + block]
    rows = w_ref.shape[2]
    return w_ref[start // rows : (start + block) // rows, m].reshape(block, HD)


def parts_of(x):
    high = x.astype(bf16)
    return high, (x - high.astype(f32)).astype(bf16)


def left_of(x):
    high, low = parts_of(x)
    return jnp.concatenate([high, high, low], axis=1)


def right_of(x):
    high, low = parts_of(x)
    return jnp.concatenate([high, low, high], axis=0)


def ortho_body(*refs):
    parts, out = refs[:-1], refs[-1]
    grads = parts[0][...].astype(f32)
    for part in parts[1:]:
        grads = grads + part[...].astype(f32)
    eye = (
        lax.broadcasted_iota(jnp.int32, (HD, HD), 0) == lax.broadcasted_iota(jnp.int32, (HD, HD), 1)
    ).astype(f32)
    raw = dot(grads, grads, (0, 0), highest)
    square = jnp.sum(jnp.sum(raw * eye, axis=0, keepdims=True), axis=1, keepdims=True)
    scale = lax.rsqrt(square + epsilon)
    gram = raw * scale * scale
    total = None
    for step in range(NS_STEPS):
        square_gram = dot(left_of(gram), right_of(gram), (1, 0))
        mix = quintic_a * eye + quintic_b * gram + quintic_c * square_gram
        right = right_of(mix)
        if step < NS_STEPS - 1:
            gram = dot(left_of(dot(left_of(gram), right, (1, 0))), right, (1, 0))
        total = mix if total is None else dot(left_of(total), right, (1, 0))
    out[...] = dot(left_of(grads * scale), right_of(total), (1, 0)).astype(out.dtype)


def finish_body(slots, group, w_ref, rows_ref, out):
    heads = w_ref.shape[1]
    for m in range(3):
        for h in range(heads):
            weights = w_ref[m, h]
            summed = weights + rows_ref[((m + h) % slots) * group + h].astype(f32)
            old = jnp.sqrt(jnp.sum(weights * weights, axis=1, keepdims=True))
            new = lax.rsqrt(jnp.sum(summed * summed, axis=1, keepdims=True) + epsilon)
            out[m, h] = summed * (old * new)


def attend_body(heads, tokens, q_ref, own_ref, back_ref, out):
    padded = own_ref.shape[0]
    span = heads * HD
    column = lax.broadcasted_iota(jnp.int32, (1, 2 * padded), 1)
    place = position()
    first = (place[0] == 0) & (place[1] == 0)
    stop = jnp.where(first, padded, padded + tokens)
    live = (column < tokens) | ((column >= padded) & (column < stop))
    for h in range(heads):
        cols = slice(h * HD, (h + 1) * HD)
        key = jnp.concatenate([own_ref[:, cols], back_ref[:, cols]], axis=0)
        vcols = slice(span + h * HD, span + (h + 1) * HD)
        value = jnp.concatenate([own_ref[:, vcols], back_ref[:, vcols]], axis=0)
        scores = dot(q_ref[:, cols], key, (1, 1)) * (HD ** (-0.5))
        scores = jnp.where(live, scores, -1e30)
        weights = jnp.exp(scores - jnp.max(scores, axis=1, keepdims=True))
        probs = (weights / jnp.sum(weights, axis=1, keepdims=True)).astype(bf16)
        out[:, cols] = dot(probs, value, (1, 0))


def assemble_body(heads, slots, out, squares):
    for h in range(heads):
        out[:, h * HD : (h + 1) * HD] = slots[h]
    fast = out[...].astype(f32)
    squares[...] = dot(jnp.ones((8, heads * HD), f32), fast * fast, (1, 1), highest)


def block_body(features, gain_ref, attended_ref, fast_ref, *refs):
    squares, out = refs[:-1], refs[-1]
    total = squares[0][...]
    for other in squares[1:]:
        total = total + other[...]
    pick = (lax.broadcasted_iota(jnp.int32, (8, HD), 0) == 0).astype(f32)
    spread = dot(total, pick, (0, 0), highest) * (1.0 / features)
    scale = lax.rsqrt(spread + epsilon)
    for h in range(fast_ref.shape[1] // HD):
        cols = slice(h * HD, (h + 1) * HD)
        out[:, cols] = (
            attended_ref[:, cols] + fast_ref[:, cols].astype(f32) * gain_ref[:, cols] * scale
        ).astype(bf16)


def on_device(queries, keys, values, rates, frame_update, fast_weights, gain):
    tokens = queries.shape[0]
    heads = queries.shape[1] // HD
    rows_local = fast_weights.shape[2]
    nz, group, nh = lax.axis_size("z"), lax.axis_size("grp"), lax.axis_size("head")
    count = nz * group
    hidden = count * rows_local
    padded = -(-tokens // 16) * 16
    span = heads * HD

    def whole(*shape):
        return pl.BlockSpec(shape, lambda i: (0,) * len(shape))

    low_shape = (count, 3, rows_local, HD)
    prepared = pl.pallas_call(
        functools.partial(prep_body, heads, group, tokens),
        grid=(1,),
        out_shape=[sds(low_shape, bf16), sds((padded, 2 * span), bf16)]
        + [sds((padded, 3 * HD), bf16)] * group,
        in_specs=[whole(1, 1), whole(*fast_weights.shape)]
        + [whole(padded, span)] * 3
        + [whole(heads, -(-padded // 128) * 128)],
        out_specs=[whole(*low_shape), whole(padded, 2 * span)]
        + [whole(padded, 3 * HD)] * group,
        compiler_params=pltpu.CompilerParams(vmem_limit_bytes=VMEM_MOST),
    )(frame_update.reshape(1, 1), fast_weights, keys, values, queries, rates.T)
    low, kv_own, token_slots = prepared[0], prepared[1], list(prepared[2:])

    weights = lax.all_to_all(low, ("z", "grp"), 0, 0, tiled=True)
    if rows_local % 16:
        weights = weights.transpose(1, 0, 2, 3).reshape(3, hidden, HD)
    for d in served(group)[1:]:
        pairs = [(s, s ^ d) for s in range(group) if s ^ d < heads]
        token_slots[d] = lax.ppermute(token_slots[d], "grp", pairs)

    last = group // 2
    early_slots = [d for d in served(group) if d != last]
    early_grads, early_fast = call(
        functools.partial(early_body, len(early_slots)),
        [sds((3, hidden, HD), f32), sds((len(early_slots), padded, HD), bf16)],
        scratch=gradient_scratch(len(early_slots), padded, hidden) + apply_scratch(padded, hidden),
        flops=1e9,
    )(*(token_slots[d] for d in early_slots), weights)
    partials = list(
        call(
            functools.partial(late_body, group, nz),
            [sds((hidden, HD), bf16)] * nz,
            scratch=[pltpu.VMEM((3, hidden, HD), bf16)] + gradient_scratch(1, padded, hidden),
            flops=5e8,
        )(token_slots[last], weights, early_grads)
    )
    weights, partials[0] = lax.optimization_barrier((weights, partials[0]))
    for d in served(nz)[1:]:
        pairs = []
        for z in range(nz):
            pairs += [
                (z * group + j, (z ^ d) * group + j)
                for j in range(heads)
                if ((z ^ d) - j) % nz < 3
            ]
        partials[d] = lax.ppermute(partials[d], ("z", "grp"), pairs)

    fast_slots = call(
        functools.partial(late_apply_body, early_slots, last),
        sds((group, padded, HD), bf16),
        scratch=apply_scratch(padded, hidden),
        flops=1e3,
        moved=1024,
    )(token_slots[last], weights, early_fast)
    kv_own, partials[0], fast_slots = lax.optimization_barrier((kv_own, partials[0], fast_slots))
    fast_slots = lax.all_to_all(fast_slots, "grp", 0, 0, tiled=True)

    ring = [(i, i + 1) for i in range(count - 1)]
    kv_back = lax.ppermute(kv_own, ("z", "grp"), ring)

    ortho = call(ortho_body, sds((hidden, HD), bf16), flops=1e9)(
        *(partials[d] for d in served(nz))
    )
    queries, ortho = lax.optimization_barrier((queries, ortho))
    rows = lax.all_to_all(
        ortho.reshape(count, rows_local, HD), ("z", "grp"), 0, 0, tiled=True
    )
    new_weights = call(
        functools.partial(finish_body, nz, group), sds(fast_weights.shape, f32), flops=1e6
    )(fast_weights, rows)

    attended = pl.pallas_call(
        functools.partial(attend_body, heads, tokens),
        grid=(1,),
        out_shape=sds((padded, span), f32),
        in_specs=[whole(padded, span)] + [whole(padded, 2 * span)] * 2,
        out_specs=whole(padded, span),
        compiler_params=pltpu.CompilerParams(vmem_limit_bytes=VMEM_LIMIT),
    )(queries, kv_own, kv_back)
    fast, squares = call(
        functools.partial(assemble_body, heads),
        [sds((padded, span), bf16), sds((8, padded), f32)],
        flops=1e7,
    )(fast_slots)
    all_squares = [squares] + [
        lax.ppermute(squares, "head", [(s, (s + d) % nh) for s in range(nh)]) for d in range(1, nh)
    ]
    block_out = pl.pallas_call(
        functools.partial(block_body, span * nh),
        grid=(1,),
        out_shape=sds((tokens, span), bf16),
        in_specs=[whole(1, span), whole(padded, span), whole(padded, span)]
        + [whole(8, padded)] * nh,
        out_specs=whole(padded, span),
        compiler_params=pltpu.CompilerParams(vmem_limit_bytes=VMEM_LIMIT),
    )(gain.reshape(1, span), attended, fast, *all_squares)
    return (block_out, new_weights)


def solution(mesh):
    group = 4
    nh = mesh.shape["head"]
    inner = Mesh(
        np.asarray(mesh.devices).reshape(mesh.shape["ctx"] // group, group, nh),
        ("z", "grp", "head"),
    )
    ctx = ("z", "grp")
    placed = (
        P(ctx, "head"),
        P(ctx, "head"),
        P(ctx, "head"),
        P(ctx, "head"),
        P(ctx),
        P(None, "head", ctx, None),
        P("head"),
    )
    return jax.shard_map(
        on_device,
        mesh=inner,
        in_specs=placed,
        out_specs=(P(ctx, "head"), P(None, "head", ctx, None)),
        check_vma=False,
    )
```

time: 69.1 us -> 60.9 us (0.88)
  waiting for transfers between devices: 14.6 us -> 8.12 us
  Pallas kernels: 17.1 us -> 14.2 us
  starting transfers between devices: 34.6 us -> 36.5 us
    ppermute x3, waiting for transfers between devices: 8.49 us -> 2.15 us  [on_device(): token_slots[d] = lax.ppermute(token_slots[d], 'grp', pairs)]
    pallas_call x3 -> x4, Pallas kernels: 10.2 us -> 7.77 us  [the longest x1 3.67 us: on_device(): call(ortho_body, sds((hidden, HD), bf16), flops=1000000000.0)]
    all_to_all x1, waiting for transfers between devices: 0.01 us -> 2.42 us  [on_device(): weights = lax.all_to_all(low, ('z', 'grp'), 0, 0, tiled=True)]
    ppermute x3, starting transfers between devices: 7.1 us -> 9.12 us  [on_device(): partials[d] = lax.ppermute(partials[d], ('z', 'grp'), pairs)]
    all_to_all x1, starting transfers between devices: 6.05 us -> 4.62 us  [on_device(): lax.all_to_all(ortho.reshape(count, rows_local, HD), ('z', 'grp'), 0, 0,...]
    ppermute x1, waiting for transfers between devices: 2.13 us -> 0.75 us  [on_device(): lax.ppermute(squares, 'head', [(s, (s + d) % nh) for s in range(nh)])]
    ppermute x3, starting transfers between devices: 6.41 us -> 7.77 us  [on_device(): token_slots[d] = lax.ppermute(token_slots[d], 'grp', pairs)]
    ppermute x3, waiting for transfers between devices: 1.16 us -> 0.01 us  [on_device(): partials[d] = lax.ppermute(partials[d], ('z', 'grp'), pairs)]
  transfers between devices with their start and end apart: 11 -> 11, of which waited for: 5 -> 5; matrix products, arithmetic and copies ran while one was open for 0% -> 0% of each run, Pallas kernels for 15% -> 16%
where the time goes in v1:
time: 60.9 us; the launch traced here: 60.3 us
  starting transfers between devices  36.5 us (60%)
  Pallas kernels  14.2 us (23%)
  waiting for transfers between devices  8.12 us (13%)
  between operations  1.48 us (2%)
    ppermute x3, starting transfers between devices, on_device(): partials[d] = lax.ppermute(partials[d], ('z', 'grp'), pairs)  9.12 us
    ppermute x3, starting transfers between devices, on_device(): token_slots[d] = lax.ppermute(token_slots[d], 'grp', pairs)  7.77 us
    all_to_all x1, starting transfers between devices, on_device(): weights = lax.all_to_all(low, ('z', 'grp'), 0, 0, tiled=True)  7.5 us
    all_to_all x1, starting transfers between devices, on_device(): lax.all_to_all(ortho.reshape(count, rows_local, HD), ('z', 'grp'), 0, 0,...  4.62 us
    pallas_call x1, Pallas kernels, on_device(): call(ortho_body, sds((hidden, HD), bf16), flops=1000000000.0)  3.67 us
    all_to_all x1, starting transfers between devices, on_device(): fast_slots = lax.all_to_all(fast_slots, 'grp', 0, 0, tiled=True)  3.51 us
    pallas_call x1, Pallas kernels, on_device(): pl.pallas_call(functools.partial(prep_body, heads, group, tokens), grid=(...  2.79 us
    all_to_all x1, waiting for transfers between devices, on_device(): lax.all_to_all(ortho.reshape(count, rows_local, HD), ('z', 'grp'), 0, 0,...  2.79 us
  transfers between devices with their start and end apart: 11, of which 5 were waited for; matrix products, arithmetic and copies ran while one was open for 0% of the time, Pallas kernels for 16%

profile of v1, /device:TPU:0, one launch (start us, length us, event | category | flops | bytes accessed | tf_op | source)
XLA Modules:
  0.0 60.3 jit_solution(9719182528129490970)
XLA Ops:
  1.3 2.8 %shard_map.86 = (bf16[16,3,32,128]{3,2,1,0:T(8,128)(2,1)}, bf16[208,768]{1,0:T(8,128)(2,1)}, bf16[208,384]{1,0:T(8,128)(2,1)}, bf16[208,384]{1,0:T(8,128)(2,1)},...) custom-call(s32[1,1]{1,0:T(1,128)} %bitcast.3.update, f32[3,3,32,128]{3,2,1,0:T(8,128)} %w_ref.3, ...), custom_call_target="tpu_custom_call" | custom-call | tf_op jit(solution)/shard_map/pallas_call | solution.py:293
  4.1 0.0 copy-start.7
  4.1 0.0 copy-start.6
  4.1 0.0 copy-start.5
  4.1 0.0 copy-start.3
  4.1 7.5 %all-to-all-start = ((bf16[16,3,32,128]{3,2,1,0:T(8,128)(2,1)}), bf16[16,3,32,128]{3,2,1,0:T(8,128)(2,1)S(1)}, u32[]{:S(2)}, u32[]{:S(2)}) async-start(bf16[16,3,32,128]{3,2,1,0:T(8,128)(2,1)} %get-tuple-element.24), calls=%async_computation | async-start | bytes 786432 | tf_op jit(solution)/shard_map/all_to_all | solution.py:307
  11.6 0.0 copy-done.7
  11.6 1.3 %collective-permute-start.1 = (bf16[208,384]{1,0:T(8,128)(2,1)S(1)}, bf16[208,384]{1,0:T(8,128)(2,1)S(1)}, u32[]{:S(2)}, u32[]{:S(2)}) collective-permute-start(bf16[208,384]{1,0:T(8,128)(2,1)S(1)} %copy-done.7), channel_id=1, source_target_pairs={{2,4},{4,2},{6,0},{3,5},{5,3},{7,1},{10,12},{12,10},{14,8},{11,13}... | collective-permute-start | bytes 479240 | tf_op jit(solution)/shard_map/ppermute | solution.py:312
  12.9 0.0 copy-done.6
  12.9 4.6 %collective-permute-start.2 = (bf16[208,384]{1,0:T(8,128)(2,1)S(1)}, bf16[208,384]{1,0:T(8,128)(2,1)S(1)}, u32[]{:S(2)}, u32[]{:S(2)}) collective-permute-start(bf16[208,384]{1,0:T(8,128)(2,1)S(1)} %copy-done.6), channel_id=1, source_target_pairs={{0,2},{2,0},{6,4},{1,3},{3,1},{7,5},{8,10},{10,8},{14,12},{9,11},{... | collective-permute-start | bytes 479240 | tf_op jit(solution)/shard_map/ppermute | solution.py:312
  17.5 0.0 copy-done.5
  17.5 1.9 %collective-permute-start = (bf16[208,384]{1,0:T(8,128)(2,1)S(1)}, bf16[208,384]{1,0:T(8,128)(2,1)S(1)}, u32[]{:S(2)}, u32[]{:S(2)}) collective-permute-start(bf16[208,384]{1,0:T(8,128)(2,1)S(1)} %copy-done.5), channel_id=1, source_target_pairs={{0,4},{4,0},{6,2},{1,5},{5,1},{7,3},{8,12},{12,8},{14,10},{9,13},{... | collective-permute-start | bytes 479240 | tf_op jit(solution)/shard_map/ppermute | solution.py:312
  19.4 2.0 %collective-permute-done.1.refs_1_ = bf16[208,384]{1,0:T(8,128)(2,1)S(1)} collective-permute-done((bf16[208,384]{1,0:T(8,128)(2,1)S(1)}, bf16[208,384]{1,0:T(8,128)(2,1)S(1)}, u32[]{:S(2)}, u32[]{:S(2)}) %collective-permute-start.1) | collective-permute-done | bytes 159776 | tf_op jit(solution)/shard_map/ppermute | solution.py:312
  21.4 0.0 collective-permute-done.2.refs_2_
  21.4 2.4 %all-to-all-done.refs_3_.w_ref = bf16[16,3,32,128]{3,2,1,0:T(8,128)(2,1)S(1)} async-done(((bf16[16,3,32,128]{3,2,1,0:T(8,128)(2,1)}), bf16[16,3,32,128]{3,2,1,0:T(8,128)(2,1)S(1)}, u32[]{:S(2)}, u32[]{:S(2)}) %all-to-all-start) | async-done | bytes 393248 | tf_op jit(solution)/shard_map/all_to_all | solution.py:307
  23.8 0.0 copy-done.3
  23.8 2.2 %shard_map.87 = (f32[3,512,128]{2,1,0:T(8,128)S(1)}, bf16[3,208,128]{2,1,0:T(8,128)(2,1)S(1)}) custom-call(bf16[208,384]{1,0:T(8,128)(2,1)S(1)} %copy-done.3, bf16[208,384]{1,0:T(8,128)(2,1)S(1)} %collective-permute-done.1.refs_1_, bf16[208,384]{1,0:T(8,128)(2,1)S(1)} %collective-permute-done.2.refs_2_, bf16[16,3,32,128]{3,2,1,0:T(8,128)(2,1)S(1)} %all-to-all-done.refs_3_.w_ref), custom_call_target="tpu_custom_call" | custom-call | flops 1000000000 | bytes 1048576 | tf_op jit(solution)/shard_map/pallas_call | solution.py:316
  26.1 0.2 collective-permute-done.token_ref
  26.2 0.8 %shard_map.88 = (bf16[512,128]{1,0:T(8,128)(2,1)S(1)}, bf16[512,128]{1,0:T(8,128)(2,1)S(1)}, bf16[512,128]{1,0:T(8,128)(2,1)S(1)}, bf16[512,128]{1,0:T(8,128)(2,1)S(1)}) custom-call(bf16[208,384]{1,0:T(8,128)(2,1)S(1)} %collective-permute-done.token_ref, bf16[16,3,32,128]{3,2,1,0:T(8,128)(2,1)S(1)} %all-to-all-done.refs_3_.w_ref, ...), custom_call_target="tpu_custom_call" | custom-call | flops 500000000 | bytes 1048576 | tf_op jit(solution)/shard_map/pallas_call | solution.py:323
  27.0 1.3 %collective-permute-start.3 = (bf16[512,128]{1,0:T(8,128)(2,1)S(1)}, bf16[512,128]{1,0:T(8,128)(2,1)S(1)}, u32[]{:S(2)}, u32[]{:S(2)}) collective-permute-start(bf16[512,128]{1,0:T(8,128)(2,1)S(1)} %get-tuple-element.35), channel_id=1, source_target_pairs={{2,26},{4,28},{8,16},{10,18},{12,20},{16,8},{18,10},{24,0},{28,4},... | collective-permute-start | bytes 393224 | tf_op jit(solution)/shard_map/ppermute | solution.py:339
  28.3 5.9 %collective-permute-start.4 = (bf16[512,128]{1,0:T(8,128)(2,1)S(1)}, bf16[512,128]{1,0:T(8,128)(2,1)S(1)}, u32[]{:S(2)}, u32[]{:S(2)}) collective-permute-start(bf16[512,128]{1,0:T(8,128)(2,1)S(1)} %get-tuple-element.36), channel_id=1, source_target_pairs={{0,16},{2,18},{4,20},{10,26},{12,28},{16,0},{20,4},{24,8},{26,10},... | collective-permute-start | bytes 393224 | tf_op jit(solution)/shard_map/ppermute | solution.py:339
  34.2 1.9 %collective-permute-start.5 = (bf16[512,128]{1,0:T(8,128)(2,1)S(1)}, bf16[512,128]{1,0:T(8,128)(2,1)S(1)}, u32[]{:S(2)}, u32[]{:S(2)}) collective-permute-start(bf16[512,128]{1,0:T(8,128)(2,1)S(1)} %get-tuple-element.37), channel_id=1, source_target_pairs={{0,8},{2,10},{8,0},{12,4},{18,26},{20,28},{24,16},{26,18},{28,20},... | collective-permute-start | bytes 393224 | tf_op jit(solution)/shard_map/ppermute | solution.py:339
  36.1 1.1 %shard_map.89 = bf16[4,208,128]{2,1,0:T(8,128)(2,1)} custom-call(bf16[208,384]{1,0:T(8,128)(2,1)S(1)} %collective-permute-done.token_ref, bf16[16,3,32,128]{3,2,1,0:T(8,128)(2,1)S(1)} %all-to-all-done.refs_3_.w_ref, bf16[3,208,128]{2,1,0:T(8,128)(2,1)S(1)} %get-tuple-element.33.early), custom_call_target="tpu_custom_call" | custom-call | flops 1000 | bytes 1024 | tf_op jit(solution)/shard_map/pallas_call | solution.py:341
  37.3 0.0 copy-start.2
  37.3 3.5 %all-to-all-start.1 = ((bf16[4,208,128]{2,1,0:T(8,128)(2,1)}), bf16[4,208,128]{2,1,0:T(8,128)(2,1)S(1)}, u32[]{:S(2)}, u32[]{:S(2)}) async-start(bf16[4,208,128]{2,1,0:T(8,128)(2,1)} %shard_map.89), calls=%async_computation.1 | async-start | bytes 425984 | tf_op jit(solution)/shard_map/all_to_all | solution.py:349
  40.8 0.0 copy-done.2
  40.8 2.4 %collective-permute-start.6 = (bf16[208,768]{1,0:T(8,128)(2,1)S(1)}, bf16[208,768]{1,0:T(8,128)(2,1)S(1)}, u32[]{:S(2)}, u32[]{:S(2)}) collective-permute-start(bf16[208,768]{1,0:T(8,128)(2,1)S(1)} %copy-done.2), channel_id=1, source_target_pairs={{0,2},{2,4},{4,6},{6,8},{8,10},{10,12},{12,14},{14,16},{16,18},{18... | collective-permute-start | bytes 958472 | tf_op jit(solution)/shard_map/ppermute | solution.py:352
  43.2 0.0 collective-permute-done.3.refs_1_
  43.2 0.0 collective-permute-done.4.refs_2_
  43.2 0.0 collective-permute-done.5.refs_3_
  43.2 3.7 %shard_map.90 = bf16[512,128]{1,0:T(8,128)(2,1)} custom-call(bf16[512,128]{1,0:T(8,128)(2,1)S(1)} %get-tuple-element.34.refs_0_, bf16[512,128]{1,0:T(8,128)(2,1)S(1)} %collective-permute-done.3.refs_1_, bf16[512,128]{1,0:T(8,128)(2,1)S(1)} %collective-permute-done.4.refs_2_, bf16[512,128]{1,0:T(8,128)(2,1)S(1)} %collective-permute-done.5.refs_3_), custom_call_target="tpu_custom_call" | custom-call | flops 1000000000 | bytes 1048576 | tf_op jit(solution)/shard_map/pallas_call | solution.py:354
  46.9 0.0 all-to-all-done.1.slots
  46.9 4.6 %all-to-all-start.2 = ((bf16[16,32,128]{2,1,0:T(8,128)(2,1)}), bf16[16,32,128]{2,1,0:T(8,128)(2,1)S(1)}, u32[]{:S(2)}, u32[]{:S(2)}) async-start(bf16[16,32,128]{2,1,0:T(8,128)(2,1)} %bitcast.2), calls=%async_computation.2 | async-start | bytes 262144 | tf_op jit(solution)/shard_map/all_to_all | solution.py:358
  51.5 0.0 copy-start.4
  51.5 0.0 copy-start
  51.5 0.4 shard_map.92
  52.0 1.6 %collective-permute-start.7 = (f32[8,208]{1,0:T(8,128)S(1)}, f32[8,208]{1,0:T(8,128)S(1)}, u32[]{:S(2)}, u32[]{:S(2)}) collective-permute-start(f32[8,208]{1,0:T(8,128)S(1)} %get-tuple-element.42.refs_0_), channel_id=1, source_target_pairs={{0,1},{1,0},{2,3},{3,2},{4,5},{5,4},{6,7},{7,6},{8,9},{9,8},{10,11... | collective-permute-start | bytes 19976 | tf_op jit(solution)/shard_map/ppermute | solution.py:379
  53.5 0.0 copy-done.4
  53.5 0.0 collective-permute-done.6.back_ref
  53.5 0.0 copy-done
  53.5 1.4 %shard_map.91.attended_ref = f32[208,384]{1,0:T(8,128)S(1)} custom-call(bf16[195,384]{1,0:T(8,128)(2,1)S(1)} %copy-done, bf16[208,768]{1,0:T(8,128)(2,1)S(1)} %copy-done.2, bf16[208,768]{1,0:T(8,128)(2,1)S(1)} %collective-permute-done.6.back_ref), custom_call_target="tpu_custom_call" | custom-call | tf_op jit(solution)/shard_map/pallas_call | solution.py:365
  54.9 0.8 %collective-permute-done.7.refs_1_ = f32[8,208]{1,0:T(8,128)S(1)} collective-permute-done((f32[8,208]{1,0:T(8,128)S(1)}, f32[8,208]{1,0:T(8,128)S(1)}, u32[]{:S(2)}, u32[]{:S(2)}) %collective-permute-start.7) | collective-permute-done | bytes 6688 | tf_op jit(solution)/shard_map/ppermute | solution.py:379
  55.6 0.0 copy-start.1
  55.7 1.0 %shard_map.93 = bf16[195,384]{1,0:T(8,128)(2,1)} custom-call(f32[1,384]{1,0:T(1,128)S(1)} %reshape.13.gain_ref, f32[208,384]{1,0:T(8,128)S(1)} %shard_map.91.attended_ref, bf16[208,384]{1,0:T(8,128)(2,1)S(1)} %get-tuple-element.41.fast_ref, f32[8,208]{1,0:T(8,128)S(1)} %get-tuple-element.42.refs_0_, f32[8,208]{1,0:T(8,128)S(1)} %collective-permute-done.7.refs_1_), custom_call_target="tpu_custom_call" | custom-call | tf_op jit(solution)/shard_map/pallas_call | solution.py:381
  56.6 2.8 %all-to-all-done.2.rows_ref = bf16[16,32,128]{2,1,0:T(8,128)(2,1)S(1)} async-done(((bf16[16,32,128]{2,1,0:T(8,128)(2,1)}), bf16[16,32,128]{2,1,0:T(8,128)(2,1)S(1)}, u32[]{:S(2)}, u32[]{:S(2)}) %all-to-all-start.2) | async-done | bytes 131104 | tf_op jit(solution)/shard_map/all_to_all | solution.py:358
  59.4 0.0 copy-done.1
  59.4 0.8 %shard_map.94 = f32[3,3,32,128]{3,2,1,0:T(8,128)} custom-call(f32[3,3,32,128]{3,2,1,0:T(8,128)S(1)} %copy-done.1, bf16[16,32,128]{2,1,0:T(8,128)(2,1)S(1)} %all-to-all-done.2.rows_ref), custom_call_target="tpu_custom_call" | custom-call | flops 1000000 | bytes 1048576 | tf_op jit(solution)/shard_map/pallas_call | solution.py:361
  (1 shorter events, 0.0 us)
Async XLA Ops:
  4.1 7.5 %copy-start.7 = (bf16[208,384]{1,0:T(8,128)(2,1)S(1)}, bf16[208,384]{1,0:T(8,128)(2,1)}, u32[]{:S(2)}) copy-start(bf16[208,384]{1,0:T(8,128)(2,1)} %get-tuple-element.27) | copy-start | bytes 479236
  4.1 8.8 %copy-start.6 = (bf16[208,384]{1,0:T(8,128)(2,1)S(1)}, bf16[208,384]{1,0:T(8,128)(2,1)}, u32[]{:S(2)}) copy-start(bf16[208,384]{1,0:T(8,128)(2,1)} %get-tuple-element.28) | copy-start | bytes 479236
  4.1 13.4 %copy-start.5 = (bf16[208,384]{1,0:T(8,128)(2,1)S(1)}, bf16[208,384]{1,0:T(8,128)(2,1)}, u32[]{:S(2)}) copy-start(bf16[208,384]{1,0:T(8,128)(2,1)} %get-tuple-element.25) | copy-start | bytes 479236
  4.1 19.7 %copy-start.3 = (bf16[208,384]{1,0:T(8,128)(2,1)S(1)}, bf16[208,384]{1,0:T(8,128)(2,1)}, u32[]{:S(2)}) copy-start(bf16[208,384]{1,0:T(8,128)(2,1)} %get-tuple-element.26.refs_0_) | copy-start | bytes 479236
  4.1 19.7 %all-to-all-start = ((bf16[16,3,32,128]{3,2,1,0:T(8,128)(2,1)}), bf16[16,3,32,128]{3,2,1,0:T(8,128)(2,1)S(1)}, u32[]{:S(2)}, u32[]{:S(2)}) async-start(bf16[16,3,32,128]{3,2,1,0:T(8,128)(2,1)} %get-tuple-element.24), calls=%async_computation | async-start | bytes 786432 | tf_op jit(solution)/shard_map/all_to_all | solution.py:307
  11.6 9.8 %collective-permute-start.1 = (bf16[208,384]{1,0:T(8,128)(2,1)S(1)}, bf16[208,384]{1,0:T(8,128)(2,1)S(1)}, u32[]{:S(2)}, u32[]{:S(2)}) collective-permute-start(bf16[208,384]{1,0:T(8,128)(2,1)S(1)} %copy-done.7), channel_id=1, source_target_pairs={{2,4},{4,2},{6,0},{3,5},{5,3},{7,1},{10,12},{12,10},{14,8},{11,13}... | collective-permute-start | bytes 479240 | tf_op jit(solution)/shard_map/ppermute | solution.py:312
  12.9 8.5 %collective-permute-start.2 = (bf16[208,384]{1,0:T(8,128)(2,1)S(1)}, bf16[208,384]{1,0:T(8,128)(2,1)S(1)}, u32[]{:S(2)}, u32[]{:S(2)}) collective-permute-start(bf16[208,384]{1,0:T(8,128)(2,1)S(1)} %copy-done.6), channel_id=1, source_target_pairs={{0,2},{2,0},{6,4},{1,3},{3,1},{7,5},{8,10},{10,8},{14,12},{9,11},{... | collective-permute-start | bytes 479240 | tf_op jit(solution)/shard_map/ppermute | solution.py:312
  17.5 8.7 %collective-permute-start = (bf16[208,384]{1,0:T(8,128)(2,1)S(1)}, bf16[208,384]{1,0:T(8,128)(2,1)S(1)}, u32[]{:S(2)}, u32[]{:S(2)}) collective-permute-start(bf16[208,384]{1,0:T(8,128)(2,1)S(1)} %copy-done.5), channel_id=1, source_target_pairs={{0,4},{4,0},{6,2},{1,5},{5,1},{7,3},{8,12},{12,8},{14,10},{9,13},{... | collective-permute-start | bytes 479240 | tf_op jit(solution)/shard_map/ppermute | solution.py:312
  27.0 16.2 %collective-permute-start.3 = (bf16[512,128]{1,0:T(8,128)(2,1)S(1)}, bf16[512,128]{1,0:T(8,128)(2,1)S(1)}, u32[]{:S(2)}, u32[]{:S(2)}) collective-permute-start(bf16[512,128]{1,0:T(8,128)(2,1)S(1)} %get-tuple-element.35), channel_id=1, source_target_pairs={{2,26},{4,28},{8,16},{10,18},{12,20},{16,8},{18,10},{24,0},{28,4},... | collective-permute-start | bytes 393224 | tf_op jit(solution)/shard_map/ppermute | solution.py:339
  28.3 14.9 %collective-permute-start.4 = (bf16[512,128]{1,0:T(8,128)(2,1)S(1)}, bf16[512,128]{1,0:T(8,128)(2,1)S(1)}, u32[]{:S(2)}, u32[]{:S(2)}) collective-permute-start(bf16[512,128]{1,0:T(8,128)(2,1)S(1)} %get-tuple-element.36), channel_id=1, source_target_pairs={{0,16},{2,18},{4,20},{10,26},{12,28},{16,0},{20,4},{24,8},{26,10},... | collective-permute-start | bytes 393224 | tf_op jit(solution)/shard_map/ppermute | solution.py:339
  34.2 9.0 %collective-permute-start.5 = (bf16[512,128]{1,0:T(8,128)(2,1)S(1)}, bf16[512,128]{1,0:T(8,128)(2,1)S(1)}, u32[]{:S(2)}, u32[]{:S(2)}) collective-permute-start(bf16[512,128]{1,0:T(8,128)(2,1)S(1)} %get-tuple-element.37), channel_id=1, source_target_pairs={{0,8},{2,10},{8,0},{12,4},{18,26},{20,28},{24,16},{26,18},{28,20},... | collective-permute-start | bytes 393224 | tf_op jit(solution)/shard_map/ppermute | solution.py:339
  37.3 3.5 %copy-start.2 = (bf16[208,768]{1,0:T(8,128)(2,1)S(1)}, bf16[208,768]{1,0:T(8,128)(2,1)}, u32[]{:S(2)}) copy-start(bf16[208,768]{1,0:T(8,128)(2,1)} %get-tuple-element.39.own_ref) | copy-start | bytes 958468
  37.3 9.6 %all-to-all-start.1 = ((bf16[4,208,128]{2,1,0:T(8,128)(2,1)}), bf16[4,208,128]{2,1,0:T(8,128)(2,1)S(1)}, u32[]{:S(2)}, u32[]{:S(2)}) async-start(bf16[4,208,128]{2,1,0:T(8,128)(2,1)} %shard_map.89), calls=%async_computation.1 | async-start | bytes 425984 | tf_op jit(solution)/shard_map/all_to_all | solution.py:349
  40.8 12.7 %collective-permute-start.6 = (bf16[208,768]{1,0:T(8,128)(2,1)S(1)}, bf16[208,768]{1,0:T(8,128)(2,1)S(1)}, u32[]{:S(2)}, u32[]{:S(2)}) collective-permute-start(bf16[208,768]{1,0:T(8,128)(2,1)S(1)} %copy-done.2), channel_id=1, source_target_pairs={{0,2},{2,4},{4,6},{6,8},{8,10},{10,12},{12,14},{14,16},{16,18},{18... | collective-permute-start | bytes 958472 | tf_op jit(solution)/shard_map/ppermute | solution.py:352
  46.9 12.6 %all-to-all-start.2 = ((bf16[16,32,128]{2,1,0:T(8,128)(2,1)}), bf16[16,32,128]{2,1,0:T(8,128)(2,1)S(1)}, u32[]{:S(2)}, u32[]{:S(2)}) async-start(bf16[16,32,128]{2,1,0:T(8,128)(2,1)} %bitcast.2), calls=%async_computation.2 | async-start | bytes 262144 | tf_op jit(solution)/shard_map/all_to_all | solution.py:358
  51.5 2.0 %copy-start.4 = (f32[384]{0:T(512)S(1)}, f32[384]{0:T(512)}, u32[]{:S(2)}) copy-start(f32[384]{0:T(512)} %param.13) | copy-start | bytes 4612
  51.5 2.0 %copy-start = (bf16[195,384]{1,0:T(8,128)(2,1)S(1)}, bf16[195,384]{1,0:T(8,128)(2,1)}, u32[]{:S(2)}) copy-start(bf16[195,384]{1,0:T(8,128)(2,1)} %q_ref.2) | copy-start | bytes 449284
  52.0 3.7 %collective-permute-start.7 = (f32[8,208]{1,0:T(8,128)S(1)}, f32[8,208]{1,0:T(8,128)S(1)}, u32[]{:S(2)}, u32[]{:S(2)}) collective-permute-start(f32[8,208]{1,0:T(8,128)S(1)} %get-tuple-element.42.refs_0_), channel_id=1, source_target_pairs={{0,1},{1,0},{2,3},{3,2},{4,5},{5,4},{6,7},{7,6},{8,9},{9,8},{10,11... | collective-permute-start | bytes 19976 | tf_op jit(solution)/shard_map/ppermute | solution.py:379
  55.6 3.8 %copy-start.1 = (f32[3,3,32,128]{3,2,1,0:T(8,128)S(1)}, f32[3,3,32,128]{3,2,1,0:T(8,128)}, u32[]{:S(2)}) copy-start(f32[3,3,32,128]{3,2,1,0:T(8,128)} %w_ref.3) | copy-start | bytes 442372

commit v2 on v1

--- a/solution.py
+++ b/solution.py
@@ -19,7 +19,6 @@
 f32 = jnp.float32
 bf16 = jnp.bfloat16
 VMEM_LIMIT = 24 * 1024 * 1024
-VMEM_MOST = 56 * 1024 * 1024
 
 
 def dot(a, b, contract, precision=None):
@@ -50,6 +49,10 @@
     return [0] + list(range(n - 1, 0, -1))
 
 
+def flip(z, group):
+    return (z & 1) * (group // 2)
+
+
 def position():
     return lax.axis_index("z"), lax.axis_index("grp")
 
@@ -58,29 +61,40 @@
     return 0.5 * jnp.tanh(0.5 * x) + 0.5
 
 
-def prep_body(heads, group, tokens, update, w_ref, k_ref, v_ref, q_ref, rate_ref, *outs):
-    w_out, kv_out = outs[:2]
-    token_outs = outs[2:]
+def cast_body(heads, group, w_ref, w_out):
+    slots = w_out.shape[0] // group
+    for head in range(heads):
+        for m in range(3):
+            low = w_ref[m, head].astype(bf16)
+            for z in range(slots):
+                for j in range(group):
+                    if min(j ^ flip(z, group), heads - 1) == head:
+                        w_out[z * group + j, m] = low
+
+
+def prep_body(
+    heads, group, tokens, last, after, update, k_ref, v_ref, q_ref, rate_ref, kv_out, *outs
+):
+    token_outs, (late_out, targets) = outs[:-2], outs[-2:]
     padded = kv_out.shape[0]
-    slots = w_out.shape[0] // group
-    for j in range(group):
-        for m in range(3):
-            low = w_ref[m, min(j, heads - 1)].astype(bf16)
-            for z in range(slots):
-                w_out[z * group + j, m] = low
     place = position()
     valid = lax.broadcasted_iota(jnp.int32, (padded, 1), 0) < tokens
     none = jnp.zeros((), bf16)
     keep = update[...].astype(f32)
-    row = lax.broadcasted_iota(jnp.int32, (heads, HD), 0)
+    lane_head = lax.broadcasted_iota(jnp.int32, (heads, heads * HD), 1) // HD
+    row = lax.broadcasted_iota(jnp.int32, (heads, heads * HD), 0)
+    rate = dot(rate_ref[...], (row == lane_head).astype(f32), (0, 0), highest)[:padded]
+    targets[...] = jnp.where(valid, ((rate * keep) * v_ref[...].astype(f32)).astype(bf16), none)
     for d in range(group):
-        head = jnp.minimum(place[1] ^ d, heads - 1)
+        head = jnp.minimum(place[1] ^ d ^ flip(place[0], group), heads - 1)
         cols = pl.ds(pl.multiple_of(head * HD, HD), HD)
-        rate = dot(rate_ref[...], (row == head).astype(f32), (0, 0), highest)[:padded]
-        target = ((rate * keep) * v_ref[:, cols].astype(f32)).astype(bf16)
         token_outs[d][:, :HD] = jnp.where(valid, k_ref[:, cols], none)
-        token_outs[d][:, HD : 2 * HD] = jnp.where(valid, target, none)
-        token_outs[d][:, 2 * HD :] = jnp.where(valid, q_ref[:, cols], none)
+        token_outs[d][:, HD : 2 * HD] = targets[:, cols]
+        query = jnp.where(valid, q_ref[:, cols], none)
+        if d == last:
+            late_out[...] = query
+        else:
+            token_outs[d][:, 2 * HD :] = query
     kv_out[:, : heads * HD] = jnp.where(valid, k_ref[...], none)
     kv_out[:, heads * HD :] = jnp.where(valid, v_ref[...], none)
 
@@ -132,11 +146,10 @@
     ]
 
 
-def apply_tokens(token_ref, w_ref, stage, act):
+def apply_tokens(query, w_ref, stage, act):
     hidden = act.shape[1]
     tall = 16
     w1, w3, w2 = (weight_rows(w_ref, m, 0, hidden) for m in range(3))
-    query = token_ref[:, 2 * HD :]
     stage[0] = dot(query, w1, (1, 1))
     stage[1] = dot(query, w3, (1, 1))
     for start in range(0, query.shape[0], tall):
@@ -157,7 +170,7 @@
     for m, grad in enumerate(gradients(token_refs, w_ref, *scratch)):
         grads[m] = grad
     for i, ref in enumerate(token_refs):
-        fast[i] = apply_tokens(ref, w_ref, staged.at[i % 2], acts.at[i % 2])
+        fast[i] = apply_tokens(ref[:, 2 * HD :], w_ref, staged.at[i % 2], acts.at[i % 2])
 
 
 def late_body(group, slots, token_ref, w_ref, early, *refs):
@@ -165,17 +178,18 @@
     outs, sums, scratch = refs[:slots], refs[slots], refs[slots + 1 :]
     for m, grad in enumerate(gradients([token_ref], w_ref, *scratch)):
         sums[m] = (early[m] + grad).astype(bf16)
+    head = place[1] ^ flip(place[0], group)
     for d in range(slots):
-        matrix = lax.rem((place[0] ^ d) - place[1] + group * slots, slots)
+        matrix = lax.rem((place[0] ^ d) - head + group * slots, slots)
         chosen = sums[jnp.minimum(matrix, 2)]
         outs[d][...] = jnp.where(matrix < 3, chosen, jnp.zeros_like(chosen))
 
 
-def late_apply_body(early_slots, last, token_ref, w_ref, early, out, staged, acts):
+def late_apply_body(early_slots, last, query_ref, w_ref, early, out, staged, acts):
     place = position()
     for i, d in enumerate(early_slots):
         out[place[1] ^ d] = early[i]
-    out[place[1] ^ last] = apply_tokens(token_ref, w_ref, staged.at[0], acts.at[0])
+    out[place[1] ^ last] = apply_tokens(query_ref[...], w_ref, staged.at[0], acts.at[0])
 
 
 def weight_rows(w_ref, m, start, block):
@@ -208,7 +222,9 @@
     eye = (
         lax.broadcasted_iota(jnp.int32, (HD, HD), 0) == lax.broadcasted_iota(jnp.int32, (HD, HD), 1)
     ).astype(f32)
-    raw = dot(grads, grads, (0, 0), highest)
+    both = jnp.concatenate(parts_of(grads), axis=1)
+    blocks = dot(both, both, (0, 0))
+    raw = (blocks[:HD, HD:] + blocks[HD:, :HD]) + blocks[:HD, :HD]
     square = jnp.sum(jnp.sum(raw * eye, axis=0, keepdims=True), axis=1, keepdims=True)
     scale = lax.rsqrt(square + epsilon)
     gram = raw * scale * scale
@@ -219,16 +235,22 @@
         right = right_of(mix)
         if step < NS_STEPS - 1:
             gram = dot(left_of(dot(left_of(gram), right, (1, 0))), right, (1, 0))
-        total = mix if total is None else dot(left_of(total), right, (1, 0))
-    out[...] = dot(left_of(grads * scale), right_of(total), (1, 0)).astype(out.dtype)
+            total = mix if total is None else dot(left_of(total), right, (1, 0))
+    ortho = dot(left_of(grads * scale), right_of(total), (1, 0))
+    out[...] = dot(left_of(ortho), right, (1, 0)).astype(out.dtype)
 
 
 def finish_body(slots, group, w_ref, rows_ref, out):
     heads = w_ref.shape[1]
+
+    def at(m, h):
+        z = (m + h) % slots
+        return z * group + (h ^ flip(z, group))
+
     for m in range(3):
         for h in range(heads):
             weights = w_ref[m, h]
-            summed = weights + rows_ref[((m + h) % slots) * group + h].astype(f32)
+            summed = weights + rows_ref[at(m, h)].astype(f32)
             old = jnp.sqrt(jnp.sum(weights * weights, axis=1, keepdims=True))
             new = lax.rsqrt(jnp.sum(summed * summed, axis=1, keepdims=True) + epsilon)
             out[m, h] = summed * (old * new)
@@ -255,8 +277,9 @@
 
 
 def assemble_body(heads, slots, out, squares):
+    side = flip(position()[0], slots.shape[0])
     for h in range(heads):
-        out[:, h * HD : (h + 1) * HD] = slots[h]
+        out[:, h * HD : (h + 1) * HD] = slots[h ^ side]
     fast = out[...].astype(f32)
     squares[...] = dot(jnp.ones((8, heads * HD), f32), fast * fast, (1, 1), highest)
 
@@ -290,28 +313,39 @@
         return pl.BlockSpec(shape, lambda i: (0,) * len(shape))
 
     low_shape = (count, 3, rows_local, HD)
+    last = group // 2
+    widths = [2 * HD if d == last else 3 * HD for d in range(group)] + [HD]
+    low = call(
+        functools.partial(cast_body, heads, group), sds(low_shape, bf16), flops=1e6
+    )(fast_weights)
     prepared = pl.pallas_call(
-        functools.partial(prep_body, heads, group, tokens),
+        functools.partial(prep_body, heads, group, tokens, last),
         grid=(1,),
-        out_shape=[sds(low_shape, bf16), sds((padded, 2 * span), bf16)]
-        + [sds((padded, 3 * HD), bf16)] * group,
-        in_specs=[whole(1, 1), whole(*fast_weights.shape)]
+        out_shape=[sds((padded, 2 * span), bf16)]
+        + [sds((padded, width), bf16) for width in widths],
+        in_specs=[pl.BlockSpec(memory_space=pl.ANY), whole(1, 1)]
         + [whole(padded, span)] * 3
         + [whole(heads, -(-padded // 128) * 128)],
-        out_specs=[whole(*low_shape), whole(padded, 2 * span)]
-        + [whole(padded, 3 * HD)] * group,
-        compiler_params=pltpu.CompilerParams(vmem_limit_bytes=VMEM_MOST),
-    )(frame_update.reshape(1, 1), fast_weights, keys, values, queries, rates.T)
-    low, kv_own, token_slots = prepared[0], prepared[1], list(prepared[2:])
+        out_specs=[whole(padded, 2 * span)] + [whole(padded, width) for width in widths],
+        scratch_shapes=[pltpu.VMEM((padded, span), bf16)],
+        compiler_params=pltpu.CompilerParams(vmem_limit_bytes=VMEM_LIMIT),
+    )(low, frame_update.reshape(1, 1), keys, values, queries, rates.T)
+    kv_own, *token_slots, late_queries = prepared
 
     weights = lax.all_to_all(low, ("z", "grp"), 0, 0, tiled=True)
     if rows_local % 16:
         weights = weights.transpose(1, 0, 2, 3).reshape(3, hidden, HD)
     for d in served(group)[1:]:
-        pairs = [(s, s ^ d) for s in range(group) if s ^ d < heads]
-        token_slots[d] = lax.ppermute(token_slots[d], "grp", pairs)
-
-    last = group // 2
+        pairs = [
+            (z * group + s, z * group + (s ^ d))
+            for z in range(nz)
+            for s in range(group)
+            if s ^ d ^ flip(z, group) < heads
+        ]
+        token_slots[d] = lax.ppermute(token_slots[d], ("z", "grp"), pairs)
+        if d == last:
+            late_queries = lax.ppermute(late_queries, ("z", "grp"), pairs)
+
     early_slots = [d for d in served(group) if d != last]
     early_grads, early_fast = call(
         functools.partial(early_body, len(early_slots)),
@@ -328,14 +362,14 @@
         )(token_slots[last], weights, early_grads)
     )
     weights, partials[0] = lax.optimization_barrier((weights, partials[0]))
+    late_queries, partials[1] = lax.optimization_barrier((late_queries, partials[1]))
     for d in served(nz)[1:]:
-        pairs = []
-        for z in range(nz):
-            pairs += [
-                (z * group + j, (z ^ d) * group + j)
-                for j in range(heads)
-                if ((z ^ d) - j) % nz < 3
-            ]
+        pairs = [
+            (z * group + (h ^ flip(z, group)), (z ^ d) * group + (h ^ flip(z ^ d, group)))
+            for z in range(nz)
+            for h in range(heads)
+            if ((z ^ d) - h) % nz < 3
+        ]
         partials[d] = lax.ppermute(partials[d], ("z", "grp"), pairs)
 
     fast_slots = call(
@@ -344,7 +378,7 @@
         scratch=apply_scratch(padded, hidden),
         flops=1e3,
         moved=1024,
-    )(token_slots[last], weights, early_fast)
+    )(late_queries, weights, early_fast)
     kv_own, partials[0], fast_slots = lax.optimization_barrier((kv_own, partials[0], fast_slots))
     fast_slots = lax.all_to_all(fast_slots, "grp", 0, 0, tiled=True)
 

time: 60.9 us -> 60.7 us (level)
  starting transfers between devices: 36.5 us -> 41.5 us
  waiting for transfers between devices: 8.12 us -> 3.6 us
  Pallas kernels: 14.2 us -> 12.5 us
  local copies, waits for them, and re-layouts: 0.04 us -> 0.93 us
    ppermute x3 -> x4, starting transfers between devices: 7.77 us -> 11.7 us  [the longest x3 7.78 us: on_device(): token_slots[d] = lax.ppermute(token_slots[d], ('z', 'grp'), pairs)]
    all_to_all x1, waiting for transfers between devices: 2.42 us -> 0.01 us  [on_device(): weights = lax.all_to_all(low, ('z', 'grp'), 0, 0, tiled=True)]
    ppermute x3 -> x4, waiting for transfers between devices: 2.15 us -> 0.01 us  [the longest x3 0.01 us: on_device(): token_slots[d] = lax.ppermute(token_slots[d], ('z', 'grp'), pairs)]
    pallas_call x1 -> x2, Pallas kernels: 2.79 us -> 1.38 us  [the longest x1 0.76 us: on_device(): call(functools.partial(cast_body, heads, group), sds(low_shape, bf16), fl...]
    ppermute x3, starting transfers between devices: 9.12 us -> 10.1 us  [on_device(): partials[d] = lax.ppermute(partials[d], ('z', 'grp'), pairs)]
    unnamed x16 -> x14, local copies, waits for them, and re-layouts: 0.04 us -> 0.93 us
  transfers between devices with their start and end apart: 11 -> 12, of which waited for: 5 -> 2; matrix products, arithmetic and copies ran while one was open for 0% -> 0% of each run, Pallas kernels for 16% -> 18%
where the time goes in v2:
time: 60.7 us; the launch traced here: 60.1 us
  starting transfers between devices  41.5 us (68%)
  Pallas kernels  12.5 us (21%)
  waiting for transfers between devices  3.6 us (6%)
  between operations  1.53 us (3%)
  local copies, waits for them, and re-layouts  0.93 us (2%)
    ppermute x3, starting transfers between devices, on_device(): partials[d] = lax.ppermute(partials[d], ('z', 'grp'), pairs)  10.1 us
    ppermute x3, starting transfers between devices, on_device(): token_slots[d] = lax.ppermute(token_slots[d], ('z', 'grp'), pairs)  7.78 us
    all_to_all x1, starting transfers between devices, on_device(): weights = lax.all_to_all(low, ('z', 'grp'), 0, 0, tiled=True)  7.49 us
    all_to_all x1, starting transfers between devices, on_device(): lax.all_to_all(ortho.reshape(count, rows_local, HD), ('z', 'grp'), 0, 0,...  4.94 us
    ppermute x1, starting transfers between devices, on_device(): late_queries = lax.ppermute(late_queries, ('z', 'grp'), pairs)  3.92 us
    pallas_call x1, Pallas kernels, on_device(): call(ortho_body, sds((hidden, HD), bf16), flops=1000000000.0)  3.42 us
    all_to_all x1, starting transfers between devices, on_device(): fast_slots = lax.all_to_all(fast_slots, 'grp', 0, 0, tiled=True)  3.37 us
    all_to_all x1, waiting for transfers between devices, on_device(): lax.all_to_all(ortho.reshape(count, rows_local, HD), ('z', 'grp'), 0, 0,...  2.79 us
  transfers between devices with their start and end apart: 12, of which 2 were waited for; matrix products, arithmetic and copies ran while one was open for 0% of the time, Pallas kernels for 18%

profile of v2, /device:TPU:0, one launch (start us, length us, event | category | flops | bytes accessed | tf_op | source)
XLA Modules:
  0.0 60.1 jit_solution(16207602062002917708)
XLA Ops:
  0.6 0.0 copy-start.1
  0.6 0.9 %copy-done.1 = f32[3,3,32,128]{3,2,1,0:T(8,128)S(1)} copy-done((f32[3,3,32,128]{3,2,1,0:T(8,128)S(1)}, f32[3,3,32,128]{3,2,1,0:T(8,128)}, u32[]{:S(2)}) %copy-start.1) | copy-done | bytes 147480
  1.5 0.8 %shard_map.86.after = bf16[16,3,32,128]{3,2,1,0:T(8,128)(2,1)} custom-call(f32[3,3,32,128]{3,2,1,0:T(8,128)S(1)} %copy-done.1), custom_call_target="tpu_custom_call" | custom-call | flops 1000000 | bytes 1048576 | tf_op jit(solution)/shard_map/pallas_call | solution.py:318
  2.3 0.0 copy-start
  2.3 0.0 copy-start.3
  2.3 0.0 copy-start.4
  2.3 7.5 %all-to-all-start = ((bf16[16,3,32,128]{3,2,1,0:T(8,128)(2,1)}), bf16[16,3,32,128]{3,2,1,0:T(8,128)(2,1)S(1)}, u32[]{:S(2)}, u32[]{:S(2)}) async-start(bf16[16,3,32,128]{3,2,1,0:T(8,128)(2,1)} %shard_map.86.after), calls=%async_computation | async-start | bytes 786432 | tf_op jit(solution)/shard_map/all_to_all | solution.py:335
  9.8 0.0 copy-start.5
  10.5 0.0 copy-done
  10.5 0.0 copy-done.3
  10.5 0.0 copy-done.4
  10.5 0.0 copy-done.5
  10.5 0.6 %shard_map.87 = (bf16[208,768]{1,0:T(8,128)(2,1)S(1)}, bf16[208,384]{1,0:T(8,128)(2,1)S(1)}, bf16[208,384]{1,0:T(8,128)(2,1)S(1)}, bf16[208,256]{1,0:T(8,128)(2,...) custom-call(bf16[16,3,32,128]{3,2,1,0:T(8,128)(2,1)} %shard_map.86.after, s32[1,1]{1,0:T(1,128)} %bitcast.3.update, ...), custom_call_target="tpu_custom_call" | custom-call | tf_op jit(solution)/shard_map/pallas_call | solution.py:321
  11.1 1.3 %collective-permute-start.1 = (bf16[208,384]{1,0:T(8,128)(2,1)S(1)}, bf16[208,384]{1,0:T(8,128)(2,1)S(1)}, u32[]{:S(2)}, u32[]{:S(2)}) collective-permute-start(bf16[208,384]{1,0:T(8,128)(2,1)S(1)} %get-tuple-element.28), channel_id=1, source_target_pairs={{2,4},{4,2},{6,0},{8,14},{10,12},{14,8},{18,20},{20,18},{22,16},{2... | collective-permute-start | bytes 479240 | tf_op jit(solution)/shard_map/ppermute | solution.py:345
  12.4 4.6 %collective-permute-start.2 = (bf16[208,384]{1,0:T(8,128)(2,1)S(1)}, bf16[208,384]{1,0:T(8,128)(2,1)S(1)}, u32[]{:S(2)}, u32[]{:S(2)}) collective-permute-start(bf16[208,384]{1,0:T(8,128)(2,1)S(1)} %get-tuple-element.29), channel_id=1, source_target_pairs={{0,2},{2,0},{6,4},{10,8},{12,14},{14,12},{16,18},{18,16},{22,20},{... | collective-permute-start | bytes 479240 | tf_op jit(solution)/shard_map/ppermute | solution.py:345
  17.0 1.9 %collective-permute-start = (bf16[208,256]{1,0:T(8,128)(2,1)S(1)}, bf16[208,256]{1,0:T(8,128)(2,1)S(1)}, u32[]{:S(2)}, u32[]{:S(2)}) collective-permute-start(bf16[208,256]{1,0:T(8,128)(2,1)S(1)} %get-tuple-element.26), channel_id=1, source_target_pairs={{0,4},{4,0},{6,2},{8,12},{10,14},{12,8},{16,20},{20,16},{22,18},{2... | collective-permute-start | bytes 319496 | tf_op jit(solution)/shard_map/ppermute | solution.py:345
  18.9 3.9 %collective-permute-start.3 = (bf16[208,128]{1,0:T(8,128)(2,1)S(1)}, bf16[208,128]{1,0:T(8,128)(2,1)S(1)}, u32[]{:S(2)}, u32[]{:S(2)}) collective-permute-start(bf16[208,128]{1,0:T(8,128)(2,1)S(1)} %get-tuple-element.33), channel_id=1, source_target_pairs={{0,4},{4,0},{6,2},{8,12},{10,14},{12,8},{16,20},{20,16},{22,18},{2... | collective-permute-start | bytes 159752 | tf_op jit(solution)/shard_map/ppermute | solution.py:347
  22.9 0.0 collective-permute-done.1.refs_1_
  22.9 0.0 collective-permute-done.2.refs_2_
  22.9 0.0 all-to-all-done.refs_3_.w_ref
  22.9 2.2 %shard_map.88 = (f32[3,512,128]{2,1,0:T(8,128)S(1)}, bf16[3,208,128]{2,1,0:T(8,128)(2,1)S(1)}) custom-call(bf16[208,384]{1,0:T(8,128)(2,1)S(1)} %get-tuple-element.27.refs_0_, bf16[208,384]{1,0:T(8,128)(2,1)S(1)} %collective-permute-done.1.refs_1_, bf16[208,384]{1,0:T(8,128)(2,1)S(1)} %collective-permute-done.2.refs_2_, ...), custom_call_target="tpu_custom_call" | custom-call | flops 1000000000 | bytes 1048576 | tf_op jit(solution)/shard_map/pallas_call | solution.py:350
  25.1 0.0 collective-permute-done.token_ref
  25.1 0.8 %shard_map.89 = (bf16[512,128]{1,0:T(8,128)(2,1)S(1)}, bf16[512,128]{1,0:T(8,128)(2,1)S(1)}, bf16[512,128]{1,0:T(8,128)(2,1)S(1)}, bf16[512,128]{1,0:T(8,128)(2,1)S(1)}) custom-call(bf16[208,256]{1,0:T(8,128)(2,1)S(1)} %collective-permute-done.token_ref, bf16[16,3,32,128]{3,2,1,0:T(8,128)(2,1)S(1)} %all-to-all-done.refs_3_.w_ref, ...), custom_call_target="tpu_custom_call" | custom-call | flops 500000000 | bytes 1048576 | tf_op jit(solution)/shard_map/pallas_call | solution.py:357
  25.9 0.0 collective-permute-done.3.query_ref
  25.9 3.4 %collective-permute-start.6 = (bf16[512,128]{1,0:T(8,128)(2,1)S(1)}, bf16[512,128]{1,0:T(8,128)(2,1)S(1)}, u32[]{:S(2)}, u32[]{:S(2)}) collective-permute-start(bf16[512,128]{1,0:T(8,128)(2,1)S(1)} %get-tuple-element.41), channel_id=1, source_target_pairs={{0,12},{2,14},{12,0},{8,4},{18,30},{20,24},{28,16},{30,18},{24,20}... | collective-permute-start | bytes 393224 | tf_op jit(solution)/shard_map/ppermute | solution.py:373
  29.3 1.3 %collective-permute-start.4 = (bf16[512,128]{1,0:T(8,128)(2,1)S(1)}, bf16[512,128]{1,0:T(8,128)(2,1)S(1)}, u32[]{:S(2)}, u32[]{:S(2)}) collective-permute-start(bf16[512,128]{1,0:T(8,128)(2,1)S(1)} %get-tuple-element.39), channel_id=1, source_target_pairs={{2,30},{4,24},{12,16},{14,18},{8,20},{16,12},{18,14},{28,0},{24,4}... | collective-permute-start | bytes 393224 | tf_op jit(solution)/shard_map/ppermute | solution.py:373
  30.6 5.5 %collective-permute-start.5 = (bf16[512,128]{1,0:T(8,128)(2,1)S(1)}, bf16[512,128]{1,0:T(8,128)(2,1)S(1)}, u32[]{:S(2)}, u32[]{:S(2)}) collective-permute-start(bf16[512,128]{1,0:T(8,128)(2,1)S(1)} %get-tuple-element.40), channel_id=1, source_target_pairs={{0,16},{2,18},{4,20},{14,30},{8,24},{16,0},{20,4},{28,12},{30,14},... | collective-permute-start | bytes 393224 | tf_op jit(solution)/shard_map/ppermute | solution.py:373
  36.1 1.1 %shard_map.90 = bf16[4,208,128]{2,1,0:T(8,128)(2,1)} custom-call(bf16[208,128]{1,0:T(8,128)(2,1)S(1)} %collective-permute-done.3.query_ref, bf16[16,3,32,128]{3,2,1,0:T(8,128)(2,1)S(1)} %all-to-all-done.refs_3_.w_ref, bf16[3,208,128]{2,1,0:T(8,128)(2,1)S(1)} %get-tuple-element.37.early), custom_call_target="tpu_custom_call" | custom-call | flops 1000 | bytes 1024 | tf_op jit(solution)/shard_map/pallas_call | solution.py:375
  37.2 3.4 %all-to-all-start.1 = ((bf16[4,208,128]{2,1,0:T(8,128)(2,1)}), bf16[4,208,128]{2,1,0:T(8,128)(2,1)S(1)}, u32[]{:S(2)}, u32[]{:S(2)}) async-start(bf16[4,208,128]{2,1,0:T(8,128)(2,1)} %shard_map.90), calls=%async_computation.1 | async-start | bytes 425984 | tf_op jit(solution)/shard_map/all_to_all | solution.py:383
  40.6 2.4 %collective-permute-start.7 = (bf16[208,768]{1,0:T(8,128)(2,1)S(1)}, bf16[208,768]{1,0:T(8,128)(2,1)S(1)}, u32[]{:S(2)}, u32[]{:S(2)}) collective-permute-start(bf16[208,768]{1,0:T(8,128)(2,1)S(1)} %get-tuple-element.43.own_ref), channel_id=1, source_target_pairs={{0,2},{2,4},{4,6},{6,8},{8,10},{10,12},{12,14},{14,16},{16,18},{18... | collective-permute-start | bytes 958472 | tf_op jit(solution)/shard_map/ppermute | solution.py:386
  42.9 0.0 collective-permute-done.6.refs_3_
  43.0 0.0 collective-permute-done.4.refs_1_
  43.0 0.0 collective-permute-done.5.refs_2_
  43.0 3.4 %shard_map.91 = bf16[512,128]{1,0:T(8,128)(2,1)} custom-call(bf16[512,128]{1,0:T(8,128)(2,1)S(1)} %get-tuple-element.38.refs_0_, bf16[512,128]{1,0:T(8,128)(2,1)S(1)} %collective-permute-done.4.refs_1_, bf16[512,128]{1,0:T(8,128)(2,1)S(1)} %collective-permute-done.5.refs_2_, bf16[512,128]{1,0:T(8,128)(2,1)S(1)} %collective-permute-done.6.refs_3_), custom_call_target="tpu_custom_call" | custom-call | flops 1000000000 | bytes 1048576 | tf_op jit(solution)/shard_map/pallas_call | solution.py:388
  46.4 0.0 all-to-all-done.1.slots
  46.4 4.9 %all-to-all-start.2 = ((bf16[16,32,128]{2,1,0:T(8,128)(2,1)}), bf16[16,32,128]{2,1,0:T(8,128)(2,1)S(1)}, u32[]{:S(2)}, u32[]{:S(2)}) async-start(bf16[16,32,128]{2,1,0:T(8,128)(2,1)} %bitcast.2), calls=%async_computation.2 | async-start | bytes 262144 | tf_op jit(solution)/shard_map/all_to_all | solution.py:392
  51.3 0.0 copy-start.6
  51.4 0.4 shard_map.93
  51.8 1.6 %collective-permute-start.8 = (f32[8,208]{1,0:T(8,128)S(1)}, f32[8,208]{1,0:T(8,128)S(1)}, u32[]{:S(2)}, u32[]{:S(2)}) collective-permute-start(f32[8,208]{1,0:T(8,128)S(1)} %get-tuple-element.46.refs_0_), channel_id=1, source_target_pairs={{0,1},{1,0},{2,3},{3,2},{4,5},{5,4},{6,7},{7,6},{8,9},{9,8},{10,11... | collective-permute-start | bytes 19976 | tf_op jit(solution)/shard_map/ppermute | solution.py:413
  53.4 0.0 copy-done.6
  53.4 0.0 collective-permute-done.7.back_ref
  53.4 1.3 %shard_map.92.attended_ref = f32[208,384]{1,0:T(8,128)S(1)} custom-call(bf16[195,384]{1,0:T(8,128)(2,1)S(1)} %copy-done, bf16[208,768]{1,0:T(8,128)(2,1)S(1)} %get-tuple-element.43.own_ref, bf16[208,768]{1,0:T(8,128)(2,1)S(1)} %collective-permute-done.7.back_ref), custom_call_target="tpu_custom_call" | custom-call | tf_op jit(solution)/shard_map/pallas_call | solution.py:399
  54.7 0.8 %collective-permute-done.8.refs_1_ = f32[8,208]{1,0:T(8,128)S(1)} collective-permute-done((f32[8,208]{1,0:T(8,128)S(1)}, f32[8,208]{1,0:T(8,128)S(1)}, u32[]{:S(2)}, u32[]{:S(2)}) %collective-permute-start.8) | collective-permute-done | bytes 6688 | tf_op jit(solution)/shard_map/ppermute | solution.py:413
  55.5 0.0 copy-start.2
  55.5 1.0 %shard_map.94 = bf16[195,384]{1,0:T(8,128)(2,1)} custom-call(f32[1,384]{1,0:T(1,128)S(1)} %reshape.13.gain_ref, f32[208,384]{1,0:T(8,128)S(1)} %shard_map.92.attended_ref, bf16[208,384]{1,0:T(8,128)(2,1)S(1)} %get-tuple-element.45.fast_ref, f32[8,208]{1,0:T(8,128)S(1)} %get-tuple-element.46.refs_0_, f32[8,208]{1,0:T(8,128)S(1)} %collective-permute-done.8.refs_1_), custom_call_target="tpu_custom_call" | custom-call | tf_op jit(solution)/shard_map/pallas_call | solution.py:415
  56.5 2.8 %all-to-all-done.2.rows_ref = bf16[16,32,128]{2,1,0:T(8,128)(2,1)S(1)} async-done(((bf16[16,32,128]{2,1,0:T(8,128)(2,1)}), bf16[16,32,128]{2,1,0:T(8,128)(2,1)S(1)}, u32[]{:S(2)}, u32[]{:S(2)}) %all-to-all-start.2) | async-done | bytes 131104 | tf_op jit(solution)/shard_map/all_to_all | solution.py:392
  59.3 0.0 copy-done.2
  59.3 0.8 %shard_map.95 = f32[3,3,32,128]{3,2,1,0:T(8,128)} custom-call(f32[3,3,32,128]{3,2,1,0:T(8,128)S(1)} %copy-done.2, bf16[16,32,128]{2,1,0:T(8,128)(2,1)S(1)} %all-to-all-done.2.rows_ref), custom_call_target="tpu_custom_call" | custom-call | flops 1000000 | bytes 1048576 | tf_op jit(solution)/shard_map/pallas_call | solution.py:395
  (1 shorter events, 0.0 us)
Async XLA Ops:
  0.6 0.9 %copy-start.1 = (f32[3,3,32,128]{3,2,1,0:T(8,128)S(1)}, f32[3,3,32,128]{3,2,1,0:T(8,128)}, u32[]{:S(2)}) copy-start(f32[3,3,32,128]{3,2,1,0:T(8,128)} %w_ref.3) | copy-start | bytes 442372
  2.3 8.2 %copy-start = (bf16[195,384]{1,0:T(8,128)(2,1)S(1)}, bf16[195,384]{1,0:T(8,128)(2,1)}, u32[]{:S(2)}) copy-start(bf16[195,384]{1,0:T(8,128)(2,1)} %q_ref.2) | copy-start | bytes 449284
  2.3 8.2 %copy-start.3 = (bf16[195,384]{1,0:T(8,128)(2,1)S(1)}, bf16[195,384]{1,0:T(8,128)(2,1)}, u32[]{:S(2)}) copy-start(bf16[195,384]{1,0:T(8,128)(2,1)} %k_ref.1) | copy-start | bytes 449284
  2.3 8.2 %copy-start.4 = (bf16[195,384]{1,0:T(8,128)(2,1)S(1)}, bf16[195,384]{1,0:T(8,128)(2,1)}, u32[]{:S(2)}) copy-start(bf16[195,384]{1,0:T(8,128)(2,1)} %v_ref.1) | copy-start | bytes 449284
  2.3 20.6 %all-to-all-start = ((bf16[16,3,32,128]{3,2,1,0:T(8,128)(2,1)}), bf16[16,3,32,128]{3,2,1,0:T(8,128)(2,1)S(1)}, u32[]{:S(2)}, u32[]{:S(2)}) async-start(bf16[16,3,32,128]{3,2,1,0:T(8,128)(2,1)} %shard_map.86.after), calls=%async_computation | async-start | bytes 786432 | tf_op jit(solution)/shard_map/all_to_all | solution.py:335
  9.8 0.7 %copy-start.5 = (f32[195,3]{0,1:T(4,128)S(1)}, f32[195,3]{0,1:T(4,128)}, u32[]{:S(2)}) copy-start(f32[195,3]{0,1:T(4,128)} %param.10) | copy-start | bytes 7024
  11.1 11.7 %collective-permute-start.1 = (bf16[208,384]{1,0:T(8,128)(2,1)S(1)}, bf16[208,384]{1,0:T(8,128)(2,1)S(1)}, u32[]{:S(2)}, u32[]{:S(2)}) collective-permute-start(bf16[208,384]{1,0:T(8,128)(2,1)S(1)} %get-tuple-element.28), channel_id=1, source_target_pairs={{2,4},{4,2},{6,0},{8,14},{10,12},{14,8},{18,20},{20,18},{22,16},{2... | collective-permute-start | bytes 479240 | tf_op jit(solution)/shard_map/ppermute | solution.py:345
  12.4 10.4 %collective-permute-start.2 = (bf16[208,384]{1,0:T(8,128)(2,1)S(1)}, bf16[208,384]{1,0:T(8,128)(2,1)S(1)}, u32[]{:S(2)}, u32[]{:S(2)}) collective-permute-start(bf16[208,384]{1,0:T(8,128)(2,1)S(1)} %get-tuple-element.29), channel_id=1, source_target_pairs={{0,2},{2,0},{6,4},{10,8},{12,14},{14,12},{16,18},{18,16},{22,20},{... | collective-permute-start | bytes 479240 | tf_op jit(solution)/shard_map/ppermute | solution.py:345
  17.0 8.1 %collective-permute-start = (bf16[208,256]{1,0:T(8,128)(2,1)S(1)}, bf16[208,256]{1,0:T(8,128)(2,1)S(1)}, u32[]{:S(2)}, u32[]{:S(2)}) collective-permute-start(bf16[208,256]{1,0:T(8,128)(2,1)S(1)} %get-tuple-element.26), channel_id=1, source_target_pairs={{0,4},{4,0},{6,2},{8,12},{10,14},{12,8},{16,20},{20,16},{22,18},{2... | collective-permute-start | bytes 319496 | tf_op jit(solution)/shard_map/ppermute | solution.py:345
  18.9 7.0 %collective-permute-start.3 = (bf16[208,128]{1,0:T(8,128)(2,1)S(1)}, bf16[208,128]{1,0:T(8,128)(2,1)S(1)}, u32[]{:S(2)}, u32[]{:S(2)}) collective-permute-start(bf16[208,128]{1,0:T(8,128)(2,1)S(1)} %get-tuple-element.33), channel_id=1, source_target_pairs={{0,4},{4,0},{6,2},{8,12},{10,14},{12,8},{16,20},{20,16},{22,18},{2... | collective-permute-start | bytes 159752 | tf_op jit(solution)/shard_map/ppermute | solution.py:347
  25.9 17.0 %collective-permute-start.6 = (bf16[512,128]{1,0:T(8,128)(2,1)S(1)}, bf16[512,128]{1,0:T(8,128)(2,1)S(1)}, u32[]{:S(2)}, u32[]{:S(2)}) collective-permute-start(bf16[512,128]{1,0:T(8,128)(2,1)S(1)} %get-tuple-element.41), channel_id=1, source_target_pairs={{0,12},{2,14},{12,0},{8,4},{18,30},{20,24},{28,16},{30,18},{24,20}... | collective-permute-start | bytes 393224 | tf_op jit(solution)/shard_map/ppermute | solution.py:373
  29.3 13.7 %collective-permute-start.4 = (bf16[512,128]{1,0:T(8,128)(2,1)S(1)}, bf16[512,128]{1,0:T(8,128)(2,1)S(1)}, u32[]{:S(2)}, u32[]{:S(2)}) collective-permute-start(bf16[512,128]{1,0:T(8,128)(2,1)S(1)} %get-tuple-element.39), channel_id=1, source_target_pairs={{2,30},{4,24},{12,16},{14,18},{8,20},{16,12},{18,14},{28,0},{24,4}... | collective-permute-start | bytes 393224 | tf_op jit(solution)/shard_map/ppermute | solution.py:373
  30.6 12.4 %collective-permute-start.5 = (bf16[512,128]{1,0:T(8,128)(2,1)S(1)}, bf16[512,128]{1,0:T(8,128)(2,1)S(1)}, u32[]{:S(2)}, u32[]{:S(2)}) collective-permute-start(bf16[512,128]{1,0:T(8,128)(2,1)S(1)} %get-tuple-element.40), channel_id=1, source_target_pairs={{0,16},{2,18},{4,20},{14,30},{8,24},{16,0},{20,4},{28,12},{30,14},... | collective-permute-start | bytes 393224 | tf_op jit(solution)/shard_map/ppermute | solution.py:373
  37.2 9.2 %all-to-all-start.1 = ((bf16[4,208,128]{2,1,0:T(8,128)(2,1)}), bf16[4,208,128]{2,1,0:T(8,128)(2,1)S(1)}, u32[]{:S(2)}, u32[]{:S(2)}) async-start(bf16[4,208,128]{2,1,0:T(8,128)(2,1)} %shard_map.90), calls=%async_computation.1 | async-start | bytes 425984 | tf_op jit(solution)/shard_map/all_to_all | solution.py:383
  40.6 12.8 %collective-permute-start.7 = (bf16[208,768]{1,0:T(8,128)(2,1)S(1)}, bf16[208,768]{1,0:T(8,128)(2,1)S(1)}, u32[]{:S(2)}, u32[]{:S(2)}) collective-permute-start(bf16[208,768]{1,0:T(8,128)(2,1)S(1)} %get-tuple-element.43.own_ref), channel_id=1, source_target_pairs={{0,2},{2,4},{4,6},{6,8},{8,10},{10,12},{12,14},{14,16},{16,18},{18... | collective-permute-start | bytes 958472 | tf_op jit(solution)/shard_map/ppermute | solution.py:386
  46.4 12.9 %all-to-all-start.2 = ((bf16[16,32,128]{2,1,0:T(8,128)(2,1)}), bf16[16,32,128]{2,1,0:T(8,128)(2,1)S(1)}, u32[]{:S(2)}, u32[]{:S(2)}) async-start(bf16[16,32,128]{2,1,0:T(8,128)(2,1)} %bitcast.2), calls=%async_computation.2 | async-start | bytes 262144 | tf_op jit(solution)/shard_map/all_to_all | solution.py:392
  51.3 2.0 %copy-start.6 = (f32[384]{0:T(512)S(1)}, f32[384]{0:T(512)}, u32[]{:S(2)}) copy-start(f32[384]{0:T(512)} %param.13) | copy-start | bytes 4612
  51.8 3.7 %collective-permute-start.8 = (f32[8,208]{1,0:T(8,128)S(1)}, f32[8,208]{1,0:T(8,128)S(1)}, u32[]{:S(2)}, u32[]{:S(2)}) collective-permute-start(f32[8,208]{1,0:T(8,128)S(1)} %get-tuple-element.46.refs_0_), channel_id=1, source_target_pairs={{0,1},{1,0},{2,3},{3,2},{4,5},{5,4},{6,7},{7,6},{8,9},{9,8},{10,11... | collective-permute-start | bytes 19976 | tf_op jit(solution)/shard_map/ppermute | solution.py:413
  55.5 3.8 %copy-start.2 = (f32[3,3,32,128]{3,2,1,0:T(8,128)S(1)}, f32[3,3,32,128]{3,2,1,0:T(8,128)}, u32[]{:S(2)}) copy-start(f32[3,3,32,128]{3,2,1,0:T(8,128)} %w_ref.3) | copy-start | bytes 442372

commit v3 on v1

--- a/solution.py
+++ b/solution.py
@@ -19,7 +19,6 @@
 f32 = jnp.float32
 bf16 = jnp.bfloat16
 VMEM_LIMIT = 24 * 1024 * 1024
-VMEM_MOST = 56 * 1024 * 1024
 
 
 def dot(a, b, contract, precision=None):
@@ -58,28 +57,33 @@
     return 0.5 * jnp.tanh(0.5 * x) + 0.5
 
 
-def prep_body(heads, group, tokens, update, w_ref, k_ref, v_ref, q_ref, rate_ref, *outs):
-    w_out, kv_out = outs[:2]
-    token_outs = outs[2:]
-    padded = kv_out.shape[0]
+def cast_body(heads, group, w_ref, w_out):
     slots = w_out.shape[0] // group
     for j in range(group):
         for m in range(3):
             low = w_ref[m, min(j, heads - 1)].astype(bf16)
             for z in range(slots):
                 w_out[z * group + j, m] = low
+
+
+def prep_body(
+    heads, group, tokens, after, update, rate_ref, k_ref, v_ref, q_ref, kv_out, *outs
+):
+    token_outs, targets = outs[:-1], outs[-1]
+    padded = kv_out.shape[0]
     place = position()
     valid = lax.broadcasted_iota(jnp.int32, (padded, 1), 0) < tokens
     none = jnp.zeros((), bf16)
     keep = update[...].astype(f32)
-    row = lax.broadcasted_iota(jnp.int32, (heads, HD), 0)
+    lane_head = lax.broadcasted_iota(jnp.int32, (heads, heads * HD), 1) // HD
+    row = lax.broadcasted_iota(jnp.int32, (heads, heads * HD), 0)
+    rate = dot(rate_ref[...], (row == lane_head).astype(f32), (0, 0), highest)[:padded]
+    targets[...] = jnp.where(valid, ((rate * keep) * v_ref[...].astype(f32)).astype(bf16), none)
     for d in range(group):
         head = jnp.minimum(place[1] ^ d, heads - 1)
         cols = pl.ds(pl.multiple_of(head * HD, HD), HD)
-        rate = dot(rate_ref[...], (row == head).astype(f32), (0, 0), highest)[:padded]
-        target = ((rate * keep) * v_ref[:, cols].astype(f32)).astype(bf16)
         token_outs[d][:, :HD] = jnp.where(valid, k_ref[:, cols], none)
-        token_outs[d][:, HD : 2 * HD] = jnp.where(valid, target, none)
+        token_outs[d][:, HD : 2 * HD] = targets[:, cols]
         token_outs[d][:, 2 * HD :] = jnp.where(valid, q_ref[:, cols], none)
     kv_out[:, : heads * HD] = jnp.where(valid, k_ref[...], none)
     kv_out[:, heads * HD :] = jnp.where(valid, v_ref[...], none)
@@ -132,11 +136,10 @@
     ]
 
 
-def apply_tokens(token_ref, w_ref, stage, act):
+def apply_tokens(query, w_ref, stage, act):
     hidden = act.shape[1]
     tall = 16
     w1, w3, w2 = (weight_rows(w_ref, m, 0, hidden) for m in range(3))
-    query = token_ref[:, 2 * HD :]
     stage[0] = dot(query, w1, (1, 1))
     stage[1] = dot(query, w3, (1, 1))
     for start in range(0, query.shape[0], tall):
@@ -157,7 +160,7 @@
     for m, grad in enumerate(gradients(token_refs, w_ref, *scratch)):
         grads[m] = grad
     for i, ref in enumerate(token_refs):
-        fast[i] = apply_tokens(ref, w_ref, staged.at[i % 2], acts.at[i % 2])
+        fast[i] = apply_tokens(ref[:, 2 * HD :], w_ref, staged.at[i % 2], acts.at[i % 2])
 
 
 def late_body(group, slots, token_ref, w_ref, early, *refs):
@@ -175,7 +178,9 @@
     place = position()
     for i, d in enumerate(early_slots):
         out[place[1] ^ d] = early[i]
-    out[place[1] ^ last] = apply_tokens(token_ref, w_ref, staged.at[0], acts.at[0])
+    out[place[1] ^ last] = apply_tokens(
+        token_ref[:, 2 * HD :], w_ref, staged.at[0], acts.at[0]
+    )
 
 
 def weight_rows(w_ref, m, start, block):
@@ -200,15 +205,30 @@
     return jnp.concatenate([high, low, high], axis=0)
 
 
-def ortho_body(*refs):
-    parts, out = refs[:-1], refs[-1]
+def ortho_body(heads, slots, *refs):
+    place = position()
+    matrix = lax.rem(place[0] - place[1] + heads * slots, slots)
+    owner = (place[1] < heads) & (matrix < 3)
+
+    @pl.when(owner)
+    def _():
+        orthogonalize(refs[:-1], refs[-1])
+
+    @pl.when(jnp.logical_not(owner))
+    def _():
+        refs[-1][...] = jnp.zeros(refs[-1].shape, refs[-1].dtype)
+
+
+def orthogonalize(parts, out):
     grads = parts[0][...].astype(f32)
     for part in parts[1:]:
         grads = grads + part[...].astype(f32)
     eye = (
         lax.broadcasted_iota(jnp.int32, (HD, HD), 0) == lax.broadcasted_iota(jnp.int32, (HD, HD), 1)
     ).astype(f32)
-    raw = dot(grads, grads, (0, 0), highest)
+    both = jnp.concatenate(parts_of(grads), axis=1)
+    blocks = dot(both, both, (0, 0))
+    raw = (blocks[:HD, HD:] + blocks[HD:, :HD]) + blocks[:HD, :HD]
     square = jnp.sum(jnp.sum(raw * eye, axis=0, keepdims=True), axis=1, keepdims=True)
     scale = lax.rsqrt(square + epsilon)
     gram = raw * scale * scale
@@ -219,8 +239,9 @@
         right = right_of(mix)
         if step < NS_STEPS - 1:
             gram = dot(left_of(dot(left_of(gram), right, (1, 0))), right, (1, 0))
-        total = mix if total is None else dot(left_of(total), right, (1, 0))
-    out[...] = dot(left_of(grads * scale), right_of(total), (1, 0)).astype(out.dtype)
+            total = mix if total is None else dot(left_of(total), right, (1, 0))
+    ortho = dot(left_of(grads * scale), right_of(total), (1, 0))
+    out[...] = dot(left_of(ortho), right, (1, 0)).astype(out.dtype)
 
 
 def finish_body(slots, group, w_ref, rows_ref, out):
@@ -290,19 +311,22 @@
         return pl.BlockSpec(shape, lambda i: (0,) * len(shape))
 
     low_shape = (count, 3, rows_local, HD)
+    low = call(
+        functools.partial(cast_body, heads, group), sds(low_shape, bf16), flops=1e6
+    )(fast_weights)
     prepared = pl.pallas_call(
         functools.partial(prep_body, heads, group, tokens),
         grid=(1,),
-        out_shape=[sds(low_shape, bf16), sds((padded, 2 * span), bf16)]
+        out_shape=[sds((padded, 2 * span), bf16)]
         + [sds((padded, 3 * HD), bf16)] * group,
-        in_specs=[whole(1, 1), whole(*fast_weights.shape)]
-        + [whole(padded, span)] * 3
-        + [whole(heads, -(-padded // 128) * 128)],
-        out_specs=[whole(*low_shape), whole(padded, 2 * span)]
-        + [whole(padded, 3 * HD)] * group,
-        compiler_params=pltpu.CompilerParams(vmem_limit_bytes=VMEM_MOST),
-    )(frame_update.reshape(1, 1), fast_weights, keys, values, queries, rates.T)
-    low, kv_own, token_slots = prepared[0], prepared[1], list(prepared[2:])
+        in_specs=[pl.BlockSpec(memory_space=pl.ANY), whole(1, 1)]
+        + [whole(heads, -(-padded // 128) * 128)]
+        + [whole(padded, span)] * 3,
+        out_specs=[whole(padded, 2 * span)] + [whole(padded, 3 * HD)] * group,
+        scratch_shapes=[pltpu.VMEM((padded, span), bf16)],
+        compiler_params=pltpu.CompilerParams(vmem_limit_bytes=VMEM_LIMIT),
+    )(low, frame_update.reshape(1, 1), rates.T, keys, values, queries)
+    kv_own, *token_slots = prepared
 
     weights = lax.all_to_all(low, ("z", "grp"), 0, 0, tiled=True)
     if rows_local % 16:
@@ -351,7 +375,7 @@
     ring = [(i, i + 1) for i in range(count - 1)]
     kv_back = lax.ppermute(kv_own, ("z", "grp"), ring)
 
-    ortho = call(ortho_body, sds((hidden, HD), bf16), flops=1e9)(
+    ortho = call(functools.partial(ortho_body, heads, nz), sds((hidden, HD), bf16), flops=1e9)(
         *(partials[d] for d in served(nz))
     )
     queries, ortho = lax.optimization_barrier((queries, ortho))

time: 60.9 us -> 59 us (0.969)
  Pallas kernels: 14.2 us -> 12.5 us
  local copies, waits for them, and re-layouts: 0.04 us -> 0.93 us
  starting transfers between devices: 36.5 us -> 35.7 us
    pallas_call x1, Pallas kernels: 2.79 us -> 0.62 us  [on_device(): pl.pallas_call(functools.partial(prep_body, heads, group, tokens), grid=(...]
    unnamed x16 -> x14, local copies, waits for them, and re-layouts: 0.04 us -> 0.93 us
    pallas_call x1 -> x2, Pallas kernels: 3.67 us -> 4.21 us  [the longest x1 3.43 us: on_device(): call(functools.partial(ortho_body, heads, nz), sds((hidden, HD), bf16), f...]
  transfers between devices with their start and end apart: 11 -> 11, of which waited for: 5 -> 5; matrix products, arithmetic and copies ran while one was open for 0% -> 0% of each run, Pallas kernels for 16% -> 17%
where the time goes in v3:
time: 59 us; the launch traced here: 58.4 us
  starting transfers between devices  35.7 us (61%)
  Pallas kernels  12.5 us (21%)
  waiting for transfers between devices  7.76 us (13%)
  between operations  1.48 us (3%)
  local copies, waits for them, and re-layouts  0.93 us (2%)
    ppermute x3, starting transfers between devices, on_device(): partials[d] = lax.ppermute(partials[d], ('z', 'grp'), pairs)  8.53 us
    ppermute x3, starting transfers between devices, on_device(): token_slots[d] = lax.ppermute(token_slots[d], 'grp', pairs)  7.77 us
    all_to_all x1, starting transfers between devices, on_device(): weights = lax.all_to_all(low, ('z', 'grp'), 0, 0, tiled=True)  7.49 us
    all_to_all x1, starting transfers between devices, on_device(): lax.all_to_all(ortho.reshape(count, rows_local, HD), ('z', 'grp'), 0, 0,...  4.61 us
    pallas_call x1, Pallas kernels, on_device(): call(functools.partial(ortho_body, heads, nz), sds((hidden, HD), bf16), f...  3.43 us
    all_to_all x1, starting transfers between devices, on_device(): fast_slots = lax.all_to_all(fast_slots, 'grp', 0, 0, tiled=True)  3.37 us
    all_to_all x1, waiting for transfers between devices, on_device(): lax.all_to_all(ortho.reshape(count, rows_local, HD), ('z', 'grp'), 0, 0,...  2.8 us
    ppermute x1, starting transfers between devices, on_device(): kv_back = lax.ppermute(kv_own, ('z', 'grp'), ring)  2.38 us
  transfers between devices with their start and end apart: 11, of which 5 were waited for; matrix products, arithmetic and copies ran while one was open for 0% of the time, Pallas kernels for 17%

profile of v3, /device:TPU:0, one launch (start us, length us, event | category | flops | bytes accessed | tf_op | source)
XLA Modules:
  0.0 58.4 jit_solution(12645879649869745527)
XLA Ops:
  0.6 0.0 copy-start.1
  0.6 0.9 %copy-done.1 = f32[3,3,32,128]{3,2,1,0:T(8,128)S(1)} copy-done((f32[3,3,32,128]{3,2,1,0:T(8,128)S(1)}, f32[3,3,32,128]{3,2,1,0:T(8,128)}, u32[]{:S(2)}) %copy-start.1) | copy-done | bytes 147480
  1.5 0.8 %shard_map.86.after = bf16[16,3,32,128]{3,2,1,0:T(8,128)(2,1)} custom-call(f32[3,3,32,128]{3,2,1,0:T(8,128)S(1)} %copy-done.1), custom_call_target="tpu_custom_call" | custom-call | flops 1000000 | bytes 1048576 | tf_op jit(solution)/shard_map/pallas_call | solution.py:314
  2.3 0.0 copy-start
  2.3 0.0 copy-start.3
  2.3 0.0 copy-start.4
  2.3 7.5 %all-to-all-start = ((bf16[16,3,32,128]{3,2,1,0:T(8,128)(2,1)}), bf16[16,3,32,128]{3,2,1,0:T(8,128)(2,1)S(1)}, u32[]{:S(2)}, u32[]{:S(2)}) async-start(bf16[16,3,32,128]{3,2,1,0:T(8,128)(2,1)} %shard_map.86.after), calls=%async_computation | async-start | bytes 786432 | tf_op jit(solution)/shard_map/all_to_all | solution.py:331
  9.8 0.0 copy-start.5
  10.5 0.0 copy-done
  10.5 0.0 copy-done.3
  10.5 0.0 copy-done.4
  10.5 0.0 copy-done.5
  10.5 0.6 %shard_map.87 = (bf16[208,768]{1,0:T(8,128)(2,1)S(1)}, bf16[208,384]{1,0:T(8,128)(2,1)S(1)}, bf16[208,384]{1,0:T(8,128)(2,1)S(1)}, bf16[208,384]{1,0:T(8,128)(2,1)S(1)}, bf16[208,384]{1,0:T(8,128)(2,1)S(1)}) custom-call(bf16[16,3,32,128]{3,2,1,0:T(8,128)(2,1)} %shard_map.86.after, s32[1,1]{1,0:T(1,128)} %bitcast.3.update, f32[3,195]{1,0:T(4,128)S(1)} %bitcast.4, ...), custom_call_target="tpu_custom_call" | custom-call | tf_op jit(solution)/shard_map/pallas_call | solution.py:317
  11.2 1.3 %collective-permute-start.1 = (bf16[208,384]{1,0:T(8,128)(2,1)S(1)}, bf16[208,384]{1,0:T(8,128)(2,1)S(1)}, u32[]{:S(2)}, u32[]{:S(2)}) collective-permute-start(bf16[208,384]{1,0:T(8,128)(2,1)S(1)} %get-tuple-element.25), channel_id=1, source_target_pairs={{2,4},{4,2},{6,0},{3,5},{5,3},{7,1},{10,12},{12,10},{14,8},{11,13}... | collective-permute-start | bytes 479240 | tf_op jit(solution)/shard_map/ppermute | solution.py:336
  12.5 4.6 %collective-permute-start.2 = (bf16[208,384]{1,0:T(8,128)(2,1)S(1)}, bf16[208,384]{1,0:T(8,128)(2,1)S(1)}, u32[]{:S(2)}, u32[]{:S(2)}) collective-permute-start(bf16[208,384]{1,0:T(8,128)(2,1)S(1)} %get-tuple-element.26), channel_id=1, source_target_pairs={{0,2},{2,0},{6,4},{1,3},{3,1},{7,5},{8,10},{10,8},{14,12},{9,11},{... | collective-permute-start | bytes 479240 | tf_op jit(solution)/shard_map/ppermute | solution.py:336
  17.0 1.9 %collective-permute-start = (bf16[208,384]{1,0:T(8,128)(2,1)S(1)}, bf16[208,384]{1,0:T(8,128)(2,1)S(1)}, u32[]{:S(2)}, u32[]{:S(2)}) collective-permute-start(bf16[208,384]{1,0:T(8,128)(2,1)S(1)} %get-tuple-element.23), channel_id=1, source_target_pairs={{0,4},{4,0},{6,2},{1,5},{5,1},{7,3},{8,12},{12,8},{14,10},{9,13},{... | collective-permute-start | bytes 479240 | tf_op jit(solution)/shard_map/ppermute | solution.py:336
  19.0 0.9 %collective-permute-done.1.refs_1_ = bf16[208,384]{1,0:T(8,128)(2,1)S(1)} collective-permute-done((bf16[208,384]{1,0:T(8,128)(2,1)S(1)}, bf16[208,384]{1,0:T(8,128)(2,1)S(1)}, u32[]{:S(2)}, u32[]{:S(2)}) %collective-permute-start.1) | collective-permute-done | bytes 159776 | tf_op jit(solution)/shard_map/ppermute | solution.py:336
  19.9 0.0 collective-permute-done.2.refs_2_
  19.9 2.2 %all-to-all-done.refs_3_.w_ref = bf16[16,3,32,128]{3,2,1,0:T(8,128)(2,1)S(1)} async-done(((bf16[16,3,32,128]{3,2,1,0:T(8,128)(2,1)}), bf16[16,3,32,128]{3,2,1,0:T(8,128)(2,1)S(1)}, u32[]{:S(2)}, u32[]{:S(2)}) %all-to-all-start) | async-done | bytes 393248 | tf_op jit(solution)/shard_map/all_to_all | solution.py:331
  22.1 2.2 %shard_map.88 = (f32[3,512,128]{2,1,0:T(8,128)S(1)}, bf16[3,208,128]{2,1,0:T(8,128)(2,1)S(1)}) custom-call(bf16[208,384]{1,0:T(8,128)(2,1)S(1)} %get-tuple-element.24.refs_0_, bf16[208,384]{1,0:T(8,128)(2,1)S(1)} %collective-permute-done.1.refs_1_, bf16[208,384]{1,0:T(8,128)(2,1)S(1)} %collective-permute-done.2.refs_2_, ...), custom_call_target="tpu_custom_call" | custom-call | flops 1000000000 | bytes 1048576 | tf_op jit(solution)/shard_map/pallas_call | solution.py:340
  24.3 1.0 %collective-permute-done.token_ref = bf16[208,384]{1,0:T(8,128)(2,1)S(1)} collective-permute-done((bf16[208,384]{1,0:T(8,128)(2,1)S(1)}, bf16[208,384]{1,0:T(8,128)(2,1)S(1)}, u32[]{:S(2)}, u32[]{:S(2)}) %collective-permute-start) | collective-permute-done | bytes 159776 | tf_op jit(solution)/shard_map/ppermute | solution.py:336
  25.4 0.8 %shard_map.89 = (bf16[512,128]{1,0:T(8,128)(2,1)S(1)}, bf16[512,128]{1,0:T(8,128)(2,1)S(1)}, bf16[512,128]{1,0:T(8,128)(2,1)S(1)}, bf16[512,128]{1,0:T(8,128)(2,1)S(1)}) custom-call(bf16[208,384]{1,0:T(8,128)(2,1)S(1)} %collective-permute-done.token_ref, bf16[16,3,32,128]{3,2,1,0:T(8,128)(2,1)S(1)} %all-to-all-done.refs_3_.w_ref, ...), custom_call_target="tpu_custom_call" | custom-call | flops 500000000 | bytes 1048576 | tf_op jit(solution)/shard_map/pallas_call | solution.py:347
  26.1 1.3 %collective-permute-start.3 = (bf16[512,128]{1,0:T(8,128)(2,1)S(1)}, bf16[512,128]{1,0:T(8,128)(2,1)S(1)}, u32[]{:S(2)}, u32[]{:S(2)}) collective-permute-start(bf16[512,128]{1,0:T(8,128)(2,1)S(1)} %get-tuple-element.33), channel_id=1, source_target_pairs={{2,26},{4,28},{8,16},{10,18},{12,20},{16,8},{18,10},{24,0},{28,4},... | collective-permute-start | bytes 393224 | tf_op jit(solution)/shard_map/ppermute | solution.py:363
  27.4 5.3 %collective-permute-start.4 = (bf16[512,128]{1,0:T(8,128)(2,1)S(1)}, bf16[512,128]{1,0:T(8,128)(2,1)S(1)}, u32[]{:S(2)}, u32[]{:S(2)}) collective-permute-start(bf16[512,128]{1,0:T(8,128)(2,1)S(1)} %get-tuple-element.34), channel_id=1, source_target_pairs={{0,16},{2,18},{4,20},{10,26},{12,28},{16,0},{20,4},{24,8},{26,10},... | collective-permute-start | bytes 393224 | tf_op jit(solution)/shard_map/ppermute | solution.py:363
  32.8 1.9 %collective-permute-start.5 = (bf16[512,128]{1,0:T(8,128)(2,1)S(1)}, bf16[512,128]{1,0:T(8,128)(2,1)S(1)}, u32[]{:S(2)}, u32[]{:S(2)}) collective-permute-start(bf16[512,128]{1,0:T(8,128)(2,1)S(1)} %get-tuple-element.35), channel_id=1, source_target_pairs={{0,8},{2,10},{8,0},{12,4},{18,26},{20,28},{24,16},{26,18},{28,20},... | collective-permute-start | bytes 393224 | tf_op jit(solution)/shard_map/ppermute | solution.py:363
  34.7 1.1 %shard_map.90 = bf16[4,208,128]{2,1,0:T(8,128)(2,1)} custom-call(bf16[208,384]{1,0:T(8,128)(2,1)S(1)} %collective-permute-done.token_ref, bf16[16,3,32,128]{3,2,1,0:T(8,128)(2,1)S(1)} %all-to-all-done.refs_3_.w_ref, bf16[3,208,128]{2,1,0:T(8,128)(2,1)S(1)} %get-tuple-element.31.early), custom_call_target="tpu_custom_call" | custom-call | flops 1000 | bytes 1024 | tf_op jit(solution)/shard_map/pallas_call | solution.py:365
  35.8 3.4 %all-to-all-start.1 = ((bf16[4,208,128]{2,1,0:T(8,128)(2,1)}), bf16[4,208,128]{2,1,0:T(8,128)(2,1)S(1)}, u32[]{:S(2)}, u32[]{:S(2)}) async-start(bf16[4,208,128]{2,1,0:T(8,128)(2,1)} %shard_map.90), calls=%async_computation.1 | async-start | bytes 425984 | tf_op jit(solution)/shard_map/all_to_all | solution.py:373
  39.2 2.4 %collective-permute-start.6 = (bf16[208,768]{1,0:T(8,128)(2,1)S(1)}, bf16[208,768]{1,0:T(8,128)(2,1)S(1)}, u32[]{:S(2)}, u32[]{:S(2)}) collective-permute-start(bf16[208,768]{1,0:T(8,128)(2,1)S(1)} %get-tuple-element.37.own_ref), channel_id=1, source_target_pairs={{0,2},{2,4},{4,6},{6,8},{8,10},{10,12},{12,14},{14,16},{16,18},{18... | collective-permute-start | bytes 958472 | tf_op jit(solution)/shard_map/ppermute | solution.py:376
  41.6 0.0 collective-permute-done.3.refs_1_
  41.6 0.0 collective-permute-done.4.refs_2_
  41.6 0.0 collective-permute-done.5.refs_3_
  41.6 3.4 %shard_map.91 = bf16[512,128]{1,0:T(8,128)(2,1)} custom-call(bf16[512,128]{1,0:T(8,128)(2,1)S(1)} %get-tuple-element.32.refs_0_, bf16[512,128]{1,0:T(8,128)(2,1)S(1)} %collective-permute-done.3.refs_1_, bf16[512,128]{1,0:T(8,128)(2,1)S(1)} %collective-permute-done.4.refs_2_, bf16[512,128]{1,0:T(8,128)(2,1)S(1)} %collective-permute-done.5.refs_3_), custom_call_target="tpu_custom_call" | custom-call | flops 1000000000 | bytes 1048576 | tf_op jit(solution)/shard_map/pallas_call | solution.py:378
  45.0 0.0 all-to-all-done.1.slots
  45.0 4.6 %all-to-all-start.2 = ((bf16[16,32,128]{2,1,0:T(8,128)(2,1)}), bf16[16,32,128]{2,1,0:T(8,128)(2,1)S(1)}, u32[]{:S(2)}, u32[]{:S(2)}) async-start(bf16[16,32,128]{2,1,0:T(8,128)(2,1)} %bitcast.2), calls=%async_computation.2 | async-start | bytes 262144 | tf_op jit(solution)/shard_map/all_to_all | solution.py:382
  49.7 0.0 copy-start.6
  49.7 0.4 shard_map.93
  50.1 1.6 %collective-permute-start.7 = (f32[8,208]{1,0:T(8,128)S(1)}, f32[8,208]{1,0:T(8,128)S(1)}, u32[]{:S(2)}, u32[]{:S(2)}) collective-permute-start(f32[8,208]{1,0:T(8,128)S(1)} %get-tuple-element.40.refs_0_), channel_id=1, source_target_pairs={{0,1},{1,0},{2,3},{3,2},{4,5},{5,4},{6,7},{7,6},{8,9},{9,8},{10,11... | collective-permute-start | bytes 19976 | tf_op jit(solution)/shard_map/ppermute | solution.py:403
  51.7 0.0 copy-done.6
  51.7 0.0 collective-permute-done.6.back_ref
  51.7 1.3 %shard_map.92.attended_ref = f32[208,384]{1,0:T(8,128)S(1)} custom-call(bf16[195,384]{1,0:T(8,128)(2,1)S(1)} %copy-done, bf16[208,768]{1,0:T(8,128)(2,1)S(1)} %get-tuple-element.37.own_ref, bf16[208,768]{1,0:T(8,128)(2,1)S(1)} %collective-permute-done.6.back_ref), custom_call_target="tpu_custom_call" | custom-call | tf_op jit(solution)/shard_map/pallas_call | solution.py:389
  53.0 0.8 %collective-permute-done.7.refs_1_ = f32[8,208]{1,0:T(8,128)S(1)} collective-permute-done((f32[8,208]{1,0:T(8,128)S(1)}, f32[8,208]{1,0:T(8,128)S(1)}, u32[]{:S(2)}, u32[]{:S(2)}) %collective-permute-start.7) | collective-permute-done | bytes 6688 | tf_op jit(solution)/shard_map/ppermute | solution.py:403
  53.8 0.0 copy-start.2
  53.8 1.0 %shard_map.94 = bf16[195,384]{1,0:T(8,128)(2,1)} custom-call(f32[1,384]{1,0:T(1,128)S(1)} %reshape.13.gain_ref, f32[208,384]{1,0:T(8,128)S(1)} %shard_map.92.attended_ref, bf16[208,384]{1,0:T(8,128)(2,1)S(1)} %get-tuple-element.39.fast_ref, f32[8,208]{1,0:T(8,128)S(1)} %get-tuple-element.40.refs_0_, f32[8,208]{1,0:T(8,128)S(1)} %collective-permute-done.7.refs_1_), custom_call_target="tpu_custom_call" | custom-call | tf_op jit(solution)/shard_map/pallas_call | solution.py:405
  54.8 2.8 %all-to-all-done.2.rows_ref = bf16[16,32,128]{2,1,0:T(8,128)(2,1)S(1)} async-done(((bf16[16,32,128]{2,1,0:T(8,128)(2,1)}), bf16[16,32,128]{2,1,0:T(8,128)(2,1)S(1)}, u32[]{:S(2)}, u32[]{:S(2)}) %all-to-all-start.2) | async-done | bytes 131104 | tf_op jit(solution)/shard_map/all_to_all | solution.py:382
  57.6 0.0 copy-done.2
  57.6 0.8 %shard_map.95 = f32[3,3,32,128]{3,2,1,0:T(8,128)} custom-call(f32[3,3,32,128]{3,2,1,0:T(8,128)S(1)} %copy-done.2, bf16[16,32,128]{2,1,0:T(8,128)(2,1)S(1)} %all-to-all-done.2.rows_ref), custom_call_target="tpu_custom_call" | custom-call | flops 1000000 | bytes 1048576 | tf_op jit(solution)/shard_map/pallas_call | solution.py:385
  (1 shorter events, 0.0 us)
Async XLA Ops:
  0.6 0.9 %copy-start.1 = (f32[3,3,32,128]{3,2,1,0:T(8,128)S(1)}, f32[3,3,32,128]{3,2,1,0:T(8,128)}, u32[]{:S(2)}) copy-start(f32[3,3,32,128]{3,2,1,0:T(8,128)} %w_ref.3) | copy-start | bytes 442372
  2.3 8.2 %copy-start = (bf16[195,384]{1,0:T(8,128)(2,1)S(1)}, bf16[195,384]{1,0:T(8,128)(2,1)}, u32[]{:S(2)}) copy-start(bf16[195,384]{1,0:T(8,128)(2,1)} %q_ref.2) | copy-start | bytes 449284
  2.3 8.2 %copy-start.3 = (bf16[195,384]{1,0:T(8,128)(2,1)S(1)}, bf16[195,384]{1,0:T(8,128)(2,1)}, u32[]{:S(2)}) copy-start(bf16[195,384]{1,0:T(8,128)(2,1)} %k_ref.1) | copy-start | bytes 449284
  2.3 8.2 %copy-start.4 = (bf16[195,384]{1,0:T(8,128)(2,1)S(1)}, bf16[195,384]{1,0:T(8,128)(2,1)}, u32[]{:S(2)}) copy-start(bf16[195,384]{1,0:T(8,128)(2,1)} %v_ref.1) | copy-start | bytes 449284
  2.3 19.8 %all-to-all-start = ((bf16[16,3,32,128]{3,2,1,0:T(8,128)(2,1)}), bf16[16,3,32,128]{3,2,1,0:T(8,128)(2,1)S(1)}, u32[]{:S(2)}, u32[]{:S(2)}) async-start(bf16[16,3,32,128]{3,2,1,0:T(8,128)(2,1)} %shard_map.86.after), calls=%async_computation | async-start | bytes 786432 | tf_op jit(solution)/shard_map/all_to_all | solution.py:331
  9.8 0.7 %copy-start.5 = (f32[195,3]{0,1:T(4,128)S(1)}, f32[195,3]{0,1:T(4,128)}, u32[]{:S(2)}) copy-start(f32[195,3]{0,1:T(4,128)} %param.10) | copy-start | bytes 7024
  11.2 8.7 %collective-permute-start.1 = (bf16[208,384]{1,0:T(8,128)(2,1)S(1)}, bf16[208,384]{1,0:T(8,128)(2,1)S(1)}, u32[]{:S(2)}, u32[]{:S(2)}) collective-permute-start(bf16[208,384]{1,0:T(8,128)(2,1)S(1)} %get-tuple-element.25), channel_id=1, source_target_pairs={{2,4},{4,2},{6,0},{3,5},{5,3},{7,1},{10,12},{12,10},{14,8},{11,13}... | collective-permute-start | bytes 479240 | tf_op jit(solution)/shard_map/ppermute | solution.py:336
  12.5 7.4 %collective-permute-start.2 = (bf16[208,384]{1,0:T(8,128)(2,1)S(1)}, bf16[208,384]{1,0:T(8,128)(2,1)S(1)}, u32[]{:S(2)}, u32[]{:S(2)}) collective-permute-start(bf16[208,384]{1,0:T(8,128)(2,1)S(1)} %get-tuple-element.26), channel_id=1, source_target_pairs={{0,2},{2,0},{6,4},{1,3},{3,1},{7,5},{8,10},{10,8},{14,12},{9,11},{... | collective-permute-start | bytes 479240 | tf_op jit(solution)/shard_map/ppermute | solution.py:336
  17.0 8.3 %collective-permute-start = (bf16[208,384]{1,0:T(8,128)(2,1)S(1)}, bf16[208,384]{1,0:T(8,128)(2,1)S(1)}, u32[]{:S(2)}, u32[]{:S(2)}) collective-permute-start(bf16[208,384]{1,0:T(8,128)(2,1)S(1)} %get-tuple-element.23), channel_id=1, source_target_pairs={{0,4},{4,0},{6,2},{1,5},{5,1},{7,3},{8,12},{12,8},{14,10},{9,13},{... | collective-permute-start | bytes 479240 | tf_op jit(solution)/shard_map/ppermute | solution.py:336
  26.1 15.4 %collective-permute-start.3 = (bf16[512,128]{1,0:T(8,128)(2,1)S(1)}, bf16[512,128]{1,0:T(8,128)(2,1)S(1)}, u32[]{:S(2)}, u32[]{:S(2)}) collective-permute-start(bf16[512,128]{1,0:T(8,128)(2,1)S(1)} %get-tuple-element.33), channel_id=1, source_target_pairs={{2,26},{4,28},{8,16},{10,18},{12,20},{16,8},{18,10},{24,0},{28,4},... | collective-permute-start | bytes 393224 | tf_op jit(solution)/shard_map/ppermute | solution.py:363
  27.4 14.2 %collective-permute-start.4 = (bf16[512,128]{1,0:T(8,128)(2,1)S(1)}, bf16[512,128]{1,0:T(8,128)(2,1)S(1)}, u32[]{:S(2)}, u32[]{:S(2)}) collective-permute-start(bf16[512,128]{1,0:T(8,128)(2,1)S(1)} %get-tuple-element.34), channel_id=1, source_target_pairs={{0,16},{2,18},{4,20},{10,26},{12,28},{16,0},{20,4},{24,8},{26,10},... | collective-permute-start | bytes 393224 | tf_op jit(solution)/shard_map/ppermute | solution.py:363
  32.8 8.8 %collective-permute-start.5 = (bf16[512,128]{1,0:T(8,128)(2,1)S(1)}, bf16[512,128]{1,0:T(8,128)(2,1)S(1)}, u32[]{:S(2)}, u32[]{:S(2)}) collective-permute-start(bf16[512,128]{1,0:T(8,128)(2,1)S(1)} %get-tuple-element.35), channel_id=1, source_target_pairs={{0,8},{2,10},{8,0},{12,4},{18,26},{20,28},{24,16},{26,18},{28,20},... | collective-permute-start | bytes 393224 | tf_op jit(solution)/shard_map/ppermute | solution.py:363
  35.8 9.2 %all-to-all-start.1 = ((bf16[4,208,128]{2,1,0:T(8,128)(2,1)}), bf16[4,208,128]{2,1,0:T(8,128)(2,1)S(1)}, u32[]{:S(2)}, u32[]{:S(2)}) async-start(bf16[4,208,128]{2,1,0:T(8,128)(2,1)} %shard_map.90), calls=%async_computation.1 | async-start | bytes 425984 | tf_op jit(solution)/shard_map/all_to_all | solution.py:373
  39.2 12.5 %collective-permute-start.6 = (bf16[208,768]{1,0:T(8,128)(2,1)S(1)}, bf16[208,768]{1,0:T(8,128)(2,1)S(1)}, u32[]{:S(2)}, u32[]{:S(2)}) collective-permute-start(bf16[208,768]{1,0:T(8,128)(2,1)S(1)} %get-tuple-element.37.own_ref), channel_id=1, source_target_pairs={{0,2},{2,4},{4,6},{6,8},{8,10},{10,12},{12,14},{14,16},{16,18},{18... | collective-permute-start | bytes 958472 | tf_op jit(solution)/shard_map/ppermute | solution.py:376
  45.0 12.6 %all-to-all-start.2 = ((bf16[16,32,128]{2,1,0:T(8,128)(2,1)}), bf16[16,32,128]{2,1,0:T(8,128)(2,1)S(1)}, u32[]{:S(2)}, u32[]{:S(2)}) async-start(bf16[16,32,128]{2,1,0:T(8,128)(2,1)} %bitcast.2), calls=%async_computation.2 | async-start | bytes 262144 | tf_op jit(solution)/shard_map/all_to_all | solution.py:382
  49.7 2.0 %copy-start.6 = (f32[384]{0:T(512)S(1)}, f32[384]{0:T(512)}, u32[]{:S(2)}) copy-start(f32[384]{0:T(512)} %param.13) | copy-start | bytes 4612
  50.1 3.7 %collective-permute-start.7 = (f32[8,208]{1,0:T(8,128)S(1)}, f32[8,208]{1,0:T(8,128)S(1)}, u32[]{:S(2)}, u32[]{:S(2)}) collective-permute-start(f32[8,208]{1,0:T(8,128)S(1)} %get-tuple-element.40.refs_0_), channel_id=1, source_target_pairs={{0,1},{1,0},{2,3},{3,2},{4,5},{5,4},{6,7},{7,6},{8,9},{9,8},{10,11... | collective-permute-start | bytes 19976 | tf_op jit(solution)/shard_map/ppermute | solution.py:403
  53.8 3.8 %copy-start.2 = (f32[3,3,32,128]{3,2,1,0:T(8,128)S(1)}, f32[3,3,32,128]{3,2,1,0:T(8,128)}, u32[]{:S(2)}) copy-start(f32[3,3,32,128]{3,2,1,0:T(8,128)} %w_ref.3) | copy-start | bytes 442372

commit v4 on v3

--- a/solution.py
+++ b/solution.py
@@ -352,7 +352,7 @@
         )(token_slots[last], weights, early_grads)
     )
     weights, partials[0] = lax.optimization_barrier((weights, partials[0]))
-    for d in served(nz)[1:]:
+    def summed(d, partial):
         pairs = []
         for z in range(nz):
             pairs += [
@@ -360,7 +360,10 @@
                 for j in range(heads)
                 if ((z ^ d) - j) % nz < 3
             ]
-        partials[d] = lax.ppermute(partials[d], ("z", "grp"), pairs)
+        return lax.ppermute(partial, ("z", "grp"), pairs)
+
+    for d in served(nz)[1:-1]:
+        partials[d] = summed(d, partials[d])
 
     fast_slots = call(
         functools.partial(late_apply_body, early_slots, last),
@@ -369,7 +372,8 @@
         flops=1e3,
         moved=1024,
     )(token_slots[last], weights, early_fast)
-    kv_own, partials[0], fast_slots = lax.optimization_barrier((kv_own, partials[0], fast_slots))
+    kv_own, partials[1], fast_slots = lax.optimization_barrier((kv_own, partials[1], fast_slots))
+    partials[1] = summed(1, partials[1])
     fast_slots = lax.all_to_all(fast_slots, "grp", 0, 0, tiled=True)
 
     ring = [(i, i + 1) for i in range(count - 1)]

time: 59 us -> 59.6 us (1.010)
  waiting for transfers between devices: 7.76 us -> 8.79 us
    all_to_all x1, starting transfers between devices: 4.61 us -> 3.51 us  [on_device(): lax.all_to_all(ortho.reshape(count, rows_local, HD), ('z', 'grp'), 0, 0,...]
    ppermute x3, waiting for transfers between devices: 0.01 us -> 1.08 us  [summed(): return lax.ppermute(partial, ('z', 'grp'), pairs)]
    ppermute x3, starting transfers between devices: 8.53 us -> 9.2 us  [summed(): return lax.ppermute(partial, ('z', 'grp'), pairs)]
  transfers between devices with their start and end apart: 11 -> 11, of which waited for: 5 -> 6; matrix products, arithmetic and copies ran while one was open for 0% -> 0% of each run, Pallas kernels for 17% -> 15%
where the time goes in v4:
time: 59.6 us; the launch traced here: 59 us
  starting transfers between devices  35.3 us (59%)
  Pallas kernels  12.5 us (21%)
  waiting for transfers between devices  8.79 us (15%)
  between operations  1.48 us (2%)
  local copies, waits for them, and re-layouts  0.93 us (2%)
    ppermute x3, starting transfers between devices, summed(): return lax.ppermute(partial, ('z', 'grp'), pairs)  9.2 us
    ppermute x3, starting transfers between devices, on_device(): token_slots[d] = lax.ppermute(token_slots[d], 'grp', pairs)  7.77 us
    all_to_all x1, starting transfers between devices, on_device(): weights = lax.all_to_all(low, ('z', 'grp'), 0, 0, tiled=True)  7.49 us
    all_to_all x1, starting transfers between devices, on_device(): lax.all_to_all(ortho.reshape(count, rows_local, HD), ('z', 'grp'), 0, 0,...  3.51 us
    pallas_call x1, Pallas kernels, on_device(): call(functools.partial(ortho_body, heads, nz), sds((hidden, HD), bf16), f...  3.42 us
    all_to_all x1, starting transfers between devices, on_device(): fast_slots = lax.all_to_all(fast_slots, 'grp', 0, 0, tiled=True)  3.39 us
    all_to_all x1, waiting for transfers between devices, on_device(): lax.all_to_all(ortho.reshape(count, rows_local, HD), ('z', 'grp'), 0, 0,...  2.76 us
    ppermute x1, starting transfers between devices, on_device(): kv_back = lax.ppermute(kv_own, ('z', 'grp'), ring)  2.38 us
  transfers between devices with their start and end apart: 11, of which 6 were waited for; matrix products, arithmetic and copies ran while one was open for 0% of the time, Pallas kernels for 15%

profile of v4, /device:TPU:0, one launch (start us, length us, event | category | flops | bytes accessed | tf_op | source)
XLA Modules:
  0.0 59.0 jit_solution(13780830299066362452)
XLA Ops:
  0.6 0.0 copy-start.1
  0.6 0.9 %copy-done.1 = f32[3,3,32,128]{3,2,1,0:T(8,128)S(1)} copy-done((f32[3,3,32,128]{3,2,1,0:T(8,128)S(1)}, f32[3,3,32,128]{3,2,1,0:T(8,128)}, u32[]{:S(2)}) %copy-start.1) | copy-done | bytes 147480
  1.5 0.8 %shard_map.86.after = bf16[16,3,32,128]{3,2,1,0:T(8,128)(2,1)} custom-call(f32[3,3,32,128]{3,2,1,0:T(8,128)S(1)} %copy-done.1), custom_call_target="tpu_custom_call" | custom-call | flops 1000000 | bytes 1048576 | tf_op jit(solution)/shard_map/pallas_call | solution.py:314
  2.3 0.0 copy-start
  2.3 0.0 copy-start.3
  2.3 0.0 copy-start.4
  2.3 7.5 %all-to-all-start = ((bf16[16,3,32,128]{3,2,1,0:T(8,128)(2,1)}), bf16[16,3,32,128]{3,2,1,0:T(8,128)(2,1)S(1)}, u32[]{:S(2)}, u32[]{:S(2)}) async-start(bf16[16,3,32,128]{3,2,1,0:T(8,128)(2,1)} %shard_map.86.after), calls=%async_computation | async-start | bytes 786432 | tf_op jit(solution)/shard_map/all_to_all | solution.py:331
  9.8 0.0 copy-start.5
  10.5 0.0 copy-done
  10.5 0.0 copy-done.3
  10.5 0.0 copy-done.4
  10.5 0.0 copy-done.5
  10.5 0.6 %shard_map.87 = (bf16[208,768]{1,0:T(8,128)(2,1)S(1)}, bf16[208,384]{1,0:T(8,128)(2,1)S(1)}, bf16[208,384]{1,0:T(8,128)(2,1)S(1)}, bf16[208,384]{1,0:T(8,128)(2,1)S(1)}, bf16[208,384]{1,0:T(8,128)(2,1)S(1)}) custom-call(bf16[16,3,32,128]{3,2,1,0:T(8,128)(2,1)} %shard_map.86.after, s32[1,1]{1,0:T(1,128)} %bitcast.3.update, f32[3,195]{1,0:T(4,128)S(1)} %bitcast.4, ...), custom_call_target="tpu_custom_call" | custom-call | tf_op jit(solution)/shard_map/pallas_call | solution.py:317
  11.2 1.3 %collective-permute-start.1 = (bf16[208,384]{1,0:T(8,128)(2,1)S(1)}, bf16[208,384]{1,0:T(8,128)(2,1)S(1)}, u32[]{:S(2)}, u32[]{:S(2)}) collective-permute-start(bf16[208,384]{1,0:T(8,128)(2,1)S(1)} %get-tuple-element.24), channel_id=1, source_target_pairs={{2,4},{4,2},{6,0},{3,5},{5,3},{7,1},{10,12},{12,10},{14,8},{11,13}... | collective-permute-start | bytes 479240 | tf_op jit(solution)/shard_map/ppermute | solution.py:336
  12.5 4.6 %collective-permute-start.2 = (bf16[208,384]{1,0:T(8,128)(2,1)S(1)}, bf16[208,384]{1,0:T(8,128)(2,1)S(1)}, u32[]{:S(2)}, u32[]{:S(2)}) collective-permute-start(bf16[208,384]{1,0:T(8,128)(2,1)S(1)} %get-tuple-element.25), channel_id=1, source_target_pairs={{0,2},{2,0},{6,4},{1,3},{3,1},{7,5},{8,10},{10,8},{14,12},{9,11},{... | collective-permute-start | bytes 479240 | tf_op jit(solution)/shard_map/ppermute | solution.py:336
  17.0 1.9 %collective-permute-start = (bf16[208,384]{1,0:T(8,128)(2,1)S(1)}, bf16[208,384]{1,0:T(8,128)(2,1)S(1)}, u32[]{:S(2)}, u32[]{:S(2)}) collective-permute-start(bf16[208,384]{1,0:T(8,128)(2,1)S(1)} %get-tuple-element.22), channel_id=1, source_target_pairs={{0,4},{4,0},{6,2},{1,5},{5,1},{7,3},{8,12},{12,8},{14,10},{9,13},{... | collective-permute-start | bytes 479240 | tf_op jit(solution)/shard_map/ppermute | solution.py:336
  19.0 0.9 %collective-permute-done.1.refs_1_ = bf16[208,384]{1,0:T(8,128)(2,1)S(1)} collective-permute-done((bf16[208,384]{1,0:T(8,128)(2,1)S(1)}, bf16[208,384]{1,0:T(8,128)(2,1)S(1)}, u32[]{:S(2)}, u32[]{:S(2)}) %collective-permute-start.1) | collective-permute-done | bytes 159776 | tf_op jit(solution)/shard_map/ppermute | solution.py:336
  19.9 0.0 collective-permute-done.2.refs_2_
  19.9 2.2 %all-to-all-done.refs_3_.w_ref = bf16[16,3,32,128]{3,2,1,0:T(8,128)(2,1)S(1)} async-done(((bf16[16,3,32,128]{3,2,1,0:T(8,128)(2,1)}), bf16[16,3,32,128]{3,2,1,0:T(8,128)(2,1)S(1)}, u32[]{:S(2)}, u32[]{:S(2)}) %all-to-all-start) | async-done | bytes 393248 | tf_op jit(solution)/shard_map/all_to_all | solution.py:331
  22.1 2.2 %shard_map.88 = (f32[3,512,128]{2,1,0:T(8,128)S(1)}, bf16[3,208,128]{2,1,0:T(8,128)(2,1)S(1)}) custom-call(bf16[208,384]{1,0:T(8,128)(2,1)S(1)} %get-tuple-element.23.refs_0_, bf16[208,384]{1,0:T(8,128)(2,1)S(1)} %collective-permute-done.1.refs_1_, bf16[208,384]{1,0:T(8,128)(2,1)S(1)} %collective-permute-done.2.refs_2_, ...), custom_call_target="tpu_custom_call" | custom-call | flops 1000000000 | bytes 1048576 | tf_op jit(solution)/shard_map/pallas_call | solution.py:340
  24.3 1.0 %collective-permute-done.token_ref = bf16[208,384]{1,0:T(8,128)(2,1)S(1)} collective-permute-done((bf16[208,384]{1,0:T(8,128)(2,1)S(1)}, bf16[208,384]{1,0:T(8,128)(2,1)S(1)}, u32[]{:S(2)}, u32[]{:S(2)}) %collective-permute-start) | collective-permute-done | bytes 159776 | tf_op jit(solution)/shard_map/ppermute | solution.py:336
  25.4 0.8 %shard_map.89 = (bf16[512,128]{1,0:T(8,128)(2,1)S(1)}, bf16[512,128]{1,0:T(8,128)(2,1)S(1)}, bf16[512,128]{1,0:T(8,128)(2,1)S(1)}, bf16[512,128]{1,0:T(8,128)(2,1)S(1)}) custom-call(bf16[208,384]{1,0:T(8,128)(2,1)S(1)} %collective-permute-done.token_ref, bf16[16,3,32,128]{3,2,1,0:T(8,128)(2,1)S(1)} %all-to-all-done.refs_3_.w_ref, ...), custom_call_target="tpu_custom_call" | custom-call | flops 500000000 | bytes 1048576 | tf_op jit(solution)/shard_map/pallas_call | solution.py:347
  26.1 1.1 %shard_map.90 = bf16[4,208,128]{2,1,0:T(8,128)(2,1)} custom-call(bf16[208,384]{1,0:T(8,128)(2,1)S(1)} %collective-permute-done.token_ref, bf16[16,3,32,128]{3,2,1,0:T(8,128)(2,1)S(1)} %all-to-all-done.refs_3_.w_ref, bf16[3,208,128]{2,1,0:T(8,128)(2,1)S(1)} %get-tuple-element.34.early), custom_call_target="tpu_custom_call" | custom-call | flops 1000 | bytes 1024 | tf_op jit(solution)/shard_map/pallas_call | solution.py:368
  27.3 3.2 %collective-permute-start.5 = (bf16[512,128]{1,0:T(8,128)(2,1)S(1)}, bf16[512,128]{1,0:T(8,128)(2,1)S(1)}, u32[]{:S(2)}, u32[]{:S(2)}) collective-permute-start(bf16[512,128]{1,0:T(8,128)(2,1)S(1)} %get-tuple-element.35), channel_id=1, source_target_pairs={{0,8},{2,10},{8,0},{12,4},{18,26},{20,28},{24,16},{26,18},{28,20},... | collective-permute-start | bytes 393224 | tf_op jit(solution)/shard_map/ppermute | solution.py:363
  30.5 1.3 %collective-permute-start.3 = (bf16[512,128]{1,0:T(8,128)(2,1)S(1)}, bf16[512,128]{1,0:T(8,128)(2,1)S(1)}, u32[]{:S(2)}, u32[]{:S(2)}) collective-permute-start(bf16[512,128]{1,0:T(8,128)(2,1)S(1)} %get-tuple-element.29), channel_id=1, source_target_pairs={{2,26},{4,28},{8,16},{10,18},{12,20},{16,8},{18,10},{24,0},{28,4},... | collective-permute-start | bytes 393224 | tf_op jit(solution)/shard_map/ppermute | solution.py:363
  31.8 4.7 %collective-permute-start.4 = (bf16[512,128]{1,0:T(8,128)(2,1)S(1)}, bf16[512,128]{1,0:T(8,128)(2,1)S(1)}, u32[]{:S(2)}, u32[]{:S(2)}) collective-permute-start(bf16[512,128]{1,0:T(8,128)(2,1)S(1)} %get-tuple-element.30), channel_id=1, source_target_pairs={{0,16},{2,18},{4,20},{10,26},{12,28},{16,0},{20,4},{24,8},{26,10},... | collective-permute-start | bytes 393224 | tf_op jit(solution)/shard_map/ppermute | solution.py:363
  36.5 3.4 %all-to-all-start.1 = ((bf16[4,208,128]{2,1,0:T(8,128)(2,1)}), bf16[4,208,128]{2,1,0:T(8,128)(2,1)S(1)}, u32[]{:S(2)}, u32[]{:S(2)}) async-start(bf16[4,208,128]{2,1,0:T(8,128)(2,1)} %shard_map.90), calls=%async_computation.1 | async-start | bytes 425984 | tf_op jit(solution)/shard_map/all_to_all | solution.py:377
  39.9 2.4 %collective-permute-start.6 = (bf16[208,768]{1,0:T(8,128)(2,1)S(1)}, bf16[208,768]{1,0:T(8,128)(2,1)S(1)}, u32[]{:S(2)}, u32[]{:S(2)}) collective-permute-start(bf16[208,768]{1,0:T(8,128)(2,1)S(1)} %get-tuple-element.37.own_ref), channel_id=1, source_target_pairs={{0,2},{2,4},{4,6},{6,8},{8,10},{10,12},{12,14},{14,16},{16,18},{18... | collective-permute-start | bytes 958472 | tf_op jit(solution)/shard_map/ppermute | solution.py:380
  42.3 0.0 collective-permute-done.5.refs_3_
  42.3 0.0 collective-permute-done.3.refs_1_
  42.3 1.1 %collective-permute-done.4.refs_2_ = bf16[512,128]{1,0:T(8,128)(2,1)S(1)} collective-permute-done((bf16[512,128]{1,0:T(8,128)(2,1)S(1)}, bf16[512,128]{1,0:T(8,128)(2,1)S(1)}, u32[]{:S(2)}, u32[]{:S(2)}) %collective-permute-start.4) | collective-permute-done | bytes 131104 | tf_op jit(solution)/shard_map/ppermute | solution.py:363
  43.4 3.4 %shard_map.91 = bf16[512,128]{1,0:T(8,128)(2,1)} custom-call(bf16[512,128]{1,0:T(8,128)(2,1)S(1)} %get-tuple-element.28.refs_0_, bf16[512,128]{1,0:T(8,128)(2,1)S(1)} %collective-permute-done.3.refs_1_, bf16[512,128]{1,0:T(8,128)(2,1)S(1)} %collective-permute-done.4.refs_2_, bf16[512,128]{1,0:T(8,128)(2,1)S(1)} %collective-permute-done.5.refs_3_), custom_call_target="tpu_custom_call" | custom-call | flops 1000000000 | bytes 1048576 | tf_op jit(solution)/shard_map/pallas_call | solution.py:382
  46.8 0.0 all-to-all-done.1.slots
  46.8 3.5 %all-to-all-start.2 = ((bf16[16,32,128]{2,1,0:T(8,128)(2,1)}), bf16[16,32,128]{2,1,0:T(8,128)(2,1)S(1)}, u32[]{:S(2)}, u32[]{:S(2)}) async-start(bf16[16,32,128]{2,1,0:T(8,128)(2,1)} %bitcast.2), calls=%async_computation.2 | async-start | bytes 262144 | tf_op jit(solution)/shard_map/all_to_all | solution.py:386
  50.3 0.0 copy-start.6
  50.3 0.4 shard_map.93
  50.7 1.6 %collective-permute-start.7 = (f32[8,208]{1,0:T(8,128)S(1)}, f32[8,208]{1,0:T(8,128)S(1)}, u32[]{:S(2)}, u32[]{:S(2)}) collective-permute-start(f32[8,208]{1,0:T(8,128)S(1)} %get-tuple-element.40.refs_0_), channel_id=1, source_target_pairs={{0,1},{1,0},{2,3},{3,2},{4,5},{5,4},{6,7},{7,6},{8,9},{9,8},{10,11... | collective-permute-start | bytes 19976 | tf_op jit(solution)/shard_map/ppermute | solution.py:407
  52.3 0.0 copy-done.6
  52.3 0.0 collective-permute-done.6.back_ref
  52.3 1.3 %shard_map.92.attended_ref = f32[208,384]{1,0:T(8,128)S(1)} custom-call(bf16[195,384]{1,0:T(8,128)(2,1)S(1)} %copy-done, bf16[208,768]{1,0:T(8,128)(2,1)S(1)} %get-tuple-element.37.own_ref, bf16[208,768]{1,0:T(8,128)(2,1)S(1)} %collective-permute-done.6.back_ref), custom_call_target="tpu_custom_call" | custom-call | tf_op jit(solution)/shard_map/pallas_call | solution.py:393
  53.7 0.8 %collective-permute-done.7.refs_1_ = f32[8,208]{1,0:T(8,128)S(1)} collective-permute-done((f32[8,208]{1,0:T(8,128)S(1)}, f32[8,208]{1,0:T(8,128)S(1)}, u32[]{:S(2)}, u32[]{:S(2)}) %collective-permute-start.7) | collective-permute-done | bytes 6688 | tf_op jit(solution)/shard_map/ppermute | solution.py:407
  54.4 0.0 copy-start.2
  54.4 1.0 %shard_map.94 = bf16[195,384]{1,0:T(8,128)(2,1)} custom-call(f32[1,384]{1,0:T(1,128)S(1)} %reshape.13.gain_ref, f32[208,384]{1,0:T(8,128)S(1)} %shard_map.92.attended_ref, bf16[208,384]{1,0:T(8,128)(2,1)S(1)} %get-tuple-element.39.fast_ref, f32[8,208]{1,0:T(8,128)S(1)} %get-tuple-element.40.refs_0_, f32[8,208]{1,0:T(8,128)S(1)} %collective-permute-done.7.refs_1_), custom_call_target="tpu_custom_call" | custom-call | tf_op jit(solution)/shard_map/pallas_call | solution.py:409
  55.4 2.8 %all-to-all-done.2.rows_ref = bf16[16,32,128]{2,1,0:T(8,128)(2,1)S(1)} async-done(((bf16[16,32,128]{2,1,0:T(8,128)(2,1)}), bf16[16,32,128]{2,1,0:T(8,128)(2,1)S(1)}, u32[]{:S(2)}, u32[]{:S(2)}) %all-to-all-start.2) | async-done | bytes 131104 | tf_op jit(solution)/shard_map/all_to_all | solution.py:386
  58.2 0.0 copy-done.2
  58.2 0.8 %shard_map.95 = f32[3,3,32,128]{3,2,1,0:T(8,128)} custom-call(f32[3,3,32,128]{3,2,1,0:T(8,128)S(1)} %copy-done.2, bf16[16,32,128]{2,1,0:T(8,128)(2,1)S(1)} %all-to-all-done.2.rows_ref), custom_call_target="tpu_custom_call" | custom-call | flops 1000000 | bytes 1048576 | tf_op jit(solution)/shard_map/pallas_call | solution.py:389
  (1 shorter events, 0.0 us)
Async XLA Ops:
  0.6 0.9 %copy-start.1 = (f32[3,3,32,128]{3,2,1,0:T(8,128)S(1)}, f32[3,3,32,128]{3,2,1,0:T(8,128)}, u32[]{:S(2)}) copy-start(f32[3,3,32,128]{3,2,1,0:T(8,128)} %w_ref.3) | copy-start | bytes 442372
  2.3 8.2 %copy-start = (bf16[195,384]{1,0:T(8,128)(2,1)S(1)}, bf16[195,384]{1,0:T(8,128)(2,1)}, u32[]{:S(2)}) copy-start(bf16[195,384]{1,0:T(8,128)(2,1)} %q_ref.2) | copy-start | bytes 449284
  2.3 8.2 %copy-start.3 = (bf16[195,384]{1,0:T(8,128)(2,1)S(1)}, bf16[195,384]{1,0:T(8,128)(2,1)}, u32[]{:S(2)}) copy-start(bf16[195,384]{1,0:T(8,128)(2,1)} %k_ref.1) | copy-start | bytes 449284
  2.3 8.2 %copy-start.4 = (bf16[195,384]{1,0:T(8,128)(2,1)S(1)}, bf16[195,384]{1,0:T(8,128)(2,1)}, u32[]{:S(2)}) copy-start(bf16[195,384]{1,0:T(8,128)(2,1)} %v_ref.1) | copy-start | bytes 449284
  2.3 19.8 %all-to-all-start = ((bf16[16,3,32,128]{3,2,1,0:T(8,128)(2,1)}), bf16[16,3,32,128]{3,2,1,0:T(8,128)(2,1)S(1)}, u32[]{:S(2)}, u32[]{:S(2)}) async-start(bf16[16,3,32,128]{3,2,1,0:T(8,128)(2,1)} %shard_map.86.after), calls=%async_computation | async-start | bytes 786432 | tf_op jit(solution)/shard_map/all_to_all | solution.py:331
  9.8 0.7 %copy-start.5 = (f32[195,3]{0,1:T(4,128)S(1)}, f32[195,3]{0,1:T(4,128)}, u32[]{:S(2)}) copy-start(f32[195,3]{0,1:T(4,128)} %param.10) | copy-start | bytes 7024
  11.2 8.7 %collective-permute-start.1 = (bf16[208,384]{1,0:T(8,128)(2,1)S(1)}, bf16[208,384]{1,0:T(8,128)(2,1)S(1)}, u32[]{:S(2)}, u32[]{:S(2)}) collective-permute-start(bf16[208,384]{1,0:T(8,128)(2,1)S(1)} %get-tuple-element.24), channel_id=1, source_target_pairs={{2,4},{4,2},{6,0},{3,5},{5,3},{7,1},{10,12},{12,10},{14,8},{11,13}... | collective-permute-start | bytes 479240 | tf_op jit(solution)/shard_map/ppermute | solution.py:336
  12.5 7.4 %collective-permute-start.2 = (bf16[208,384]{1,0:T(8,128)(2,1)S(1)}, bf16[208,384]{1,0:T(8,128)(2,1)S(1)}, u32[]{:S(2)}, u32[]{:S(2)}) collective-permute-start(bf16[208,384]{1,0:T(8,128)(2,1)S(1)} %get-tuple-element.25), channel_id=1, source_target_pairs={{0,2},{2,0},{6,4},{1,3},{3,1},{7,5},{8,10},{10,8},{14,12},{9,11},{... | collective-permute-start | bytes 479240 | tf_op jit(solution)/shard_map/ppermute | solution.py:336
  17.0 8.3 %collective-permute-start = (bf16[208,384]{1,0:T(8,128)(2,1)S(1)}, bf16[208,384]{1,0:T(8,128)(2,1)S(1)}, u32[]{:S(2)}, u32[]{:S(2)}) collective-permute-start(bf16[208,384]{1,0:T(8,128)(2,1)S(1)} %get-tuple-element.22), channel_id=1, source_target_pairs={{0,4},{4,0},{6,2},{1,5},{5,1},{7,3},{8,12},{12,8},{14,10},{9,13},{... | collective-permute-start | bytes 479240 | tf_op jit(solution)/shard_map/ppermute | solution.py:336
  27.3 15.0 %collective-permute-start.5 = (bf16[512,128]{1,0:T(8,128)(2,1)S(1)}, bf16[512,128]{1,0:T(8,128)(2,1)S(1)}, u32[]{:S(2)}, u32[]{:S(2)}) collective-permute-start(bf16[512,128]{1,0:T(8,128)(2,1)S(1)} %get-tuple-element.35), channel_id=1, source_target_pairs={{0,8},{2,10},{8,0},{12,4},{18,26},{20,28},{24,16},{26,18},{28,20},... | collective-permute-start | bytes 393224 | tf_op jit(solution)/shard_map/ppermute | solution.py:363
  30.5 11.8 %collective-permute-start.3 = (bf16[512,128]{1,0:T(8,128)(2,1)S(1)}, bf16[512,128]{1,0:T(8,128)(2,1)S(1)}, u32[]{:S(2)}, u32[]{:S(2)}) collective-permute-start(bf16[512,128]{1,0:T(8,128)(2,1)S(1)} %get-tuple-element.29), channel_id=1, source_target_pairs={{2,26},{4,28},{8,16},{10,18},{12,20},{16,8},{18,10},{24,0},{28,4},... | collective-permute-start | bytes 393224 | tf_op jit(solution)/shard_map/ppermute | solution.py:363
  31.8 11.6 %collective-permute-start.4 = (bf16[512,128]{1,0:T(8,128)(2,1)S(1)}, bf16[512,128]{1,0:T(8,128)(2,1)S(1)}, u32[]{:S(2)}, u32[]{:S(2)}) collective-permute-start(bf16[512,128]{1,0:T(8,128)(2,1)S(1)} %get-tuple-element.30), channel_id=1, source_target_pairs={{0,16},{2,18},{4,20},{10,26},{12,28},{16,0},{20,4},{24,8},{26,10},... | collective-permute-start | bytes 393224 | tf_op jit(solution)/shard_map/ppermute | solution.py:363
  36.5 10.3 %all-to-all-start.1 = ((bf16[4,208,128]{2,1,0:T(8,128)(2,1)}), bf16[4,208,128]{2,1,0:T(8,128)(2,1)S(1)}, u32[]{:S(2)}, u32[]{:S(2)}) async-start(bf16[4,208,128]{2,1,0:T(8,128)(2,1)} %shard_map.90), calls=%async_computation.1 | async-start | bytes 425984 | tf_op jit(solution)/shard_map/all_to_all | solution.py:377
  39.9 12.4 %collective-permute-start.6 = (bf16[208,768]{1,0:T(8,128)(2,1)S(1)}, bf16[208,768]{1,0:T(8,128)(2,1)S(1)}, u32[]{:S(2)}, u32[]{:S(2)}) collective-permute-start(bf16[208,768]{1,0:T(8,128)(2,1)S(1)} %get-tuple-element.37.own_ref), channel_id=1, source_target_pairs={{0,2},{2,4},{4,6},{6,8},{8,10},{10,12},{12,14},{14,16},{16,18},{18... | collective-permute-start | bytes 958472 | tf_op jit(solution)/shard_map/ppermute | solution.py:380
  46.8 11.4 %all-to-all-start.2 = ((bf16[16,32,128]{2,1,0:T(8,128)(2,1)}), bf16[16,32,128]{2,1,0:T(8,128)(2,1)S(1)}, u32[]{:S(2)}, u32[]{:S(2)}) async-start(bf16[16,32,128]{2,1,0:T(8,128)(2,1)} %bitcast.2), calls=%async_computation.2 | async-start | bytes 262144 | tf_op jit(solution)/shard_map/all_to_all | solution.py:386
  50.3 2.0 %copy-start.6 = (f32[384]{0:T(512)S(1)}, f32[384]{0:T(512)}, u32[]{:S(2)}) copy-start(f32[384]{0:T(512)} %param.13) | copy-start | bytes 4612
  50.7 3.7 %collective-permute-start.7 = (f32[8,208]{1,0:T(8,128)S(1)}, f32[8,208]{1,0:T(8,128)S(1)}, u32[]{:S(2)}, u32[]{:S(2)}) collective-permute-start(f32[8,208]{1,0:T(8,128)S(1)} %get-tuple-element.40.refs_0_), channel_id=1, source_target_pairs={{0,1},{1,0},{2,3},{3,2},{4,5},{5,4},{6,7},{7,6},{8,9},{9,8},{10,11... | collective-permute-start | bytes 19976 | tf_op jit(solution)/shard_map/ppermute | solution.py:407
  54.4 3.8 %copy-start.2 = (f32[3,3,32,128]{3,2,1,0:T(8,128)S(1)}, f32[3,3,32,128]{3,2,1,0:T(8,128)}, u32[]{:S(2)}) copy-start(f32[3,3,32,128]{3,2,1,0:T(8,128)} %w_ref.3) | copy-start | bytes 442372

commit v5 on v3

--- a/solution.py
+++ b/solution.py
@@ -47,6 +47,10 @@
 
 def served(n):
     return [0] + list(range(n - 1, 0, -1))
+
+
+def first_owner(h):
+    return h & 1
 
 
 def position():
@@ -78,24 +82,25 @@
     lane_head = lax.broadcasted_iota(jnp.int32, (heads, heads * HD), 1) // HD
     row = lax.broadcasted_iota(jnp.int32, (heads, heads * HD), 0)
     rate = dot(rate_ref[...], (row == lane_head).astype(f32), (0, 0), highest)[:padded]
-    targets[...] = jnp.where(valid, ((rate * keep) * v_ref[...].astype(f32)).astype(bf16), none)
+    targets[...] = ((rate * keep) * v_ref[...].astype(f32)).astype(bf16)
     for d in range(group):
         head = jnp.minimum(place[1] ^ d, heads - 1)
         cols = pl.ds(pl.multiple_of(head * HD, HD), HD)
-        token_outs[d][:, :HD] = jnp.where(valid, k_ref[:, cols], none)
-        token_outs[d][:, HD : 2 * HD] = targets[:, cols]
-        token_outs[d][:, 2 * HD :] = jnp.where(valid, q_ref[:, cols], none)
+        for i, source in enumerate((k_ref, targets, q_ref)):
+            token_outs[d][:, i * HD : (i + 1) * HD] = source[:tokens, cols]
     kv_out[:, : heads * HD] = jnp.where(valid, k_ref[...], none)
     kv_out[:, heads * HD :] = jnp.where(valid, v_ref[...], none)
 
 
 def gradients(token_refs, w_ref, k_all, t_all, staged, deltas):
-    padded = token_refs[0].shape[0]
+    tokens = token_refs[0].shape[0]
+    padded = -(-tokens // 16) * 16
     width = k_all.shape[0]
     filled = len(token_refs) * padded
     for i, ref in enumerate(token_refs):
-        k_all[i * padded : (i + 1) * padded] = ref[:, :HD]
-        t_all[i * padded : (i + 1) * padded] = ref[:, HD : 2 * HD]
+        for part, rows in enumerate((k_all, t_all)):
+            rows[(i + 1) * padded - 16 : (i + 1) * padded] = jnp.zeros((16, HD), bf16)
+            rows[i * padded : i * padded + tokens] = ref[:, part * HD : (part + 1) * HD]
     if width > filled:
         k_all[filled:] = jnp.zeros((width - filled, HD), bf16)
         t_all[filled:] = jnp.zeros((width - filled, HD), bf16)
@@ -136,10 +141,13 @@
     ]
 
 
-def apply_tokens(query, w_ref, stage, act):
+def apply_tokens(token_ref, w_ref, stage, act, held):
     hidden = act.shape[1]
     tall = 16
     w1, w3, w2 = (weight_rows(w_ref, m, 0, hidden) for m in range(3))
+    held[held.shape[0] - 16 :] = jnp.zeros((16, HD), bf16)
+    held[: token_ref.shape[0]] = token_ref[:, 2 * HD :]
+    query = held[...]
     stage[0] = dot(query, w1, (1, 1))
     stage[1] = dot(query, w3, (1, 1))
     for start in range(0, query.shape[0], tall):
@@ -150,17 +158,21 @@
 
 
 def apply_scratch(padded, hidden):
-    return [pltpu.VMEM((2, 2, padded, hidden), f32), pltpu.VMEM((2, padded, hidden), bf16)]
+    return [
+        pltpu.VMEM((2, 2, padded, hidden), f32),
+        pltpu.VMEM((2, padded, hidden), bf16),
+        pltpu.VMEM((2, padded, HD), bf16),
+    ]
 
 
 def early_body(count, *refs):
     token_refs, w_ref = refs[:count], refs[count]
     grads, fast = refs[count + 1 : count + 3]
-    scratch, (staged, acts) = refs[count + 3 : -2], refs[-2:]
+    scratch, (staged, acts, held) = refs[count + 3 : -3], refs[-3:]
     for m, grad in enumerate(gradients(token_refs, w_ref, *scratch)):
         grads[m] = grad
     for i, ref in enumerate(token_refs):
-        fast[i] = apply_tokens(ref[:, 2 * HD :], w_ref, staged.at[i % 2], acts.at[i % 2])
+        fast[i] = apply_tokens(ref, w_ref, *(buffer.at[i % 2] for buffer in (staged, acts, held)))
 
 
 def late_body(group, slots, token_ref, w_ref, early, *refs):
@@ -169,17 +181,17 @@
     for m, grad in enumerate(gradients([token_ref], w_ref, *scratch)):
         sums[m] = (early[m] + grad).astype(bf16)
     for d in range(slots):
-        matrix = lax.rem((place[0] ^ d) - place[1] + group * slots, slots)
+        matrix = lax.rem((place[0] ^ d) - first_owner(place[1]) + slots, slots)
         chosen = sums[jnp.minimum(matrix, 2)]
         outs[d][...] = jnp.where(matrix < 3, chosen, jnp.zeros_like(chosen))
 
 
-def late_apply_body(early_slots, last, token_ref, w_ref, early, out, staged, acts):
+def late_apply_body(early_slots, last, token_ref, w_ref, early, out, staged, acts, held):
     place = position()
     for i, d in enumerate(early_slots):
         out[place[1] ^ d] = early[i]
     out[place[1] ^ last] = apply_tokens(
-        token_ref[:, 2 * HD :], w_ref, staged.at[0], acts.at[0]
+        token_ref, w_ref, staged.at[0], acts.at[0], held.at[0]
     )
 
 
@@ -207,7 +219,7 @@
 
 def ortho_body(heads, slots, *refs):
     place = position()
-    matrix = lax.rem(place[0] - place[1] + heads * slots, slots)
+    matrix = lax.rem(place[0] - first_owner(place[1]) + slots, slots)
     owner = (place[1] < heads) & (matrix < 3)
 
     @pl.when(owner)
@@ -249,7 +261,7 @@
     for m in range(3):
         for h in range(heads):
             weights = w_ref[m, h]
-            summed = weights + rows_ref[((m + h) % slots) * group + h].astype(f32)
+            summed = weights + rows_ref[((m + first_owner(h)) % slots) * group + h].astype(f32)
             old = jnp.sqrt(jnp.sum(weights * weights, axis=1, keepdims=True))
             new = lax.rsqrt(jnp.sum(summed * summed, axis=1, keepdims=True) + epsilon)
             out[m, h] = summed * (old * new)
@@ -318,11 +330,11 @@
         functools.partial(prep_body, heads, group, tokens),
         grid=(1,),
         out_shape=[sds((padded, 2 * span), bf16)]
-        + [sds((padded, 3 * HD), bf16)] * group,
+        + [sds((tokens, 3 * HD), bf16)] * group,
         in_specs=[pl.BlockSpec(memory_space=pl.ANY), whole(1, 1)]
         + [whole(heads, -(-padded // 128) * 128)]
         + [whole(padded, span)] * 3,
-        out_specs=[whole(padded, 2 * span)] + [whole(padded, 3 * HD)] * group,
+        out_specs=[whole(padded, 2 * span)] + [whole(tokens, 3 * HD)] * group,
         scratch_shapes=[pltpu.VMEM((padded, span), bf16)],
         compiler_params=pltpu.CompilerParams(vmem_limit_bytes=VMEM_LIMIT),
     )(low, frame_update.reshape(1, 1), rates.T, keys, values, queries)
@@ -358,7 +370,7 @@
             pairs += [
                 (z * group + j, (z ^ d) * group + j)
                 for j in range(heads)
-                if ((z ^ d) - j) % nz < 3
+                if ((z ^ d) - first_owner(j)) % nz < 3
             ]
         partials[d] = lax.ppermute(partials[d], ("z", "grp"), pairs)
 

time: 59 us -> 58.9 us (level)
  no operation moved by 1% of the time
where the time goes in v5:
time: 58.9 us; the launch traced here: 58.3 us
  starting transfers between devices  35.7 us (61%)
  Pallas kernels  12.5 us (21%)
  waiting for transfers between devices  7.65 us (13%)
  between operations  1.48 us (3%)
  local copies, waits for them, and re-layouts  0.93 us (2%)
    ppermute x3, starting transfers between devices, on_device(): partials[d] = lax.ppermute(partials[d], ('z', 'grp'), pairs)  8.51 us
    ppermute x3, starting transfers between devices, on_device(): token_slots[d] = lax.ppermute(token_slots[d], 'grp', pairs)  7.78 us
    all_to_all x1, starting transfers between devices, on_device(): weights = lax.all_to_all(low, ('z', 'grp'), 0, 0, tiled=True)  7.49 us
    all_to_all x1, starting transfers between devices, on_device(): lax.all_to_all(ortho.reshape(count, rows_local, HD), ('z', 'grp'), 0, 0,...  4.61 us
    pallas_call x1, Pallas kernels, on_device(): call(functools.partial(ortho_body, heads, nz), sds((hidden, HD), bf16), f...  3.44 us
    all_to_all x1, starting transfers between devices, on_device(): fast_slots = lax.all_to_all(fast_slots, 'grp', 0, 0, tiled=True)  3.37 us
    all_to_all x1, waiting for transfers between devices, on_device(): lax.all_to_all(ortho.reshape(count, rows_local, HD), ('z', 'grp'), 0, 0,...  2.8 us
    ppermute x1, starting transfers between devices, on_device(): kv_back = lax.ppermute(kv_own, ('z', 'grp'), ring)  2.38 us
  transfers between devices with their start and end apart: 11, of which 5 were waited for; matrix products, arithmetic and copies ran while one was open for 0% of the time, Pallas kernels for 17%

profile of v5, /device:TPU:0, one launch (start us, length us, event | category | flops | bytes accessed | tf_op | source)
XLA Modules:
  0.0 58.3 jit_solution(14287260918026211595)
XLA Ops:
  0.6 0.0 copy-start.1
  0.6 0.9 %copy-done.1 = f32[3,3,32,128]{3,2,1,0:T(8,128)S(1)} copy-done((f32[3,3,32,128]{3,2,1,0:T(8,128)S(1)}, f32[3,3,32,128]{3,2,1,0:T(8,128)}, u32[]{:S(2)}) %copy-start.1) | copy-done | bytes 147480
  1.5 0.8 %shard_map.86.after = bf16[16,3,32,128]{3,2,1,0:T(8,128)(2,1)} custom-call(f32[3,3,32,128]{3,2,1,0:T(8,128)S(1)} %copy-done.1), custom_call_target="tpu_custom_call" | custom-call | flops 1000000 | bytes 1048576 | tf_op jit(solution)/shard_map/pallas_call | solution.py:326
  2.3 0.0 copy-start
  2.3 0.0 copy-start.3
  2.3 0.0 copy-start.4
  2.3 7.5 %all-to-all-start = ((bf16[16,3,32,128]{3,2,1,0:T(8,128)(2,1)}), bf16[16,3,32,128]{3,2,1,0:T(8,128)(2,1)S(1)}, u32[]{:S(2)}, u32[]{:S(2)}) async-start(bf16[16,3,32,128]{3,2,1,0:T(8,128)(2,1)} %shard_map.86.after), calls=%async_computation | async-start | bytes 786432 | tf_op jit(solution)/shard_map/all_to_all | solution.py:343
  9.8 0.0 copy-start.5
  10.5 0.0 copy-done
  10.5 0.0 copy-done.3
  10.5 0.0 copy-done.4
  10.5 0.0 copy-done.5
  10.5 0.6 %shard_map.87 = (bf16[208,768]{1,0:T(8,128)(2,1)S(1)}, bf16[195,384]{1,0:T(8,128)(2,1)S(1)}, bf16[195,384]{1,0:T(8,128)(2,1)S(1)}, bf16[195,384]{1,0:T(8,128)(2,1)S(1)}, bf16[195,384]{1,0:T(8,128)(2,1)S(1)}) custom-call(bf16[16,3,32,128]{3,2,1,0:T(8,128)(2,1)} %shard_map.86.after, s32[1,1]{1,0:T(1,128)} %bitcast.3.update, f32[3,195]{1,0:T(4,128)S(1)} %bitcast.4, ...), custom_call_target="tpu_custom_call" | custom-call | tf_op jit(solution)/shard_map/pallas_call | solution.py:329
  11.1 1.3 %collective-permute-start.1 = (bf16[195,384]{1,0:T(8,128)(2,1)S(1)}, bf16[195,384]{1,0:T(8,128)(2,1)S(1)}, u32[]{:S(2)}, u32[]{:S(2)}) collective-permute-start(bf16[195,384]{1,0:T(8,128)(2,1)S(1)} %get-tuple-element.25), channel_id=1, source_target_pairs={{2,4},{4,2},{6,0},{3,5},{5,3},{7,1},{10,12},{12,10},{14,8},{11,13}... | collective-permute-start | bytes 449288 | tf_op jit(solution)/shard_map/ppermute | solution.py:348
  12.4 4.6 %collective-permute-start.2 = (bf16[195,384]{1,0:T(8,128)(2,1)S(1)}, bf16[195,384]{1,0:T(8,128)(2,1)S(1)}, u32[]{:S(2)}, u32[]{:S(2)}) collective-permute-start(bf16[195,384]{1,0:T(8,128)(2,1)S(1)} %get-tuple-element.26), channel_id=1, source_target_pairs={{0,2},{2,0},{6,4},{1,3},{3,1},{7,5},{8,10},{10,8},{14,12},{9,11},{... | collective-permute-start | bytes 449288 | tf_op jit(solution)/shard_map/ppermute | solution.py:348
  17.0 1.9 %collective-permute-start = (bf16[195,384]{1,0:T(8,128)(2,1)S(1)}, bf16[195,384]{1,0:T(8,128)(2,1)S(1)}, u32[]{:S(2)}, u32[]{:S(2)}) collective-permute-start(bf16[195,384]{1,0:T(8,128)(2,1)S(1)} %get-tuple-element.23), channel_id=1, source_target_pairs={{0,4},{4,0},{6,2},{1,5},{5,1},{7,3},{8,12},{12,8},{14,10},{9,13},{... | collective-permute-start | bytes 449288 | tf_op jit(solution)/shard_map/ppermute | solution.py:348
  18.9 0.8 %collective-permute-done.1.refs_1_ = bf16[195,384]{1,0:T(8,128)(2,1)S(1)} collective-permute-done((bf16[195,384]{1,0:T(8,128)(2,1)S(1)}, bf16[195,384]{1,0:T(8,128)(2,1)S(1)}, u32[]{:S(2)}, u32[]{:S(2)}) %collective-permute-start.1) | collective-permute-done | bytes 149792 | tf_op jit(solution)/shard_map/ppermute | solution.py:348
  19.7 0.0 collective-permute-done.2.refs_2_
  19.7 2.3 %all-to-all-done.refs_3_.w_ref = bf16[16,3,32,128]{3,2,1,0:T(8,128)(2,1)S(1)} async-done(((bf16[16,3,32,128]{3,2,1,0:T(8,128)(2,1)}), bf16[16,3,32,128]{3,2,1,0:T(8,128)(2,1)S(1)}, u32[]{:S(2)}, u32[]{:S(2)}) %all-to-all-start) | async-done | bytes 393248 | tf_op jit(solution)/shard_map/all_to_all | solution.py:343
  22.0 2.2 %shard_map.88 = (f32[3,512,128]{2,1,0:T(8,128)S(1)}, bf16[3,208,128]{2,1,0:T(8,128)(2,1)S(1)}) custom-call(bf16[195,384]{1,0:T(8,128)(2,1)S(1)} %get-tuple-element.24.refs_0_, bf16[195,384]{1,0:T(8,128)(2,1)S(1)} %collective-permute-done.1.refs_1_, bf16[195,384]{1,0:T(8,128)(2,1)S(1)} %collective-permute-done.2.refs_2_, ...), custom_call_target="tpu_custom_call" | custom-call | flops 1000000000 | bytes 1048576 | tf_op jit(solution)/shard_map/pallas_call | solution.py:352
  24.3 0.9 %collective-permute-done.token_ref = bf16[195,384]{1,0:T(8,128)(2,1)S(1)} collective-permute-done((bf16[195,384]{1,0:T(8,128)(2,1)S(1)}, bf16[195,384]{1,0:T(8,128)(2,1)S(1)}, u32[]{:S(2)}, u32[]{:S(2)}) %collective-permute-start) | collective-permute-done | bytes 149792 | tf_op jit(solution)/shard_map/ppermute | solution.py:348
  25.2 0.8 %shard_map.89 = (bf16[512,128]{1,0:T(8,128)(2,1)S(1)}, bf16[512,128]{1,0:T(8,128)(2,1)S(1)}, bf16[512,128]{1,0:T(8,128)(2,1)S(1)}, bf16[512,128]{1,0:T(8,128)(2,1)S(1)}) custom-call(bf16[195,384]{1,0:T(8,128)(2,1)S(1)} %collective-permute-done.token_ref, bf16[16,3,32,128]{3,2,1,0:T(8,128)(2,1)S(1)} %all-to-all-done.refs_3_.w_ref, ...), custom_call_target="tpu_custom_call" | custom-call | flops 500000000 | bytes 1048576 | tf_op jit(solution)/shard_map/pallas_call | solution.py:359
  26.0 1.3 %collective-permute-start.3 = (bf16[512,128]{1,0:T(8,128)(2,1)S(1)}, bf16[512,128]{1,0:T(8,128)(2,1)S(1)}, u32[]{:S(2)}, u32[]{:S(2)}) collective-permute-start(bf16[512,128]{1,0:T(8,128)(2,1)S(1)} %get-tuple-element.33), channel_id=1, source_target_pairs={{2,26},{8,16},{10,18},{12,20},{16,8},{18,10},{20,12},{24,0},{28,4}... | collective-permute-start | bytes 393224 | tf_op jit(solution)/shard_map/ppermute | solution.py:375
  27.3 5.3 %collective-permute-start.4 = (bf16[512,128]{1,0:T(8,128)(2,1)S(1)}, bf16[512,128]{1,0:T(8,128)(2,1)S(1)}, u32[]{:S(2)}, u32[]{:S(2)}) collective-permute-start(bf16[512,128]{1,0:T(8,128)(2,1)S(1)} %get-tuple-element.34), channel_id=1, source_target_pairs={{0,16},{2,18},{4,20},{10,26},{16,0},{20,4},{24,8},{26,10},{28,12},... | collective-permute-start | bytes 393224 | tf_op jit(solution)/shard_map/ppermute | solution.py:375
  32.6 1.9 %collective-permute-start.5 = (bf16[512,128]{1,0:T(8,128)(2,1)S(1)}, bf16[512,128]{1,0:T(8,128)(2,1)S(1)}, u32[]{:S(2)}, u32[]{:S(2)}) collective-permute-start(bf16[512,128]{1,0:T(8,128)(2,1)S(1)} %get-tuple-element.35), channel_id=1, source_target_pairs={{0,8},{2,10},{4,12},{8,0},{12,4},{18,26},{24,16},{26,18},{28,20},{... | collective-permute-start | bytes 393224 | tf_op jit(solution)/shard_map/ppermute | solution.py:375
  34.5 1.1 %shard_map.90 = bf16[4,208,128]{2,1,0:T(8,128)(2,1)} custom-call(bf16[195,384]{1,0:T(8,128)(2,1)S(1)} %collective-permute-done.token_ref, bf16[16,3,32,128]{3,2,1,0:T(8,128)(2,1)S(1)} %all-to-all-done.refs_3_.w_ref, bf16[3,208,128]{2,1,0:T(8,128)(2,1)S(1)} %get-tuple-element.31.early), custom_call_target="tpu_custom_call" | custom-call | flops 1000 | bytes 1024 | tf_op jit(solution)/shard_map/pallas_call | solution.py:377
  35.6 3.4 %all-to-all-start.1 = ((bf16[4,208,128]{2,1,0:T(8,128)(2,1)}), bf16[4,208,128]{2,1,0:T(8,128)(2,1)S(1)}, u32[]{:S(2)}, u32[]{:S(2)}) async-start(bf16[4,208,128]{2,1,0:T(8,128)(2,1)} %shard_map.90), calls=%async_computation.1 | async-start | bytes 425984 | tf_op jit(solution)/shard_map/all_to_all | solution.py:385
  39.0 2.4 %collective-permute-start.6 = (bf16[208,768]{1,0:T(8,128)(2,1)S(1)}, bf16[208,768]{1,0:T(8,128)(2,1)S(1)}, u32[]{:S(2)}, u32[]{:S(2)}) collective-permute-start(bf16[208,768]{1,0:T(8,128)(2,1)S(1)} %get-tuple-element.37.own_ref), channel_id=1, source_target_pairs={{0,2},{2,4},{4,6},{6,8},{8,10},{10,12},{12,14},{14,16},{16,18},{18... | collective-permute-start | bytes 958472 | tf_op jit(solution)/shard_map/ppermute | solution.py:388
  41.4 0.0 collective-permute-done.3.refs_1_
  41.4 0.0 collective-permute-done.4.refs_2_
  41.4 0.0 collective-permute-done.5.refs_3_
  41.5 3.4 %shard_map.91 = bf16[512,128]{1,0:T(8,128)(2,1)} custom-call(bf16[512,128]{1,0:T(8,128)(2,1)S(1)} %get-tuple-element.32.refs_0_, bf16[512,128]{1,0:T(8,128)(2,1)S(1)} %collective-permute-done.3.refs_1_, bf16[512,128]{1,0:T(8,128)(2,1)S(1)} %collective-permute-done.4.refs_2_, bf16[512,128]{1,0:T(8,128)(2,1)S(1)} %collective-permute-done.5.refs_3_), custom_call_target="tpu_custom_call" | custom-call | flops 1000000000 | bytes 1048576 | tf_op jit(solution)/shard_map/pallas_call | solution.py:390
  44.9 0.0 all-to-all-done.1.slots
  44.9 4.6 %all-to-all-start.2 = ((bf16[16,32,128]{2,1,0:T(8,128)(2,1)}), bf16[16,32,128]{2,1,0:T(8,128)(2,1)S(1)}, u32[]{:S(2)}, u32[]{:S(2)}) async-start(bf16[16,32,128]{2,1,0:T(8,128)(2,1)} %bitcast.2), calls=%async_computation.2 | async-start | bytes 262144 | tf_op jit(solution)/shard_map/all_to_all | solution.py:394
  49.5 0.0 copy-start.6
  49.5 0.4 shard_map.93
  50.0 1.6 %collective-permute-start.7 = (f32[8,208]{1,0:T(8,128)S(1)}, f32[8,208]{1,0:T(8,128)S(1)}, u32[]{:S(2)}, u32[]{:S(2)}) collective-permute-start(f32[8,208]{1,0:T(8,128)S(1)} %get-tuple-element.40.refs_0_), channel_id=1, source_target_pairs={{0,1},{1,0},{2,3},{3,2},{4,5},{5,4},{6,7},{7,6},{8,9},{9,8},{10,11... | collective-permute-start | bytes 19976 | tf_op jit(solution)/shard_map/ppermute | solution.py:415
  51.5 0.0 copy-done.6
  51.5 0.0 collective-permute-done.6.back_ref
  51.5 1.3 %shard_map.92.attended_ref = f32[208,384]{1,0:T(8,128)S(1)} custom-call(bf16[195,384]{1,0:T(8,128)(2,1)S(1)} %copy-done, bf16[208,768]{1,0:T(8,128)(2,1)S(1)} %get-tuple-element.37.own_ref, bf16[208,768]{1,0:T(8,128)(2,1)S(1)} %collective-permute-done.6.back_ref), custom_call_target="tpu_custom_call" | custom-call | tf_op jit(solution)/shard_map/pallas_call | solution.py:401
  52.9 0.8 %collective-permute-done.7.refs_1_ = f32[8,208]{1,0:T(8,128)S(1)} collective-permute-done((f32[8,208]{1,0:T(8,128)S(1)}, f32[8,208]{1,0:T(8,128)S(1)}, u32[]{:S(2)}, u32[]{:S(2)}) %collective-permute-start.7) | collective-permute-done | bytes 6688 | tf_op jit(solution)/shard_map/ppermute | solution.py:415
  53.6 0.0 copy-start.2
  53.6 1.0 %shard_map.94 = bf16[195,384]{1,0:T(8,128)(2,1)} custom-call(f32[1,384]{1,0:T(1,128)S(1)} %reshape.13.gain_ref, f32[208,384]{1,0:T(8,128)S(1)} %shard_map.92.attended_ref, bf16[208,384]{1,0:T(8,128)(2,1)S(1)} %get-tuple-element.39.fast_ref, f32[8,208]{1,0:T(8,128)S(1)} %get-tuple-element.40.refs_0_, f32[8,208]{1,0:T(8,128)S(1)} %collective-permute-done.7.refs_1_), custom_call_target="tpu_custom_call" | custom-call | tf_op jit(solution)/shard_map/pallas_call | solution.py:417
  54.6 2.8 %all-to-all-done.2.rows_ref = bf16[16,32,128]{2,1,0:T(8,128)(2,1)S(1)} async-done(((bf16[16,32,128]{2,1,0:T(8,128)(2,1)}), bf16[16,32,128]{2,1,0:T(8,128)(2,1)S(1)}, u32[]{:S(2)}, u32[]{:S(2)}) %all-to-all-start.2) | async-done | bytes 131104 | tf_op jit(solution)/shard_map/all_to_all | solution.py:394
  57.4 0.0 copy-done.2
  57.4 0.8 %shard_map.95 = f32[3,3,32,128]{3,2,1,0:T(8,128)} custom-call(f32[3,3,32,128]{3,2,1,0:T(8,128)S(1)} %copy-done.2, bf16[16,32,128]{2,1,0:T(8,128)(2,1)S(1)} %all-to-all-done.2.rows_ref), custom_call_target="tpu_custom_call" | custom-call | flops 1000000 | bytes 1048576 | tf_op jit(solution)/shard_map/pallas_call | solution.py:397
  (1 shorter events, 0.0 us)
Async XLA Ops:
  0.6 0.9 %copy-start.1 = (f32[3,3,32,128]{3,2,1,0:T(8,128)S(1)}, f32[3,3,32,128]{3,2,1,0:T(8,128)}, u32[]{:S(2)}) copy-start(f32[3,3,32,128]{3,2,1,0:T(8,128)} %w_ref.3) | copy-start | bytes 442372
  2.3 8.2 %copy-start = (bf16[195,384]{1,0:T(8,128)(2,1)S(1)}, bf16[195,384]{1,0:T(8,128)(2,1)}, u32[]{:S(2)}) copy-start(bf16[195,384]{1,0:T(8,128)(2,1)} %q_ref.2) | copy-start | bytes 449284
  2.3 8.2 %copy-start.3 = (bf16[195,384]{1,0:T(8,128)(2,1)S(1)}, bf16[195,384]{1,0:T(8,128)(2,1)}, u32[]{:S(2)}) copy-start(bf16[195,384]{1,0:T(8,128)(2,1)} %k_ref.1) | copy-start | bytes 449284
  2.3 8.2 %copy-start.4 = (bf16[195,384]{1,0:T(8,128)(2,1)S(1)}, bf16[195,384]{1,0:T(8,128)(2,1)}, u32[]{:S(2)}) copy-start(bf16[195,384]{1,0:T(8,128)(2,1)} %v_ref.1) | copy-start | bytes 449284
  2.3 19.7 %all-to-all-start = ((bf16[16,3,32,128]{3,2,1,0:T(8,128)(2,1)}), bf16[16,3,32,128]{3,2,1,0:T(8,128)(2,1)S(1)}, u32[]{:S(2)}, u32[]{:S(2)}) async-start(bf16[16,3,32,128]{3,2,1,0:T(8,128)(2,1)} %shard_map.86.after), calls=%async_computation | async-start | bytes 786432 | tf_op jit(solution)/shard_map/all_to_all | solution.py:343
  9.8 0.7 %copy-start.5 = (f32[195,3]{0,1:T(4,128)S(1)}, f32[195,3]{0,1:T(4,128)}, u32[]{:S(2)}) copy-start(f32[195,3]{0,1:T(4,128)} %param.10) | copy-start | bytes 7024
  11.1 8.6 %collective-permute-start.1 = (bf16[195,384]{1,0:T(8,128)(2,1)S(1)}, bf16[195,384]{1,0:T(8,128)(2,1)S(1)}, u32[]{:S(2)}, u32[]{:S(2)}) collective-permute-start(bf16[195,384]{1,0:T(8,128)(2,1)S(1)} %get-tuple-element.25), channel_id=1, source_target_pairs={{2,4},{4,2},{6,0},{3,5},{5,3},{7,1},{10,12},{12,10},{14,8},{11,13}... | collective-permute-start | bytes 449288 | tf_op jit(solution)/shard_map/ppermute | solution.py:348
  12.4 7.3 %collective-permute-start.2 = (bf16[195,384]{1,0:T(8,128)(2,1)S(1)}, bf16[195,384]{1,0:T(8,128)(2,1)S(1)}, u32[]{:S(2)}, u32[]{:S(2)}) collective-permute-start(bf16[195,384]{1,0:T(8,128)(2,1)S(1)} %get-tuple-element.26), channel_id=1, source_target_pairs={{0,2},{2,0},{6,4},{1,3},{3,1},{7,5},{8,10},{10,8},{14,12},{9,11},{... | collective-permute-start | bytes 449288 | tf_op jit(solution)/shard_map/ppermute | solution.py:348
  17.0 8.2 %collective-permute-start = (bf16[195,384]{1,0:T(8,128)(2,1)S(1)}, bf16[195,384]{1,0:T(8,128)(2,1)S(1)}, u32[]{:S(2)}, u32[]{:S(2)}) collective-permute-start(bf16[195,384]{1,0:T(8,128)(2,1)S(1)} %get-tuple-element.23), channel_id=1, source_target_pairs={{0,4},{4,0},{6,2},{1,5},{5,1},{7,3},{8,12},{12,8},{14,10},{9,13},{... | collective-permute-start | bytes 449288 | tf_op jit(solution)/shard_map/ppermute | solution.py:348
  26.0 15.4 %collective-permute-start.3 = (bf16[512,128]{1,0:T(8,128)(2,1)S(1)}, bf16[512,128]{1,0:T(8,128)(2,1)S(1)}, u32[]{:S(2)}, u32[]{:S(2)}) collective-permute-start(bf16[512,128]{1,0:T(8,128)(2,1)S(1)} %get-tuple-element.33), channel_id=1, source_target_pairs={{2,26},{8,16},{10,18},{12,20},{16,8},{18,10},{20,12},{24,0},{28,4}... | collective-permute-start | bytes 393224 | tf_op jit(solution)/shard_map/ppermute | solution.py:375
  27.3 14.1 %collective-permute-start.4 = (bf16[512,128]{1,0:T(8,128)(2,1)S(1)}, bf16[512,128]{1,0:T(8,128)(2,1)S(1)}, u32[]{:S(2)}, u32[]{:S(2)}) collective-permute-start(bf16[512,128]{1,0:T(8,128)(2,1)S(1)} %get-tuple-element.34), channel_id=1, source_target_pairs={{0,16},{2,18},{4,20},{10,26},{16,0},{20,4},{24,8},{26,10},{28,12},... | collective-permute-start | bytes 393224 | tf_op jit(solution)/shard_map/ppermute | solution.py:375
  32.6 8.8 %collective-permute-start.5 = (bf16[512,128]{1,0:T(8,128)(2,1)S(1)}, bf16[512,128]{1,0:T(8,128)(2,1)S(1)}, u32[]{:S(2)}, u32[]{:S(2)}) collective-permute-start(bf16[512,128]{1,0:T(8,128)(2,1)S(1)} %get-tuple-element.35), channel_id=1, source_target_pairs={{0,8},{2,10},{4,12},{8,0},{12,4},{18,26},{24,16},{26,18},{28,20},{... | collective-permute-start | bytes 393224 | tf_op jit(solution)/shard_map/ppermute | solution.py:375
  35.6 9.2 %all-to-all-start.1 = ((bf16[4,208,128]{2,1,0:T(8,128)(2,1)}), bf16[4,208,128]{2,1,0:T(8,128)(2,1)S(1)}, u32[]{:S(2)}, u32[]{:S(2)}) async-start(bf16[4,208,128]{2,1,0:T(8,128)(2,1)} %shard_map.90), calls=%async_computation.1 | async-start | bytes 425984 | tf_op jit(solution)/shard_map/all_to_all | solution.py:385
  39.0 12.5 %collective-permute-start.6 = (bf16[208,768]{1,0:T(8,128)(2,1)S(1)}, bf16[208,768]{1,0:T(8,128)(2,1)S(1)}, u32[]{:S(2)}, u32[]{:S(2)}) collective-permute-start(bf16[208,768]{1,0:T(8,128)(2,1)S(1)} %get-tuple-element.37.own_ref), channel_id=1, source_target_pairs={{0,2},{2,4},{4,6},{6,8},{8,10},{10,12},{12,14},{14,16},{16,18},{18... | collective-permute-start | bytes 958472 | tf_op jit(solution)/shard_map/ppermute | solution.py:388
  44.9 12.6 %all-to-all-start.2 = ((bf16[16,32,128]{2,1,0:T(8,128)(2,1)}), bf16[16,32,128]{2,1,0:T(8,128)(2,1)S(1)}, u32[]{:S(2)}, u32[]{:S(2)}) async-start(bf16[16,32,128]{2,1,0:T(8,128)(2,1)} %bitcast.2), calls=%async_computation.2 | async-start | bytes 262144 | tf_op jit(solution)/shard_map/all_to_all | solution.py:394
  49.5 2.0 %copy-start.6 = (f32[384]{0:T(512)S(1)}, f32[384]{0:T(512)}, u32[]{:S(2)}) copy-start(f32[384]{0:T(512)} %param.13) | copy-start | bytes 4612
  50.0 3.7 %collective-permute-start.7 = (f32[8,208]{1,0:T(8,128)S(1)}, f32[8,208]{1,0:T(8,128)S(1)}, u32[]{:S(2)}, u32[]{:S(2)}) collective-permute-start(f32[8,208]{1,0:T(8,128)S(1)} %get-tuple-element.40.refs_0_), channel_id=1, source_target_pairs={{0,1},{1,0},{2,3},{3,2},{4,5},{5,4},{6,7},{7,6},{8,9},{9,8},{10,11... | collective-permute-start | bytes 19976 | tf_op jit(solution)/shard_map/ppermute | solution.py:415
  53.6 3.8 %copy-start.2 = (f32[3,3,32,128]{3,2,1,0:T(8,128)S(1)}, f32[3,3,32,128]{3,2,1,0:T(8,128)}, u32[]{:S(2)}) copy-start(f32[3,3,32,128]{3,2,1,0:T(8,128)} %w_ref.3) | copy-start | bytes 442372

commit v6 on v5

--- a/solution.py
+++ b/solution.py
@@ -47,6 +47,10 @@
 
 def served(n):
     return [0] + list(range(n - 1, 0, -1))
+
+
+def summed_order(n):
+    return [0] + list(range(n // 2, n)) + list(range(1, n // 2))
 
 
 def first_owner(h):
@@ -364,7 +368,7 @@
         )(token_slots[last], weights, early_grads)
     )
     weights, partials[0] = lax.optimization_barrier((weights, partials[0]))
-    for d in served(nz)[1:]:
+    for d in summed_order(nz)[1:]:
         pairs = []
         for z in range(nz):
             pairs += [
@@ -388,7 +392,7 @@
     kv_back = lax.ppermute(kv_own, ("z", "grp"), ring)
 
     ortho = call(functools.partial(ortho_body, heads, nz), sds((hidden, HD), bf16), flops=1e9)(
-        *(partials[d] for d in served(nz))
+        *(partials[d] for d in summed_order(nz))
     )
     queries, ortho = lax.optimization_barrier((queries, ortho))
     rows = lax.all_to_all(

time: 58.9 us -> 59.5 us (1.010)
  starting transfers between devices: 35.7 us -> 36.4 us
    ppermute x3, starting transfers between devices: 8.51 us -> 9.21 us  [on_device(): partials[d] = lax.ppermute(partials[d], ('z', 'grp'), pairs)]
where the time goes in v6:
time: 59.5 us; the launch traced here: 58.9 us
  starting transfers between devices  36.4 us (61%)
  Pallas kernels  12.5 us (21%)
  waiting for transfers between devices  7.64 us (13%)
  between operations  1.48 us (2%)
  local copies, waits for them, and re-layouts  0.93 us (2%)
    ppermute x3, starting transfers between devices, on_device(): partials[d] = lax.ppermute(partials[d], ('z', 'grp'), pairs)  9.21 us
    ppermute x3, starting transfers between devices, on_device(): token_slots[d] = lax.ppermute(token_slots[d], 'grp', pairs)  7.78 us
    all_to_all x1, starting transfers between devices, on_device(): weights = lax.all_to_all(low, ('z', 'grp'), 0, 0, tiled=True)  7.49 us
    all_to_all x1, starting transfers between devices, on_device(): lax.all_to_all(ortho.reshape(count, rows_local, HD), ('z', 'grp'), 0, 0,...  4.56 us
    pallas_call x1, Pallas kernels, on_device(): call(functools.partial(ortho_body, heads, nz), sds((hidden, HD), bf16), f...  3.43 us
    all_to_all x1, starting transfers between devices, on_device(): fast_slots = lax.all_to_all(fast_slots, 'grp', 0, 0, tiled=True)  3.37 us
    all_to_all x1, waiting for transfers between devices, on_device(): lax.all_to_all(ortho.reshape(count, rows_local, HD), ('z', 'grp'), 0, 0,...  2.8 us
    ppermute x1, starting transfers between devices, on_device(): kv_back = lax.ppermute(kv_own, ('z', 'grp'), ring)  2.38 us
  transfers between devices with their start and end apart: 11, of which 5 were waited for; matrix products, arithmetic and copies ran while one was open for 0% of the time, Pallas kernels for 17%

profile of v6, /device:TPU:0, one launch (start us, length us, event | category | flops | bytes accessed | tf_op | source)
XLA Modules:
  0.0 58.9 jit_solution(3820925456996295768)
XLA Ops:
  0.6 0.0 copy-start.1
  0.6 0.9 %copy-done.1 = f32[3,3,32,128]{3,2,1,0:T(8,128)S(1)} copy-done((f32[3,3,32,128]{3,2,1,0:T(8,128)S(1)}, f32[3,3,32,128]{3,2,1,0:T(8,128)}, u32[]{:S(2)}) %copy-start.1) | copy-done | bytes 147480
  1.5 0.8 %shard_map.86.after = bf16[16,3,32,128]{3,2,1,0:T(8,128)(2,1)} custom-call(f32[3,3,32,128]{3,2,1,0:T(8,128)S(1)} %copy-done.1), custom_call_target="tpu_custom_call" | custom-call | flops 1000000 | bytes 1048576 | tf_op jit(solution)/shard_map/pallas_call | solution.py:330
  2.3 0.0 copy-start
  2.3 0.0 copy-start.3
  2.3 0.0 copy-start.4
  2.3 7.5 %all-to-all-start = ((bf16[16,3,32,128]{3,2,1,0:T(8,128)(2,1)}), bf16[16,3,32,128]{3,2,1,0:T(8,128)(2,1)S(1)}, u32[]{:S(2)}, u32[]{:S(2)}) async-start(bf16[16,3,32,128]{3,2,1,0:T(8,128)(2,1)} %shard_map.86.after), calls=%async_computation | async-start | bytes 786432 | tf_op jit(solution)/shard_map/all_to_all | solution.py:347
  9.8 0.0 copy-start.5
  10.5 0.0 copy-done
  10.5 0.0 copy-done.3
  10.5 0.0 copy-done.4
  10.5 0.0 copy-done.5
  10.5 0.6 %shard_map.87 = (bf16[208,768]{1,0:T(8,128)(2,1)S(1)}, bf16[195,384]{1,0:T(8,128)(2,1)S(1)}, bf16[195,384]{1,0:T(8,128)(2,1)S(1)}, bf16[195,384]{1,0:T(8,128)(2,1)S(1)}, bf16[195,384]{1,0:T(8,128)(2,1)S(1)}) custom-call(bf16[16,3,32,128]{3,2,1,0:T(8,128)(2,1)} %shard_map.86.after, s32[1,1]{1,0:T(1,128)} %bitcast.3.update, f32[3,195]{1,0:T(4,128)S(1)} %bitcast.4, ...), custom_call_target="tpu_custom_call" | custom-call | tf_op jit(solution)/shard_map/pallas_call | solution.py:333
  11.1 1.3 %collective-permute-start.1 = (bf16[195,384]{1,0:T(8,128)(2,1)S(1)}, bf16[195,384]{1,0:T(8,128)(2,1)S(1)}, u32[]{:S(2)}, u32[]{:S(2)}) collective-permute-start(bf16[195,384]{1,0:T(8,128)(2,1)S(1)} %get-tuple-element.25), channel_id=1, source_target_pairs={{2,4},{4,2},{6,0},{3,5},{5,3},{7,1},{10,12},{12,10},{14,8},{11,13}... | collective-permute-start | bytes 449288 | tf_op jit(solution)/shard_map/ppermute | solution.py:352
  12.4 4.6 %collective-permute-start.2 = (bf16[195,384]{1,0:T(8,128)(2,1)S(1)}, bf16[195,384]{1,0:T(8,128)(2,1)S(1)}, u32[]{:S(2)}, u32[]{:S(2)}) collective-permute-start(bf16[195,384]{1,0:T(8,128)(2,1)S(1)} %get-tuple-element.26), channel_id=1, source_target_pairs={{0,2},{2,0},{6,4},{1,3},{3,1},{7,5},{8,10},{10,8},{14,12},{9,11},{... | collective-permute-start | bytes 449288 | tf_op jit(solution)/shard_map/ppermute | solution.py:352
  17.0 1.9 %collective-permute-start = (bf16[195,384]{1,0:T(8,128)(2,1)S(1)}, bf16[195,384]{1,0:T(8,128)(2,1)S(1)}, u32[]{:S(2)}, u32[]{:S(2)}) collective-permute-start(bf16[195,384]{1,0:T(8,128)(2,1)S(1)} %get-tuple-element.23), channel_id=1, source_target_pairs={{0,4},{4,0},{6,2},{1,5},{5,1},{7,3},{8,12},{12,8},{14,10},{9,13},{... | collective-permute-start | bytes 449288 | tf_op jit(solution)/shard_map/ppermute | solution.py:352
  18.9 0.8 %collective-permute-done.1.refs_1_ = bf16[195,384]{1,0:T(8,128)(2,1)S(1)} collective-permute-done((bf16[195,384]{1,0:T(8,128)(2,1)S(1)}, bf16[195,384]{1,0:T(8,128)(2,1)S(1)}, u32[]{:S(2)}, u32[]{:S(2)}) %collective-permute-start.1) | collective-permute-done | bytes 149792 | tf_op jit(solution)/shard_map/ppermute | solution.py:352
  19.7 0.0 collective-permute-done.2.refs_2_
  19.7 2.3 %all-to-all-done.refs_3_.w_ref = bf16[16,3,32,128]{3,2,1,0:T(8,128)(2,1)S(1)} async-done(((bf16[16,3,32,128]{3,2,1,0:T(8,128)(2,1)}), bf16[16,3,32,128]{3,2,1,0:T(8,128)(2,1)S(1)}, u32[]{:S(2)}, u32[]{:S(2)}) %all-to-all-start) | async-done | bytes 393248 | tf_op jit(solution)/shard_map/all_to_all | solution.py:347
  22.0 2.2 %shard_map.88 = (f32[3,512,128]{2,1,0:T(8,128)S(1)}, bf16[3,208,128]{2,1,0:T(8,128)(2,1)S(1)}) custom-call(bf16[195,384]{1,0:T(8,128)(2,1)S(1)} %get-tuple-element.24.refs_0_, bf16[195,384]{1,0:T(8,128)(2,1)S(1)} %collective-permute-done.1.refs_1_, bf16[195,384]{1,0:T(8,128)(2,1)S(1)} %collective-permute-done.2.refs_2_, ...), custom_call_target="tpu_custom_call" | custom-call | flops 1000000000 | bytes 1048576 | tf_op jit(solution)/shard_map/pallas_call | solution.py:356
  24.3 0.9 %collective-permute-done.token_ref = bf16[195,384]{1,0:T(8,128)(2,1)S(1)} collective-permute-done((bf16[195,384]{1,0:T(8,128)(2,1)S(1)}, bf16[195,384]{1,0:T(8,128)(2,1)S(1)}, u32[]{:S(2)}, u32[]{:S(2)}) %collective-permute-start) | collective-permute-done | bytes 149792 | tf_op jit(solution)/shard_map/ppermute | solution.py:352
  25.2 0.8 %shard_map.89 = (bf16[512,128]{1,0:T(8,128)(2,1)S(1)}, bf16[512,128]{1,0:T(8,128)(2,1)S(1)}, bf16[512,128]{1,0:T(8,128)(2,1)S(1)}, bf16[512,128]{1,0:T(8,128)(2,1)S(1)}) custom-call(bf16[195,384]{1,0:T(8,128)(2,1)S(1)} %collective-permute-done.token_ref, bf16[16,3,32,128]{3,2,1,0:T(8,128)(2,1)S(1)} %all-to-all-done.refs_3_.w_ref, ...), custom_call_target="tpu_custom_call" | custom-call | flops 500000000 | bytes 1048576 | tf_op jit(solution)/shard_map/pallas_call | solution.py:363
  26.0 4.1 %collective-permute-start.3 = (bf16[512,128]{1,0:T(8,128)(2,1)S(1)}, bf16[512,128]{1,0:T(8,128)(2,1)S(1)}, u32[]{:S(2)}, u32[]{:S(2)}) collective-permute-start(bf16[512,128]{1,0:T(8,128)(2,1)S(1)} %get-tuple-element.33), channel_id=1, source_target_pairs={{0,16},{2,18},{4,20},{10,26},{16,0},{20,4},{24,8},{26,10},{28,12},... | collective-permute-start | bytes 393224 | tf_op jit(solution)/shard_map/ppermute | solution.py:379
  30.1 1.3 %collective-permute-start.4 = (bf16[512,128]{1,0:T(8,128)(2,1)S(1)}, bf16[512,128]{1,0:T(8,128)(2,1)S(1)}, u32[]{:S(2)}, u32[]{:S(2)}) collective-permute-start(bf16[512,128]{1,0:T(8,128)(2,1)S(1)} %get-tuple-element.34), channel_id=1, source_target_pairs={{2,26},{8,16},{10,18},{12,20},{16,8},{18,10},{20,12},{24,0},{28,4}... | collective-permute-start | bytes 393224 | tf_op jit(solution)/shard_map/ppermute | solution.py:379
  31.4 3.8 %collective-permute-start.5 = (bf16[512,128]{1,0:T(8,128)(2,1)S(1)}, bf16[512,128]{1,0:T(8,128)(2,1)S(1)}, u32[]{:S(2)}, u32[]{:S(2)}) collective-permute-start(bf16[512,128]{1,0:T(8,128)(2,1)S(1)} %get-tuple-element.35), channel_id=1, source_target_pairs={{0,8},{2,10},{4,12},{8,0},{12,4},{18,26},{24,16},{26,18},{28,20},{... | collective-permute-start | bytes 393224 | tf_op jit(solution)/shard_map/ppermute | solution.py:379
  35.2 1.1 %shard_map.90 = bf16[4,208,128]{2,1,0:T(8,128)(2,1)} custom-call(bf16[195,384]{1,0:T(8,128)(2,1)S(1)} %collective-permute-done.token_ref, bf16[16,3,32,128]{3,2,1,0:T(8,128)(2,1)S(1)} %all-to-all-done.refs_3_.w_ref, bf16[3,208,128]{2,1,0:T(8,128)(2,1)S(1)} %get-tuple-element.31.early), custom_call_target="tpu_custom_call" | custom-call | flops 1000 | bytes 1024 | tf_op jit(solution)/shard_map/pallas_call | solution.py:381
  36.4 3.4 %all-to-all-start.1 = ((bf16[4,208,128]{2,1,0:T(8,128)(2,1)}), bf16[4,208,128]{2,1,0:T(8,128)(2,1)S(1)}, u32[]{:S(2)}, u32[]{:S(2)}) async-start(bf16[4,208,128]{2,1,0:T(8,128)(2,1)} %shard_map.90), calls=%async_computation.1 | async-start | bytes 425984 | tf_op jit(solution)/shard_map/all_to_all | solution.py:389
  39.7 2.4 %collective-permute-start.6 = (bf16[208,768]{1,0:T(8,128)(2,1)S(1)}, bf16[208,768]{1,0:T(8,128)(2,1)S(1)}, u32[]{:S(2)}, u32[]{:S(2)}) collective-permute-start(bf16[208,768]{1,0:T(8,128)(2,1)S(1)} %get-tuple-element.37.own_ref), channel_id=1, source_target_pairs={{0,2},{2,4},{4,6},{6,8},{8,10},{10,12},{12,14},{14,16},{16,18},{18... | collective-permute-start | bytes 958472 | tf_op jit(solution)/shard_map/ppermute | solution.py:392
  42.1 0.0 collective-permute-done.3.refs_1_
  42.1 0.0 collective-permute-done.4.refs_2_
  42.1 0.0 collective-permute-done.5.refs_3_
  42.2 3.4 %shard_map.91 = bf16[512,128]{1,0:T(8,128)(2,1)} custom-call(bf16[512,128]{1,0:T(8,128)(2,1)S(1)} %get-tuple-element.32.refs_0_, bf16[512,128]{1,0:T(8,128)(2,1)S(1)} %collective-permute-done.3.refs_1_, bf16[512,128]{1,0:T(8,128)(2,1)S(1)} %collective-permute-done.4.refs_2_, bf16[512,128]{1,0:T(8,128)(2,1)S(1)} %collective-permute-done.5.refs_3_), custom_call_target="tpu_custom_call" | custom-call | flops 1000000000 | bytes 1048576 | tf_op jit(solution)/shard_map/pallas_call | solution.py:394
  45.6 0.0 all-to-all-done.1.slots
  45.6 4.6 %all-to-all-start.2 = ((bf16[16,32,128]{2,1,0:T(8,128)(2,1)}), bf16[16,32,128]{2,1,0:T(8,128)(2,1)S(1)}, u32[]{:S(2)}, u32[]{:S(2)}) async-start(bf16[16,32,128]{2,1,0:T(8,128)(2,1)} %bitcast.2), calls=%async_computation.2 | async-start | bytes 262144 | tf_op jit(solution)/shard_map/all_to_all | solution.py:398
  50.2 0.0 copy-start.6
  50.2 0.4 shard_map.93
  50.6 1.6 %collective-permute-start.7 = (f32[8,208]{1,0:T(8,128)S(1)}, f32[8,208]{1,0:T(8,128)S(1)}, u32[]{:S(2)}, u32[]{:S(2)}) collective-permute-start(f32[8,208]{1,0:T(8,128)S(1)} %get-tuple-element.40.refs_0_), channel_id=1, source_target_pairs={{0,1},{1,0},{2,3},{3,2},{4,5},{5,4},{6,7},{7,6},{8,9},{9,8},{10,11... | collective-permute-start | bytes 19976 | tf_op jit(solution)/shard_map/ppermute | solution.py:419
  52.2 0.0 copy-done.6
  52.2 0.0 collective-permute-done.6.back_ref
  52.2 1.3 %shard_map.92.attended_ref = f32[208,384]{1,0:T(8,128)S(1)} custom-call(bf16[195,384]{1,0:T(8,128)(2,1)S(1)} %copy-done, bf16[208,768]{1,0:T(8,128)(2,1)S(1)} %get-tuple-element.37.own_ref, bf16[208,768]{1,0:T(8,128)(2,1)S(1)} %collective-permute-done.6.back_ref), custom_call_target="tpu_custom_call" | custom-call | tf_op jit(solution)/shard_map/pallas_call | solution.py:405
  53.5 0.8 %collective-permute-done.7.refs_1_ = f32[8,208]{1,0:T(8,128)S(1)} collective-permute-done((f32[8,208]{1,0:T(8,128)S(1)}, f32[8,208]{1,0:T(8,128)S(1)}, u32[]{:S(2)}, u32[]{:S(2)}) %collective-permute-start.7) | collective-permute-done | bytes 6688 | tf_op jit(solution)/shard_map/ppermute | solution.py:419
  54.3 0.0 copy-start.2
  54.3 1.0 %shard_map.94 = bf16[195,384]{1,0:T(8,128)(2,1)} custom-call(f32[1,384]{1,0:T(1,128)S(1)} %reshape.13.gain_ref, f32[208,384]{1,0:T(8,128)S(1)} %shard_map.92.attended_ref, bf16[208,384]{1,0:T(8,128)(2,1)S(1)} %get-tuple-element.39.fast_ref, f32[8,208]{1,0:T(8,128)S(1)} %get-tuple-element.40.refs_0_, f32[8,208]{1,0:T(8,128)S(1)} %collective-permute-done.7.refs_1_), custom_call_target="tpu_custom_call" | custom-call | tf_op jit(solution)/shard_map/pallas_call | solution.py:421
  55.3 2.8 %all-to-all-done.2.rows_ref = bf16[16,32,128]{2,1,0:T(8,128)(2,1)S(1)} async-done(((bf16[16,32,128]{2,1,0:T(8,128)(2,1)}), bf16[16,32,128]{2,1,0:T(8,128)(2,1)S(1)}, u32[]{:S(2)}, u32[]{:S(2)}) %all-to-all-start.2) | async-done | bytes 131104 | tf_op jit(solution)/shard_map/all_to_all | solution.py:398
  58.1 0.0 copy-done.2
  58.1 0.8 %shard_map.95 = f32[3,3,32,128]{3,2,1,0:T(8,128)} custom-call(f32[3,3,32,128]{3,2,1,0:T(8,128)S(1)} %copy-done.2, bf16[16,32,128]{2,1,0:T(8,128)(2,1)S(1)} %all-to-all-done.2.rows_ref), custom_call_target="tpu_custom_call" | custom-call | flops 1000000 | bytes 1048576 | tf_op jit(solution)/shard_map/pallas_call | solution.py:401
  (1 shorter events, 0.0 us)
Async XLA Ops:
  0.6 0.9 %copy-start.1 = (f32[3,3,32,128]{3,2,1,0:T(8,128)S(1)}, f32[3,3,32,128]{3,2,1,0:T(8,128)}, u32[]{:S(2)}) copy-start(f32[3,3,32,128]{3,2,1,0:T(8,128)} %w_ref.3) | copy-start | bytes 442372
  2.3 8.2 %copy-start = (bf16[195,384]{1,0:T(8,128)(2,1)S(1)}, bf16[195,384]{1,0:T(8,128)(2,1)}, u32[]{:S(2)}) copy-start(bf16[195,384]{1,0:T(8,128)(2,1)} %q_ref.2) | copy-start | bytes 449284
  2.3 8.2 %copy-start.3 = (bf16[195,384]{1,0:T(8,128)(2,1)S(1)}, bf16[195,384]{1,0:T(8,128)(2,1)}, u32[]{:S(2)}) copy-start(bf16[195,384]{1,0:T(8,128)(2,1)} %k_ref.1) | copy-start | bytes 449284
  2.3 8.2 %copy-start.4 = (bf16[195,384]{1,0:T(8,128)(2,1)S(1)}, bf16[195,384]{1,0:T(8,128)(2,1)}, u32[]{:S(2)}) copy-start(bf16[195,384]{1,0:T(8,128)(2,1)} %v_ref.1) | copy-start | bytes 449284
  2.3 19.7 %all-to-all-start = ((bf16[16,3,32,128]{3,2,1,0:T(8,128)(2,1)}), bf16[16,3,32,128]{3,2,1,0:T(8,128)(2,1)S(1)}, u32[]{:S(2)}, u32[]{:S(2)}) async-start(bf16[16,3,32,128]{3,2,1,0:T(8,128)(2,1)} %shard_map.86.after), calls=%async_computation | async-start | bytes 786432 | tf_op jit(solution)/shard_map/all_to_all | solution.py:347
  9.8 0.7 %copy-start.5 = (f32[195,3]{0,1:T(4,128)S(1)}, f32[195,3]{0,1:T(4,128)}, u32[]{:S(2)}) copy-start(f32[195,3]{0,1:T(4,128)} %param.10) | copy-start | bytes 7024
  11.1 8.6 %collective-permute-start.1 = (bf16[195,384]{1,0:T(8,128)(2,1)S(1)}, bf16[195,384]{1,0:T(8,128)(2,1)S(1)}, u32[]{:S(2)}, u32[]{:S(2)}) collective-permute-start(bf16[195,384]{1,0:T(8,128)(2,1)S(1)} %get-tuple-element.25), channel_id=1, source_target_pairs={{2,4},{4,2},{6,0},{3,5},{5,3},{7,1},{10,12},{12,10},{14,8},{11,13}... | collective-permute-start | bytes 449288 | tf_op jit(solution)/shard_map/ppermute | solution.py:352
  12.4 7.3 %collective-permute-start.2 = (bf16[195,384]{1,0:T(8,128)(2,1)S(1)}, bf16[195,384]{1,0:T(8,128)(2,1)S(1)}, u32[]{:S(2)}, u32[]{:S(2)}) collective-permute-start(bf16[195,384]{1,0:T(8,128)(2,1)S(1)} %get-tuple-element.26), channel_id=1, source_target_pairs={{0,2},{2,0},{6,4},{1,3},{3,1},{7,5},{8,10},{10,8},{14,12},{9,11},{... | collective-permute-start | bytes 449288 | tf_op jit(solution)/shard_map/ppermute | solution.py:352
  17.0 8.2 %collective-permute-start = (bf16[195,384]{1,0:T(8,128)(2,1)S(1)}, bf16[195,384]{1,0:T(8,128)(2,1)S(1)}, u32[]{:S(2)}, u32[]{:S(2)}) collective-permute-start(bf16[195,384]{1,0:T(8,128)(2,1)S(1)} %get-tuple-element.23), channel_id=1, source_target_pairs={{0,4},{4,0},{6,2},{1,5},{5,1},{7,3},{8,12},{12,8},{14,10},{9,13},{... | collective-permute-start | bytes 449288 | tf_op jit(solution)/shard_map/ppermute | solution.py:352
  26.0 16.1 %collective-permute-start.3 = (bf16[512,128]{1,0:T(8,128)(2,1)S(1)}, bf16[512,128]{1,0:T(8,128)(2,1)S(1)}, u32[]{:S(2)}, u32[]{:S(2)}) collective-permute-start(bf16[512,128]{1,0:T(8,128)(2,1)S(1)} %get-tuple-element.33), channel_id=1, source_target_pairs={{0,16},{2,18},{4,20},{10,26},{16,0},{20,4},{24,8},{26,10},{28,12},... | collective-permute-start | bytes 393224 | tf_op jit(solution)/shard_map/ppermute | solution.py:379
  30.1 12.0 %collective-permute-start.4 = (bf16[512,128]{1,0:T(8,128)(2,1)S(1)}, bf16[512,128]{1,0:T(8,128)(2,1)S(1)}, u32[]{:S(2)}, u32[]{:S(2)}) collective-permute-start(bf16[512,128]{1,0:T(8,128)(2,1)S(1)} %get-tuple-element.34), channel_id=1, source_target_pairs={{2,26},{8,16},{10,18},{12,20},{16,8},{18,10},{20,12},{24,0},{28,4}... | collective-permute-start | bytes 393224 | tf_op jit(solution)/shard_map/ppermute | solution.py:379
  31.4 10.7 %collective-permute-start.5 = (bf16[512,128]{1,0:T(8,128)(2,1)S(1)}, bf16[512,128]{1,0:T(8,128)(2,1)S(1)}, u32[]{:S(2)}, u32[]{:S(2)}) collective-permute-start(bf16[512,128]{1,0:T(8,128)(2,1)S(1)} %get-tuple-element.35), channel_id=1, source_target_pairs={{0,8},{2,10},{4,12},{8,0},{12,4},{18,26},{24,16},{26,18},{28,20},{... | collective-permute-start | bytes 393224 | tf_op jit(solution)/shard_map/ppermute | solution.py:379
  36.4 9.2 %all-to-all-start.1 = ((bf16[4,208,128]{2,1,0:T(8,128)(2,1)}), bf16[4,208,128]{2,1,0:T(8,128)(2,1)S(1)}, u32[]{:S(2)}, u32[]{:S(2)}) async-start(bf16[4,208,128]{2,1,0:T(8,128)(2,1)} %shard_map.90), calls=%async_computation.1 | async-start | bytes 425984 | tf_op jit(solution)/shard_map/all_to_all | solution.py:389
  39.7 12.4 %collective-permute-start.6 = (bf16[208,768]{1,0:T(8,128)(2,1)S(1)}, bf16[208,768]{1,0:T(8,128)(2,1)S(1)}, u32[]{:S(2)}, u32[]{:S(2)}) collective-permute-start(bf16[208,768]{1,0:T(8,128)(2,1)S(1)} %get-tuple-element.37.own_ref), channel_id=1, source_target_pairs={{0,2},{2,4},{4,6},{6,8},{8,10},{10,12},{12,14},{14,16},{16,18},{18... | collective-permute-start | bytes 958472 | tf_op jit(solution)/shard_map/ppermute | solution.py:392
  45.6 12.5 %all-to-all-start.2 = ((bf16[16,32,128]{2,1,0:T(8,128)(2,1)}), bf16[16,32,128]{2,1,0:T(8,128)(2,1)S(1)}, u32[]{:S(2)}, u32[]{:S(2)}) async-start(bf16[16,32,128]{2,1,0:T(8,128)(2,1)} %bitcast.2), calls=%async_computation.2 | async-start | bytes 262144 | tf_op jit(solution)/shard_map/all_to_all | solution.py:398
  50.2 2.0 %copy-start.6 = (f32[384]{0:T(512)S(1)}, f32[384]{0:T(512)}, u32[]{:S(2)}) copy-start(f32[384]{0:T(512)} %param.13) | copy-start | bytes 4612
  50.6 3.7 %collective-permute-start.7 = (f32[8,208]{1,0:T(8,128)S(1)}, f32[8,208]{1,0:T(8,128)S(1)}, u32[]{:S(2)}, u32[]{:S(2)}) collective-permute-start(f32[8,208]{1,0:T(8,128)S(1)} %get-tuple-element.40.refs_0_), channel_id=1, source_target_pairs={{0,1},{1,0},{2,3},{3,2},{4,5},{5,4},{6,7},{7,6},{8,9},{9,8},{10,11... | collective-permute-start | bytes 19976 | tf_op jit(solution)/shard_map/ppermute | solution.py:419
  54.3 3.8 %copy-start.2 = (f32[3,3,32,128]{3,2,1,0:T(8,128)S(1)}, f32[3,3,32,128]{3,2,1,0:T(8,128)}, u32[]{:S(2)}) copy-start(f32[3,3,32,128]{3,2,1,0:T(8,128)} %w_ref.3) | copy-start | bytes 442372

commit v7 on v5

--- a/solution.py
+++ b/solution.py
@@ -267,7 +267,7 @@
             out[m, h] = summed * (old * new)
 
 
-def attend_body(heads, tokens, q_ref, own_ref, back_ref, out):
+def attend_body(heads, tokens, q_ref, own_ref, inside_ref, behind_ref, out):
     padded = own_ref.shape[0]
     span = heads * HD
     column = lax.broadcasted_iota(jnp.int32, (1, 2 * padded), 1)
@@ -275,11 +275,15 @@
     first = (place[0] == 0) & (place[1] == 0)
     stop = jnp.where(first, padded, padded + tokens)
     live = (column < tokens) | ((column >= padded) & (column < stop))
+
+    def back(cols):
+        return inside_ref[:, cols] + behind_ref[:, cols]
+
     for h in range(heads):
         cols = slice(h * HD, (h + 1) * HD)
-        key = jnp.concatenate([own_ref[:, cols], back_ref[:, cols]], axis=0)
+        key = jnp.concatenate([own_ref[:, cols], back(cols)], axis=0)
         vcols = slice(span + h * HD, span + (h + 1) * HD)
-        value = jnp.concatenate([own_ref[:, vcols], back_ref[:, vcols]], axis=0)
+        value = jnp.concatenate([own_ref[:, vcols], back(vcols)], axis=0)
         scores = dot(q_ref[:, cols], key, (1, 1)) * (HD ** (-0.5))
         scores = jnp.where(live, scores, -1e30)
         weights = jnp.exp(scores - jnp.max(scores, axis=1, keepdims=True))
@@ -347,6 +351,8 @@
         pairs = [(s, s ^ d) for s in range(group) if s ^ d < heads]
         token_slots[d] = lax.ppermute(token_slots[d], "grp", pairs)
 
+    inside = lax.ppermute(kv_own, "grp", [(j, j + 1) for j in range(group - 1)])
+
     last = group // 2
     early_slots = [d for d in served(group) if d != last]
     early_grads, early_fast = call(
@@ -363,7 +369,7 @@
             flops=5e8,
         )(token_slots[last], weights, early_grads)
     )
-    weights, partials[0] = lax.optimization_barrier((weights, partials[0]))
+    weights, inside, partials[0] = lax.optimization_barrier((weights, inside, partials[0]))
     for d in served(nz)[1:]:
         pairs = []
         for z in range(nz):
@@ -384,8 +390,9 @@
     kv_own, partials[0], fast_slots = lax.optimization_barrier((kv_own, partials[0], fast_slots))
     fast_slots = lax.all_to_all(fast_slots, "grp", 0, 0, tiled=True)
 
-    ring = [(i, i + 1) for i in range(count - 1)]
-    kv_back = lax.ppermute(kv_own, ("z", "grp"), ring)
+    behind = lax.ppermute(
+        kv_own, ("z", "grp"), [((z + 1) * group - 1, (z + 1) * group) for z in range(nz - 1)]
+    )
 
     ortho = call(functools.partial(ortho_body, heads, nz), sds((hidden, HD), bf16), flops=1e9)(
         *(partials[d] for d in served(nz))
@@ -402,10 +409,10 @@
         functools.partial(attend_body, heads, tokens),
         grid=(1,),
         out_shape=sds((padded, span), f32),
-        in_specs=[whole(padded, span)] + [whole(padded, 2 * span)] * 2,
+        in_specs=[whole(padded, span)] + [whole(padded, 2 * span)] * 3,
         out_specs=whole(padded, span),
         compiler_params=pltpu.CompilerParams(vmem_limit_bytes=VMEM_LIMIT),
-    )(queries, kv_own, kv_back)
+    )(queries, kv_own, inside, behind)
     fast, squares = call(
         functools.partial(assemble_body, heads),
         [sds((padded, span), bf16), sds((8, padded), f32)],

time: 58.9 us -> 59 us (level)
    all_to_all x1, waiting for transfers between devices: 2.32 us -> 0.63 us  [on_device(): weights = lax.all_to_all(low, ('z', 'grp'), 0, 0, tiled=True)]
    all_to_all x1, waiting for transfers between devices: 0.01 us -> 1.13 us  [on_device(): fast_slots = lax.all_to_all(fast_slots, 'grp', 0, 0, tiled=True)]
    all_to_all x1, starting transfers between devices: 4.61 us -> 3.51 us  [on_device(): lax.all_to_all(ortho.reshape(count, rows_local, HD), ('z', 'grp'), 0, 0,...]
    ppermute x3, waiting for transfers between devices: 1.74 us -> 2.48 us  [on_device(): token_slots[d] = lax.ppermute(token_slots[d], 'grp', pairs)]
    ppermute x1 -> x2, starting transfers between devices: 2.38 us -> 2.62 us  [the longest x1 1.94 us: on_device(): inside = lax.ppermute(kv_own, 'grp', [(j, j + 1) for j in range(group - 1)])]
  transfers between devices with their start and end apart: 11 -> 12, of which waited for: 5 -> 6; matrix products, arithmetic and copies ran while one was open for 0% -> 0% of each run, Pallas kernels for 17% -> 19%
where the time goes in v7:
time: 59 us; the launch traced here: 58.4 us
  starting transfers between devices  35.5 us (60%)
  Pallas kernels  12.5 us (21%)
  waiting for transfers between devices  8 us (14%)
  between operations  1.5 us (3%)
  local copies, waits for them, and re-layouts  0.93 us (2%)
    ppermute x3, starting transfers between devices, on_device(): partials[d] = lax.ppermute(partials[d], ('z', 'grp'), pairs)  8.66 us
    ppermute x3, starting transfers between devices, on_device(): token_slots[d] = lax.ppermute(token_slots[d], 'grp', pairs)  8.27 us
    all_to_all x1, starting transfers between devices, on_device(): weights = lax.all_to_all(low, ('z', 'grp'), 0, 0, tiled=True)  7.49 us
    all_to_all x1, starting transfers between devices, on_device(): lax.all_to_all(ortho.reshape(count, rows_local, HD), ('z', 'grp'), 0, 0,...  3.51 us
    pallas_call x1, Pallas kernels, on_device(): call(functools.partial(ortho_body, heads, nz), sds((hidden, HD), bf16), f...  3.41 us
    all_to_all x1, starting transfers between devices, on_device(): fast_slots = lax.all_to_all(fast_slots, 'grp', 0, 0, tiled=True)  3.37 us
    all_to_all x1, waiting for transfers between devices, on_device(): lax.all_to_all(ortho.reshape(count, rows_local, HD), ('z', 'grp'), 0, 0,...  2.76 us
    ppermute x3, waiting for transfers between devices, on_device(): token_slots[d] = lax.ppermute(token_slots[d], 'grp', pairs)  2.48 us
  transfers between devices with their start and end apart: 12, of which 6 were waited for; matrix products, arithmetic and copies ran while one was open for 0% of the time, Pallas kernels for 19%

profile of v7, /device:TPU:0, one launch (start us, length us, event | category | flops | bytes accessed | tf_op | source)
XLA Modules:
  0.0 58.4 jit_solution(7625720479495706265)
XLA Ops:
  0.6 0.0 copy-start.1
  0.6 0.9 %copy-done.1 = f32[3,3,32,128]{3,2,1,0:T(8,128)S(1)} copy-done((f32[3,3,32,128]{3,2,1,0:T(8,128)S(1)}, f32[3,3,32,128]{3,2,1,0:T(8,128)}, u32[]{:S(2)}) %copy-start.1) | copy-done | bytes 147480
  1.5 0.8 %shard_map.86.after = bf16[16,3,32,128]{3,2,1,0:T(8,128)(2,1)} custom-call(f32[3,3,32,128]{3,2,1,0:T(8,128)S(1)} %copy-done.1), custom_call_target="tpu_custom_call" | custom-call | flops 1000000 | bytes 1048576 | tf_op jit(solution)/shard_map/pallas_call | solution.py:330
  2.3 0.0 copy-start
  2.3 0.0 copy-start.3
  2.3 0.0 copy-start.4
  2.3 7.5 %all-to-all-start = ((bf16[16,3,32,128]{3,2,1,0:T(8,128)(2,1)}), bf16[16,3,32,128]{3,2,1,0:T(8,128)(2,1)S(1)}, u32[]{:S(2)}, u32[]{:S(2)}) async-start(bf16[16,3,32,128]{3,2,1,0:T(8,128)(2,1)} %shard_map.86.after), calls=%async_computation | async-start | bytes 786432 | tf_op jit(solution)/shard_map/all_to_all | solution.py:347
  9.8 0.0 copy-start.5
  10.5 0.0 copy-done
  10.5 0.0 copy-done.3
  10.5 0.0 copy-done.4
  10.5 0.0 copy-done.5
  10.5 0.6 %shard_map.87 = (bf16[208,768]{1,0:T(8,128)(2,1)S(1)}, bf16[195,384]{1,0:T(8,128)(2,1)S(1)}, bf16[195,384]{1,0:T(8,128)(2,1)S(1)}, bf16[195,384]{1,0:T(8,128)(2,1)S(1)}, bf16[195,384]{1,0:T(8,128)(2,1)S(1)}) custom-call(bf16[16,3,32,128]{3,2,1,0:T(8,128)(2,1)} %shard_map.86.after, s32[1,1]{1,0:T(1,128)} %bitcast.3.update, f32[3,195]{1,0:T(4,128)S(1)} %bitcast.4, ...), custom_call_target="tpu_custom_call" | custom-call | tf_op jit(solution)/shard_map/pallas_call | solution.py:333
  11.1 1.3 %collective-permute-start.2 = (bf16[195,384]{1,0:T(8,128)(2,1)S(1)}, bf16[195,384]{1,0:T(8,128)(2,1)S(1)}, u32[]{:S(2)}, u32[]{:S(2)}) collective-permute-start(bf16[195,384]{1,0:T(8,128)(2,1)S(1)} %get-tuple-element.26), channel_id=1, source_target_pairs={{2,4},{4,2},{6,0},{3,5},{5,3},{7,1},{10,12},{12,10},{14,8},{11,13}... | collective-permute-start | bytes 449288 | tf_op jit(solution)/shard_map/ppermute | solution.py:352
  12.4 4.6 %collective-permute-start.3 = (bf16[195,384]{1,0:T(8,128)(2,1)S(1)}, bf16[195,384]{1,0:T(8,128)(2,1)S(1)}, u32[]{:S(2)}, u32[]{:S(2)}) collective-permute-start(bf16[195,384]{1,0:T(8,128)(2,1)S(1)} %get-tuple-element.27), channel_id=1, source_target_pairs={{0,2},{2,0},{6,4},{1,3},{3,1},{7,5},{8,10},{10,8},{14,12},{9,11},{... | collective-permute-start | bytes 449288 | tf_op jit(solution)/shard_map/ppermute | solution.py:352
  17.0 1.9 %collective-permute-start = (bf16[208,768]{1,0:T(8,128)(2,1)S(1)}, bf16[208,768]{1,0:T(8,128)(2,1)S(1)}, u32[]{:S(2)}, u32[]{:S(2)}) collective-permute-start(bf16[208,768]{1,0:T(8,128)(2,1)S(1)} %get-tuple-element.38.own_ref), channel_id=1, source_target_pairs={{0,2},{2,4},{4,6},{1,3},{3,5},{5,7},{8,10},{10,12},{12,14},{9,11},... | collective-permute-start | bytes 958472 | tf_op jit(solution)/shard_map/ppermute | solution.py:354
  18.9 2.4 %collective-permute-start.1 = (bf16[195,384]{1,0:T(8,128)(2,1)S(1)}, bf16[195,384]{1,0:T(8,128)(2,1)S(1)}, u32[]{:S(2)}, u32[]{:S(2)}) collective-permute-start(bf16[195,384]{1,0:T(8,128)(2,1)S(1)} %get-tuple-element.24), channel_id=1, source_target_pairs={{0,4},{4,0},{6,2},{1,5},{5,1},{7,3},{8,12},{12,8},{14,10},{9,13},{... | collective-permute-start | bytes 449288 | tf_op jit(solution)/shard_map/ppermute | solution.py:352
  21.4 0.0 collective-permute-done.2.refs_1_
  21.4 0.0 collective-permute-done.3.refs_2_
  21.4 0.6 %all-to-all-done.refs_3_.w_ref = bf16[16,3,32,128]{3,2,1,0:T(8,128)(2,1)S(1)} async-done(((bf16[16,3,32,128]{3,2,1,0:T(8,128)(2,1)}), bf16[16,3,32,128]{3,2,1,0:T(8,128)(2,1)S(1)}, u32[]{:S(2)}, u32[]{:S(2)}) %all-to-all-start) | async-done | bytes 393248 | tf_op jit(solution)/shard_map/all_to_all | solution.py:347
  22.0 2.2 %shard_map.88 = (f32[3,512,128]{2,1,0:T(8,128)S(1)}, bf16[3,208,128]{2,1,0:T(8,128)(2,1)S(1)}) custom-call(bf16[195,384]{1,0:T(8,128)(2,1)S(1)} %get-tuple-element.25.refs_0_, bf16[195,384]{1,0:T(8,128)(2,1)S(1)} %collective-permute-done.2.refs_1_, bf16[195,384]{1,0:T(8,128)(2,1)S(1)} %collective-permute-done.3.refs_2_, ...), custom_call_target="tpu_custom_call" | custom-call | flops 1000000000 | bytes 1048576 | tf_op jit(solution)/shard_map/pallas_call | solution.py:358
  24.2 2.5 %collective-permute-done.1.token_ref = bf16[195,384]{1,0:T(8,128)(2,1)S(1)} collective-permute-done((bf16[195,384]{1,0:T(8,128)(2,1)S(1)}, bf16[195,384]{1,0:T(8,128)(2,1)S(1)}, u32[]{:S(2)}, u32[]{:S(2)}) %collective-permute-start.1) | collective-permute-done | bytes 149792 | tf_op jit(solution)/shard_map/ppermute | solution.py:352
  26.7 0.8 %shard_map.89 = (bf16[512,128]{1,0:T(8,128)(2,1)S(1)}, bf16[512,128]{1,0:T(8,128)(2,1)S(1)}, bf16[512,128]{1,0:T(8,128)(2,1)S(1)}, bf16[512,128]{1,0:T(8,128)(2,1)S(1)}) custom-call(bf16[195,384]{1,0:T(8,128)(2,1)S(1)} %collective-permute-done.1.token_ref, bf16[16,3,32,128]{3,2,1,0:T(8,128)(2,1)S(1)} %all-to-all-done.refs_3_.w_ref, ...), custom_call_target="tpu_custom_call" | custom-call | flops 500000000 | bytes 1048576 | tf_op jit(solution)/shard_map/pallas_call | solution.py:365
  27.5 1.3 %collective-permute-start.4 = (bf16[512,128]{1,0:T(8,128)(2,1)S(1)}, bf16[512,128]{1,0:T(8,128)(2,1)S(1)}, u32[]{:S(2)}, u32[]{:S(2)}) collective-permute-start(bf16[512,128]{1,0:T(8,128)(2,1)S(1)} %get-tuple-element.34), channel_id=1, source_target_pairs={{2,26},{8,16},{10,18},{12,20},{16,8},{18,10},{20,12},{24,0},{28,4}... | collective-permute-start | bytes 393224 | tf_op jit(solution)/shard_map/ppermute | solution.py:381
  28.8 5.4 %collective-permute-start.5 = (bf16[512,128]{1,0:T(8,128)(2,1)S(1)}, bf16[512,128]{1,0:T(8,128)(2,1)S(1)}, u32[]{:S(2)}, u32[]{:S(2)}) collective-permute-start(bf16[512,128]{1,0:T(8,128)(2,1)S(1)} %get-tuple-element.35), channel_id=1, source_target_pairs={{0,16},{2,18},{4,20},{10,26},{16,0},{20,4},{24,8},{26,10},{28,12},... | collective-permute-start | bytes 393224 | tf_op jit(solution)/shard_map/ppermute | solution.py:381
  34.3 1.9 %collective-permute-start.6 = (bf16[512,128]{1,0:T(8,128)(2,1)S(1)}, bf16[512,128]{1,0:T(8,128)(2,1)S(1)}, u32[]{:S(2)}, u32[]{:S(2)}) collective-permute-start(bf16[512,128]{1,0:T(8,128)(2,1)S(1)} %get-tuple-element.36), channel_id=1, source_target_pairs={{0,8},{2,10},{4,12},{8,0},{12,4},{18,26},{24,16},{26,18},{28,20},{... | collective-permute-start | bytes 393224 | tf_op jit(solution)/shard_map/ppermute | solution.py:381
  36.2 0.0 collective-permute-done.inside_ref
  36.2 1.1 %shard_map.90 = bf16[4,208,128]{2,1,0:T(8,128)(2,1)} custom-call(bf16[195,384]{1,0:T(8,128)(2,1)S(1)} %collective-permute-done.1.token_ref, bf16[16,3,32,128]{3,2,1,0:T(8,128)(2,1)S(1)} %all-to-all-done.refs_3_.w_ref, bf16[3,208,128]{2,1,0:T(8,128)(2,1)S(1)} %get-tuple-element.32.early), custom_call_target="tpu_custom_call" | custom-call | flops 1000 | bytes 1024 | tf_op jit(solution)/shard_map/pallas_call | solution.py:383
  37.3 3.4 %all-to-all-start.1 = ((bf16[4,208,128]{2,1,0:T(8,128)(2,1)}), bf16[4,208,128]{2,1,0:T(8,128)(2,1)S(1)}, u32[]{:S(2)}, u32[]{:S(2)}) async-start(bf16[4,208,128]{2,1,0:T(8,128)(2,1)} %shard_map.90), calls=%async_computation.1 | async-start | bytes 425984 | tf_op jit(solution)/shard_map/all_to_all | solution.py:391
  40.7 0.7 %collective-permute-start.7 = (bf16[208,768]{1,0:T(8,128)(2,1)S(1)}, bf16[208,768]{1,0:T(8,128)(2,1)S(1)}, u32[]{:S(2)}, u32[]{:S(2)}) collective-permute-start(bf16[208,768]{1,0:T(8,128)(2,1)S(1)} %get-tuple-element.38.own_ref), channel_id=1, source_target_pairs={{6,8},{14,16},{22,24},{7,9},{15,17},{23,25}} | collective-permute-start | bytes 958472 | tf_op jit(solution)/shard_map/ppermute | solution.py:393
  41.4 0.0 collective-permute-done.4.refs_1_
  41.4 0.0 collective-permute-done.5.refs_2_
  41.4 0.2 collective-permute-done.6.refs_3_
  41.6 3.4 %shard_map.91 = bf16[512,128]{1,0:T(8,128)(2,1)} custom-call(bf16[512,128]{1,0:T(8,128)(2,1)S(1)} %get-tuple-element.33.refs_0_, bf16[512,128]{1,0:T(8,128)(2,1)S(1)} %collective-permute-done.4.refs_1_, bf16[512,128]{1,0:T(8,128)(2,1)S(1)} %collective-permute-done.5.refs_2_, bf16[512,128]{1,0:T(8,128)(2,1)S(1)} %collective-permute-done.6.refs_3_), custom_call_target="tpu_custom_call" | custom-call | flops 1000000000 | bytes 1048576 | tf_op jit(solution)/shard_map/pallas_call | solution.py:397
  45.0 1.1 %all-to-all-done.1.slots = bf16[4,208,128]{2,1,0:T(8,128)(2,1)S(1)} async-done(((bf16[4,208,128]{2,1,0:T(8,128)(2,1)}), bf16[4,208,128]{2,1,0:T(8,128)(2,1)S(1)}, u32[]{:S(2)}, u32[]{:S(2)}) %all-to-all-start.1) | async-done | bytes 213024 | tf_op jit(solution)/shard_map/all_to_all | solution.py:391
  46.2 3.5 %all-to-all-start.2 = ((bf16[16,32,128]{2,1,0:T(8,128)(2,1)}), bf16[16,32,128]{2,1,0:T(8,128)(2,1)S(1)}, u32[]{:S(2)}, u32[]{:S(2)}) async-start(bf16[16,32,128]{2,1,0:T(8,128)(2,1)} %bitcast.2), calls=%async_computation.2 | async-start | bytes 262144 | tf_op jit(solution)/shard_map/all_to_all | solution.py:401
  49.7 0.0 copy-start.6
  49.7 0.4 shard_map.93
  50.1 1.6 %collective-permute-start.8 = (f32[8,208]{1,0:T(8,128)S(1)}, f32[8,208]{1,0:T(8,128)S(1)}, u32[]{:S(2)}, u32[]{:S(2)}) collective-permute-start(f32[8,208]{1,0:T(8,128)S(1)} %get-tuple-element.42.refs_0_), channel_id=1, source_target_pairs={{0,1},{1,0},{2,3},{3,2},{4,5},{5,4},{6,7},{7,6},{8,9},{9,8},{10,11... | collective-permute-start | bytes 19976 | tf_op jit(solution)/shard_map/ppermute | solution.py:422
  51.7 0.0 copy-done.6
  51.7 0.0 collective-permute-done.7.behind_ref
  51.7 1.4 %shard_map.92.attended_ref = f32[208,384]{1,0:T(8,128)S(1)} custom-call(bf16[195,384]{1,0:T(8,128)(2,1)S(1)} %copy-done, bf16[208,768]{1,0:T(8,128)(2,1)S(1)} %get-tuple-element.38.own_ref, bf16[208,768]{1,0:T(8,128)(2,1)S(1)} %collective-permute-done.inside_ref, bf16[208,768]{1,0:T(8,128)(2,1)S(1)} %collective-permute-done.7.behind_ref), custom_call_target="tpu_custom_call" | custom-call | tf_op jit(solution)/shard_map/pallas_call | solution.py:408
  53.1 0.8 %collective-permute-done.8.refs_1_ = f32[8,208]{1,0:T(8,128)S(1)} collective-permute-done((f32[8,208]{1,0:T(8,128)S(1)}, f32[8,208]{1,0:T(8,128)S(1)}, u32[]{:S(2)}, u32[]{:S(2)}) %collective-permute-start.8) | collective-permute-done | bytes 6688 | tf_op jit(solution)/shard_map/ppermute | solution.py:422
  53.8 0.0 copy-start.2
  53.8 1.0 %shard_map.94 = bf16[195,384]{1,0:T(8,128)(2,1)} custom-call(f32[1,384]{1,0:T(1,128)S(1)} %reshape.13.gain_ref, f32[208,384]{1,0:T(8,128)S(1)} %shard_map.92.attended_ref, bf16[208,384]{1,0:T(8,128)(2,1)S(1)} %get-tuple-element.41.fast_ref, f32[8,208]{1,0:T(8,128)S(1)} %get-tuple-element.42.refs_0_, f32[8,208]{1,0:T(8,128)S(1)} %collective-permute-done.8.refs_1_), custom_call_target="tpu_custom_call" | custom-call | tf_op jit(solution)/shard_map/pallas_call | solution.py:424
  54.8 2.8 %all-to-all-done.2.rows_ref = bf16[16,32,128]{2,1,0:T(8,128)(2,1)S(1)} async-done(((bf16[16,32,128]{2,1,0:T(8,128)(2,1)}), bf16[16,32,128]{2,1,0:T(8,128)(2,1)S(1)}, u32[]{:S(2)}, u32[]{:S(2)}) %all-to-all-start.2) | async-done | bytes 131104 | tf_op jit(solution)/shard_map/all_to_all | solution.py:401
  57.6 0.0 copy-done.2
  57.6 0.8 %shard_map.95 = f32[3,3,32,128]{3,2,1,0:T(8,128)} custom-call(f32[3,3,32,128]{3,2,1,0:T(8,128)S(1)} %copy-done.2, bf16[16,32,128]{2,1,0:T(8,128)(2,1)S(1)} %all-to-all-done.2.rows_ref), custom_call_target="tpu_custom_call" | custom-call | flops 1000000 | bytes 1048576 | tf_op jit(solution)/shard_map/pallas_call | solution.py:404
  (1 shorter events, 0.0 us)
Async XLA Ops:
  0.6 0.9 %copy-start.1 = (f32[3,3,32,128]{3,2,1,0:T(8,128)S(1)}, f32[3,3,32,128]{3,2,1,0:T(8,128)}, u32[]{:S(2)}) copy-start(f32[3,3,32,128]{3,2,1,0:T(8,128)} %w_ref.3) | copy-start | bytes 442372
  2.3 8.2 %copy-start = (bf16[195,384]{1,0:T(8,128)(2,1)S(1)}, bf16[195,384]{1,0:T(8,128)(2,1)}, u32[]{:S(2)}) copy-start(bf16[195,384]{1,0:T(8,128)(2,1)} %q_ref.2) | copy-start | bytes 449284
  2.3 8.2 %copy-start.3 = (bf16[195,384]{1,0:T(8,128)(2,1)S(1)}, bf16[195,384]{1,0:T(8,128)(2,1)}, u32[]{:S(2)}) copy-start(bf16[195,384]{1,0:T(8,128)(2,1)} %k_ref.1) | copy-start | bytes 449284
  2.3 8.2 %copy-start.4 = (bf16[195,384]{1,0:T(8,128)(2,1)S(1)}, bf16[195,384]{1,0:T(8,128)(2,1)}, u32[]{:S(2)}) copy-start(bf16[195,384]{1,0:T(8,128)(2,1)} %v_ref.1) | copy-start | bytes 449284
  2.3 19.7 %all-to-all-start = ((bf16[16,3,32,128]{3,2,1,0:T(8,128)(2,1)}), bf16[16,3,32,128]{3,2,1,0:T(8,128)(2,1)S(1)}, u32[]{:S(2)}, u32[]{:S(2)}) async-start(bf16[16,3,32,128]{3,2,1,0:T(8,128)(2,1)} %shard_map.86.after), calls=%async_computation | async-start | bytes 786432 | tf_op jit(solution)/shard_map/all_to_all | solution.py:347
  9.8 0.7 %copy-start.5 = (f32[195,3]{0,1:T(4,128)S(1)}, f32[195,3]{0,1:T(4,128)}, u32[]{:S(2)}) copy-start(f32[195,3]{0,1:T(4,128)} %param.10) | copy-start | bytes 7024
  11.1 10.2 %collective-permute-start.2 = (bf16[195,384]{1,0:T(8,128)(2,1)S(1)}, bf16[195,384]{1,0:T(8,128)(2,1)S(1)}, u32[]{:S(2)}, u32[]{:S(2)}) collective-permute-start(bf16[195,384]{1,0:T(8,128)(2,1)S(1)} %get-tuple-element.26), channel_id=1, source_target_pairs={{2,4},{4,2},{6,0},{3,5},{5,3},{7,1},{10,12},{12,10},{14,8},{11,13}... | collective-permute-start | bytes 449288 | tf_op jit(solution)/shard_map/ppermute | solution.py:352
  12.4 9.0 %collective-permute-start.3 = (bf16[195,384]{1,0:T(8,128)(2,1)S(1)}, bf16[195,384]{1,0:T(8,128)(2,1)S(1)}, u32[]{:S(2)}, u32[]{:S(2)}) collective-permute-start(bf16[195,384]{1,0:T(8,128)(2,1)S(1)} %get-tuple-element.27), channel_id=1, source_target_pairs={{0,2},{2,0},{6,4},{1,3},{3,1},{7,5},{8,10},{10,8},{14,12},{9,11},{... | collective-permute-start | bytes 449288 | tf_op jit(solution)/shard_map/ppermute | solution.py:352
  17.0 19.2 %collective-permute-start = (bf16[208,768]{1,0:T(8,128)(2,1)S(1)}, bf16[208,768]{1,0:T(8,128)(2,1)S(1)}, u32[]{:S(2)}, u32[]{:S(2)}) collective-permute-start(bf16[208,768]{1,0:T(8,128)(2,1)S(1)} %get-tuple-element.38.own_ref), channel_id=1, source_target_pairs={{0,2},{2,4},{4,6},{1,3},{3,5},{5,7},{8,10},{10,12},{12,14},{9,11},... | collective-permute-start | bytes 958472 | tf_op jit(solution)/shard_map/ppermute | solution.py:354
  18.9 7.8 %collective-permute-start.1 = (bf16[195,384]{1,0:T(8,128)(2,1)S(1)}, bf16[195,384]{1,0:T(8,128)(2,1)S(1)}, u32[]{:S(2)}, u32[]{:S(2)}) collective-permute-start(bf16[195,384]{1,0:T(8,128)(2,1)S(1)} %get-tuple-element.24), channel_id=1, source_target_pairs={{0,4},{4,0},{6,2},{1,5},{5,1},{7,3},{8,12},{12,8},{14,10},{9,13},{... | collective-permute-start | bytes 449288 | tf_op jit(solution)/shard_map/ppermute | solution.py:352
  27.5 13.9 %collective-permute-start.4 = (bf16[512,128]{1,0:T(8,128)(2,1)S(1)}, bf16[512,128]{1,0:T(8,128)(2,1)S(1)}, u32[]{:S(2)}, u32[]{:S(2)}) collective-permute-start(bf16[512,128]{1,0:T(8,128)(2,1)S(1)} %get-tuple-element.34), channel_id=1, source_target_pairs={{2,26},{8,16},{10,18},{12,20},{16,8},{18,10},{20,12},{24,0},{28,4}... | collective-permute-start | bytes 393224 | tf_op jit(solution)/shard_map/ppermute | solution.py:381
  28.8 12.6 %collective-permute-start.5 = (bf16[512,128]{1,0:T(8,128)(2,1)S(1)}, bf16[512,128]{1,0:T(8,128)(2,1)S(1)}, u32[]{:S(2)}, u32[]{:S(2)}) collective-permute-start(bf16[512,128]{1,0:T(8,128)(2,1)S(1)} %get-tuple-element.35), channel_id=1, source_target_pairs={{0,16},{2,18},{4,20},{10,26},{16,0},{20,4},{24,8},{26,10},{28,12},... | collective-permute-start | bytes 393224 | tf_op jit(solution)/shard_map/ppermute | solution.py:381
  34.3 7.4 %collective-permute-start.6 = (bf16[512,128]{1,0:T(8,128)(2,1)S(1)}, bf16[512,128]{1,0:T(8,128)(2,1)S(1)}, u32[]{:S(2)}, u32[]{:S(2)}) collective-permute-start(bf16[512,128]{1,0:T(8,128)(2,1)S(1)} %get-tuple-element.36), channel_id=1, source_target_pairs={{0,8},{2,10},{4,12},{8,0},{12,4},{18,26},{24,16},{26,18},{28,20},{... | collective-permute-start | bytes 393224 | tf_op jit(solution)/shard_map/ppermute | solution.py:381
  37.3 8.9 %all-to-all-start.1 = ((bf16[4,208,128]{2,1,0:T(8,128)(2,1)}), bf16[4,208,128]{2,1,0:T(8,128)(2,1)S(1)}, u32[]{:S(2)}, u32[]{:S(2)}) async-start(bf16[4,208,128]{2,1,0:T(8,128)(2,1)} %shard_map.90), calls=%async_computation.1 | async-start | bytes 425984 | tf_op jit(solution)/shard_map/all_to_all | solution.py:391
  40.7 11.0 %collective-permute-start.7 = (bf16[208,768]{1,0:T(8,128)(2,1)S(1)}, bf16[208,768]{1,0:T(8,128)(2,1)S(1)}, u32[]{:S(2)}, u32[]{:S(2)}) collective-permute-start(bf16[208,768]{1,0:T(8,128)(2,1)S(1)} %get-tuple-element.38.own_ref), channel_id=1, source_target_pairs={{6,8},{14,16},{22,24},{7,9},{15,17},{23,25}} | collective-permute-start | bytes 958472 | tf_op jit(solution)/shard_map/ppermute | solution.py:393
  46.2 11.4 %all-to-all-start.2 = ((bf16[16,32,128]{2,1,0:T(8,128)(2,1)}), bf16[16,32,128]{2,1,0:T(8,128)(2,1)S(1)}, u32[]{:S(2)}, u32[]{:S(2)}) async-start(bf16[16,32,128]{2,1,0:T(8,128)(2,1)} %bitcast.2), calls=%async_computation.2 | async-start | bytes 262144 | tf_op jit(solution)/shard_map/all_to_all | solution.py:401
  49.7 2.0 %copy-start.6 = (f32[384]{0:T(512)S(1)}, f32[384]{0:T(512)}, u32[]{:S(2)}) copy-start(f32[384]{0:T(512)} %param.13) | copy-start | bytes 4612
  50.1 3.7 %collective-permute-start.8 = (f32[8,208]{1,0:T(8,128)S(1)}, f32[8,208]{1,0:T(8,128)S(1)}, u32[]{:S(2)}, u32[]{:S(2)}) collective-permute-start(f32[8,208]{1,0:T(8,128)S(1)} %get-tuple-element.42.refs_0_), channel_id=1, source_target_pairs={{0,1},{1,0},{2,3},{3,2},{4,5},{5,4},{6,7},{7,6},{8,9},{9,8},{10,11... | collective-permute-start | bytes 19976 | tf_op jit(solution)/shard_map/ppermute | solution.py:422
  53.8 3.8 %copy-start.2 = (f32[3,3,32,128]{3,2,1,0:T(8,128)S(1)}, f32[3,3,32,128]{3,2,1,0:T(8,128)}, u32[]{:S(2)}) copy-start(f32[3,3,32,128]{3,2,1,0:T(8,128)} %w_ref.3) | copy-start | bytes 442372

commit v8 on v5

--- a/solution.py
+++ b/solution.py
@@ -67,7 +67,7 @@
         for m in range(3):
             low = w_ref[m, min(j, heads - 1)].astype(bf16)
             for z in range(slots):
-                w_out[z * group + j, m] = low
+                w_out[j * slots + z, m] = low
 
 
 def prep_body(
@@ -261,7 +261,7 @@
     for m in range(3):
         for h in range(heads):
             weights = w_ref[m, h]
-            summed = weights + rows_ref[((m + first_owner(h)) % slots) * group + h].astype(f32)
+            summed = weights + rows_ref[h * slots + (m + first_owner(h)) % slots].astype(f32)
             old = jnp.sqrt(jnp.sum(weights * weights, axis=1, keepdims=True))
             new = lax.rsqrt(jnp.sum(summed * summed, axis=1, keepdims=True) + epsilon)
             out[m, h] = summed * (old * new)
@@ -340,7 +340,7 @@
     )(low, frame_update.reshape(1, 1), rates.T, keys, values, queries)
     kv_own, *token_slots = prepared
 
-    weights = lax.all_to_all(low, ("z", "grp"), 0, 0, tiled=True)
+    weights = lax.all_to_all(low, ("grp", "z"), 0, 0, tiled=True)
     if rows_local % 16:
         weights = weights.transpose(1, 0, 2, 3).reshape(3, hidden, HD)
     for d in served(group)[1:]:
@@ -392,7 +392,7 @@
     )
     queries, ortho = lax.optimization_barrier((queries, ortho))
     rows = lax.all_to_all(
-        ortho.reshape(count, rows_local, HD), ("z", "grp"), 0, 0, tiled=True
+        ortho.reshape(count, rows_local, HD), ("grp", "z"), 0, 0, tiled=True
     )
     new_weights = call(
         functools.partial(finish_body, nz, group), sds(fast_weights.shape, f32), flops=1e6

time: 58.9 us -> 58.2 us (0.988)
  waiting for transfers between devices: 7.65 us -> 6.89 us
    all_to_all x2, waiting for transfers between devices: 5.12 us -> 4.1 us  [the longest x1 2.22 us: on_device(): lax.all_to_all(ortho.reshape(count, rows_local, HD), ('grp', 'z'), 0, 0,...]
  transfers between devices with their start and end apart: 11 -> 11, of which waited for: 5 -> 5; matrix products, arithmetic and copies ran while one was open for 0% -> 0% of each run, Pallas kernels for 17% -> 18%
where the time goes in v8:
time: 58.2 us; the launch traced here: 57.6 us
  starting transfers between devices  35.8 us (62%)
  Pallas kernels  12.5 us (21%)
  waiting for transfers between devices  6.89 us (12%)
  between operations  1.48 us (3%)
  local copies, waits for them, and re-layouts  0.93 us (2%)
    ppermute x3, starting transfers between devices, on_device(): partials[d] = lax.ppermute(partials[d], ('z', 'grp'), pairs)  8.61 us
    ppermute x3, starting transfers between devices, on_device(): token_slots[d] = lax.ppermute(token_slots[d], 'grp', pairs)  7.79 us
    all_to_all x1, starting transfers between devices, on_device(): weights = lax.all_to_all(low, ('grp', 'z'), 0, 0, tiled=True)  7.49 us
    all_to_all x1, starting transfers between devices, on_device(): lax.all_to_all(ortho.reshape(count, rows_local, HD), ('grp', 'z'), 0, 0,...  4.61 us
    pallas_call x1, Pallas kernels, on_device(): call(functools.partial(ortho_body, heads, nz), sds((hidden, HD), bf16), f...  3.44 us
    all_to_all x1, starting transfers between devices, on_device(): fast_slots = lax.all_to_all(fast_slots, 'grp', 0, 0, tiled=True)  3.37 us
    ppermute x1, starting transfers between devices, on_device(): kv_back = lax.ppermute(kv_own, ('z', 'grp'), ring)  2.38 us
    pallas_call x1, Pallas kernels, on_device(): call(functools.partial(early_body, len(early_slots)), [sds((3, hidden, HD...  2.24 us
  transfers between devices with their start and end apart: 11, of which 5 were waited for; matrix products, arithmetic and copies ran while one was open for 0% of the time, Pallas kernels for 18%

profile of v8, /device:TPU:0, one launch (start us, length us, event | category | flops | bytes accessed | tf_op | source)
XLA Modules:
  0.0 57.6 jit_solution(5090512144908433228)
XLA Ops:
  0.6 0.0 copy-start.1
  0.6 0.9 %copy-done.1 = f32[3,3,32,128]{3,2,1,0:T(8,128)S(1)} copy-done((f32[3,3,32,128]{3,2,1,0:T(8,128)S(1)}, f32[3,3,32,128]{3,2,1,0:T(8,128)}, u32[]{:S(2)}) %copy-start.1) | copy-done | bytes 147480
  1.5 0.8 %shard_map.86.after = bf16[16,3,32,128]{3,2,1,0:T(8,128)(2,1)} custom-call(f32[3,3,32,128]{3,2,1,0:T(8,128)S(1)} %copy-done.1), custom_call_target="tpu_custom_call" | custom-call | flops 1000000 | bytes 1048576 | tf_op jit(solution)/shard_map/pallas_call | solution.py:326
  2.3 0.0 copy-start
  2.3 0.0 copy-start.3
  2.3 0.0 copy-start.4
  2.3 7.5 %all-to-all-start = ((bf16[16,3,32,128]{3,2,1,0:T(8,128)(2,1)}), bf16[16,3,32,128]{3,2,1,0:T(8,128)(2,1)S(1)}, u32[]{:S(2)}, u32[]{:S(2)}) async-start(bf16[16,3,32,128]{3,2,1,0:T(8,128)(2,1)} %shard_map.86.after), calls=%async_computation | async-start | bytes 786432 | tf_op jit(solution)/shard_map/all_to_all | solution.py:343
  9.8 0.0 copy-start.5
  10.5 0.0 copy-done
  10.5 0.0 copy-done.3
  10.5 0.0 copy-done.4
  10.5 0.0 copy-done.5
  10.5 0.6 %shard_map.87 = (bf16[208,768]{1,0:T(8,128)(2,1)S(1)}, bf16[195,384]{1,0:T(8,128)(2,1)S(1)}, bf16[195,384]{1,0:T(8,128)(2,1)S(1)}, bf16[195,384]{1,0:T(8,128)(2,1)S(1)}, bf16[195,384]{1,0:T(8,128)(2,1)S(1)}) custom-call(bf16[16,3,32,128]{3,2,1,0:T(8,128)(2,1)} %shard_map.86.after, s32[1,1]{1,0:T(1,128)} %bitcast.3.update, f32[3,195]{1,0:T(4,128)S(1)} %bitcast.4, ...), custom_call_target="tpu_custom_call" | custom-call | tf_op jit(solution)/shard_map/pallas_call | solution.py:329
  11.1 1.3 %collective-permute-start.1 = (bf16[195,384]{1,0:T(8,128)(2,1)S(1)}, bf16[195,384]{1,0:T(8,128)(2,1)S(1)}, u32[]{:S(2)}, u32[]{:S(2)}) collective-permute-start(bf16[195,384]{1,0:T(8,128)(2,1)S(1)} %get-tuple-element.25), channel_id=1, source_target_pairs={{2,4},{4,2},{6,0},{3,5},{5,3},{7,1},{10,12},{12,10},{14,8},{11,13}... | collective-permute-start | bytes 449288 | tf_op jit(solution)/shard_map/ppermute | solution.py:348
  12.4 4.6 %collective-permute-start.2 = (bf16[195,384]{1,0:T(8,128)(2,1)S(1)}, bf16[195,384]{1,0:T(8,128)(2,1)S(1)}, u32[]{:S(2)}, u32[]{:S(2)}) collective-permute-start(bf16[195,384]{1,0:T(8,128)(2,1)S(1)} %get-tuple-element.26), channel_id=1, source_target_pairs={{0,2},{2,0},{6,4},{1,3},{3,1},{7,5},{8,10},{10,8},{14,12},{9,11},{... | collective-permute-start | bytes 449288 | tf_op jit(solution)/shard_map/ppermute | solution.py:348
  17.0 1.9 %collective-permute-start = (bf16[195,384]{1,0:T(8,128)(2,1)S(1)}, bf16[195,384]{1,0:T(8,128)(2,1)S(1)}, u32[]{:S(2)}, u32[]{:S(2)}) collective-permute-start(bf16[195,384]{1,0:T(8,128)(2,1)S(1)} %get-tuple-element.23), channel_id=1, source_target_pairs={{0,4},{4,0},{6,2},{1,5},{5,1},{7,3},{8,12},{12,8},{14,10},{9,13},{... | collective-permute-start | bytes 449288 | tf_op jit(solution)/shard_map/ppermute | solution.py:348
  18.9 1.9 %collective-permute-done.1.refs_1_ = bf16[195,384]{1,0:T(8,128)(2,1)S(1)} collective-permute-done((bf16[195,384]{1,0:T(8,128)(2,1)S(1)}, bf16[195,384]{1,0:T(8,128)(2,1)S(1)}, u32[]{:S(2)}, u32[]{:S(2)}) %collective-permute-start.1) | collective-permute-done | bytes 149792 | tf_op jit(solution)/shard_map/ppermute | solution.py:348
  20.8 0.0 collective-permute-done.2.refs_2_
  20.8 1.9 %all-to-all-done.refs_3_.w_ref = bf16[16,3,32,128]{3,2,1,0:T(8,128)(2,1)S(1)} async-done(((bf16[16,3,32,128]{3,2,1,0:T(8,128)(2,1)}), bf16[16,3,32,128]{3,2,1,0:T(8,128)(2,1)S(1)}, u32[]{:S(2)}, u32[]{:S(2)}) %all-to-all-start) | async-done | bytes 393248 | tf_op jit(solution)/shard_map/all_to_all | solution.py:343
  22.7 2.2 %shard_map.88 = (f32[3,512,128]{2,1,0:T(8,128)S(1)}, bf16[3,208,128]{2,1,0:T(8,128)(2,1)S(1)}) custom-call(bf16[195,384]{1,0:T(8,128)(2,1)S(1)} %get-tuple-element.24.refs_0_, bf16[195,384]{1,0:T(8,128)(2,1)S(1)} %collective-permute-done.1.refs_1_, bf16[195,384]{1,0:T(8,128)(2,1)S(1)} %collective-permute-done.2.refs_2_, ...), custom_call_target="tpu_custom_call" | custom-call | flops 1000000000 | bytes 1048576 | tf_op jit(solution)/shard_map/pallas_call | solution.py:352
  24.9 0.1 collective-permute-done.token_ref
  25.1 0.8 %shard_map.89 = (bf16[512,128]{1,0:T(8,128)(2,1)S(1)}, bf16[512,128]{1,0:T(8,128)(2,1)S(1)}, bf16[512,128]{1,0:T(8,128)(2,1)S(1)}, bf16[512,128]{1,0:T(8,128)(2,1)S(1)}) custom-call(bf16[195,384]{1,0:T(8,128)(2,1)S(1)} %collective-permute-done.token_ref, bf16[16,3,32,128]{3,2,1,0:T(8,128)(2,1)S(1)} %all-to-all-done.refs_3_.w_ref, ...), custom_call_target="tpu_custom_call" | custom-call | flops 500000000 | bytes 1048576 | tf_op jit(solution)/shard_map/pallas_call | solution.py:359
  25.8 1.3 %collective-permute-start.3 = (bf16[512,128]{1,0:T(8,128)(2,1)S(1)}, bf16[512,128]{1,0:T(8,128)(2,1)S(1)}, u32[]{:S(2)}, u32[]{:S(2)}) collective-permute-start(bf16[512,128]{1,0:T(8,128)(2,1)S(1)} %get-tuple-element.33), channel_id=1, source_target_pairs={{2,26},{8,16},{10,18},{12,20},{16,8},{18,10},{20,12},{24,0},{28,4}... | collective-permute-start | bytes 393224 | tf_op jit(solution)/shard_map/ppermute | solution.py:375
  27.1 5.4 %collective-permute-start.4 = (bf16[512,128]{1,0:T(8,128)(2,1)S(1)}, bf16[512,128]{1,0:T(8,128)(2,1)S(1)}, u32[]{:S(2)}, u32[]{:S(2)}) collective-permute-start(bf16[512,128]{1,0:T(8,128)(2,1)S(1)} %get-tuple-element.34), channel_id=1, source_target_pairs={{0,16},{2,18},{4,20},{10,26},{16,0},{20,4},{24,8},{26,10},{28,12},... | collective-permute-start | bytes 393224 | tf_op jit(solution)/shard_map/ppermute | solution.py:375
  32.5 1.9 %collective-permute-start.5 = (bf16[512,128]{1,0:T(8,128)(2,1)S(1)}, bf16[512,128]{1,0:T(8,128)(2,1)S(1)}, u32[]{:S(2)}, u32[]{:S(2)}) collective-permute-start(bf16[512,128]{1,0:T(8,128)(2,1)S(1)} %get-tuple-element.35), channel_id=1, source_target_pairs={{0,8},{2,10},{4,12},{8,0},{12,4},{18,26},{24,16},{26,18},{28,20},{... | collective-permute-start | bytes 393224 | tf_op jit(solution)/shard_map/ppermute | solution.py:375
  34.5 1.1 %shard_map.90 = bf16[4,208,128]{2,1,0:T(8,128)(2,1)} custom-call(bf16[195,384]{1,0:T(8,128)(2,1)S(1)} %collective-permute-done.token_ref, bf16[16,3,32,128]{3,2,1,0:T(8,128)(2,1)S(1)} %all-to-all-done.refs_3_.w_ref, bf16[3,208,128]{2,1,0:T(8,128)(2,1)S(1)} %get-tuple-element.31.early), custom_call_target="tpu_custom_call" | custom-call | flops 1000 | bytes 1024 | tf_op jit(solution)/shard_map/pallas_call | solution.py:377
  35.6 3.4 %all-to-all-start.1 = ((bf16[4,208,128]{2,1,0:T(8,128)(2,1)}), bf16[4,208,128]{2,1,0:T(8,128)(2,1)S(1)}, u32[]{:S(2)}, u32[]{:S(2)}) async-start(bf16[4,208,128]{2,1,0:T(8,128)(2,1)} %shard_map.90), calls=%async_computation.1 | async-start | bytes 425984 | tf_op jit(solution)/shard_map/all_to_all | solution.py:385
  39.0 2.4 %collective-permute-start.6 = (bf16[208,768]{1,0:T(8,128)(2,1)S(1)}, bf16[208,768]{1,0:T(8,128)(2,1)S(1)}, u32[]{:S(2)}, u32[]{:S(2)}) collective-permute-start(bf16[208,768]{1,0:T(8,128)(2,1)S(1)} %get-tuple-element.37.own_ref), channel_id=1, source_target_pairs={{0,2},{2,4},{4,6},{6,8},{8,10},{10,12},{12,14},{14,16},{16,18},{18... | collective-permute-start | bytes 958472 | tf_op jit(solution)/shard_map/ppermute | solution.py:388
  41.4 0.0 collective-permute-done.3.refs_1_
  41.4 0.0 collective-permute-done.4.refs_2_
  41.4 0.0 collective-permute-done.5.refs_3_
  41.4 3.4 %shard_map.91 = bf16[512,128]{1,0:T(8,128)(2,1)} custom-call(bf16[512,128]{1,0:T(8,128)(2,1)S(1)} %get-tuple-element.32.refs_0_, bf16[512,128]{1,0:T(8,128)(2,1)S(1)} %collective-permute-done.3.refs_1_, bf16[512,128]{1,0:T(8,128)(2,1)S(1)} %collective-permute-done.4.refs_2_, bf16[512,128]{1,0:T(8,128)(2,1)S(1)} %collective-permute-done.5.refs_3_), custom_call_target="tpu_custom_call" | custom-call | flops 1000000000 | bytes 1048576 | tf_op jit(solution)/shard_map/pallas_call | solution.py:390
  44.8 0.0 all-to-all-done.1.slots
  44.8 4.6 %all-to-all-start.2 = ((bf16[16,32,128]{2,1,0:T(8,128)(2,1)}), bf16[16,32,128]{2,1,0:T(8,128)(2,1)S(1)}, u32[]{:S(2)}, u32[]{:S(2)}) async-start(bf16[16,32,128]{2,1,0:T(8,128)(2,1)} %bitcast.2), calls=%async_computation.2 | async-start | bytes 262144 | tf_op jit(solution)/shard_map/all_to_all | solution.py:394
  49.4 0.0 copy-start.6
  49.5 0.4 shard_map.93
  49.9 1.6 %collective-permute-start.7 = (f32[8,208]{1,0:T(8,128)S(1)}, f32[8,208]{1,0:T(8,128)S(1)}, u32[]{:S(2)}, u32[]{:S(2)}) collective-permute-start(f32[8,208]{1,0:T(8,128)S(1)} %get-tuple-element.40.refs_0_), channel_id=1, source_target_pairs={{0,1},{1,0},{2,3},{3,2},{4,5},{5,4},{6,7},{7,6},{8,9},{9,8},{10,11... | collective-permute-start | bytes 19976 | tf_op jit(solution)/shard_map/ppermute | solution.py:415
  51.5 0.0 copy-done.6
  51.5 0.0 collective-permute-done.6.back_ref
  51.5 1.3 %shard_map.92.attended_ref = f32[208,384]{1,0:T(8,128)S(1)} custom-call(bf16[195,384]{1,0:T(8,128)(2,1)S(1)} %copy-done, bf16[208,768]{1,0:T(8,128)(2,1)S(1)} %get-tuple-element.37.own_ref, bf16[208,768]{1,0:T(8,128)(2,1)S(1)} %collective-permute-done.6.back_ref), custom_call_target="tpu_custom_call" | custom-call | tf_op jit(solution)/shard_map/pallas_call | solution.py:401
  52.8 0.8 %collective-permute-done.7.refs_1_ = f32[8,208]{1,0:T(8,128)S(1)} collective-permute-done((f32[8,208]{1,0:T(8,128)S(1)}, f32[8,208]{1,0:T(8,128)S(1)}, u32[]{:S(2)}, u32[]{:S(2)}) %collective-permute-start.7) | collective-permute-done | bytes 6688 | tf_op jit(solution)/shard_map/ppermute | solution.py:415
  53.6 0.0 copy-start.2
  53.6 1.0 %shard_map.94 = bf16[195,384]{1,0:T(8,128)(2,1)} custom-call(f32[1,384]{1,0:T(1,128)S(1)} %reshape.13.gain_ref, f32[208,384]{1,0:T(8,128)S(1)} %shard_map.92.attended_ref, bf16[208,384]{1,0:T(8,128)(2,1)S(1)} %get-tuple-element.39.fast_ref, f32[8,208]{1,0:T(8,128)S(1)} %get-tuple-element.40.refs_0_, f32[8,208]{1,0:T(8,128)S(1)} %collective-permute-done.7.refs_1_), custom_call_target="tpu_custom_call" | custom-call | tf_op jit(solution)/shard_map/pallas_call | solution.py:417
  54.6 2.2 %all-to-all-done.2.rows_ref = bf16[16,32,128]{2,1,0:T(8,128)(2,1)S(1)} async-done(((bf16[16,32,128]{2,1,0:T(8,128)(2,1)}), bf16[16,32,128]{2,1,0:T(8,128)(2,1)S(1)}, u32[]{:S(2)}, u32[]{:S(2)}) %all-to-all-start.2) | async-done | bytes 131104 | tf_op jit(solution)/shard_map/all_to_all | solution.py:394
  56.8 0.0 copy-done.2
  56.8 0.8 %shard_map.95 = f32[3,3,32,128]{3,2,1,0:T(8,128)} custom-call(f32[3,3,32,128]{3,2,1,0:T(8,128)S(1)} %copy-done.2, bf16[16,32,128]{2,1,0:T(8,128)(2,1)S(1)} %all-to-all-done.2.rows_ref), custom_call_target="tpu_custom_call" | custom-call | flops 1000000 | bytes 1048576 | tf_op jit(solution)/shard_map/pallas_call | solution.py:397
  (1 shorter events, 0.0 us)
Async XLA Ops:
  0.6 0.9 %copy-start.1 = (f32[3,3,32,128]{3,2,1,0:T(8,128)S(1)}, f32[3,3,32,128]{3,2,1,0:T(8,128)}, u32[]{:S(2)}) copy-start(f32[3,3,32,128]{3,2,1,0:T(8,128)} %w_ref.3) | copy-start | bytes 442372
  2.3 8.2 %copy-start = (bf16[195,384]{1,0:T(8,128)(2,1)S(1)}, bf16[195,384]{1,0:T(8,128)(2,1)}, u32[]{:S(2)}) copy-start(bf16[195,384]{1,0:T(8,128)(2,1)} %q_ref.2) | copy-start | bytes 449284
  2.3 8.2 %copy-start.3 = (bf16[195,384]{1,0:T(8,128)(2,1)S(1)}, bf16[195,384]{1,0:T(8,128)(2,1)}, u32[]{:S(2)}) copy-start(bf16[195,384]{1,0:T(8,128)(2,1)} %k_ref.1) | copy-start | bytes 449284
  2.3 8.2 %copy-start.4 = (bf16[195,384]{1,0:T(8,128)(2,1)S(1)}, bf16[195,384]{1,0:T(8,128)(2,1)}, u32[]{:S(2)}) copy-start(bf16[195,384]{1,0:T(8,128)(2,1)} %v_ref.1) | copy-start | bytes 449284
  2.3 20.4 %all-to-all-start = ((bf16[16,3,32,128]{3,2,1,0:T(8,128)(2,1)}), bf16[16,3,32,128]{3,2,1,0:T(8,128)(2,1)S(1)}, u32[]{:S(2)}, u32[]{:S(2)}) async-start(bf16[16,3,32,128]{3,2,1,0:T(8,128)(2,1)} %shard_map.86.after), calls=%async_computation | async-start | bytes 786432 | tf_op jit(solution)/shard_map/all_to_all | solution.py:343
  9.8 0.7 %copy-start.5 = (f32[195,3]{0,1:T(4,128)S(1)}, f32[195,3]{0,1:T(4,128)}, u32[]{:S(2)}) copy-start(f32[195,3]{0,1:T(4,128)} %param.10) | copy-start | bytes 7024
  11.1 9.7 %collective-permute-start.1 = (bf16[195,384]{1,0:T(8,128)(2,1)S(1)}, bf16[195,384]{1,0:T(8,128)(2,1)S(1)}, u32[]{:S(2)}, u32[]{:S(2)}) collective-permute-start(bf16[195,384]{1,0:T(8,128)(2,1)S(1)} %get-tuple-element.25), channel_id=1, source_target_pairs={{2,4},{4,2},{6,0},{3,5},{5,3},{7,1},{10,12},{12,10},{14,8},{11,13}... | collective-permute-start | bytes 449288 | tf_op jit(solution)/shard_map/ppermute | solution.py:348
  12.4 8.4 %collective-permute-start.2 = (bf16[195,384]{1,0:T(8,128)(2,1)S(1)}, bf16[195,384]{1,0:T(8,128)(2,1)S(1)}, u32[]{:S(2)}, u32[]{:S(2)}) collective-permute-start(bf16[195,384]{1,0:T(8,128)(2,1)S(1)} %get-tuple-element.26), channel_id=1, source_target_pairs={{0,2},{2,0},{6,4},{1,3},{3,1},{7,5},{8,10},{10,8},{14,12},{9,11},{... | collective-permute-start | bytes 449288 | tf_op jit(solution)/shard_map/ppermute | solution.py:348
  17.0 8.1 %collective-permute-start = (bf16[195,384]{1,0:T(8,128)(2,1)S(1)}, bf16[195,384]{1,0:T(8,128)(2,1)S(1)}, u32[]{:S(2)}, u32[]{:S(2)}) collective-permute-start(bf16[195,384]{1,0:T(8,128)(2,1)S(1)} %get-tuple-element.23), channel_id=1, source_target_pairs={{0,4},{4,0},{6,2},{1,5},{5,1},{7,3},{8,12},{12,8},{14,10},{9,13},{... | collective-permute-start | bytes 449288 | tf_op jit(solution)/shard_map/ppermute | solution.py:348
  25.8 15.5 %collective-permute-start.3 = (bf16[512,128]{1,0:T(8,128)(2,1)S(1)}, bf16[512,128]{1,0:T(8,128)(2,1)S(1)}, u32[]{:S(2)}, u32[]{:S(2)}) collective-permute-start(bf16[512,128]{1,0:T(8,128)(2,1)S(1)} %get-tuple-element.33), channel_id=1, source_target_pairs={{2,26},{8,16},{10,18},{12,20},{16,8},{18,10},{20,12},{24,0},{28,4}... | collective-permute-start | bytes 393224 | tf_op jit(solution)/shard_map/ppermute | solution.py:375
  27.1 14.2 %collective-permute-start.4 = (bf16[512,128]{1,0:T(8,128)(2,1)S(1)}, bf16[512,128]{1,0:T(8,128)(2,1)S(1)}, u32[]{:S(2)}, u32[]{:S(2)}) collective-permute-start(bf16[512,128]{1,0:T(8,128)(2,1)S(1)} %get-tuple-element.34), channel_id=1, source_target_pairs={{0,16},{2,18},{4,20},{10,26},{16,0},{20,4},{24,8},{26,10},{28,12},... | collective-permute-start | bytes 393224 | tf_op jit(solution)/shard_map/ppermute | solution.py:375
  32.5 8.8 %collective-permute-start.5 = (bf16[512,128]{1,0:T(8,128)(2,1)S(1)}, bf16[512,128]{1,0:T(8,128)(2,1)S(1)}, u32[]{:S(2)}, u32[]{:S(2)}) collective-permute-start(bf16[512,128]{1,0:T(8,128)(2,1)S(1)} %get-tuple-element.35), channel_id=1, source_target_pairs={{0,8},{2,10},{4,12},{8,0},{12,4},{18,26},{24,16},{26,18},{28,20},{... | collective-permute-start | bytes 393224 | tf_op jit(solution)/shard_map/ppermute | solution.py:375
  35.6 9.2 %all-to-all-start.1 = ((bf16[4,208,128]{2,1,0:T(8,128)(2,1)}), bf16[4,208,128]{2,1,0:T(8,128)(2,1)S(1)}, u32[]{:S(2)}, u32[]{:S(2)}) async-start(bf16[4,208,128]{2,1,0:T(8,128)(2,1)} %shard_map.90), calls=%async_computation.1 | async-start | bytes 425984 | tf_op jit(solution)/shard_map/all_to_all | solution.py:385
  39.0 12.5 %collective-permute-start.6 = (bf16[208,768]{1,0:T(8,128)(2,1)S(1)}, bf16[208,768]{1,0:T(8,128)(2,1)S(1)}, u32[]{:S(2)}, u32[]{:S(2)}) collective-permute-start(bf16[208,768]{1,0:T(8,128)(2,1)S(1)} %get-tuple-element.37.own_ref), channel_id=1, source_target_pairs={{0,2},{2,4},{4,6},{6,8},{8,10},{10,12},{12,14},{14,16},{16,18},{18... | collective-permute-start | bytes 958472 | tf_op jit(solution)/shard_map/ppermute | solution.py:388
  44.8 12.0 %all-to-all-start.2 = ((bf16[16,32,128]{2,1,0:T(8,128)(2,1)}), bf16[16,32,128]{2,1,0:T(8,128)(2,1)S(1)}, u32[]{:S(2)}, u32[]{:S(2)}) async-start(bf16[16,32,128]{2,1,0:T(8,128)(2,1)} %bitcast.2), calls=%async_computation.2 | async-start | bytes 262144 | tf_op jit(solution)/shard_map/all_to_all | solution.py:394
  49.4 2.0 %copy-start.6 = (f32[384]{0:T(512)S(1)}, f32[384]{0:T(512)}, u32[]{:S(2)}) copy-start(f32[384]{0:T(512)} %param.13) | copy-start | bytes 4612
  49.9 3.7 %collective-permute-start.7 = (f32[8,208]{1,0:T(8,128)S(1)}, f32[8,208]{1,0:T(8,128)S(1)}, u32[]{:S(2)}, u32[]{:S(2)}) collective-permute-start(f32[8,208]{1,0:T(8,128)S(1)} %get-tuple-element.40.refs_0_), channel_id=1, source_target_pairs={{0,1},{1,0},{2,3},{3,2},{4,5},{5,4},{6,7},{7,6},{8,9},{9,8},{10,11... | collective-permute-start | bytes 19976 | tf_op jit(solution)/shard_map/ppermute | solution.py:415
  53.6 3.2 %copy-start.2 = (f32[3,3,32,128]{3,2,1,0:T(8,128)S(1)}, f32[3,3,32,128]{3,2,1,0:T(8,128)}, u32[]{:S(2)}) copy-start(f32[3,3,32,128]{3,2,1,0:T(8,128)} %w_ref.3) | copy-start | bytes 442372

commit v9 on v8

--- a/solution.py
+++ b/solution.py
@@ -53,8 +53,20 @@
     return h & 1
 
 
+GROUP = ("x", "core")
+ORDER = ("core", "x", "z")
+
+
 def position():
-    return lax.axis_index("z"), lax.axis_index("grp")
+    return lax.axis_index("z"), lax.axis_index("x") * 2 + lax.axis_index("core")
+
+
+def index_of(z, j, slots):
+    index = 0
+    for name in ORDER:
+        size, at = {"z": (slots, z), "x": (2, j // 2), "core": (2, j % 2)}[name]
+        index = index * size + at
+    return index
 
 
 def sigmoid(x):
@@ -67,7 +79,7 @@
         for m in range(3):
             low = w_ref[m, min(j, heads - 1)].astype(bf16)
             for z in range(slots):
-                w_out[j * slots + z, m] = low
+                w_out[index_of(z, j, slots), m] = low
 
 
 def prep_body(
@@ -261,7 +273,7 @@
     for m in range(3):
         for h in range(heads):
             weights = w_ref[m, h]
-            summed = weights + rows_ref[h * slots + (m + first_owner(h)) % slots].astype(f32)
+            summed = weights + rows_ref[index_of((m + first_owner(h)) % slots, h, slots)].astype(f32)
             old = jnp.sqrt(jnp.sum(weights * weights, axis=1, keepdims=True))
             new = lax.rsqrt(jnp.sum(summed * summed, axis=1, keepdims=True) + epsilon)
             out[m, h] = summed * (old * new)
@@ -313,7 +325,8 @@
     tokens = queries.shape[0]
     heads = queries.shape[1] // HD
     rows_local = fast_weights.shape[2]
-    nz, group, nh = lax.axis_size("z"), lax.axis_size("grp"), lax.axis_size("head")
+    nz, nh = lax.axis_size("z"), lax.axis_size("head")
+    group = lax.axis_size("x") * lax.axis_size("core")
     count = nz * group
     hidden = count * rows_local
     padded = -(-tokens // 16) * 16
@@ -340,12 +353,12 @@
     )(low, frame_update.reshape(1, 1), rates.T, keys, values, queries)
     kv_own, *token_slots = prepared
 
-    weights = lax.all_to_all(low, ("grp", "z"), 0, 0, tiled=True)
+    weights = lax.all_to_all(low, ORDER, 0, 0, tiled=True)
     if rows_local % 16:
         weights = weights.transpose(1, 0, 2, 3).reshape(3, hidden, HD)
     for d in served(group)[1:]:
         pairs = [(s, s ^ d) for s in range(group) if s ^ d < heads]
-        token_slots[d] = lax.ppermute(token_slots[d], "grp", pairs)
+        token_slots[d] = lax.ppermute(token_slots[d], GROUP, pairs)
 
     last = group // 2
     early_slots = [d for d in served(group) if d != last]
@@ -372,7 +385,7 @@
                 for j in range(heads)
                 if ((z ^ d) - first_owner(j)) % nz < 3
             ]
-        partials[d] = lax.ppermute(partials[d], ("z", "grp"), pairs)
+        partials[d] = lax.ppermute(partials[d], ("z", *GROUP), pairs)
 
     fast_slots = call(
         functools.partial(late_apply_body, early_slots, last),
@@ -382,17 +395,17 @@
         moved=1024,
     )(token_slots[last], weights, early_fast)
     kv_own, partials[0], fast_slots = lax.optimization_barrier((kv_own, partials[0], fast_slots))
-    fast_slots = lax.all_to_all(fast_slots, "grp", 0, 0, tiled=True)
+    fast_slots = lax.all_to_all(fast_slots, GROUP, 0, 0, tiled=True)
 
     ring = [(i, i + 1) for i in range(count - 1)]
-    kv_back = lax.ppermute(kv_own, ("z", "grp"), ring)
+    kv_back = lax.ppermute(kv_own, ("z", *GROUP), ring)
 
     ortho = call(functools.partial(ortho_body, heads, nz), sds((hidden, HD), bf16), flops=1e9)(
         *(partials[d] for d in served(nz))
     )
     queries, ortho = lax.optimization_barrier((queries, ortho))
     rows = lax.all_to_all(
-        ortho.reshape(count, rows_local, HD), ("grp", "z"), 0, 0, tiled=True
+        ortho.reshape(count, rows_local, HD), ORDER, 0, 0, tiled=True
     )
     new_weights = call(
         functools.partial(finish_body, nz, group), sds(fast_weights.shape, f32), flops=1e6
@@ -427,13 +440,12 @@
 
 
 def solution(mesh):
-    group = 4
     nh = mesh.shape["head"]
     inner = Mesh(
-        np.asarray(mesh.devices).reshape(mesh.shape["ctx"] // group, group, nh),
-        ("z", "grp", "head"),
-    )
-    ctx = ("z", "grp")
+        np.asarray(mesh.devices).reshape(mesh.shape["ctx"] // 4, 2, 2, nh),
+        ("z", *GROUP, "head"),
+    )
+    ctx = ("z", *GROUP)
     placed = (
         P(ctx, "head"),
         P(ctx, "head"),

time: 58.2 us -> 58.7 us (level)
    all_to_all x3, waiting for transfers between devices: 4.1 us -> 4.74 us  [the longest x1 2.45 us: on_device(): lax.all_to_all(ortho.reshape(count, rows_local, HD), ORDER, 0, 0, tiled=T...]
  transfers between devices with their start and end apart: 11 -> 11, of which waited for: 5 -> 5; matrix products, arithmetic and copies ran while one was open for 0% -> 0% of each run, Pallas kernels for 18% -> 17%
where the time goes in v9:
time: 58.7 us; the launch traced here: 58.1 us
  starting transfers between devices  35.8 us (61%)
  Pallas kernels  12.5 us (21%)
  waiting for transfers between devices  7.38 us (13%)
  between operations  1.48 us (3%)
  local copies, waits for them, and re-layouts  0.93 us (2%)
    ppermute x3, starting transfers between devices, on_device(): partials[d] = lax.ppermute(partials[d], ('z', *GROUP), pairs)  8.56 us
    ppermute x3, starting transfers between devices, on_device(): token_slots[d] = lax.ppermute(token_slots[d], GROUP, pairs)  7.79 us
    all_to_all x1, starting transfers between devices, on_device(): weights = lax.all_to_all(low, ORDER, 0, 0, tiled=True)  7.49 us
    all_to_all x1, starting transfers between devices, on_device(): lax.all_to_all(ortho.reshape(count, rows_local, HD), ORDER, 0, 0, tiled=T...  4.62 us
    pallas_call x1, Pallas kernels, on_device(): call(functools.partial(ortho_body, heads, nz), sds((hidden, HD), bf16), f...  3.44 us
    all_to_all x1, starting transfers between devices, on_device(): fast_slots = lax.all_to_all(fast_slots, GROUP, 0, 0, tiled=True)  3.37 us
    all_to_all x1, waiting for transfers between devices, on_device(): lax.all_to_all(ortho.reshape(count, rows_local, HD), ORDER, 0, 0, tiled=T...  2.45 us
    ppermute x1, starting transfers between devices, on_device(): kv_back = lax.ppermute(kv_own, ('z', *GROUP), ring)  2.38 us
  transfers between devices with their start and end apart: 11, of which 5 were waited for; matrix products, arithmetic and copies ran while one was open for 0% of the time, Pallas kernels for 17%

profile of v9, /device:TPU:0, one launch (start us, length us, event | category | flops | bytes accessed | tf_op | source)
XLA Modules:
  0.0 58.1 jit_solution(13881934950181952184)
XLA Ops:
  0.6 0.0 copy-start.1
  0.6 0.9 %copy-done.1 = f32[3,3,32,128]{3,2,1,0:T(8,128)S(1)} copy-done((f32[3,3,32,128]{3,2,1,0:T(8,128)S(1)}, f32[3,3,32,128]{3,2,1,0:T(8,128)}, u32[]{:S(2)}) %copy-start.1) | copy-done | bytes 147480
  1.5 0.8 %shard_map.86.after = bf16[16,3,32,128]{3,2,1,0:T(8,128)(2,1)} custom-call(f32[3,3,32,128]{3,2,1,0:T(8,128)S(1)} %copy-done.1), custom_call_target="tpu_custom_call" | custom-call | flops 1000000 | bytes 1048576 | tf_op jit(solution)/shard_map/pallas_call | solution.py:339
  2.3 0.0 copy-start
  2.3 0.0 copy-start.3
  2.3 0.0 copy-start.4
  2.3 7.5 %all-to-all-start = ((bf16[16,3,32,128]{3,2,1,0:T(8,128)(2,1)}), bf16[16,3,32,128]{3,2,1,0:T(8,128)(2,1)S(1)}, u32[]{:S(2)}, u32[]{:S(2)}) async-start(bf16[16,3,32,128]{3,2,1,0:T(8,128)(2,1)} %shard_map.86.after), calls=%async_computation | async-start | bytes 786432 | tf_op jit(solution)/shard_map/all_to_all | solution.py:356
  9.8 0.0 copy-start.5
  10.5 0.0 copy-done
  10.5 0.0 copy-done.3
  10.5 0.0 copy-done.4
  10.5 0.0 copy-done.5
  10.5 0.6 %shard_map.87 = (bf16[208,768]{1,0:T(8,128)(2,1)S(1)}, bf16[195,384]{1,0:T(8,128)(2,1)S(1)}, bf16[195,384]{1,0:T(8,128)(2,1)S(1)}, bf16[195,384]{1,0:T(8,128)(2,1)S(1)}, bf16[195,384]{1,0:T(8,128)(2,1)S(1)}) custom-call(bf16[16,3,32,128]{3,2,1,0:T(8,128)(2,1)} %shard_map.86.after, s32[1,1]{1,0:T(1,128)} %bitcast.3.update, f32[3,195]{1,0:T(4,128)S(1)} %bitcast.4, ...), custom_call_target="tpu_custom_call" | custom-call | tf_op jit(solution)/shard_map/pallas_call | solution.py:342
  11.1 1.3 %collective-permute-start.1 = (bf16[195,384]{1,0:T(8,128)(2,1)S(1)}, bf16[195,384]{1,0:T(8,128)(2,1)S(1)}, u32[]{:S(2)}, u32[]{:S(2)}) collective-permute-start(bf16[195,384]{1,0:T(8,128)(2,1)S(1)} %get-tuple-element.25), channel_id=1, source_target_pairs={{2,4},{4,2},{6,0},{3,5},{5,3},{7,1},{10,12},{12,10},{14,8},{11,13}... | collective-permute-start | bytes 449288 | tf_op jit(solution)/shard_map/ppermute | solution.py:361
  12.4 4.6 %collective-permute-start.2 = (bf16[195,384]{1,0:T(8,128)(2,1)S(1)}, bf16[195,384]{1,0:T(8,128)(2,1)S(1)}, u32[]{:S(2)}, u32[]{:S(2)}) collective-permute-start(bf16[195,384]{1,0:T(8,128)(2,1)S(1)} %get-tuple-element.26), channel_id=1, source_target_pairs={{0,2},{2,0},{6,4},{1,3},{3,1},{7,5},{8,10},{10,8},{14,12},{9,11},{... | collective-permute-start | bytes 449288 | tf_op jit(solution)/shard_map/ppermute | solution.py:361
  17.0 1.9 %collective-permute-start = (bf16[195,384]{1,0:T(8,128)(2,1)S(1)}, bf16[195,384]{1,0:T(8,128)(2,1)S(1)}, u32[]{:S(2)}, u32[]{:S(2)}) collective-permute-start(bf16[195,384]{1,0:T(8,128)(2,1)S(1)} %get-tuple-element.23), channel_id=1, source_target_pairs={{0,4},{4,0},{6,2},{1,5},{5,1},{7,3},{8,12},{12,8},{14,10},{9,13},{... | collective-permute-start | bytes 449288 | tf_op jit(solution)/shard_map/ppermute | solution.py:361
  18.9 1.5 %collective-permute-done.1.refs_1_ = bf16[195,384]{1,0:T(8,128)(2,1)S(1)} collective-permute-done((bf16[195,384]{1,0:T(8,128)(2,1)S(1)}, bf16[195,384]{1,0:T(8,128)(2,1)S(1)}, u32[]{:S(2)}, u32[]{:S(2)}) %collective-permute-start.1) | collective-permute-done | bytes 149792 | tf_op jit(solution)/shard_map/ppermute | solution.py:361
  20.4 0.0 collective-permute-done.2.refs_2_
  20.4 2.3 %all-to-all-done.refs_3_.w_ref = bf16[16,3,32,128]{3,2,1,0:T(8,128)(2,1)S(1)} async-done(((bf16[16,3,32,128]{3,2,1,0:T(8,128)(2,1)}), bf16[16,3,32,128]{3,2,1,0:T(8,128)(2,1)S(1)}, u32[]{:S(2)}, u32[]{:S(2)}) %all-to-all-start) | async-done | bytes 393248 | tf_op jit(solution)/shard_map/all_to_all | solution.py:356
  22.7 2.2 %shard_map.88 = (f32[3,512,128]{2,1,0:T(8,128)S(1)}, bf16[3,208,128]{2,1,0:T(8,128)(2,1)S(1)}) custom-call(bf16[195,384]{1,0:T(8,128)(2,1)S(1)} %get-tuple-element.24.refs_0_, bf16[195,384]{1,0:T(8,128)(2,1)S(1)} %collective-permute-done.1.refs_1_, bf16[195,384]{1,0:T(8,128)(2,1)S(1)} %collective-permute-done.2.refs_2_, ...), custom_call_target="tpu_custom_call" | custom-call | flops 1000000000 | bytes 1048576 | tf_op jit(solution)/shard_map/pallas_call | solution.py:365
  24.9 0.4 collective-permute-done.token_ref
  25.3 0.8 %shard_map.89 = (bf16[512,128]{1,0:T(8,128)(2,1)S(1)}, bf16[512,128]{1,0:T(8,128)(2,1)S(1)}, bf16[512,128]{1,0:T(8,128)(2,1)S(1)}, bf16[512,128]{1,0:T(8,128)(2,1)S(1)}) custom-call(bf16[195,384]{1,0:T(8,128)(2,1)S(1)} %collective-permute-done.token_ref, bf16[16,3,32,128]{3,2,1,0:T(8,128)(2,1)S(1)} %all-to-all-done.refs_3_.w_ref, ...), custom_call_target="tpu_custom_call" | custom-call | flops 500000000 | bytes 1048576 | tf_op jit(solution)/shard_map/pallas_call | solution.py:372
  26.1 1.3 %collective-permute-start.3 = (bf16[512,128]{1,0:T(8,128)(2,1)S(1)}, bf16[512,128]{1,0:T(8,128)(2,1)S(1)}, u32[]{:S(2)}, u32[]{:S(2)}) collective-permute-start(bf16[512,128]{1,0:T(8,128)(2,1)S(1)} %get-tuple-element.33), channel_id=1, source_target_pairs={{2,26},{8,16},{10,18},{12,20},{16,8},{18,10},{20,12},{24,0},{28,4}... | collective-permute-start | bytes 393224 | tf_op jit(solution)/shard_map/ppermute | solution.py:388
  27.4 5.3 %collective-permute-start.4 = (bf16[512,128]{1,0:T(8,128)(2,1)S(1)}, bf16[512,128]{1,0:T(8,128)(2,1)S(1)}, u32[]{:S(2)}, u32[]{:S(2)}) collective-permute-start(bf16[512,128]{1,0:T(8,128)(2,1)S(1)} %get-tuple-element.34), channel_id=1, source_target_pairs={{0,16},{2,18},{4,20},{10,26},{16,0},{20,4},{24,8},{26,10},{28,12},... | collective-permute-start | bytes 393224 | tf_op jit(solution)/shard_map/ppermute | solution.py:388
  32.8 1.9 %collective-permute-start.5 = (bf16[512,128]{1,0:T(8,128)(2,1)S(1)}, bf16[512,128]{1,0:T(8,128)(2,1)S(1)}, u32[]{:S(2)}, u32[]{:S(2)}) collective-permute-start(bf16[512,128]{1,0:T(8,128)(2,1)S(1)} %get-tuple-element.35), channel_id=1, source_target_pairs={{0,8},{2,10},{4,12},{8,0},{12,4},{18,26},{24,16},{26,18},{28,20},{... | collective-permute-start | bytes 393224 | tf_op jit(solution)/shard_map/ppermute | solution.py:388
  34.7 1.1 %shard_map.90 = bf16[4,208,128]{2,1,0:T(8,128)(2,1)} custom-call(bf16[195,384]{1,0:T(8,128)(2,1)S(1)} %collective-permute-done.token_ref, bf16[16,3,32,128]{3,2,1,0:T(8,128)(2,1)S(1)} %all-to-all-done.refs_3_.w_ref, bf16[3,208,128]{2,1,0:T(8,128)(2,1)S(1)} %get-tuple-element.31.early), custom_call_target="tpu_custom_call" | custom-call | flops 1000 | bytes 1024 | tf_op jit(solution)/shard_map/pallas_call | solution.py:390
  35.8 3.4 %all-to-all-start.1 = ((bf16[4,208,128]{2,1,0:T(8,128)(2,1)}), bf16[4,208,128]{2,1,0:T(8,128)(2,1)S(1)}, u32[]{:S(2)}, u32[]{:S(2)}) async-start(bf16[4,208,128]{2,1,0:T(8,128)(2,1)} %shard_map.90), calls=%async_computation.1 | async-start | bytes 425984 | tf_op jit(solution)/shard_map/all_to_all | solution.py:398
  39.2 2.4 %collective-permute-start.6 = (bf16[208,768]{1,0:T(8,128)(2,1)S(1)}, bf16[208,768]{1,0:T(8,128)(2,1)S(1)}, u32[]{:S(2)}, u32[]{:S(2)}) collective-permute-start(bf16[208,768]{1,0:T(8,128)(2,1)S(1)} %get-tuple-element.37.own_ref), channel_id=1, source_target_pairs={{0,2},{2,4},{4,6},{6,8},{8,10},{10,12},{12,14},{14,16},{16,18},{18... | collective-permute-start | bytes 958472 | tf_op jit(solution)/shard_map/ppermute | solution.py:401
  41.6 0.0 collective-permute-done.3.refs_1_
  41.6 0.0 collective-permute-done.4.refs_2_
  41.6 0.0 collective-permute-done.5.refs_3_
  41.6 3.4 %shard_map.91 = bf16[512,128]{1,0:T(8,128)(2,1)} custom-call(bf16[512,128]{1,0:T(8,128)(2,1)S(1)} %get-tuple-element.32.refs_0_, bf16[512,128]{1,0:T(8,128)(2,1)S(1)} %collective-permute-done.3.refs_1_, bf16[512,128]{1,0:T(8,128)(2,1)S(1)} %collective-permute-done.4.refs_2_, bf16[512,128]{1,0:T(8,128)(2,1)S(1)} %collective-permute-done.5.refs_3_), custom_call_target="tpu_custom_call" | custom-call | flops 1000000000 | bytes 1048576 | tf_op jit(solution)/shard_map/pallas_call | solution.py:403
  45.0 0.0 all-to-all-done.1.slots
  45.0 4.6 %all-to-all-start.2 = ((bf16[16,32,128]{2,1,0:T(8,128)(2,1)}), bf16[16,32,128]{2,1,0:T(8,128)(2,1)S(1)}, u32[]{:S(2)}, u32[]{:S(2)}) async-start(bf16[16,32,128]{2,1,0:T(8,128)(2,1)} %bitcast.2), calls=%async_computation.2 | async-start | bytes 262144 | tf_op jit(solution)/shard_map/all_to_all | solution.py:407
  49.7 0.0 copy-start.6
  49.7 0.4 shard_map.93
  50.1 1.6 %collective-permute-start.7 = (f32[8,208]{1,0:T(8,128)S(1)}, f32[8,208]{1,0:T(8,128)S(1)}, u32[]{:S(2)}, u32[]{:S(2)}) collective-permute-start(f32[8,208]{1,0:T(8,128)S(1)} %get-tuple-element.40.refs_0_), channel_id=1, source_target_pairs={{0,1},{1,0},{2,3},{3,2},{4,5},{5,4},{6,7},{7,6},{8,9},{9,8},{10,11... | collective-permute-start | bytes 19976 | tf_op jit(solution)/shard_map/ppermute | solution.py:428
  51.7 0.0 copy-done.6
  51.7 0.0 collective-permute-done.6.back_ref
  51.7 1.3 %shard_map.92.attended_ref = f32[208,384]{1,0:T(8,128)S(1)} custom-call(bf16[195,384]{1,0:T(8,128)(2,1)S(1)} %copy-done, bf16[208,768]{1,0:T(8,128)(2,1)S(1)} %get-tuple-element.37.own_ref, bf16[208,768]{1,0:T(8,128)(2,1)S(1)} %collective-permute-done.6.back_ref), custom_call_target="tpu_custom_call" | custom-call | tf_op jit(solution)/shard_map/pallas_call | solution.py:414
  53.0 0.8 %collective-permute-done.7.refs_1_ = f32[8,208]{1,0:T(8,128)S(1)} collective-permute-done((f32[8,208]{1,0:T(8,128)S(1)}, f32[8,208]{1,0:T(8,128)S(1)}, u32[]{:S(2)}, u32[]{:S(2)}) %collective-permute-start.7) | collective-permute-done | bytes 6688 | tf_op jit(solution)/shard_map/ppermute | solution.py:428
  53.8 0.0 copy-start.2
  53.8 1.0 %shard_map.94 = bf16[195,384]{1,0:T(8,128)(2,1)} custom-call(f32[1,384]{1,0:T(1,128)S(1)} %reshape.13.gain_ref, f32[208,384]{1,0:T(8,128)S(1)} %shard_map.92.attended_ref, bf16[208,384]{1,0:T(8,128)(2,1)S(1)} %get-tuple-element.39.fast_ref, f32[8,208]{1,0:T(8,128)S(1)} %get-tuple-element.40.refs_0_, f32[8,208]{1,0:T(8,128)S(1)} %collective-permute-done.7.refs_1_), custom_call_target="tpu_custom_call" | custom-call | tf_op jit(solution)/shard_map/pallas_call | solution.py:430
  54.8 2.4 %all-to-all-done.2.rows_ref = bf16[16,32,128]{2,1,0:T(8,128)(2,1)S(1)} async-done(((bf16[16,32,128]{2,1,0:T(8,128)(2,1)}), bf16[16,32,128]{2,1,0:T(8,128)(2,1)S(1)}, u32[]{:S(2)}, u32[]{:S(2)}) %all-to-all-start.2) | async-done | bytes 131104 | tf_op jit(solution)/shard_map/all_to_all | solution.py:407
  57.2 0.0 copy-done.2
  57.2 0.8 %shard_map.95 = f32[3,3,32,128]{3,2,1,0:T(8,128)} custom-call(f32[3,3,32,128]{3,2,1,0:T(8,128)S(1)} %copy-done.2, bf16[16,32,128]{2,1,0:T(8,128)(2,1)S(1)} %all-to-all-done.2.rows_ref), custom_call_target="tpu_custom_call" | custom-call | flops 1000000 | bytes 1048576 | tf_op jit(solution)/shard_map/pallas_call | solution.py:410
  (1 shorter events, 0.0 us)
Async XLA Ops:
  0.6 0.9 %copy-start.1 = (f32[3,3,32,128]{3,2,1,0:T(8,128)S(1)}, f32[3,3,32,128]{3,2,1,0:T(8,128)}, u32[]{:S(2)}) copy-start(f32[3,3,32,128]{3,2,1,0:T(8,128)} %w_ref.3) | copy-start | bytes 442372
  2.3 8.2 %copy-start = (bf16[195,384]{1,0:T(8,128)(2,1)S(1)}, bf16[195,384]{1,0:T(8,128)(2,1)}, u32[]{:S(2)}) copy-start(bf16[195,384]{1,0:T(8,128)(2,1)} %q_ref.2) | copy-start | bytes 449284
  2.3 8.2 %copy-start.3 = (bf16[195,384]{1,0:T(8,128)(2,1)S(1)}, bf16[195,384]{1,0:T(8,128)(2,1)}, u32[]{:S(2)}) copy-start(bf16[195,384]{1,0:T(8,128)(2,1)} %k_ref.1) | copy-start | bytes 449284
  2.3 8.2 %copy-start.4 = (bf16[195,384]{1,0:T(8,128)(2,1)S(1)}, bf16[195,384]{1,0:T(8,128)(2,1)}, u32[]{:S(2)}) copy-start(bf16[195,384]{1,0:T(8,128)(2,1)} %v_ref.1) | copy-start | bytes 449284
  2.3 20.4 %all-to-all-start = ((bf16[16,3,32,128]{3,2,1,0:T(8,128)(2,1)}), bf16[16,3,32,128]{3,2,1,0:T(8,128)(2,1)S(1)}, u32[]{:S(2)}, u32[]{:S(2)}) async-start(bf16[16,3,32,128]{3,2,1,0:T(8,128)(2,1)} %shard_map.86.after), calls=%async_computation | async-start | bytes 786432 | tf_op jit(solution)/shard_map/all_to_all | solution.py:356
  9.8 0.7 %copy-start.5 = (f32[195,3]{0,1:T(4,128)S(1)}, f32[195,3]{0,1:T(4,128)}, u32[]{:S(2)}) copy-start(f32[195,3]{0,1:T(4,128)} %param.10) | copy-start | bytes 7024
  11.1 9.3 %collective-permute-start.1 = (bf16[195,384]{1,0:T(8,128)(2,1)S(1)}, bf16[195,384]{1,0:T(8,128)(2,1)S(1)}, u32[]{:S(2)}, u32[]{:S(2)}) collective-permute-start(bf16[195,384]{1,0:T(8,128)(2,1)S(1)} %get-tuple-element.25), channel_id=1, source_target_pairs={{2,4},{4,2},{6,0},{3,5},{5,3},{7,1},{10,12},{12,10},{14,8},{11,13}... | collective-permute-start | bytes 449288 | tf_op jit(solution)/shard_map/ppermute | solution.py:361
  12.4 8.0 %collective-permute-start.2 = (bf16[195,384]{1,0:T(8,128)(2,1)S(1)}, bf16[195,384]{1,0:T(8,128)(2,1)S(1)}, u32[]{:S(2)}, u32[]{:S(2)}) collective-permute-start(bf16[195,384]{1,0:T(8,128)(2,1)S(1)} %get-tuple-element.26), channel_id=1, source_target_pairs={{0,2},{2,0},{6,4},{1,3},{3,1},{7,5},{8,10},{10,8},{14,12},{9,11},{... | collective-permute-start | bytes 449288 | tf_op jit(solution)/shard_map/ppermute | solution.py:361
  17.0 8.3 %collective-permute-start = (bf16[195,384]{1,0:T(8,128)(2,1)S(1)}, bf16[195,384]{1,0:T(8,128)(2,1)S(1)}, u32[]{:S(2)}, u32[]{:S(2)}) collective-permute-start(bf16[195,384]{1,0:T(8,128)(2,1)S(1)} %get-tuple-element.23), channel_id=1, source_target_pairs={{0,4},{4,0},{6,2},{1,5},{5,1},{7,3},{8,12},{12,8},{14,10},{9,13},{... | collective-permute-start | bytes 449288 | tf_op jit(solution)/shard_map/ppermute | solution.py:361
  26.1 15.5 %collective-permute-start.3 = (bf16[512,128]{1,0:T(8,128)(2,1)S(1)}, bf16[512,128]{1,0:T(8,128)(2,1)S(1)}, u32[]{:S(2)}, u32[]{:S(2)}) collective-permute-start(bf16[512,128]{1,0:T(8,128)(2,1)S(1)} %get-tuple-element.33), channel_id=1, source_target_pairs={{2,26},{8,16},{10,18},{12,20},{16,8},{18,10},{20,12},{24,0},{28,4}... | collective-permute-start | bytes 393224 | tf_op jit(solution)/shard_map/ppermute | solution.py:388
  27.4 14.2 %collective-permute-start.4 = (bf16[512,128]{1,0:T(8,128)(2,1)S(1)}, bf16[512,128]{1,0:T(8,128)(2,1)S(1)}, u32[]{:S(2)}, u32[]{:S(2)}) collective-permute-start(bf16[512,128]{1,0:T(8,128)(2,1)S(1)} %get-tuple-element.34), channel_id=1, source_target_pairs={{0,16},{2,18},{4,20},{10,26},{16,0},{20,4},{24,8},{26,10},{28,12},... | collective-permute-start | bytes 393224 | tf_op jit(solution)/shard_map/ppermute | solution.py:388
  32.8 8.8 %collective-permute-start.5 = (bf16[512,128]{1,0:T(8,128)(2,1)S(1)}, bf16[512,128]{1,0:T(8,128)(2,1)S(1)}, u32[]{:S(2)}, u32[]{:S(2)}) collective-permute-start(bf16[512,128]{1,0:T(8,128)(2,1)S(1)} %get-tuple-element.35), channel_id=1, source_target_pairs={{0,8},{2,10},{4,12},{8,0},{12,4},{18,26},{24,16},{26,18},{28,20},{... | collective-permute-start | bytes 393224 | tf_op jit(solution)/shard_map/ppermute | solution.py:388
  35.8 9.2 %all-to-all-start.1 = ((bf16[4,208,128]{2,1,0:T(8,128)(2,1)}), bf16[4,208,128]{2,1,0:T(8,128)(2,1)S(1)}, u32[]{:S(2)}, u32[]{:S(2)}) async-start(bf16[4,208,128]{2,1,0:T(8,128)(2,1)} %shard_map.90), calls=%async_computation.1 | async-start | bytes 425984 | tf_op jit(solution)/shard_map/all_to_all | solution.py:398
  39.2 12.5 %collective-permute-start.6 = (bf16[208,768]{1,0:T(8,128)(2,1)S(1)}, bf16[208,768]{1,0:T(8,128)(2,1)S(1)}, u32[]{:S(2)}, u32[]{:S(2)}) collective-permute-start(bf16[208,768]{1,0:T(8,128)(2,1)S(1)} %get-tuple-element.37.own_ref), channel_id=1, source_target_pairs={{0,2},{2,4},{4,6},{6,8},{8,10},{10,12},{12,14},{14,16},{16,18},{18... | collective-permute-start | bytes 958472 | tf_op jit(solution)/shard_map/ppermute | solution.py:401
  45.0 12.2 %all-to-all-start.2 = ((bf16[16,32,128]{2,1,0:T(8,128)(2,1)}), bf16[16,32,128]{2,1,0:T(8,128)(2,1)S(1)}, u32[]{:S(2)}, u32[]{:S(2)}) async-start(bf16[16,32,128]{2,1,0:T(8,128)(2,1)} %bitcast.2), calls=%async_computation.2 | async-start | bytes 262144 | tf_op jit(solution)/shard_map/all_to_all | solution.py:407
  49.7 2.0 %copy-start.6 = (f32[384]{0:T(512)S(1)}, f32[384]{0:T(512)}, u32[]{:S(2)}) copy-start(f32[384]{0:T(512)} %param.13) | copy-start | bytes 4612
  50.1 3.7 %collective-permute-start.7 = (f32[8,208]{1,0:T(8,128)S(1)}, f32[8,208]{1,0:T(8,128)S(1)}, u32[]{:S(2)}, u32[]{:S(2)}) collective-permute-start(f32[8,208]{1,0:T(8,128)S(1)} %get-tuple-element.40.refs_0_), channel_id=1, source_target_pairs={{0,1},{1,0},{2,3},{3,2},{4,5},{5,4},{6,7},{7,6},{8,9},{9,8},{10,11... | collective-permute-start | bytes 19976 | tf_op jit(solution)/shard_map/ppermute | solution.py:428
  53.8 3.4 %copy-start.2 = (f32[3,3,32,128]{3,2,1,0:T(8,128)S(1)}, f32[3,3,32,128]{3,2,1,0:T(8,128)}, u32[]{:S(2)}) copy-start(f32[3,3,32,128]{3,2,1,0:T(8,128)} %w_ref.3) | copy-start | bytes 442372

commit v10 on v9

--- a/solution.py
+++ b/solution.py
@@ -54,7 +54,7 @@
 
 
 GROUP = ("x", "core")
-ORDER = ("core", "x", "z")
+ORDER = ("x", "z", "core")
 
 
 def position():

time: 58.7 us -> 58.7 us (level)
  no operation moved by 1% of the time
where the time goes in v10:
time: 58.7 us; the launch traced here: 58.1 us
  starting transfers between devices  35.6 us (61%)
  Pallas kernels  12.5 us (21%)
  waiting for transfers between devices  7.63 us (13%)
  between operations  1.48 us (3%)
  local copies, waits for them, and re-layouts  0.93 us (2%)
    ppermute x3, starting transfers between devices, on_device(): partials[d] = lax.ppermute(partials[d], ('z', *GROUP), pairs)  8.35 us
    ppermute x3, starting transfers between devices, on_device(): token_slots[d] = lax.ppermute(token_slots[d], GROUP, pairs)  7.78 us
    all_to_all x1, starting transfers between devices, on_device(): weights = lax.all_to_all(low, ORDER, 0, 0, tiled=True)  7.49 us
    all_to_all x1, starting transfers between devices, on_device(): lax.all_to_all(ortho.reshape(count, rows_local, HD), ORDER, 0, 0, tiled=T...  4.62 us
    pallas_call x1, Pallas kernels, on_device(): call(functools.partial(ortho_body, heads, nz), sds((hidden, HD), bf16), f...  3.44 us
    all_to_all x1, starting transfers between devices, on_device(): fast_slots = lax.all_to_all(fast_slots, GROUP, 0, 0, tiled=True)  3.37 us
    all_to_all x1, waiting for transfers between devices, on_device(): lax.all_to_all(ortho.reshape(count, rows_local, HD), ORDER, 0, 0, tiled=T...  2.8 us
    ppermute x1, starting transfers between devices, on_device(): kv_back = lax.ppermute(kv_own, ('z', *GROUP), ring)  2.38 us
  transfers between devices with their start and end apart: 11, of which 5 were waited for; matrix products, arithmetic and copies ran while one was open for 0% of the time, Pallas kernels for 17%

profile of v10, /device:TPU:0, one launch (start us, length us, event | category | flops | bytes accessed | tf_op | source)
XLA Modules:
  0.0 58.1 jit_solution(3935173598625429191)
XLA Ops:
  0.6 0.0 copy-start.1
  0.6 0.9 %copy-done.1 = f32[3,3,32,128]{3,2,1,0:T(8,128)S(1)} copy-done((f32[3,3,32,128]{3,2,1,0:T(8,128)S(1)}, f32[3,3,32,128]{3,2,1,0:T(8,128)}, u32[]{:S(2)}) %copy-start.1) | copy-done | bytes 147480
  1.5 0.8 %shard_map.86.after = bf16[16,3,32,128]{3,2,1,0:T(8,128)(2,1)} custom-call(f32[3,3,32,128]{3,2,1,0:T(8,128)S(1)} %copy-done.1), custom_call_target="tpu_custom_call" | custom-call | flops 1000000 | bytes 1048576 | tf_op jit(solution)/shard_map/pallas_call | solution.py:339
  2.3 0.0 copy-start
  2.3 0.0 copy-start.3
  2.3 0.0 copy-start.4
  2.3 7.5 %all-to-all-start = ((bf16[16,3,32,128]{3,2,1,0:T(8,128)(2,1)}), bf16[16,3,32,128]{3,2,1,0:T(8,128)(2,1)S(1)}, u32[]{:S(2)}, u32[]{:S(2)}) async-start(bf16[16,3,32,128]{3,2,1,0:T(8,128)(2,1)} %shard_map.86.after), calls=%async_computation | async-start | bytes 786432 | tf_op jit(solution)/shard_map/all_to_all | solution.py:356
  9.8 0.0 copy-start.5
  10.5 0.0 copy-done
  10.5 0.0 copy-done.3
  10.5 0.0 copy-done.4
  10.5 0.0 copy-done.5
  10.5 0.6 %shard_map.87 = (bf16[208,768]{1,0:T(8,128)(2,1)S(1)}, bf16[195,384]{1,0:T(8,128)(2,1)S(1)}, bf16[195,384]{1,0:T(8,128)(2,1)S(1)}, bf16[195,384]{1,0:T(8,128)(2,1)S(1)}, bf16[195,384]{1,0:T(8,128)(2,1)S(1)}) custom-call(bf16[16,3,32,128]{3,2,1,0:T(8,128)(2,1)} %shard_map.86.after, s32[1,1]{1,0:T(1,128)} %bitcast.3.update, f32[3,195]{1,0:T(4,128)S(1)} %bitcast.4, ...), custom_call_target="tpu_custom_call" | custom-call | tf_op jit(solution)/shard_map/pallas_call | solution.py:342
  11.1 1.3 %collective-permute-start.1 = (bf16[195,384]{1,0:T(8,128)(2,1)S(1)}, bf16[195,384]{1,0:T(8,128)(2,1)S(1)}, u32[]{:S(2)}, u32[]{:S(2)}) collective-permute-start(bf16[195,384]{1,0:T(8,128)(2,1)S(1)} %get-tuple-element.25), channel_id=1, source_target_pairs={{2,4},{4,2},{6,0},{3,5},{5,3},{7,1},{10,12},{12,10},{14,8},{11,13}... | collective-permute-start | bytes 449288 | tf_op jit(solution)/shard_map/ppermute | solution.py:361
  12.4 4.6 %collective-permute-start.2 = (bf16[195,384]{1,0:T(8,128)(2,1)S(1)}, bf16[195,384]{1,0:T(8,128)(2,1)S(1)}, u32[]{:S(2)}, u32[]{:S(2)}) collective-permute-start(bf16[195,384]{1,0:T(8,128)(2,1)S(1)} %get-tuple-element.26), channel_id=1, source_target_pairs={{0,2},{2,0},{6,4},{1,3},{3,1},{7,5},{8,10},{10,8},{14,12},{9,11},{... | collective-permute-start | bytes 449288 | tf_op jit(solution)/shard_map/ppermute | solution.py:361
  17.0 1.9 %collective-permute-start = (bf16[195,384]{1,0:T(8,128)(2,1)S(1)}, bf16[195,384]{1,0:T(8,128)(2,1)S(1)}, u32[]{:S(2)}, u32[]{:S(2)}) collective-permute-start(bf16[195,384]{1,0:T(8,128)(2,1)S(1)} %get-tuple-element.23), channel_id=1, source_target_pairs={{0,4},{4,0},{6,2},{1,5},{5,1},{7,3},{8,12},{12,8},{14,10},{9,13},{... | collective-permute-start | bytes 449288 | tf_op jit(solution)/shard_map/ppermute | solution.py:361
  18.9 1.1 %collective-permute-done.1.refs_1_ = bf16[195,384]{1,0:T(8,128)(2,1)S(1)} collective-permute-done((bf16[195,384]{1,0:T(8,128)(2,1)S(1)}, bf16[195,384]{1,0:T(8,128)(2,1)S(1)}, u32[]{:S(2)}, u32[]{:S(2)}) %collective-permute-start.1) | collective-permute-done | bytes 149792 | tf_op jit(solution)/shard_map/ppermute | solution.py:361
  20.0 0.0 collective-permute-done.2.refs_2_
  20.0 2.1 %all-to-all-done.refs_3_.w_ref = bf16[16,3,32,128]{3,2,1,0:T(8,128)(2,1)S(1)} async-done(((bf16[16,3,32,128]{3,2,1,0:T(8,128)(2,1)}), bf16[16,3,32,128]{3,2,1,0:T(8,128)(2,1)S(1)}, u32[]{:S(2)}, u32[]{:S(2)}) %all-to-all-start) | async-done | bytes 393248 | tf_op jit(solution)/shard_map/all_to_all | solution.py:356
  22.1 2.2 %shard_map.88 = (f32[3,512,128]{2,1,0:T(8,128)S(1)}, bf16[3,208,128]{2,1,0:T(8,128)(2,1)S(1)}) custom-call(bf16[195,384]{1,0:T(8,128)(2,1)S(1)} %get-tuple-element.24.refs_0_, bf16[195,384]{1,0:T(8,128)(2,1)S(1)} %collective-permute-done.1.refs_1_, bf16[195,384]{1,0:T(8,128)(2,1)S(1)} %collective-permute-done.2.refs_2_, ...), custom_call_target="tpu_custom_call" | custom-call | flops 1000000000 | bytes 1048576 | tf_op jit(solution)/shard_map/pallas_call | solution.py:365
  24.3 0.9 %collective-permute-done.token_ref = bf16[195,384]{1,0:T(8,128)(2,1)S(1)} collective-permute-done((bf16[195,384]{1,0:T(8,128)(2,1)S(1)}, bf16[195,384]{1,0:T(8,128)(2,1)S(1)}, u32[]{:S(2)}, u32[]{:S(2)}) %collective-permute-start) | collective-permute-done | bytes 149792 | tf_op jit(solution)/shard_map/ppermute | solution.py:361
  25.2 0.8 %shard_map.89 = (bf16[512,128]{1,0:T(8,128)(2,1)S(1)}, bf16[512,128]{1,0:T(8,128)(2,1)S(1)}, bf16[512,128]{1,0:T(8,128)(2,1)S(1)}, bf16[512,128]{1,0:T(8,128)(2,1)S(1)}) custom-call(bf16[195,384]{1,0:T(8,128)(2,1)S(1)} %collective-permute-done.token_ref, bf16[16,3,32,128]{3,2,1,0:T(8,128)(2,1)S(1)} %all-to-all-done.refs_3_.w_ref, ...), custom_call_target="tpu_custom_call" | custom-call | flops 500000000 | bytes 1048576 | tf_op jit(solution)/shard_map/pallas_call | solution.py:372
  26.0 1.3 %collective-permute-start.3 = (bf16[512,128]{1,0:T(8,128)(2,1)S(1)}, bf16[512,128]{1,0:T(8,128)(2,1)S(1)}, u32[]{:S(2)}, u32[]{:S(2)}) collective-permute-start(bf16[512,128]{1,0:T(8,128)(2,1)S(1)} %get-tuple-element.33), channel_id=1, source_target_pairs={{2,26},{8,16},{10,18},{12,20},{16,8},{18,10},{20,12},{24,0},{28,4}... | collective-permute-start | bytes 393224 | tf_op jit(solution)/shard_map/ppermute | solution.py:388
  27.3 5.1 %collective-permute-start.4 = (bf16[512,128]{1,0:T(8,128)(2,1)S(1)}, bf16[512,128]{1,0:T(8,128)(2,1)S(1)}, u32[]{:S(2)}, u32[]{:S(2)}) collective-permute-start(bf16[512,128]{1,0:T(8,128)(2,1)S(1)} %get-tuple-element.34), channel_id=1, source_target_pairs={{0,16},{2,18},{4,20},{10,26},{16,0},{20,4},{24,8},{26,10},{28,12},... | collective-permute-start | bytes 393224 | tf_op jit(solution)/shard_map/ppermute | solution.py:388
  32.4 1.9 %collective-permute-start.5 = (bf16[512,128]{1,0:T(8,128)(2,1)S(1)}, bf16[512,128]{1,0:T(8,128)(2,1)S(1)}, u32[]{:S(2)}, u32[]{:S(2)}) collective-permute-start(bf16[512,128]{1,0:T(8,128)(2,1)S(1)} %get-tuple-element.35), channel_id=1, source_target_pairs={{0,8},{2,10},{4,12},{8,0},{12,4},{18,26},{24,16},{26,18},{28,20},{... | collective-permute-start | bytes 393224 | tf_op jit(solution)/shard_map/ppermute | solution.py:388
  34.4 1.1 %shard_map.90 = bf16[4,208,128]{2,1,0:T(8,128)(2,1)} custom-call(bf16[195,384]{1,0:T(8,128)(2,1)S(1)} %collective-permute-done.token_ref, bf16[16,3,32,128]{3,2,1,0:T(8,128)(2,1)S(1)} %all-to-all-done.refs_3_.w_ref, bf16[3,208,128]{2,1,0:T(8,128)(2,1)S(1)} %get-tuple-element.31.early), custom_call_target="tpu_custom_call" | custom-call | flops 1000 | bytes 1024 | tf_op jit(solution)/shard_map/pallas_call | solution.py:390
  35.5 3.4 %all-to-all-start.1 = ((bf16[4,208,128]{2,1,0:T(8,128)(2,1)}), bf16[4,208,128]{2,1,0:T(8,128)(2,1)S(1)}, u32[]{:S(2)}, u32[]{:S(2)}) async-start(bf16[4,208,128]{2,1,0:T(8,128)(2,1)} %shard_map.90), calls=%async_computation.1 | async-start | bytes 425984 | tf_op jit(solution)/shard_map/all_to_all | solution.py:398
  38.9 2.4 %collective-permute-start.6 = (bf16[208,768]{1,0:T(8,128)(2,1)S(1)}, bf16[208,768]{1,0:T(8,128)(2,1)S(1)}, u32[]{:S(2)}, u32[]{:S(2)}) collective-permute-start(bf16[208,768]{1,0:T(8,128)(2,1)S(1)} %get-tuple-element.37.own_ref), channel_id=1, source_target_pairs={{0,2},{2,4},{4,6},{6,8},{8,10},{10,12},{12,14},{14,16},{16,18},{18... | collective-permute-start | bytes 958472 | tf_op jit(solution)/shard_map/ppermute | solution.py:401
  41.3 0.0 collective-permute-done.3.refs_1_
  41.3 0.0 collective-permute-done.4.refs_2_
  41.3 0.0 collective-permute-done.5.refs_3_
  41.3 3.4 %shard_map.91 = bf16[512,128]{1,0:T(8,128)(2,1)} custom-call(bf16[512,128]{1,0:T(8,128)(2,1)S(1)} %get-tuple-element.32.refs_0_, bf16[512,128]{1,0:T(8,128)(2,1)S(1)} %collective-permute-done.3.refs_1_, bf16[512,128]{1,0:T(8,128)(2,1)S(1)} %collective-permute-done.4.refs_2_, bf16[512,128]{1,0:T(8,128)(2,1)S(1)} %collective-permute-done.5.refs_3_), custom_call_target="tpu_custom_call" | custom-call | flops 1000000000 | bytes 1048576 | tf_op jit(solution)/shard_map/pallas_call | solution.py:403
  44.7 0.0 all-to-all-done.1.slots
  44.7 4.6 %all-to-all-start.2 = ((bf16[16,32,128]{2,1,0:T(8,128)(2,1)}), bf16[16,32,128]{2,1,0:T(8,128)(2,1)S(1)}, u32[]{:S(2)}, u32[]{:S(2)}) async-start(bf16[16,32,128]{2,1,0:T(8,128)(2,1)} %bitcast.2), calls=%async_computation.2 | async-start | bytes 262144 | tf_op jit(solution)/shard_map/all_to_all | solution.py:407
  49.4 0.0 copy-start.6
  49.4 0.4 shard_map.93
  49.8 1.6 %collective-permute-start.7 = (f32[8,208]{1,0:T(8,128)S(1)}, f32[8,208]{1,0:T(8,128)S(1)}, u32[]{:S(2)}, u32[]{:S(2)}) collective-permute-start(f32[8,208]{1,0:T(8,128)S(1)} %get-tuple-element.40.refs_0_), channel_id=1, source_target_pairs={{0,1},{1,0},{2,3},{3,2},{4,5},{5,4},{6,7},{7,6},{8,9},{9,8},{10,11... | collective-permute-start | bytes 19976 | tf_op jit(solution)/shard_map/ppermute | solution.py:428
  51.4 0.0 copy-done.6
  51.4 0.0 collective-permute-done.6.back_ref
  51.4 1.3 %shard_map.92.attended_ref = f32[208,384]{1,0:T(8,128)S(1)} custom-call(bf16[195,384]{1,0:T(8,128)(2,1)S(1)} %copy-done, bf16[208,768]{1,0:T(8,128)(2,1)S(1)} %get-tuple-element.37.own_ref, bf16[208,768]{1,0:T(8,128)(2,1)S(1)} %collective-permute-done.6.back_ref), custom_call_target="tpu_custom_call" | custom-call | tf_op jit(solution)/shard_map/pallas_call | solution.py:414
  52.7 0.8 %collective-permute-done.7.refs_1_ = f32[8,208]{1,0:T(8,128)S(1)} collective-permute-done((f32[8,208]{1,0:T(8,128)S(1)}, f32[8,208]{1,0:T(8,128)S(1)}, u32[]{:S(2)}, u32[]{:S(2)}) %collective-permute-start.7) | collective-permute-done | bytes 6688 | tf_op jit(solution)/shard_map/ppermute | solution.py:428
  53.5 0.0 copy-start.2
  53.5 1.0 %shard_map.94 = bf16[195,384]{1,0:T(8,128)(2,1)} custom-call(f32[1,384]{1,0:T(1,128)S(1)} %reshape.13.gain_ref, f32[208,384]{1,0:T(8,128)S(1)} %shard_map.92.attended_ref, bf16[208,384]{1,0:T(8,128)(2,1)S(1)} %get-tuple-element.39.fast_ref, f32[8,208]{1,0:T(8,128)S(1)} %get-tuple-element.40.refs_0_, f32[8,208]{1,0:T(8,128)S(1)} %collective-permute-done.7.refs_1_), custom_call_target="tpu_custom_call" | custom-call | tf_op jit(solution)/shard_map/pallas_call | solution.py:430
  54.5 2.8 %all-to-all-done.2.rows_ref = bf16[16,32,128]{2,1,0:T(8,128)(2,1)S(1)} async-done(((bf16[16,32,128]{2,1,0:T(8,128)(2,1)}), bf16[16,32,128]{2,1,0:T(8,128)(2,1)S(1)}, u32[]{:S(2)}, u32[]{:S(2)}) %all-to-all-start.2) | async-done | bytes 131104 | tf_op jit(solution)/shard_map/all_to_all | solution.py:407
  57.3 0.0 copy-done.2
  57.3 0.8 %shard_map.95 = f32[3,3,32,128]{3,2,1,0:T(8,128)} custom-call(f32[3,3,32,128]{3,2,1,0:T(8,128)S(1)} %copy-done.2, bf16[16,32,128]{2,1,0:T(8,128)(2,1)S(1)} %all-to-all-done.2.rows_ref), custom_call_target="tpu_custom_call" | custom-call | flops 1000000 | bytes 1048576 | tf_op jit(solution)/shard_map/pallas_call | solution.py:410
  (1 shorter events, 0.0 us)
Async XLA Ops:
  0.6 0.9 %copy-start.1 = (f32[3,3,32,128]{3,2,1,0:T(8,128)S(1)}, f32[3,3,32,128]{3,2,1,0:T(8,128)}, u32[]{:S(2)}) copy-start(f32[3,3,32,128]{3,2,1,0:T(8,128)} %w_ref.3) | copy-start | bytes 442372
  2.3 8.2 %copy-start = (bf16[195,384]{1,0:T(8,128)(2,1)S(1)}, bf16[195,384]{1,0:T(8,128)(2,1)}, u32[]{:S(2)}) copy-start(bf16[195,384]{1,0:T(8,128)(2,1)} %q_ref.2) | copy-start | bytes 449284
  2.3 8.2 %copy-start.3 = (bf16[195,384]{1,0:T(8,128)(2,1)S(1)}, bf16[195,384]{1,0:T(8,128)(2,1)}, u32[]{:S(2)}) copy-start(bf16[195,384]{1,0:T(8,128)(2,1)} %k_ref.1) | copy-start | bytes 449284
  2.3 8.2 %copy-start.4 = (bf16[195,384]{1,0:T(8,128)(2,1)S(1)}, bf16[195,384]{1,0:T(8,128)(2,1)}, u32[]{:S(2)}) copy-start(bf16[195,384]{1,0:T(8,128)(2,1)} %v_ref.1) | copy-start | bytes 449284
  2.3 19.8 %all-to-all-start = ((bf16[16,3,32,128]{3,2,1,0:T(8,128)(2,1)}), bf16[16,3,32,128]{3,2,1,0:T(8,128)(2,1)S(1)}, u32[]{:S(2)}, u32[]{:S(2)}) async-start(bf16[16,3,32,128]{3,2,1,0:T(8,128)(2,1)} %shard_map.86.after), calls=%async_computation | async-start | bytes 786432 | tf_op jit(solution)/shard_map/all_to_all | solution.py:356
  9.8 0.7 %copy-start.5 = (f32[195,3]{0,1:T(4,128)S(1)}, f32[195,3]{0,1:T(4,128)}, u32[]{:S(2)}) copy-start(f32[195,3]{0,1:T(4,128)} %param.10) | copy-start | bytes 7024
  11.1 8.9 %collective-permute-start.1 = (bf16[195,384]{1,0:T(8,128)(2,1)S(1)}, bf16[195,384]{1,0:T(8,128)(2,1)S(1)}, u32[]{:S(2)}, u32[]{:S(2)}) collective-permute-start(bf16[195,384]{1,0:T(8,128)(2,1)S(1)} %get-tuple-element.25), channel_id=1, source_target_pairs={{2,4},{4,2},{6,0},{3,5},{5,3},{7,1},{10,12},{12,10},{14,8},{11,13}... | collective-permute-start | bytes 449288 | tf_op jit(solution)/shard_map/ppermute | solution.py:361
  12.4 7.6 %collective-permute-start.2 = (bf16[195,384]{1,0:T(8,128)(2,1)S(1)}, bf16[195,384]{1,0:T(8,128)(2,1)S(1)}, u32[]{:S(2)}, u32[]{:S(2)}) collective-permute-start(bf16[195,384]{1,0:T(8,128)(2,1)S(1)} %get-tuple-element.26), channel_id=1, source_target_pairs={{0,2},{2,0},{6,4},{1,3},{3,1},{7,5},{8,10},{10,8},{14,12},{9,11},{... | collective-permute-start | bytes 449288 | tf_op jit(solution)/shard_map/ppermute | solution.py:361
  17.0 8.2 %collective-permute-start = (bf16[195,384]{1,0:T(8,128)(2,1)S(1)}, bf16[195,384]{1,0:T(8,128)(2,1)S(1)}, u32[]{:S(2)}, u32[]{:S(2)}) collective-permute-start(bf16[195,384]{1,0:T(8,128)(2,1)S(1)} %get-tuple-element.23), channel_id=1, source_target_pairs={{0,4},{4,0},{6,2},{1,5},{5,1},{7,3},{8,12},{12,8},{14,10},{9,13},{... | collective-permute-start | bytes 449288 | tf_op jit(solution)/shard_map/ppermute | solution.py:361
  26.0 15.3 %collective-permute-start.3 = (bf16[512,128]{1,0:T(8,128)(2,1)S(1)}, bf16[512,128]{1,0:T(8,128)(2,1)S(1)}, u32[]{:S(2)}, u32[]{:S(2)}) collective-permute-start(bf16[512,128]{1,0:T(8,128)(2,1)S(1)} %get-tuple-element.33), channel_id=1, source_target_pairs={{2,26},{8,16},{10,18},{12,20},{16,8},{18,10},{20,12},{24,0},{28,4}... | collective-permute-start | bytes 393224 | tf_op jit(solution)/shard_map/ppermute | solution.py:388
  27.3 14.0 %collective-permute-start.4 = (bf16[512,128]{1,0:T(8,128)(2,1)S(1)}, bf16[512,128]{1,0:T(8,128)(2,1)S(1)}, u32[]{:S(2)}, u32[]{:S(2)}) collective-permute-start(bf16[512,128]{1,0:T(8,128)(2,1)S(1)} %get-tuple-element.34), channel_id=1, source_target_pairs={{0,16},{2,18},{4,20},{10,26},{16,0},{20,4},{24,8},{26,10},{28,12},... | collective-permute-start | bytes 393224 | tf_op jit(solution)/shard_map/ppermute | solution.py:388
  32.4 8.8 %collective-permute-start.5 = (bf16[512,128]{1,0:T(8,128)(2,1)S(1)}, bf16[512,128]{1,0:T(8,128)(2,1)S(1)}, u32[]{:S(2)}, u32[]{:S(2)}) collective-permute-start(bf16[512,128]{1,0:T(8,128)(2,1)S(1)} %get-tuple-element.35), channel_id=1, source_target_pairs={{0,8},{2,10},{4,12},{8,0},{12,4},{18,26},{24,16},{26,18},{28,20},{... | collective-permute-start | bytes 393224 | tf_op jit(solution)/shard_map/ppermute | solution.py:388
  35.5 9.2 %all-to-all-start.1 = ((bf16[4,208,128]{2,1,0:T(8,128)(2,1)}), bf16[4,208,128]{2,1,0:T(8,128)(2,1)S(1)}, u32[]{:S(2)}, u32[]{:S(2)}) async-start(bf16[4,208,128]{2,1,0:T(8,128)(2,1)} %shard_map.90), calls=%async_computation.1 | async-start | bytes 425984 | tf_op jit(solution)/shard_map/all_to_all | solution.py:398
  38.9 12.5 %collective-permute-start.6 = (bf16[208,768]{1,0:T(8,128)(2,1)S(1)}, bf16[208,768]{1,0:T(8,128)(2,1)S(1)}, u32[]{:S(2)}, u32[]{:S(2)}) collective-permute-start(bf16[208,768]{1,0:T(8,128)(2,1)S(1)} %get-tuple-element.37.own_ref), channel_id=1, source_target_pairs={{0,2},{2,4},{4,6},{6,8},{8,10},{10,12},{12,14},{14,16},{16,18},{18... | collective-permute-start | bytes 958472 | tf_op jit(solution)/shard_map/ppermute | solution.py:401
  44.7 12.6 %all-to-all-start.2 = ((bf16[16,32,128]{2,1,0:T(8,128)(2,1)}), bf16[16,32,128]{2,1,0:T(8,128)(2,1)S(1)}, u32[]{:S(2)}, u32[]{:S(2)}) async-start(bf16[16,32,128]{2,1,0:T(8,128)(2,1)} %bitcast.2), calls=%async_computation.2 | async-start | bytes 262144 | tf_op jit(solution)/shard_map/all_to_all | solution.py:407
  49.4 2.0 %copy-start.6 = (f32[384]{0:T(512)S(1)}, f32[384]{0:T(512)}, u32[]{:S(2)}) copy-start(f32[384]{0:T(512)} %param.13) | copy-start | bytes 4612
  49.8 3.7 %collective-permute-start.7 = (f32[8,208]{1,0:T(8,128)S(1)}, f32[8,208]{1,0:T(8,128)S(1)}, u32[]{:S(2)}, u32[]{:S(2)}) collective-permute-start(f32[8,208]{1,0:T(8,128)S(1)} %get-tuple-element.40.refs_0_), channel_id=1, source_target_pairs={{0,1},{1,0},{2,3},{3,2},{4,5},{5,4},{6,7},{7,6},{8,9},{9,8},{10,11... | collective-permute-start | bytes 19976 | tf_op jit(solution)/shard_map/ppermute | solution.py:428
  53.5 3.8 %copy-start.2 = (f32[3,3,32,128]{3,2,1,0:T(8,128)S(1)}, f32[3,3,32,128]{3,2,1,0:T(8,128)}, u32[]{:S(2)}) copy-start(f32[3,3,32,128]{3,2,1,0:T(8,128)} %w_ref.3) | copy-start | bytes 442372

commit v11 on v8

--- a/solution.py
+++ b/solution.py
@@ -2,11 +2,10 @@
 
 import jax
 import jax.numpy as jnp
-import numpy as np
 from jax import lax
 from jax.experimental import pallas as pl
 from jax.experimental.pallas import tpu as pltpu
-from jax.sharding import Mesh, PartitionSpec as P
+from jax.sharding import PartitionSpec as P
 
 HD = 128
 NS_STEPS = 5
@@ -53,8 +52,19 @@
     return h & 1
 
 
+GROUP = 4
+
+
 def position():
-    return lax.axis_index("z"), lax.axis_index("grp")
+    return lax.axis_index("ctx") // GROUP, lax.axis_index("ctx") % GROUP
+
+
+def index_of(z, j, slots):
+    return (slots - 1 - z) * GROUP + j
+
+
+def listed(slots):
+    return [z * GROUP + j for z in reversed(range(slots)) for j in range(GROUP)]
 
 
 def sigmoid(x):
@@ -67,7 +77,7 @@
         for m in range(3):
             low = w_ref[m, min(j, heads - 1)].astype(bf16)
             for z in range(slots):
-                w_out[j * slots + z, m] = low
+                w_out[index_of(z, j, slots), m] = low
 
 
 def prep_body(
@@ -261,7 +271,7 @@
     for m in range(3):
         for h in range(heads):
             weights = w_ref[m, h]
-            summed = weights + rows_ref[h * slots + (m + first_owner(h)) % slots].astype(f32)
+            summed = weights + rows_ref[index_of((m + first_owner(h)) % slots, h, slots)].astype(f32)
             old = jnp.sqrt(jnp.sum(weights * weights, axis=1, keepdims=True))
             new = lax.rsqrt(jnp.sum(summed * summed, axis=1, keepdims=True) + epsilon)
             out[m, h] = summed * (old * new)
@@ -313,7 +323,8 @@
     tokens = queries.shape[0]
     heads = queries.shape[1] // HD
     rows_local = fast_weights.shape[2]
-    nz, group, nh = lax.axis_size("z"), lax.axis_size("grp"), lax.axis_size("head")
+    group, nh = GROUP, lax.axis_size("head")
+    nz = lax.axis_size("ctx") // group
     count = nz * group
     hidden = count * rows_local
     padded = -(-tokens // 16) * 16
@@ -340,12 +351,12 @@
     )(low, frame_update.reshape(1, 1), rates.T, keys, values, queries)
     kv_own, *token_slots = prepared
 
-    weights = lax.all_to_all(low, ("grp", "z"), 0, 0, tiled=True)
+    weights = lax.all_to_all(low, "ctx", 0, 0, tiled=True, axis_index_groups=[listed(nz)])
     if rows_local % 16:
         weights = weights.transpose(1, 0, 2, 3).reshape(3, hidden, HD)
     for d in served(group)[1:]:
-        pairs = [(s, s ^ d) for s in range(group) if s ^ d < heads]
-        token_slots[d] = lax.ppermute(token_slots[d], "grp", pairs)
+        pairs = [(s, s ^ d) for s in range(count) if (s ^ d) % group < heads]
+        token_slots[d] = lax.ppermute(token_slots[d], "ctx", pairs)
 
     last = group // 2
     early_slots = [d for d in served(group) if d != last]
@@ -372,7 +383,7 @@
                 for j in range(heads)
                 if ((z ^ d) - first_owner(j)) % nz < 3
             ]
-        partials[d] = lax.ppermute(partials[d], ("z", "grp"), pairs)
+        partials[d] = lax.ppermute(partials[d], "ctx", pairs)
 
     fast_slots = call(
         functools.partial(late_apply_body, early_slots, last),
@@ -382,17 +393,21 @@
         moved=1024,
     )(token_slots[last], weights, early_fast)
     kv_own, partials[0], fast_slots = lax.optimization_barrier((kv_own, partials[0], fast_slots))
-    fast_slots = lax.all_to_all(fast_slots, "grp", 0, 0, tiled=True)
+    fast_slots = lax.all_to_all(
+        fast_slots, "ctx", 0, 0, tiled=True,
+        axis_index_groups=[[z * group + j for j in range(group)] for z in range(nz)],
+    )
 
     ring = [(i, i + 1) for i in range(count - 1)]
-    kv_back = lax.ppermute(kv_own, ("z", "grp"), ring)
+    kv_back = lax.ppermute(kv_own, "ctx", ring)
 
     ortho = call(functools.partial(ortho_body, heads, nz), sds((hidden, HD), bf16), flops=1e9)(
         *(partials[d] for d in served(nz))
     )
     queries, ortho = lax.optimization_barrier((queries, ortho))
     rows = lax.all_to_all(
-        ortho.reshape(count, rows_local, HD), ("grp", "z"), 0, 0, tiled=True
+        ortho.reshape(count, rows_local, HD), "ctx", 0, 0, tiled=True,
+        axis_index_groups=[listed(nz)],
     )
     new_weights = call(
         functools.partial(finish_body, nz, group), sds(fast_weights.shape, f32), flops=1e6
@@ -427,26 +442,19 @@
 
 
 def solution(mesh):
-    group = 4
-    nh = mesh.shape["head"]
-    inner = Mesh(
-        np.asarray(mesh.devices).reshape(mesh.shape["ctx"] // group, group, nh),
-        ("z", "grp", "head"),
-    )
-    ctx = ("z", "grp")
     placed = (
-        P(ctx, "head"),
-        P(ctx, "head"),
-        P(ctx, "head"),
-        P(ctx, "head"),
-        P(ctx),
-        P(None, "head", ctx, None),
+        P("ctx", "head"),
+        P("ctx", "head"),
+        P("ctx", "head"),
+        P("ctx", "head"),
+        P("ctx"),
+        P(None, "head", "ctx", None),
         P("head"),
     )
     return jax.shard_map(
         on_device,
-        mesh=inner,
+        mesh=mesh,
         in_specs=placed,
-        out_specs=(P(ctx, "head"), P(None, "head", ctx, None)),
+        out_specs=(P("ctx", "head"), P(None, "head", "ctx", None)),
         check_vma=False,
     )

time: 58.2 us -> 58 us (level)
  waiting for transfers between devices: 6.89 us -> 4.41 us
  starting transfers between devices: 35.8 us -> 38.1 us
    all_to_all x3, waiting for transfers between devices: 4.1 us -> 0.01 us  [the longest x1 0.01 us: on_device(): lax.all_to_all(low, 'ctx', 0, 0, tiled=True, axis_index_groups=[listed(nz)])]
    all_to_all x3, starting transfers between devices: 15.5 us -> 18.9 us  [the longest x1 8.6 us: on_device(): lax.all_to_all(low, 'ctx', 0, 0, tiled=True, axis_index_groups=[listed(nz)])]
    ppermute x7, waiting for transfers between devices: 2.01 us -> 3.63 us  [the longest x3 3.62 us: on_device(): token_slots[d] = lax.ppermute(token_slots[d], 'ctx', pairs)]
    ppermute x7, starting transfers between devices: 18.8 us -> 17.7 us  [the longest x3 7.93 us: on_device(): partials[d] = lax.ppermute(partials[d], 'ctx', pairs)]
  transfers between devices with their start and end apart: 11 -> 11, of which waited for: 5 -> 3; matrix products, arithmetic and copies ran while one was open for 0% -> 0% of each run, Pallas kernels for 18% -> 18%
where the time goes in v11:
time: 58 us; the launch traced here: 57.4 us
  starting transfers between devices  38.1 us (66%)
  Pallas kernels  12.5 us (22%)
  waiting for transfers between devices  4.41 us (8%)
  between operations  1.46 us (3%)
  local copies, waits for them, and re-layouts  0.93 us (2%)
    all_to_all x1, starting transfers between devices, on_device(): lax.all_to_all(low, 'ctx', 0, 0, tiled=True, axis_index_groups=[listed(nz)])  8.6 us
    ppermute x3, starting transfers between devices, on_device(): partials[d] = lax.ppermute(partials[d], 'ctx', pairs)  7.93 us
    ppermute x3, starting transfers between devices, on_device(): token_slots[d] = lax.ppermute(token_slots[d], 'ctx', pairs)  7.34 us
    all_to_all x1, starting transfers between devices, on_device(): lax.all_to_all(ortho.reshape(count, rows_local, HD), 'ctx', 0, 0, tiled=T...  6.89 us
    ppermute x3, waiting for transfers between devices, on_device(): token_slots[d] = lax.ppermute(token_slots[d], 'ctx', pairs)  3.62 us
    pallas_call x1, Pallas kernels, on_device(): call(functools.partial(ortho_body, heads, nz), sds((hidden, HD), bf16), f...  3.44 us
    all_to_all x1, starting transfers between devices, on_device(): lax.all_to_all(fast_slots, 'ctx', 0, 0, tiled=True, axis_index_groups=[[z...  3.37 us
    ppermute x1, starting transfers between devices, on_device(): kv_back = lax.ppermute(kv_own, 'ctx', ring)  2.38 us
  transfers between devices with their start and end apart: 11, of which 3 were waited for; matrix products, arithmetic and copies ran while one was open for 0% of the time, Pallas kernels for 18%

profile of v11, /device:TPU:0, one launch (start us, length us, event | category | flops | bytes accessed | tf_op | source)
XLA Modules:
  0.0 57.4 jit_solution(17587275763659240481)
XLA Ops:
  0.6 0.0 copy-start.1
  0.6 0.9 %copy-done.1 = f32[3,3,32,128]{3,2,1,0:T(8,128)S(1)} copy-done((f32[3,3,32,128]{3,2,1,0:T(8,128)S(1)}, f32[3,3,32,128]{3,2,1,0:T(8,128)}, u32[]{:S(2)}) %copy-start.1) | copy-done | bytes 147480
  1.5 0.8 %shard_map.86.after = bf16[16,3,32,128]{3,2,1,0:T(8,128)(2,1)} custom-call(f32[3,3,32,128]{3,2,1,0:T(8,128)S(1)} %copy-done.1), custom_call_target="tpu_custom_call" | custom-call | flops 1000000 | bytes 1048576 | tf_op jit(solution)/shard_map/pallas_call | solution.py:337
  2.3 0.0 copy-start
  2.3 0.0 copy-start.3
  2.3 0.0 copy-start.4
  2.3 8.6 %all-to-all-start = ((bf16[16,3,32,128]{3,2,1,0:T(8,128)(2,1)}), bf16[16,3,32,128]{3,2,1,0:T(8,128)(2,1)S(1)}, u32[]{:S(2)}, u32[]{:S(2)}) async-start(bf16[16,3,32,128]{3,2,1,0:T(8,128)(2,1)} %shard_map.86.after), calls=%async_computation | async-start | bytes 786432 | tf_op jit(solution)/shard_map/all_to_all | solution.py:354
  10.9 0.0 copy-start.5
  11.6 0.0 copy-done
  11.6 0.0 copy-done.3
  11.6 0.0 copy-done.4
  11.6 0.0 copy-done.5
  11.6 0.6 %shard_map.87 = (bf16[208,768]{1,0:T(8,128)(2,1)S(1)}, bf16[195,384]{1,0:T(8,128)(2,1)S(1)}, bf16[195,384]{1,0:T(8,128)(2,1)S(1)}, bf16[195,384]{1,0:T(8,128)(2,1)S(1)}, bf16[195,384]{1,0:T(8,128)(2,1)S(1)}) custom-call(bf16[16,3,32,128]{3,2,1,0:T(8,128)(2,1)} %shard_map.86.after, s32[1,1]{1,0:T(1,128)} %bitcast.3.update, f32[3,195]{1,0:T(4,128)S(1)} %bitcast.4, ...), custom_call_target="tpu_custom_call" | custom-call | tf_op jit(solution)/shard_map/pallas_call | solution.py:340
  12.2 1.3 %collective-permute-start.1 = (bf16[195,384]{1,0:T(8,128)(2,1)S(1)}, bf16[195,384]{1,0:T(8,128)(2,1)S(1)}, u32[]{:S(2)}, u32[]{:S(2)}) collective-permute-start(bf16[195,384]{1,0:T(8,128)(2,1)S(1)} %get-tuple-element.25), channel_id=1, source_target_pairs={{2,4},{4,2},{6,0},{10,12},{12,10},{14,8},{18,20},{20,18},{22,16},{... | collective-permute-start | bytes 449288 | tf_op jit(solution)/shard_map/ppermute | solution.py:359
  13.5 4.1 %collective-permute-start.2 = (bf16[195,384]{1,0:T(8,128)(2,1)S(1)}, bf16[195,384]{1,0:T(8,128)(2,1)S(1)}, u32[]{:S(2)}, u32[]{:S(2)}) collective-permute-start(bf16[195,384]{1,0:T(8,128)(2,1)S(1)} %get-tuple-element.26), channel_id=1, source_target_pairs={{0,2},{2,0},{6,4},{8,10},{10,8},{14,12},{16,18},{18,16},{22,20},{2... | collective-permute-start | bytes 449288 | tf_op jit(solution)/shard_map/ppermute | solution.py:359
  17.7 1.9 %collective-permute-start = (bf16[195,384]{1,0:T(8,128)(2,1)S(1)}, bf16[195,384]{1,0:T(8,128)(2,1)S(1)}, u32[]{:S(2)}, u32[]{:S(2)}) collective-permute-start(bf16[195,384]{1,0:T(8,128)(2,1)S(1)} %get-tuple-element.23), channel_id=1, source_target_pairs={{0,4},{4,0},{6,2},{8,12},{12,8},{14,10},{16,20},{20,16},{22,18},{2... | collective-permute-start | bytes 449288 | tf_op jit(solution)/shard_map/ppermute | solution.py:359
  19.6 2.1 %collective-permute-done.1.refs_1_ = bf16[195,384]{1,0:T(8,128)(2,1)S(1)} collective-permute-done((bf16[195,384]{1,0:T(8,128)(2,1)S(1)}, bf16[195,384]{1,0:T(8,128)(2,1)S(1)}, u32[]{:S(2)}, u32[]{:S(2)}) %collective-permute-start.1) | collective-permute-done | bytes 149792 | tf_op jit(solution)/shard_map/ppermute | solution.py:359
  21.7 0.0 collective-permute-done.2.refs_2_
  21.7 0.0 all-to-all-done.refs_3_.w_ref
  21.7 2.2 %shard_map.88 = (f32[3,512,128]{2,1,0:T(8,128)S(1)}, bf16[3,208,128]{2,1,0:T(8,128)(2,1)S(1)}) custom-call(bf16[195,384]{1,0:T(8,128)(2,1)S(1)} %get-tuple-element.24.refs_0_, bf16[195,384]{1,0:T(8,128)(2,1)S(1)} %collective-permute-done.1.refs_1_, bf16[195,384]{1,0:T(8,128)(2,1)S(1)} %collective-permute-done.2.refs_2_, ...), custom_call_target="tpu_custom_call" | custom-call | flops 1000000000 | bytes 1048576 | tf_op jit(solution)/shard_map/pallas_call | solution.py:363
  23.9 1.5 %collective-permute-done.token_ref = bf16[195,384]{1,0:T(8,128)(2,1)S(1)} collective-permute-done((bf16[195,384]{1,0:T(8,128)(2,1)S(1)}, bf16[195,384]{1,0:T(8,128)(2,1)S(1)}, u32[]{:S(2)}, u32[]{:S(2)}) %collective-permute-start) | collective-permute-done | bytes 149792 | tf_op jit(solution)/shard_map/ppermute | solution.py:359
  25.5 0.8 %shard_map.89 = (bf16[512,128]{1,0:T(8,128)(2,1)S(1)}, bf16[512,128]{1,0:T(8,128)(2,1)S(1)}, bf16[512,128]{1,0:T(8,128)(2,1)S(1)}, bf16[512,128]{1,0:T(8,128)(2,1)S(1)}) custom-call(bf16[195,384]{1,0:T(8,128)(2,1)S(1)} %collective-permute-done.token_ref, bf16[16,3,32,128]{3,2,1,0:T(8,128)(2,1)S(1)} %all-to-all-done.refs_3_.w_ref, ...), custom_call_target="tpu_custom_call" | custom-call | flops 500000000 | bytes 1048576 | tf_op jit(solution)/shard_map/pallas_call | solution.py:370
  26.2 1.3 %collective-permute-start.3 = (bf16[512,128]{1,0:T(8,128)(2,1)S(1)}, bf16[512,128]{1,0:T(8,128)(2,1)S(1)}, u32[]{:S(2)}, u32[]{:S(2)}) collective-permute-start(bf16[512,128]{1,0:T(8,128)(2,1)S(1)} %get-tuple-element.33), channel_id=1, source_target_pairs={{2,26},{8,16},{10,18},{12,20},{16,8},{18,10},{20,12},{24,0},{28,4}... | collective-permute-start | bytes 393224 | tf_op jit(solution)/shard_map/ppermute | solution.py:386
  27.5 4.7 %collective-permute-start.4 = (bf16[512,128]{1,0:T(8,128)(2,1)S(1)}, bf16[512,128]{1,0:T(8,128)(2,1)S(1)}, u32[]{:S(2)}, u32[]{:S(2)}) collective-permute-start(bf16[512,128]{1,0:T(8,128)(2,1)S(1)} %get-tuple-element.34), channel_id=1, source_target_pairs={{0,16},{2,18},{4,20},{10,26},{16,0},{20,4},{24,8},{26,10},{28,12},... | collective-permute-start | bytes 393224 | tf_op jit(solution)/shard_map/ppermute | solution.py:386
  32.3 1.9 %collective-permute-start.5 = (bf16[512,128]{1,0:T(8,128)(2,1)S(1)}, bf16[512,128]{1,0:T(8,128)(2,1)S(1)}, u32[]{:S(2)}, u32[]{:S(2)}) collective-permute-start(bf16[512,128]{1,0:T(8,128)(2,1)S(1)} %get-tuple-element.35), channel_id=1, source_target_pairs={{0,8},{2,10},{4,12},{8,0},{12,4},{18,26},{24,16},{26,18},{28,20},{... | collective-permute-start | bytes 393224 | tf_op jit(solution)/shard_map/ppermute | solution.py:386
  34.2 1.1 %shard_map.90 = bf16[4,208,128]{2,1,0:T(8,128)(2,1)} custom-call(bf16[195,384]{1,0:T(8,128)(2,1)S(1)} %collective-permute-done.token_ref, bf16[16,3,32,128]{3,2,1,0:T(8,128)(2,1)S(1)} %all-to-all-done.refs_3_.w_ref, bf16[3,208,128]{2,1,0:T(8,128)(2,1)S(1)} %get-tuple-element.31.early), custom_call_target="tpu_custom_call" | custom-call | flops 1000 | bytes 1024 | tf_op jit(solution)/shard_map/pallas_call | solution.py:388
  35.3 3.4 %all-to-all-start.1 = ((bf16[4,208,128]{2,1,0:T(8,128)(2,1)}), bf16[4,208,128]{2,1,0:T(8,128)(2,1)S(1)}, u32[]{:S(2)}, u32[]{:S(2)}) async-start(bf16[4,208,128]{2,1,0:T(8,128)(2,1)} %shard_map.90), calls=%async_computation.1 | async-start | bytes 425984 | tf_op jit(solution)/shard_map/all_to_all | solution.py:396
  38.7 2.4 %collective-permute-start.6 = (bf16[208,768]{1,0:T(8,128)(2,1)S(1)}, bf16[208,768]{1,0:T(8,128)(2,1)S(1)}, u32[]{:S(2)}, u32[]{:S(2)}) collective-permute-start(bf16[208,768]{1,0:T(8,128)(2,1)S(1)} %get-tuple-element.37.own_ref), channel_id=1, source_target_pairs={{0,2},{2,4},{4,6},{6,8},{8,10},{10,12},{12,14},{14,16},{16,18},{18... | collective-permute-start | bytes 958472 | tf_op jit(solution)/shard_map/ppermute | solution.py:402
  41.1 0.0 collective-permute-done.3.refs_1_
  41.1 0.0 collective-permute-done.4.refs_2_
  41.1 0.0 collective-permute-done.5.refs_3_
  41.1 3.4 %shard_map.91 = bf16[512,128]{1,0:T(8,128)(2,1)} custom-call(bf16[512,128]{1,0:T(8,128)(2,1)S(1)} %get-tuple-element.32.refs_0_, bf16[512,128]{1,0:T(8,128)(2,1)S(1)} %collective-permute-done.3.refs_1_, bf16[512,128]{1,0:T(8,128)(2,1)S(1)} %collective-permute-done.4.refs_2_, bf16[512,128]{1,0:T(8,128)(2,1)S(1)} %collective-permute-done.5.refs_3_), custom_call_target="tpu_custom_call" | custom-call | flops 1000000000 | bytes 1048576 | tf_op jit(solution)/shard_map/pallas_call | solution.py:404
  44.5 0.0 all-to-all-done.1.slots
  44.5 6.9 %all-to-all-start.2 = ((bf16[16,32,128]{2,1,0:T(8,128)(2,1)}), bf16[16,32,128]{2,1,0:T(8,128)(2,1)S(1)}, u32[]{:S(2)}, u32[]{:S(2)}) async-start(bf16[16,32,128]{2,1,0:T(8,128)(2,1)} %bitcast.2), calls=%async_computation.2 | async-start | bytes 262144 | tf_op jit(solution)/shard_map/all_to_all | solution.py:408
  51.4 0.0 copy-start.6
  51.4 0.4 shard_map.93
  51.9 1.6 %collective-permute-start.7 = (f32[8,208]{1,0:T(8,128)S(1)}, f32[8,208]{1,0:T(8,128)S(1)}, u32[]{:S(2)}, u32[]{:S(2)}) collective-permute-start(f32[8,208]{1,0:T(8,128)S(1)} %get-tuple-element.40.refs_0_), channel_id=1, source_target_pairs={{0,1},{1,0},{2,3},{3,2},{4,5},{5,4},{6,7},{7,6},{8,9},{9,8},{10,11... | collective-permute-start | bytes 19976 | tf_op jit(solution)/shard_map/ppermute | solution.py:430
  53.4 0.0 copy-done.6
  53.4 0.0 collective-permute-done.6.back_ref
  53.5 1.3 %shard_map.92.attended_ref = f32[208,384]{1,0:T(8,128)S(1)} custom-call(bf16[195,384]{1,0:T(8,128)(2,1)S(1)} %copy-done, bf16[208,768]{1,0:T(8,128)(2,1)S(1)} %get-tuple-element.37.own_ref, bf16[208,768]{1,0:T(8,128)(2,1)S(1)} %collective-permute-done.6.back_ref), custom_call_target="tpu_custom_call" | custom-call | tf_op jit(solution)/shard_map/pallas_call | solution.py:416
  54.8 0.8 %collective-permute-done.7.refs_1_ = f32[8,208]{1,0:T(8,128)S(1)} collective-permute-done((f32[8,208]{1,0:T(8,128)S(1)}, f32[8,208]{1,0:T(8,128)S(1)}, u32[]{:S(2)}, u32[]{:S(2)}) %collective-permute-start.7) | collective-permute-done | bytes 6688 | tf_op jit(solution)/shard_map/ppermute | solution.py:430
  55.6 0.0 copy-start.2
  55.6 1.0 %shard_map.94 = bf16[195,384]{1,0:T(8,128)(2,1)} custom-call(f32[1,384]{1,0:T(1,128)S(1)} %reshape.13.gain_ref, f32[208,384]{1,0:T(8,128)S(1)} %shard_map.92.attended_ref, bf16[208,384]{1,0:T(8,128)(2,1)S(1)} %get-tuple-element.39.fast_ref, f32[8,208]{1,0:T(8,128)S(1)} %get-tuple-element.40.refs_0_, f32[8,208]{1,0:T(8,128)S(1)} %collective-permute-done.7.refs_1_), custom_call_target="tpu_custom_call" | custom-call | tf_op jit(solution)/shard_map/pallas_call | solution.py:432
  56.6 0.0 all-to-all-done.2.rows_ref
  56.6 0.0 copy-done.2
  56.6 0.8 %shard_map.95 = f32[3,3,32,128]{3,2,1,0:T(8,128)} custom-call(f32[3,3,32,128]{3,2,1,0:T(8,128)S(1)} %copy-done.2, bf16[16,32,128]{2,1,0:T(8,128)(2,1)S(1)} %all-to-all-done.2.rows_ref), custom_call_target="tpu_custom_call" | custom-call | flops 1000000 | bytes 1048576 | tf_op jit(solution)/shard_map/pallas_call | solution.py:412
  (1 shorter events, 0.0 us)
Async XLA Ops:
  0.6 0.9 %copy-start.1 = (f32[3,3,32,128]{3,2,1,0:T(8,128)S(1)}, f32[3,3,32,128]{3,2,1,0:T(8,128)}, u32[]{:S(2)}) copy-start(f32[3,3,32,128]{3,2,1,0:T(8,128)} %w_ref.3) | copy-start | bytes 442372
  2.3 9.3 %copy-start = (bf16[195,384]{1,0:T(8,128)(2,1)S(1)}, bf16[195,384]{1,0:T(8,128)(2,1)}, u32[]{:S(2)}) copy-start(bf16[195,384]{1,0:T(8,128)(2,1)} %q_ref.2) | copy-start | bytes 449284
  2.3 9.3 %copy-start.3 = (bf16[195,384]{1,0:T(8,128)(2,1)S(1)}, bf16[195,384]{1,0:T(8,128)(2,1)}, u32[]{:S(2)}) copy-start(bf16[195,384]{1,0:T(8,128)(2,1)} %k_ref.1) | copy-start | bytes 449284
  2.3 9.3 %copy-start.4 = (bf16[195,384]{1,0:T(8,128)(2,1)S(1)}, bf16[195,384]{1,0:T(8,128)(2,1)}, u32[]{:S(2)}) copy-start(bf16[195,384]{1,0:T(8,128)(2,1)} %v_ref.1) | copy-start | bytes 449284
  2.3 19.3 %all-to-all-start = ((bf16[16,3,32,128]{3,2,1,0:T(8,128)(2,1)}), bf16[16,3,32,128]{3,2,1,0:T(8,128)(2,1)S(1)}, u32[]{:S(2)}, u32[]{:S(2)}) async-start(bf16[16,3,32,128]{3,2,1,0:T(8,128)(2,1)} %shard_map.86.after), calls=%async_computation | async-start | bytes 786432 | tf_op jit(solution)/shard_map/all_to_all | solution.py:354
  10.9 0.7 %copy-start.5 = (f32[195,3]{0,1:T(4,128)S(1)}, f32[195,3]{0,1:T(4,128)}, u32[]{:S(2)}) copy-start(f32[195,3]{0,1:T(4,128)} %param.10) | copy-start | bytes 7024
  12.2 9.4 %collective-permute-start.1 = (bf16[195,384]{1,0:T(8,128)(2,1)S(1)}, bf16[195,384]{1,0:T(8,128)(2,1)S(1)}, u32[]{:S(2)}, u32[]{:S(2)}) collective-permute-start(bf16[195,384]{1,0:T(8,128)(2,1)S(1)} %get-tuple-element.25), channel_id=1, source_target_pairs={{2,4},{4,2},{6,0},{10,12},{12,10},{14,8},{18,20},{20,18},{22,16},{... | collective-permute-start | bytes 449288 | tf_op jit(solution)/shard_map/ppermute | solution.py:359
  13.5 8.1 %collective-permute-start.2 = (bf16[195,384]{1,0:T(8,128)(2,1)S(1)}, bf16[195,384]{1,0:T(8,128)(2,1)S(1)}, u32[]{:S(2)}, u32[]{:S(2)}) collective-permute-start(bf16[195,384]{1,0:T(8,128)(2,1)S(1)} %get-tuple-element.26), channel_id=1, source_target_pairs={{0,2},{2,0},{6,4},{8,10},{10,8},{14,12},{16,18},{18,16},{22,20},{2... | collective-permute-start | bytes 449288 | tf_op jit(solution)/shard_map/ppermute | solution.py:359
  17.7 7.8 %collective-permute-start = (bf16[195,384]{1,0:T(8,128)(2,1)S(1)}, bf16[195,384]{1,0:T(8,128)(2,1)S(1)}, u32[]{:S(2)}, u32[]{:S(2)}) collective-permute-start(bf16[195,384]{1,0:T(8,128)(2,1)S(1)} %get-tuple-element.23), channel_id=1, source_target_pairs={{0,4},{4,0},{6,2},{8,12},{12,8},{14,10},{16,20},{20,16},{22,18},{2... | collective-permute-start | bytes 449288 | tf_op jit(solution)/shard_map/ppermute | solution.py:359
  26.2 14.8 %collective-permute-start.3 = (bf16[512,128]{1,0:T(8,128)(2,1)S(1)}, bf16[512,128]{1,0:T(8,128)(2,1)S(1)}, u32[]{:S(2)}, u32[]{:S(2)}) collective-permute-start(bf16[512,128]{1,0:T(8,128)(2,1)S(1)} %get-tuple-element.33), channel_id=1, source_target_pairs={{2,26},{8,16},{10,18},{12,20},{16,8},{18,10},{20,12},{24,0},{28,4}... | collective-permute-start | bytes 393224 | tf_op jit(solution)/shard_map/ppermute | solution.py:386
  27.5 13.6 %collective-permute-start.4 = (bf16[512,128]{1,0:T(8,128)(2,1)S(1)}, bf16[512,128]{1,0:T(8,128)(2,1)S(1)}, u32[]{:S(2)}, u32[]{:S(2)}) collective-permute-start(bf16[512,128]{1,0:T(8,128)(2,1)S(1)} %get-tuple-element.34), channel_id=1, source_target_pairs={{0,16},{2,18},{4,20},{10,26},{16,0},{20,4},{24,8},{26,10},{28,12},... | collective-permute-start | bytes 393224 | tf_op jit(solution)/shard_map/ppermute | solution.py:386
  32.3 8.8 %collective-permute-start.5 = (bf16[512,128]{1,0:T(8,128)(2,1)S(1)}, bf16[512,128]{1,0:T(8,128)(2,1)S(1)}, u32[]{:S(2)}, u32[]{:S(2)}) collective-permute-start(bf16[512,128]{1,0:T(8,128)(2,1)S(1)} %get-tuple-element.35), channel_id=1, source_target_pairs={{0,8},{2,10},{4,12},{8,0},{12,4},{18,26},{24,16},{26,18},{28,20},{... | collective-permute-start | bytes 393224 | tf_op jit(solution)/shard_map/ppermute | solution.py:386
  35.3 9.2 %all-to-all-start.1 = ((bf16[4,208,128]{2,1,0:T(8,128)(2,1)}), bf16[4,208,128]{2,1,0:T(8,128)(2,1)S(1)}, u32[]{:S(2)}, u32[]{:S(2)}) async-start(bf16[4,208,128]{2,1,0:T(8,128)(2,1)} %shard_map.90), calls=%async_computation.1 | async-start | bytes 425984 | tf_op jit(solution)/shard_map/all_to_all | solution.py:396
  38.7 14.8 %collective-permute-start.6 = (bf16[208,768]{1,0:T(8,128)(2,1)S(1)}, bf16[208,768]{1,0:T(8,128)(2,1)S(1)}, u32[]{:S(2)}, u32[]{:S(2)}) collective-permute-start(bf16[208,768]{1,0:T(8,128)(2,1)S(1)} %get-tuple-element.37.own_ref), channel_id=1, source_target_pairs={{0,2},{2,4},{4,6},{6,8},{8,10},{10,12},{12,14},{14,16},{16,18},{18... | collective-permute-start | bytes 958472 | tf_op jit(solution)/shard_map/ppermute | solution.py:402
  44.5 12.0 %all-to-all-start.2 = ((bf16[16,32,128]{2,1,0:T(8,128)(2,1)}), bf16[16,32,128]{2,1,0:T(8,128)(2,1)S(1)}, u32[]{:S(2)}, u32[]{:S(2)}) async-start(bf16[16,32,128]{2,1,0:T(8,128)(2,1)} %bitcast.2), calls=%async_computation.2 | async-start | bytes 262144 | tf_op jit(solution)/shard_map/all_to_all | solution.py:408
  51.4 2.0 %copy-start.6 = (f32[384]{0:T(512)S(1)}, f32[384]{0:T(512)}, u32[]{:S(2)}) copy-start(f32[384]{0:T(512)} %param.13) | copy-start | bytes 4612
  51.9 3.7 %collective-permute-start.7 = (f32[8,208]{1,0:T(8,128)S(1)}, f32[8,208]{1,0:T(8,128)S(1)}, u32[]{:S(2)}, u32[]{:S(2)}) collective-permute-start(f32[8,208]{1,0:T(8,128)S(1)} %get-tuple-element.40.refs_0_), channel_id=1, source_target_pairs={{0,1},{1,0},{2,3},{3,2},{4,5},{5,4},{6,7},{7,6},{8,9},{9,8},{10,11... | collective-permute-start | bytes 19976 | tf_op jit(solution)/shard_map/ppermute | solution.py:430
  55.6 1.0 %copy-start.2 = (f32[3,3,32,128]{3,2,1,0:T(8,128)S(1)}, f32[3,3,32,128]{3,2,1,0:T(8,128)}, u32[]{:S(2)}) copy-start(f32[3,3,32,128]{3,2,1,0:T(8,128)} %w_ref.3) | copy-start | bytes 442372

commit v12 on v11

--- a/solution.py
+++ b/solution.py
@@ -60,11 +60,11 @@
 
 
 def index_of(z, j, slots):
-    return (slots - 1 - z) * GROUP + j
+    return (slots // 2 - 1 - z) % slots * GROUP + j
 
 
 def listed(slots):
-    return [z * GROUP + j for z in reversed(range(slots)) for j in range(GROUP)]
+    return [(slots // 2 - 1 - i) % slots * GROUP + j for i in range(slots) for j in range(GROUP)]
 
 
 def sigmoid(x):

time: 58 us -> 56.7 us (0.978)
  starting transfers between devices: 38.1 us -> 36 us
  waiting for transfers between devices: 4.41 us -> 5.16 us
    all_to_all x1, starting transfers between devices: 6.89 us -> 5.32 us  [on_device(): lax.all_to_all(ortho.reshape(count, rows_local, HD), 'ctx', 0, 0, tiled=T...]
    all_to_all x1, waiting for transfers between devices: 0.01 us -> 0.65 us  [on_device(): lax.all_to_all(ortho.reshape(count, rows_local, HD), 'ctx', 0, 0, tiled=T...]
    all_to_all x1, starting transfers between devices: 8.6 us -> 7.96 us  [on_device(): lax.all_to_all(low, 'ctx', 0, 0, tiled=True, axis_index_groups=[listed(nz)])]
  transfers between devices with their start and end apart: 11 -> 11, of which waited for: 3 -> 4; matrix products, arithmetic and copies ran while one was open for 0% -> 0% of each run, Pallas kernels for 18% -> 18%
where the time goes in v12:
time: 56.7 us; the launch traced here: 56.1 us
  starting transfers between devices  36 us (63%)
  Pallas kernels  12.5 us (22%)
  waiting for transfers between devices  5.16 us (9%)
  between operations  1.46 us (3%)
  local copies, waits for them, and re-layouts  0.93 us (2%)
    ppermute x3, starting transfers between devices, on_device(): partials[d] = lax.ppermute(partials[d], 'ctx', pairs)  8.08 us
    all_to_all x1, starting transfers between devices, on_device(): lax.all_to_all(low, 'ctx', 0, 0, tiled=True, axis_index_groups=[listed(nz)])  7.96 us
    ppermute x3, starting transfers between devices, on_device(): token_slots[d] = lax.ppermute(token_slots[d], 'ctx', pairs)  7.33 us
    all_to_all x1, starting transfers between devices, on_device(): lax.all_to_all(ortho.reshape(count, rows_local, HD), 'ctx', 0, 0, tiled=T...  5.32 us
    ppermute x3, waiting for transfers between devices, on_device(): token_slots[d] = lax.ppermute(token_slots[d], 'ctx', pairs)  3.72 us
    pallas_call x1, Pallas kernels, on_device(): call(functools.partial(ortho_body, heads, nz), sds((hidden, HD), bf16), f...  3.44 us
    all_to_all x1, starting transfers between devices, on_device(): lax.all_to_all(fast_slots, 'ctx', 0, 0, tiled=True, axis_index_groups=[[z...  3.37 us
    ppermute x1, starting transfers between devices, on_device(): kv_back = lax.ppermute(kv_own, 'ctx', ring)  2.38 us
  transfers between devices with their start and end apart: 11, of which 4 were waited for; matrix products, arithmetic and copies ran while one was open for 0% of the time, Pallas kernels for 18%

profile of v12, /device:TPU:0, one launch (start us, length us, event | category | flops | bytes accessed | tf_op | source)
XLA Modules:
  0.0 56.1 jit_solution(3779046420394889036)
XLA Ops:
  0.6 0.0 copy-start.1
  0.6 0.9 %copy-done.1 = f32[3,3,32,128]{3,2,1,0:T(8,128)S(1)} copy-done((f32[3,3,32,128]{3,2,1,0:T(8,128)S(1)}, f32[3,3,32,128]{3,2,1,0:T(8,128)}, u32[]{:S(2)}) %copy-start.1) | copy-done | bytes 147480
  1.5 0.8 %shard_map.86.after = bf16[16,3,32,128]{3,2,1,0:T(8,128)(2,1)} custom-call(f32[3,3,32,128]{3,2,1,0:T(8,128)S(1)} %copy-done.1), custom_call_target="tpu_custom_call" | custom-call | flops 1000000 | bytes 1048576 | tf_op jit(solution)/shard_map/pallas_call | solution.py:337
  2.3 0.0 copy-start
  2.3 0.0 copy-start.3
  2.3 0.0 copy-start.4
  2.3 8.0 %all-to-all-start = ((bf16[16,3,32,128]{3,2,1,0:T(8,128)(2,1)}), bf16[16,3,32,128]{3,2,1,0:T(8,128)(2,1)S(1)}, u32[]{:S(2)}, u32[]{:S(2)}) async-start(bf16[16,3,32,128]{3,2,1,0:T(8,128)(2,1)} %shard_map.86.after), calls=%async_computation | async-start | bytes 786432 | tf_op jit(solution)/shard_map/all_to_all | solution.py:354
  10.3 0.0 copy-start.5
  11.0 0.0 copy-done
  11.0 0.0 copy-done.3
  11.0 0.0 copy-done.4
  11.0 0.0 copy-done.5
  11.0 0.6 %shard_map.87 = (bf16[208,768]{1,0:T(8,128)(2,1)S(1)}, bf16[195,384]{1,0:T(8,128)(2,1)S(1)}, bf16[195,384]{1,0:T(8,128)(2,1)S(1)}, bf16[195,384]{1,0:T(8,128)(2,1)S(1)}, bf16[195,384]{1,0:T(8,128)(2,1)S(1)}) custom-call(bf16[16,3,32,128]{3,2,1,0:T(8,128)(2,1)} %shard_map.86.after, s32[1,1]{1,0:T(1,128)} %bitcast.3.update, f32[3,195]{1,0:T(4,128)S(1)} %bitcast.4, ...), custom_call_target="tpu_custom_call" | custom-call | tf_op jit(solution)/shard_map/pallas_call | solution.py:340
  11.6 1.3 %collective-permute-start.1 = (bf16[195,384]{1,0:T(8,128)(2,1)S(1)}, bf16[195,384]{1,0:T(8,128)(2,1)S(1)}, u32[]{:S(2)}, u32[]{:S(2)}) collective-permute-start(bf16[195,384]{1,0:T(8,128)(2,1)S(1)} %get-tuple-element.25), channel_id=1, source_target_pairs={{2,4},{4,2},{6,0},{10,12},{12,10},{14,8},{18,20},{20,18},{22,16},{... | collective-permute-start | bytes 449288 | tf_op jit(solution)/shard_map/ppermute | solution.py:359
  12.9 4.1 %collective-permute-start.2 = (bf16[195,384]{1,0:T(8,128)(2,1)S(1)}, bf16[195,384]{1,0:T(8,128)(2,1)S(1)}, u32[]{:S(2)}, u32[]{:S(2)}) collective-permute-start(bf16[195,384]{1,0:T(8,128)(2,1)S(1)} %get-tuple-element.26), channel_id=1, source_target_pairs={{0,2},{2,0},{6,4},{8,10},{10,8},{14,12},{16,18},{18,16},{22,20},{2... | collective-permute-start | bytes 449288 | tf_op jit(solution)/shard_map/ppermute | solution.py:359
  17.0 1.9 %collective-permute-start = (bf16[195,384]{1,0:T(8,128)(2,1)S(1)}, bf16[195,384]{1,0:T(8,128)(2,1)S(1)}, u32[]{:S(2)}, u32[]{:S(2)}) collective-permute-start(bf16[195,384]{1,0:T(8,128)(2,1)S(1)} %get-tuple-element.23), channel_id=1, source_target_pairs={{0,4},{4,0},{6,2},{8,12},{12,8},{14,10},{16,20},{20,16},{22,18},{2... | collective-permute-start | bytes 449288 | tf_op jit(solution)/shard_map/ppermute | solution.py:359
  18.9 1.6 %collective-permute-done.1.refs_1_ = bf16[195,384]{1,0:T(8,128)(2,1)S(1)} collective-permute-done((bf16[195,384]{1,0:T(8,128)(2,1)S(1)}, bf16[195,384]{1,0:T(8,128)(2,1)S(1)}, u32[]{:S(2)}, u32[]{:S(2)}) %collective-permute-start.1) | collective-permute-done | bytes 149792 | tf_op jit(solution)/shard_map/ppermute | solution.py:359
  20.5 0.0 collective-permute-done.2.refs_2_
  20.5 0.0 all-to-all-done.refs_3_.w_ref
  20.5 2.2 %shard_map.88 = (f32[3,512,128]{2,1,0:T(8,128)S(1)}, bf16[3,208,128]{2,1,0:T(8,128)(2,1)S(1)}) custom-call(bf16[195,384]{1,0:T(8,128)(2,1)S(1)} %get-tuple-element.24.refs_0_, bf16[195,384]{1,0:T(8,128)(2,1)S(1)} %collective-permute-done.1.refs_1_, bf16[195,384]{1,0:T(8,128)(2,1)S(1)} %collective-permute-done.2.refs_2_, ...), custom_call_target="tpu_custom_call" | custom-call | flops 1000000000 | bytes 1048576 | tf_op jit(solution)/shard_map/pallas_call | solution.py:363
  22.8 2.1 %collective-permute-done.token_ref = bf16[195,384]{1,0:T(8,128)(2,1)S(1)} collective-permute-done((bf16[195,384]{1,0:T(8,128)(2,1)S(1)}, bf16[195,384]{1,0:T(8,128)(2,1)S(1)}, u32[]{:S(2)}, u32[]{:S(2)}) %collective-permute-start) | collective-permute-done | bytes 149792 | tf_op jit(solution)/shard_map/ppermute | solution.py:359
  24.9 0.8 %shard_map.89 = (bf16[512,128]{1,0:T(8,128)(2,1)S(1)}, bf16[512,128]{1,0:T(8,128)(2,1)S(1)}, bf16[512,128]{1,0:T(8,128)(2,1)S(1)}, bf16[512,128]{1,0:T(8,128)(2,1)S(1)}) custom-call(bf16[195,384]{1,0:T(8,128)(2,1)S(1)} %collective-permute-done.token_ref, bf16[16,3,32,128]{3,2,1,0:T(8,128)(2,1)S(1)} %all-to-all-done.refs_3_.w_ref, ...), custom_call_target="tpu_custom_call" | custom-call | flops 500000000 | bytes 1048576 | tf_op jit(solution)/shard_map/pallas_call | solution.py:370
  25.7 1.3 %collective-permute-start.3 = (bf16[512,128]{1,0:T(8,128)(2,1)S(1)}, bf16[512,128]{1,0:T(8,128)(2,1)S(1)}, u32[]{:S(2)}, u32[]{:S(2)}) collective-permute-start(bf16[512,128]{1,0:T(8,128)(2,1)S(1)} %get-tuple-element.33), channel_id=1, source_target_pairs={{2,26},{8,16},{10,18},{12,20},{16,8},{18,10},{20,12},{24,0},{28,4}... | collective-permute-start | bytes 393224 | tf_op jit(solution)/shard_map/ppermute | solution.py:386
  27.0 4.9 %collective-permute-start.4 = (bf16[512,128]{1,0:T(8,128)(2,1)S(1)}, bf16[512,128]{1,0:T(8,128)(2,1)S(1)}, u32[]{:S(2)}, u32[]{:S(2)}) collective-permute-start(bf16[512,128]{1,0:T(8,128)(2,1)S(1)} %get-tuple-element.34), channel_id=1, source_target_pairs={{0,16},{2,18},{4,20},{10,26},{16,0},{20,4},{24,8},{26,10},{28,12},... | collective-permute-start | bytes 393224 | tf_op jit(solution)/shard_map/ppermute | solution.py:386
  31.8 1.9 %collective-permute-start.5 = (bf16[512,128]{1,0:T(8,128)(2,1)S(1)}, bf16[512,128]{1,0:T(8,128)(2,1)S(1)}, u32[]{:S(2)}, u32[]{:S(2)}) collective-permute-start(bf16[512,128]{1,0:T(8,128)(2,1)S(1)} %get-tuple-element.35), channel_id=1, source_target_pairs={{0,8},{2,10},{4,12},{8,0},{12,4},{18,26},{24,16},{26,18},{28,20},{... | collective-permute-start | bytes 393224 | tf_op jit(solution)/shard_map/ppermute | solution.py:386
  33.8 1.1 %shard_map.90 = bf16[4,208,128]{2,1,0:T(8,128)(2,1)} custom-call(bf16[195,384]{1,0:T(8,128)(2,1)S(1)} %collective-permute-done.token_ref, bf16[16,3,32,128]{3,2,1,0:T(8,128)(2,1)S(1)} %all-to-all-done.refs_3_.w_ref, bf16[3,208,128]{2,1,0:T(8,128)(2,1)S(1)} %get-tuple-element.31.early), custom_call_target="tpu_custom_call" | custom-call | flops 1000 | bytes 1024 | tf_op jit(solution)/shard_map/pallas_call | solution.py:388
  34.9 3.4 %all-to-all-start.1 = ((bf16[4,208,128]{2,1,0:T(8,128)(2,1)}), bf16[4,208,128]{2,1,0:T(8,128)(2,1)S(1)}, u32[]{:S(2)}, u32[]{:S(2)}) async-start(bf16[4,208,128]{2,1,0:T(8,128)(2,1)} %shard_map.90), calls=%async_computation.1 | async-start | bytes 425984 | tf_op jit(solution)/shard_map/all_to_all | solution.py:396
  38.3 2.4 %collective-permute-start.6 = (bf16[208,768]{1,0:T(8,128)(2,1)S(1)}, bf16[208,768]{1,0:T(8,128)(2,1)S(1)}, u32[]{:S(2)}, u32[]{:S(2)}) collective-permute-start(bf16[208,768]{1,0:T(8,128)(2,1)S(1)} %get-tuple-element.37.own_ref), channel_id=1, source_target_pairs={{0,2},{2,4},{4,6},{6,8},{8,10},{10,12},{12,14},{14,16},{16,18},{18... | collective-permute-start | bytes 958472 | tf_op jit(solution)/shard_map/ppermute | solution.py:402
  40.7 0.0 collective-permute-done.3.refs_1_
  40.7 0.0 collective-permute-done.4.refs_2_
  40.7 0.0 collective-permute-done.5.refs_3_
  40.7 3.4 %shard_map.91 = bf16[512,128]{1,0:T(8,128)(2,1)} custom-call(bf16[512,128]{1,0:T(8,128)(2,1)S(1)} %get-tuple-element.32.refs_0_, bf16[512,128]{1,0:T(8,128)(2,1)S(1)} %collective-permute-done.3.refs_1_, bf16[512,128]{1,0:T(8,128)(2,1)S(1)} %collective-permute-done.4.refs_2_, bf16[512,128]{1,0:T(8,128)(2,1)S(1)} %collective-permute-done.5.refs_3_), custom_call_target="tpu_custom_call" | custom-call | flops 1000000000 | bytes 1048576 | tf_op jit(solution)/shard_map/pallas_call | solution.py:404
  44.1 0.0 all-to-all-done.1.slots
  44.1 5.3 %all-to-all-start.2 = ((bf16[16,32,128]{2,1,0:T(8,128)(2,1)}), bf16[16,32,128]{2,1,0:T(8,128)(2,1)S(1)}, u32[]{:S(2)}, u32[]{:S(2)}) async-start(bf16[16,32,128]{2,1,0:T(8,128)(2,1)} %bitcast.2), calls=%async_computation.2 | async-start | bytes 262144 | tf_op jit(solution)/shard_map/all_to_all | solution.py:408
  49.5 0.0 copy-start.6
  49.5 0.4 shard_map.93
  49.9 1.6 %collective-permute-start.7 = (f32[8,208]{1,0:T(8,128)S(1)}, f32[8,208]{1,0:T(8,128)S(1)}, u32[]{:S(2)}, u32[]{:S(2)}) collective-permute-start(f32[8,208]{1,0:T(8,128)S(1)} %get-tuple-element.40.refs_0_), channel_id=1, source_target_pairs={{0,1},{1,0},{2,3},{3,2},{4,5},{5,4},{6,7},{7,6},{8,9},{9,8},{10,11... | collective-permute-start | bytes 19976 | tf_op jit(solution)/shard_map/ppermute | solution.py:430
  51.5 0.0 copy-done.6
  51.5 0.0 collective-permute-done.6.back_ref
  51.5 1.3 %shard_map.92.attended_ref = f32[208,384]{1,0:T(8,128)S(1)} custom-call(bf16[195,384]{1,0:T(8,128)(2,1)S(1)} %copy-done, bf16[208,768]{1,0:T(8,128)(2,1)S(1)} %get-tuple-element.37.own_ref, bf16[208,768]{1,0:T(8,128)(2,1)S(1)} %collective-permute-done.6.back_ref), custom_call_target="tpu_custom_call" | custom-call | tf_op jit(solution)/shard_map/pallas_call | solution.py:416
  52.8 0.8 %collective-permute-done.7.refs_1_ = f32[8,208]{1,0:T(8,128)S(1)} collective-permute-done((f32[8,208]{1,0:T(8,128)S(1)}, f32[8,208]{1,0:T(8,128)S(1)}, u32[]{:S(2)}, u32[]{:S(2)}) %collective-permute-start.7) | collective-permute-done | bytes 6688 | tf_op jit(solution)/shard_map/ppermute | solution.py:430
  53.6 0.0 copy-start.2
  53.6 1.0 %shard_map.94 = bf16[195,384]{1,0:T(8,128)(2,1)} custom-call(f32[1,384]{1,0:T(1,128)S(1)} %reshape.13.gain_ref, f32[208,384]{1,0:T(8,128)S(1)} %shard_map.92.attended_ref, bf16[208,384]{1,0:T(8,128)(2,1)S(1)} %get-tuple-element.39.fast_ref, f32[8,208]{1,0:T(8,128)S(1)} %get-tuple-element.40.refs_0_, f32[8,208]{1,0:T(8,128)S(1)} %collective-permute-done.7.refs_1_), custom_call_target="tpu_custom_call" | custom-call | tf_op jit(solution)/shard_map/pallas_call | solution.py:432
  54.6 0.6 %all-to-all-done.2.rows_ref = bf16[16,32,128]{2,1,0:T(8,128)(2,1)S(1)} async-done(((bf16[16,32,128]{2,1,0:T(8,128)(2,1)}), bf16[16,32,128]{2,1,0:T(8,128)(2,1)S(1)}, u32[]{:S(2)}, u32[]{:S(2)}) %all-to-all-start.2) | async-done | bytes 131104 | tf_op jit(solution)/shard_map/all_to_all | solution.py:408
  55.2 0.0 copy-done.2
  55.2 0.8 %shard_map.95 = f32[3,3,32,128]{3,2,1,0:T(8,128)} custom-call(f32[3,3,32,128]{3,2,1,0:T(8,128)S(1)} %copy-done.2, bf16[16,32,128]{2,1,0:T(8,128)(2,1)S(1)} %all-to-all-done.2.rows_ref), custom_call_target="tpu_custom_call" | custom-call | flops 1000000 | bytes 1048576 | tf_op jit(solution)/shard_map/pallas_call | solution.py:412
  (1 shorter events, 0.0 us)
Async XLA Ops:
  0.6 0.9 %copy-start.1 = (f32[3,3,32,128]{3,2,1,0:T(8,128)S(1)}, f32[3,3,32,128]{3,2,1,0:T(8,128)}, u32[]{:S(2)}) copy-start(f32[3,3,32,128]{3,2,1,0:T(8,128)} %w_ref.3) | copy-start | bytes 442372
  2.3 8.6 %copy-start = (bf16[195,384]{1,0:T(8,128)(2,1)S(1)}, bf16[195,384]{1,0:T(8,128)(2,1)}, u32[]{:S(2)}) copy-start(bf16[195,384]{1,0:T(8,128)(2,1)} %q_ref.2) | copy-start | bytes 449284
  2.3 8.6 %copy-start.3 = (bf16[195,384]{1,0:T(8,128)(2,1)S(1)}, bf16[195,384]{1,0:T(8,128)(2,1)}, u32[]{:S(2)}) copy-start(bf16[195,384]{1,0:T(8,128)(2,1)} %k_ref.1) | copy-start | bytes 449284
  2.3 8.7 %copy-start.4 = (bf16[195,384]{1,0:T(8,128)(2,1)S(1)}, bf16[195,384]{1,0:T(8,128)(2,1)}, u32[]{:S(2)}) copy-start(bf16[195,384]{1,0:T(8,128)(2,1)} %v_ref.1) | copy-start | bytes 449284
  2.3 18.2 %all-to-all-start = ((bf16[16,3,32,128]{3,2,1,0:T(8,128)(2,1)}), bf16[16,3,32,128]{3,2,1,0:T(8,128)(2,1)S(1)}, u32[]{:S(2)}, u32[]{:S(2)}) async-start(bf16[16,3,32,128]{3,2,1,0:T(8,128)(2,1)} %shard_map.86.after), calls=%async_computation | async-start | bytes 786432 | tf_op jit(solution)/shard_map/all_to_all | solution.py:354
  10.3 0.7 %copy-start.5 = (f32[195,3]{0,1:T(4,128)S(1)}, f32[195,3]{0,1:T(4,128)}, u32[]{:S(2)}) copy-start(f32[195,3]{0,1:T(4,128)} %param.10) | copy-start | bytes 7024
  11.6 8.9 %collective-permute-start.1 = (bf16[195,384]{1,0:T(8,128)(2,1)S(1)}, bf16[195,384]{1,0:T(8,128)(2,1)S(1)}, u32[]{:S(2)}, u32[]{:S(2)}) collective-permute-start(bf16[195,384]{1,0:T(8,128)(2,1)S(1)} %get-tuple-element.25), channel_id=1, source_target_pairs={{2,4},{4,2},{6,0},{10,12},{12,10},{14,8},{18,20},{20,18},{22,16},{... | collective-permute-start | bytes 449288 | tf_op jit(solution)/shard_map/ppermute | solution.py:359
  12.9 7.6 %collective-permute-start.2 = (bf16[195,384]{1,0:T(8,128)(2,1)S(1)}, bf16[195,384]{1,0:T(8,128)(2,1)S(1)}, u32[]{:S(2)}, u32[]{:S(2)}) collective-permute-start(bf16[195,384]{1,0:T(8,128)(2,1)S(1)} %get-tuple-element.26), channel_id=1, source_target_pairs={{0,2},{2,0},{6,4},{8,10},{10,8},{14,12},{16,18},{18,16},{22,20},{2... | collective-permute-start | bytes 449288 | tf_op jit(solution)/shard_map/ppermute | solution.py:359
  17.0 7.9 %collective-permute-start = (bf16[195,384]{1,0:T(8,128)(2,1)S(1)}, bf16[195,384]{1,0:T(8,128)(2,1)S(1)}, u32[]{:S(2)}, u32[]{:S(2)}) collective-permute-start(bf16[195,384]{1,0:T(8,128)(2,1)S(1)} %get-tuple-element.23), channel_id=1, source_target_pairs={{0,4},{4,0},{6,2},{8,12},{12,8},{14,10},{16,20},{20,16},{22,18},{2... | collective-permute-start | bytes 449288 | tf_op jit(solution)/shard_map/ppermute | solution.py:359
  25.7 15.0 %collective-permute-start.3 = (bf16[512,128]{1,0:T(8,128)(2,1)S(1)}, bf16[512,128]{1,0:T(8,128)(2,1)S(1)}, u32[]{:S(2)}, u32[]{:S(2)}) collective-permute-start(bf16[512,128]{1,0:T(8,128)(2,1)S(1)} %get-tuple-element.33), channel_id=1, source_target_pairs={{2,26},{8,16},{10,18},{12,20},{16,8},{18,10},{20,12},{24,0},{28,4}... | collective-permute-start | bytes 393224 | tf_op jit(solution)/shard_map/ppermute | solution.py:386
  27.0 13.7 %collective-permute-start.4 = (bf16[512,128]{1,0:T(8,128)(2,1)S(1)}, bf16[512,128]{1,0:T(8,128)(2,1)S(1)}, u32[]{:S(2)}, u32[]{:S(2)}) collective-permute-start(bf16[512,128]{1,0:T(8,128)(2,1)S(1)} %get-tuple-element.34), channel_id=1, source_target_pairs={{0,16},{2,18},{4,20},{10,26},{16,0},{20,4},{24,8},{26,10},{28,12},... | collective-permute-start | bytes 393224 | tf_op jit(solution)/shard_map/ppermute | solution.py:386
  31.8 8.8 %collective-permute-start.5 = (bf16[512,128]{1,0:T(8,128)(2,1)S(1)}, bf16[512,128]{1,0:T(8,128)(2,1)S(1)}, u32[]{:S(2)}, u32[]{:S(2)}) collective-permute-start(bf16[512,128]{1,0:T(8,128)(2,1)S(1)} %get-tuple-element.35), channel_id=1, source_target_pairs={{0,8},{2,10},{4,12},{8,0},{12,4},{18,26},{24,16},{26,18},{28,20},{... | collective-permute-start | bytes 393224 | tf_op jit(solution)/shard_map/ppermute | solution.py:386
  34.9 9.2 %all-to-all-start.1 = ((bf16[4,208,128]{2,1,0:T(8,128)(2,1)}), bf16[4,208,128]{2,1,0:T(8,128)(2,1)S(1)}, u32[]{:S(2)}, u32[]{:S(2)}) async-start(bf16[4,208,128]{2,1,0:T(8,128)(2,1)} %shard_map.90), calls=%async_computation.1 | async-start | bytes 425984 | tf_op jit(solution)/shard_map/all_to_all | solution.py:396
  38.3 13.2 %collective-permute-start.6 = (bf16[208,768]{1,0:T(8,128)(2,1)S(1)}, bf16[208,768]{1,0:T(8,128)(2,1)S(1)}, u32[]{:S(2)}, u32[]{:S(2)}) collective-permute-start(bf16[208,768]{1,0:T(8,128)(2,1)S(1)} %get-tuple-element.37.own_ref), channel_id=1, source_target_pairs={{0,2},{2,4},{4,6},{6,8},{8,10},{10,12},{12,14},{14,16},{16,18},{18... | collective-permute-start | bytes 958472 | tf_op jit(solution)/shard_map/ppermute | solution.py:402
  44.1 11.1 %all-to-all-start.2 = ((bf16[16,32,128]{2,1,0:T(8,128)(2,1)}), bf16[16,32,128]{2,1,0:T(8,128)(2,1)S(1)}, u32[]{:S(2)}, u32[]{:S(2)}) async-start(bf16[16,32,128]{2,1,0:T(8,128)(2,1)} %bitcast.2), calls=%async_computation.2 | async-start | bytes 262144 | tf_op jit(solution)/shard_map/all_to_all | solution.py:408
  49.5 2.0 %copy-start.6 = (f32[384]{0:T(512)S(1)}, f32[384]{0:T(512)}, u32[]{:S(2)}) copy-start(f32[384]{0:T(512)} %param.13) | copy-start | bytes 4612
  49.9 3.7 %collective-permute-start.7 = (f32[8,208]{1,0:T(8,128)S(1)}, f32[8,208]{1,0:T(8,128)S(1)}, u32[]{:S(2)}, u32[]{:S(2)}) collective-permute-start(f32[8,208]{1,0:T(8,128)S(1)} %get-tuple-element.40.refs_0_), channel_id=1, source_target_pairs={{0,1},{1,0},{2,3},{3,2},{4,5},{5,4},{6,7},{7,6},{8,9},{9,8},{10,11... | collective-permute-start | bytes 19976 | tf_op jit(solution)/shard_map/ppermute | solution.py:430
  53.6 1.6 %copy-start.2 = (f32[3,3,32,128]{3,2,1,0:T(8,128)S(1)}, f32[3,3,32,128]{3,2,1,0:T(8,128)}, u32[]{:S(2)}) copy-start(f32[3,3,32,128]{3,2,1,0:T(8,128)} %w_ref.3) | copy-start | bytes 442372

commit v13 on v12

--- a/solution.py
+++ b/solution.py
@@ -48,8 +48,13 @@
     return [0] + list(range(n - 1, 0, -1))
 
 
-def first_owner(h):
-    return h & 1
+def owner(m, h):
+    return m + (h & 1) * min(m, 1)
+
+
+def owned(z, h):
+    odd = h & 1
+    return jnp.where((odd == 1) & (z == 1), 3, z - odd * jnp.minimum(z, 1))
 
 
 GROUP = 4
@@ -191,7 +196,7 @@
     for m, grad in enumerate(gradients([token_ref], w_ref, *scratch)):
         sums[m] = (early[m] + grad).astype(bf16)
     for d in range(slots):
-        matrix = lax.rem((place[0] ^ d) - first_owner(place[1]) + slots, slots)
+        matrix = owned(place[0] ^ d, place[1])
         chosen = sums[jnp.minimum(matrix, 2)]
         outs[d][...] = jnp.where(matrix < 3, chosen, jnp.zeros_like(chosen))
 
@@ -227,16 +232,15 @@
     return jnp.concatenate([high, low, high], axis=0)
 
 
-def ortho_body(heads, slots, *refs):
+def ortho_body(heads, *refs):
     place = position()
-    matrix = lax.rem(place[0] - first_owner(place[1]) + slots, slots)
-    owner = (place[1] < heads) & (matrix < 3)
-
-    @pl.when(owner)
+    busy = (place[1] < heads) & (owned(*place) < 3)
+
+    @pl.when(busy)
     def _():
         orthogonalize(refs[:-1], refs[-1])
 
-    @pl.when(jnp.logical_not(owner))
+    @pl.when(jnp.logical_not(busy))
     def _():
         refs[-1][...] = jnp.zeros(refs[-1].shape, refs[-1].dtype)
 
@@ -271,7 +275,7 @@
     for m in range(3):
         for h in range(heads):
             weights = w_ref[m, h]
-            summed = weights + rows_ref[index_of((m + first_owner(h)) % slots, h, slots)].astype(f32)
+            summed = weights + rows_ref[index_of(owner(m, h), h, slots)].astype(f32)
             old = jnp.sqrt(jnp.sum(weights * weights, axis=1, keepdims=True))
             new = lax.rsqrt(jnp.sum(summed * summed, axis=1, keepdims=True) + epsilon)
             out[m, h] = summed * (old * new)
@@ -381,7 +385,7 @@
             pairs += [
                 (z * group + j, (z ^ d) * group + j)
                 for j in range(heads)
-                if ((z ^ d) - first_owner(j)) % nz < 3
+                if (z ^ d) in [owner(m, j) for m in range(3)]
             ]
         partials[d] = lax.ppermute(partials[d], "ctx", pairs)
 
@@ -401,7 +405,7 @@
     ring = [(i, i + 1) for i in range(count - 1)]
     kv_back = lax.ppermute(kv_own, "ctx", ring)
 
-    ortho = call(functools.partial(ortho_body, heads, nz), sds((hidden, HD), bf16), flops=1e9)(
+    ortho = call(functools.partial(ortho_body, heads), sds((hidden, HD), bf16), flops=1e9)(
         *(partials[d] for d in served(nz))
     )
     queries, ortho = lax.optimization_barrier((queries, ortho))

time: 56.7 us -> 56.8 us (level)
  transfers between devices with their start and end apart: 11 -> 11, of which waited for: 4 -> 5; matrix products, arithmetic and copies ran while one was open for 0% -> 0% of each run, Pallas kernels for 18% -> 18%
where the time goes in v13:
time: 56.8 us; the launch traced here: 56.1 us
  starting transfers between devices  35.9 us (63%)
  Pallas kernels  12.6 us (22%)
  waiting for transfers between devices  5.27 us (9%)
  between operations  1.46 us (3%)
  local copies, waits for them, and re-layouts  0.93 us (2%)
    ppermute x3, starting transfers between devices, on_device(): partials[d] = lax.ppermute(partials[d], 'ctx', pairs)  8.08 us
    all_to_all x1, starting transfers between devices, on_device(): lax.all_to_all(low, 'ctx', 0, 0, tiled=True, axis_index_groups=[listed(nz)])  7.96 us
    ppermute x3, starting transfers between devices, on_device(): token_slots[d] = lax.ppermute(token_slots[d], 'ctx', pairs)  7.33 us
    all_to_all x1, starting transfers between devices, on_device(): lax.all_to_all(ortho.reshape(count, rows_local, HD), 'ctx', 0, 0, tiled=T...  5.25 us
    ppermute x3, waiting for transfers between devices, on_device(): token_slots[d] = lax.ppermute(token_slots[d], 'ctx', pairs)  3.72 us
    pallas_call x1, Pallas kernels, on_device(): call(functools.partial(ortho_body, heads), sds((hidden, HD), bf16), flops...  3.42 us
    all_to_all x1, starting transfers between devices, on_device(): lax.all_to_all(fast_slots, 'ctx', 0, 0, tiled=True, axis_index_groups=[[z...  3.37 us
    ppermute x1, starting transfers between devices, on_device(): kv_back = lax.ppermute(kv_own, 'ctx', ring)  2.38 us
  transfers between devices with their start and end apart: 11, of which 5 were waited for; matrix products, arithmetic and copies ran while one was open for 0% of the time, Pallas kernels for 18%

profile of v13, /device:TPU:0, one launch (start us, length us, event | category | flops | bytes accessed | tf_op | source)
XLA Modules:
  0.0 56.1 jit_solution(1268960783427894141)
XLA Ops:
  0.6 0.0 copy-start.1
  0.6 0.9 %copy-done.1 = f32[3,3,32,128]{3,2,1,0:T(8,128)S(1)} copy-done((f32[3,3,32,128]{3,2,1,0:T(8,128)S(1)}, f32[3,3,32,128]{3,2,1,0:T(8,128)}, u32[]{:S(2)}) %copy-start.1) | copy-done | bytes 147480
  1.5 0.8 %shard_map.86.after = bf16[16,3,32,128]{3,2,1,0:T(8,128)(2,1)} custom-call(f32[3,3,32,128]{3,2,1,0:T(8,128)S(1)} %copy-done.1), custom_call_target="tpu_custom_call" | custom-call | flops 1000000 | bytes 1048576 | tf_op jit(solution)/shard_map/pallas_call | solution.py:341
  2.3 0.0 copy-start
  2.3 0.0 copy-start.3
  2.3 0.0 copy-start.4
  2.3 8.0 %all-to-all-start = ((bf16[16,3,32,128]{3,2,1,0:T(8,128)(2,1)}), bf16[16,3,32,128]{3,2,1,0:T(8,128)(2,1)S(1)}, u32[]{:S(2)}, u32[]{:S(2)}) async-start(bf16[16,3,32,128]{3,2,1,0:T(8,128)(2,1)} %shard_map.86.after), calls=%async_computation | async-start | bytes 786432 | tf_op jit(solution)/shard_map/all_to_all | solution.py:358
  10.3 0.0 copy-start.5
  11.0 0.0 copy-done
  11.0 0.0 copy-done.3
  11.0 0.0 copy-done.4
  11.0 0.0 copy-done.5
  11.0 0.6 %shard_map.87 = (bf16[208,768]{1,0:T(8,128)(2,1)S(1)}, bf16[195,384]{1,0:T(8,128)(2,1)S(1)}, bf16[195,384]{1,0:T(8,128)(2,1)S(1)}, bf16[195,384]{1,0:T(8,128)(2,1)S(1)}, bf16[195,384]{1,0:T(8,128)(2,1)S(1)}) custom-call(bf16[16,3,32,128]{3,2,1,0:T(8,128)(2,1)} %shard_map.86.after, s32[1,1]{1,0:T(1,128)} %bitcast.3.update, f32[3,195]{1,0:T(4,128)S(1)} %bitcast.4, ...), custom_call_target="tpu_custom_call" | custom-call | tf_op jit(solution)/shard_map/pallas_call | solution.py:344
  11.6 1.3 %collective-permute-start.1 = (bf16[195,384]{1,0:T(8,128)(2,1)S(1)}, bf16[195,384]{1,0:T(8,128)(2,1)S(1)}, u32[]{:S(2)}, u32[]{:S(2)}) collective-permute-start(bf16[195,384]{1,0:T(8,128)(2,1)S(1)} %get-tuple-element.25), channel_id=1, source_target_pairs={{2,4},{4,2},{6,0},{10,12},{12,10},{14,8},{18,20},{20,18},{22,16},{... | collective-permute-start | bytes 449288 | tf_op jit(solution)/shard_map/ppermute | solution.py:363
  12.9 4.1 %collective-permute-start.2 = (bf16[195,384]{1,0:T(8,128)(2,1)S(1)}, bf16[195,384]{1,0:T(8,128)(2,1)S(1)}, u32[]{:S(2)}, u32[]{:S(2)}) collective-permute-start(bf16[195,384]{1,0:T(8,128)(2,1)S(1)} %get-tuple-element.26), channel_id=1, source_target_pairs={{0,2},{2,0},{6,4},{8,10},{10,8},{14,12},{16,18},{18,16},{22,20},{2... | collective-permute-start | bytes 449288 | tf_op jit(solution)/shard_map/ppermute | solution.py:363
  17.0 1.9 %collective-permute-start = (bf16[195,384]{1,0:T(8,128)(2,1)S(1)}, bf16[195,384]{1,0:T(8,128)(2,1)S(1)}, u32[]{:S(2)}, u32[]{:S(2)}) collective-permute-start(bf16[195,384]{1,0:T(8,128)(2,1)S(1)} %get-tuple-element.23), channel_id=1, source_target_pairs={{0,4},{4,0},{6,2},{8,12},{12,8},{14,10},{16,20},{20,16},{22,18},{2... | collective-permute-start | bytes 449288 | tf_op jit(solution)/shard_map/ppermute | solution.py:363
  18.9 1.6 %collective-permute-done.1.refs_1_ = bf16[195,384]{1,0:T(8,128)(2,1)S(1)} collective-permute-done((bf16[195,384]{1,0:T(8,128)(2,1)S(1)}, bf16[195,384]{1,0:T(8,128)(2,1)S(1)}, u32[]{:S(2)}, u32[]{:S(2)}) %collective-permute-start.1) | collective-permute-done | bytes 149792 | tf_op jit(solution)/shard_map/ppermute | solution.py:363
  20.5 0.0 collective-permute-done.2.refs_2_
  20.5 0.0 all-to-all-done.refs_3_.w_ref
  20.5 2.2 %shard_map.88 = (f32[3,512,128]{2,1,0:T(8,128)S(1)}, bf16[3,208,128]{2,1,0:T(8,128)(2,1)S(1)}) custom-call(bf16[195,384]{1,0:T(8,128)(2,1)S(1)} %get-tuple-element.24.refs_0_, bf16[195,384]{1,0:T(8,128)(2,1)S(1)} %collective-permute-done.1.refs_1_, bf16[195,384]{1,0:T(8,128)(2,1)S(1)} %collective-permute-done.2.refs_2_, ...), custom_call_target="tpu_custom_call" | custom-call | flops 1000000000 | bytes 1048576 | tf_op jit(solution)/shard_map/pallas_call | solution.py:367
  22.8 2.1 %collective-permute-done.token_ref = bf16[195,384]{1,0:T(8,128)(2,1)S(1)} collective-permute-done((bf16[195,384]{1,0:T(8,128)(2,1)S(1)}, bf16[195,384]{1,0:T(8,128)(2,1)S(1)}, u32[]{:S(2)}, u32[]{:S(2)}) %collective-permute-start) | collective-permute-done | bytes 149792 | tf_op jit(solution)/shard_map/ppermute | solution.py:363
  24.9 0.8 %shard_map.89 = (bf16[512,128]{1,0:T(8,128)(2,1)S(1)}, bf16[512,128]{1,0:T(8,128)(2,1)S(1)}, bf16[512,128]{1,0:T(8,128)(2,1)S(1)}, bf16[512,128]{1,0:T(8,128)(2,1)S(1)}) custom-call(bf16[195,384]{1,0:T(8,128)(2,1)S(1)} %collective-permute-done.token_ref, bf16[16,3,32,128]{3,2,1,0:T(8,128)(2,1)S(1)} %all-to-all-done.refs_3_.w_ref, ...), custom_call_target="tpu_custom_call" | custom-call | flops 500000000 | bytes 1048576 | tf_op jit(solution)/shard_map/pallas_call | solution.py:374
  25.7 1.3 %collective-permute-start.3 = (bf16[512,128]{1,0:T(8,128)(2,1)S(1)}, bf16[512,128]{1,0:T(8,128)(2,1)S(1)}, u32[]{:S(2)}, u32[]{:S(2)}) collective-permute-start(bf16[512,128]{1,0:T(8,128)(2,1)S(1)} %get-tuple-element.33), channel_id=1, source_target_pairs={{2,26},{8,16},{10,18},{12,20},{16,8},{20,12},{24,0},{26,2},{28,4},... | collective-permute-start | bytes 393224 | tf_op jit(solution)/shard_map/ppermute | solution.py:390
  27.0 4.9 %collective-permute-start.4 = (bf16[512,128]{1,0:T(8,128)(2,1)S(1)}, bf16[512,128]{1,0:T(8,128)(2,1)S(1)}, u32[]{:S(2)}, u32[]{:S(2)}) collective-permute-start(bf16[512,128]{1,0:T(8,128)(2,1)S(1)} %get-tuple-element.34), channel_id=1, source_target_pairs={{0,16},{2,18},{4,20},{10,26},{16,0},{18,2},{20,4},{24,8},{28,12},{... | collective-permute-start | bytes 393224 | tf_op jit(solution)/shard_map/ppermute | solution.py:390
  31.9 1.9 %collective-permute-start.5 = (bf16[512,128]{1,0:T(8,128)(2,1)S(1)}, bf16[512,128]{1,0:T(8,128)(2,1)S(1)}, u32[]{:S(2)}, u32[]{:S(2)}) collective-permute-start(bf16[512,128]{1,0:T(8,128)(2,1)S(1)} %get-tuple-element.35), channel_id=1, source_target_pairs={{0,8},{4,12},{8,0},{10,2},{12,4},{18,26},{24,16},{26,18},{28,20},{... | collective-permute-start | bytes 393224 | tf_op jit(solution)/shard_map/ppermute | solution.py:390
  33.8 1.1 %shard_map.90 = bf16[4,208,128]{2,1,0:T(8,128)(2,1)} custom-call(bf16[195,384]{1,0:T(8,128)(2,1)S(1)} %collective-permute-done.token_ref, bf16[16,3,32,128]{3,2,1,0:T(8,128)(2,1)S(1)} %all-to-all-done.refs_3_.w_ref, bf16[3,208,128]{2,1,0:T(8,128)(2,1)S(1)} %get-tuple-element.31.early), custom_call_target="tpu_custom_call" | custom-call | flops 1000 | bytes 1024 | tf_op jit(solution)/shard_map/pallas_call | solution.py:392
  35.0 3.4 %all-to-all-start.1 = ((bf16[4,208,128]{2,1,0:T(8,128)(2,1)}), bf16[4,208,128]{2,1,0:T(8,128)(2,1)S(1)}, u32[]{:S(2)}, u32[]{:S(2)}) async-start(bf16[4,208,128]{2,1,0:T(8,128)(2,1)} %shard_map.90), calls=%async_computation.1 | async-start | bytes 425984 | tf_op jit(solution)/shard_map/all_to_all | solution.py:400
  38.3 2.4 %collective-permute-start.6 = (bf16[208,768]{1,0:T(8,128)(2,1)S(1)}, bf16[208,768]{1,0:T(8,128)(2,1)S(1)}, u32[]{:S(2)}, u32[]{:S(2)}) collective-permute-start(bf16[208,768]{1,0:T(8,128)(2,1)S(1)} %get-tuple-element.37.own_ref), channel_id=1, source_target_pairs={{0,2},{2,4},{4,6},{6,8},{8,10},{10,12},{12,14},{14,16},{16,18},{18... | collective-permute-start | bytes 958472 | tf_op jit(solution)/shard_map/ppermute | solution.py:406
  40.7 0.0 collective-permute-done.3.refs_1_
  40.7 0.0 collective-permute-done.4.refs_2_
  40.7 0.1 collective-permute-done.5.refs_3_
  40.9 3.4 %shard_map.91 = bf16[512,128]{1,0:T(8,128)(2,1)} custom-call(bf16[512,128]{1,0:T(8,128)(2,1)S(1)} %get-tuple-element.32.refs_0_, bf16[512,128]{1,0:T(8,128)(2,1)S(1)} %collective-permute-done.3.refs_1_, bf16[512,128]{1,0:T(8,128)(2,1)S(1)} %collective-permute-done.4.refs_2_, bf16[512,128]{1,0:T(8,128)(2,1)S(1)} %collective-permute-done.5.refs_3_), custom_call_target="tpu_custom_call" | custom-call | flops 1000000000 | bytes 1048576 | tf_op jit(solution)/shard_map/pallas_call | solution.py:408
  44.3 0.0 all-to-all-done.1.slots
  44.3 5.2 %all-to-all-start.2 = ((bf16[16,32,128]{2,1,0:T(8,128)(2,1)}), bf16[16,32,128]{2,1,0:T(8,128)(2,1)S(1)}, u32[]{:S(2)}, u32[]{:S(2)}) async-start(bf16[16,32,128]{2,1,0:T(8,128)(2,1)} %bitcast.2), calls=%async_computation.2 | async-start | bytes 262144 | tf_op jit(solution)/shard_map/all_to_all | solution.py:412
  49.5 0.0 copy-start.6
  49.5 0.4 shard_map.93
  50.0 1.6 %collective-permute-start.7 = (f32[8,208]{1,0:T(8,128)S(1)}, f32[8,208]{1,0:T(8,128)S(1)}, u32[]{:S(2)}, u32[]{:S(2)}) collective-permute-start(f32[8,208]{1,0:T(8,128)S(1)} %get-tuple-element.40.refs_0_), channel_id=1, source_target_pairs={{0,1},{1,0},{2,3},{3,2},{4,5},{5,4},{6,7},{7,6},{8,9},{9,8},{10,11... | collective-permute-start | bytes 19976 | tf_op jit(solution)/shard_map/ppermute | solution.py:434
  51.5 0.0 copy-done.6
  51.5 0.0 collective-permute-done.6.back_ref
  51.5 1.3 %shard_map.92.attended_ref = f32[208,384]{1,0:T(8,128)S(1)} custom-call(bf16[195,384]{1,0:T(8,128)(2,1)S(1)} %copy-done, bf16[208,768]{1,0:T(8,128)(2,1)S(1)} %get-tuple-element.37.own_ref, bf16[208,768]{1,0:T(8,128)(2,1)S(1)} %collective-permute-done.6.back_ref), custom_call_target="tpu_custom_call" | custom-call | tf_op jit(solution)/shard_map/pallas_call | solution.py:420
  52.9 0.8 %collective-permute-done.7.refs_1_ = f32[8,208]{1,0:T(8,128)S(1)} collective-permute-done((f32[8,208]{1,0:T(8,128)S(1)}, f32[8,208]{1,0:T(8,128)S(1)}, u32[]{:S(2)}, u32[]{:S(2)}) %collective-permute-start.7) | collective-permute-done | bytes 6688 | tf_op jit(solution)/shard_map/ppermute | solution.py:434
  53.7 0.0 copy-start.2
  53.7 1.0 %shard_map.94 = bf16[195,384]{1,0:T(8,128)(2,1)} custom-call(f32[1,384]{1,0:T(1,128)S(1)} %reshape.13.gain_ref, f32[208,384]{1,0:T(8,128)S(1)} %shard_map.92.attended_ref, bf16[208,384]{1,0:T(8,128)(2,1)S(1)} %get-tuple-element.39.fast_ref, f32[8,208]{1,0:T(8,128)S(1)} %get-tuple-element.40.refs_0_, f32[8,208]{1,0:T(8,128)S(1)} %collective-permute-done.7.refs_1_), custom_call_target="tpu_custom_call" | custom-call | tf_op jit(solution)/shard_map/pallas_call | solution.py:436
  54.7 0.6 %all-to-all-done.2.rows_ref = bf16[16,32,128]{2,1,0:T(8,128)(2,1)S(1)} async-done(((bf16[16,32,128]{2,1,0:T(8,128)(2,1)}), bf16[16,32,128]{2,1,0:T(8,128)(2,1)S(1)}, u32[]{:S(2)}, u32[]{:S(2)}) %all-to-all-start.2) | async-done | bytes 131104 | tf_op jit(solution)/shard_map/all_to_all | solution.py:412
  55.3 0.0 copy-done.2
  55.3 0.8 %shard_map.95 = f32[3,3,32,128]{3,2,1,0:T(8,128)} custom-call(f32[3,3,32,128]{3,2,1,0:T(8,128)S(1)} %copy-done.2, bf16[16,32,128]{2,1,0:T(8,128)(2,1)S(1)} %all-to-all-done.2.rows_ref), custom_call_target="tpu_custom_call" | custom-call | flops 1000000 | bytes 1048576 | tf_op jit(solution)/shard_map/pallas_call | solution.py:416
  (1 shorter events, 0.0 us)
Async XLA Ops:
  0.6 0.9 %copy-start.1 = (f32[3,3,32,128]{3,2,1,0:T(8,128)S(1)}, f32[3,3,32,128]{3,2,1,0:T(8,128)}, u32[]{:S(2)}) copy-start(f32[3,3,32,128]{3,2,1,0:T(8,128)} %w_ref.3) | copy-start | bytes 442372
  2.3 8.6 %copy-start = (bf16[195,384]{1,0:T(8,128)(2,1)S(1)}, bf16[195,384]{1,0:T(8,128)(2,1)}, u32[]{:S(2)}) copy-start(bf16[195,384]{1,0:T(8,128)(2,1)} %q_ref.2) | copy-start | bytes 449284
  2.3 8.6 %copy-start.3 = (bf16[195,384]{1,0:T(8,128)(2,1)S(1)}, bf16[195,384]{1,0:T(8,128)(2,1)}, u32[]{:S(2)}) copy-start(bf16[195,384]{1,0:T(8,128)(2,1)} %k_ref.1) | copy-start | bytes 449284
  2.3 8.7 %copy-start.4 = (bf16[195,384]{1,0:T(8,128)(2,1)S(1)}, bf16[195,384]{1,0:T(8,128)(2,1)}, u32[]{:S(2)}) copy-start(bf16[195,384]{1,0:T(8,128)(2,1)} %v_ref.1) | copy-start | bytes 449284
  2.3 18.2 %all-to-all-start = ((bf16[16,3,32,128]{3,2,1,0:T(8,128)(2,1)}), bf16[16,3,32,128]{3,2,1,0:T(8,128)(2,1)S(1)}, u32[]{:S(2)}, u32[]{:S(2)}) async-start(bf16[16,3,32,128]{3,2,1,0:T(8,128)(2,1)} %shard_map.86.after), calls=%async_computation | async-start | bytes 786432 | tf_op jit(solution)/shard_map/all_to_all | solution.py:358
  10.3 0.7 %copy-start.5 = (f32[195,3]{0,1:T(4,128)S(1)}, f32[195,3]{0,1:T(4,128)}, u32[]{:S(2)}) copy-start(f32[195,3]{0,1:T(4,128)} %param.10) | copy-start | bytes 7024
  11.6 8.9 %collective-permute-start.1 = (bf16[195,384]{1,0:T(8,128)(2,1)S(1)}, bf16[195,384]{1,0:T(8,128)(2,1)S(1)}, u32[]{:S(2)}, u32[]{:S(2)}) collective-permute-start(bf16[195,384]{1,0:T(8,128)(2,1)S(1)} %get-tuple-element.25), channel_id=1, source_target_pairs={{2,4},{4,2},{6,0},{10,12},{12,10},{14,8},{18,20},{20,18},{22,16},{... | collective-permute-start | bytes 449288 | tf_op jit(solution)/shard_map/ppermute | solution.py:363
  12.9 7.6 %collective-permute-start.2 = (bf16[195,384]{1,0:T(8,128)(2,1)S(1)}, bf16[195,384]{1,0:T(8,128)(2,1)S(1)}, u32[]{:S(2)}, u32[]{:S(2)}) collective-permute-start(bf16[195,384]{1,0:T(8,128)(2,1)S(1)} %get-tuple-element.26), channel_id=1, source_target_pairs={{0,2},{2,0},{6,4},{8,10},{10,8},{14,12},{16,18},{18,16},{22,20},{2... | collective-permute-start | bytes 449288 | tf_op jit(solution)/shard_map/ppermute | solution.py:363
  17.0 7.9 %collective-permute-start = (bf16[195,384]{1,0:T(8,128)(2,1)S(1)}, bf16[195,384]{1,0:T(8,128)(2,1)S(1)}, u32[]{:S(2)}, u32[]{:S(2)}) collective-permute-start(bf16[195,384]{1,0:T(8,128)(2,1)S(1)} %get-tuple-element.23), channel_id=1, source_target_pairs={{0,4},{4,0},{6,2},{8,12},{12,8},{14,10},{16,20},{20,16},{22,18},{2... | collective-permute-start | bytes 449288 | tf_op jit(solution)/shard_map/ppermute | solution.py:363
  25.7 15.0 %collective-permute-start.3 = (bf16[512,128]{1,0:T(8,128)(2,1)S(1)}, bf16[512,128]{1,0:T(8,128)(2,1)S(1)}, u32[]{:S(2)}, u32[]{:S(2)}) collective-permute-start(bf16[512,128]{1,0:T(8,128)(2,1)S(1)} %get-tuple-element.33), channel_id=1, source_target_pairs={{2,26},{8,16},{10,18},{12,20},{16,8},{20,12},{24,0},{26,2},{28,4},... | collective-permute-start | bytes 393224 | tf_op jit(solution)/shard_map/ppermute | solution.py:390
  27.0 13.7 %collective-permute-start.4 = (bf16[512,128]{1,0:T(8,128)(2,1)S(1)}, bf16[512,128]{1,0:T(8,128)(2,1)S(1)}, u32[]{:S(2)}, u32[]{:S(2)}) collective-permute-start(bf16[512,128]{1,0:T(8,128)(2,1)S(1)} %get-tuple-element.34), channel_id=1, source_target_pairs={{0,16},{2,18},{4,20},{10,26},{16,0},{18,2},{20,4},{24,8},{28,12},{... | collective-permute-start | bytes 393224 | tf_op jit(solution)/shard_map/ppermute | solution.py:390
  31.9 8.9 %collective-permute-start.5 = (bf16[512,128]{1,0:T(8,128)(2,1)S(1)}, bf16[512,128]{1,0:T(8,128)(2,1)S(1)}, u32[]{:S(2)}, u32[]{:S(2)}) collective-permute-start(bf16[512,128]{1,0:T(8,128)(2,1)S(1)} %get-tuple-element.35), channel_id=1, source_target_pairs={{0,8},{4,12},{8,0},{10,2},{12,4},{18,26},{24,16},{26,18},{28,20},{... | collective-permute-start | bytes 393224 | tf_op jit(solution)/shard_map/ppermute | solution.py:390
  35.0 9.3 %all-to-all-start.1 = ((bf16[4,208,128]{2,1,0:T(8,128)(2,1)}), bf16[4,208,128]{2,1,0:T(8,128)(2,1)S(1)}, u32[]{:S(2)}, u32[]{:S(2)}) async-start(bf16[4,208,128]{2,1,0:T(8,128)(2,1)} %shard_map.90), calls=%async_computation.1 | async-start | bytes 425984 | tf_op jit(solution)/shard_map/all_to_all | solution.py:400
  38.3 13.2 %collective-permute-start.6 = (bf16[208,768]{1,0:T(8,128)(2,1)S(1)}, bf16[208,768]{1,0:T(8,128)(2,1)S(1)}, u32[]{:S(2)}, u32[]{:S(2)}) collective-permute-start(bf16[208,768]{1,0:T(8,128)(2,1)S(1)} %get-tuple-element.37.own_ref), channel_id=1, source_target_pairs={{0,2},{2,4},{4,6},{6,8},{8,10},{10,12},{12,14},{14,16},{16,18},{18... | collective-permute-start | bytes 958472 | tf_op jit(solution)/shard_map/ppermute | solution.py:406
  44.3 11.0 %all-to-all-start.2 = ((bf16[16,32,128]{2,1,0:T(8,128)(2,1)}), bf16[16,32,128]{2,1,0:T(8,128)(2,1)S(1)}, u32[]{:S(2)}, u32[]{:S(2)}) async-start(bf16[16,32,128]{2,1,0:T(8,128)(2,1)} %bitcast.2), calls=%async_computation.2 | async-start | bytes 262144 | tf_op jit(solution)/shard_map/all_to_all | solution.py:412
  49.5 2.0 %copy-start.6 = (f32[384]{0:T(512)S(1)}, f32[384]{0:T(512)}, u32[]{:S(2)}) copy-start(f32[384]{0:T(512)} %param.13) | copy-start | bytes 4612
  50.0 3.7 %collective-permute-start.7 = (f32[8,208]{1,0:T(8,128)S(1)}, f32[8,208]{1,0:T(8,128)S(1)}, u32[]{:S(2)}, u32[]{:S(2)}) collective-permute-start(f32[8,208]{1,0:T(8,128)S(1)} %get-tuple-element.40.refs_0_), channel_id=1, source_target_pairs={{0,1},{1,0},{2,3},{3,2},{4,5},{5,4},{6,7},{7,6},{8,9},{9,8},{10,11... | collective-permute-start | bytes 19976 | tf_op jit(solution)/shard_map/ppermute | solution.py:434
  53.7 1.6 %copy-start.2 = (f32[3,3,32,128]{3,2,1,0:T(8,128)S(1)}, f32[3,3,32,128]{3,2,1,0:T(8,128)}, u32[]{:S(2)}) copy-start(f32[3,3,32,128]{3,2,1,0:T(8,128)} %w_ref.3) | copy-start | bytes 442372

commit v14 on v12

--- a/solution.py
+++ b/solution.py
@@ -60,11 +60,11 @@
 
 
 def index_of(z, j, slots):
-    return (slots // 2 - 1 - z) % slots * GROUP + j
+    return (slots // 2 - z) % slots * GROUP + j
 
 
 def listed(slots):
-    return [(slots // 2 - 1 - i) % slots * GROUP + j for i in range(slots) for j in range(GROUP)]
+    return [(slots // 2 - i) % slots * GROUP + j for i in range(slots) for j in range(GROUP)]
 
 
 def sigmoid(x):

time: 56.7 us -> 56.4 us (level)
  waiting for transfers between devices: 5.16 us -> 4.42 us
    all_to_all x1, starting transfers between devices: 5.32 us -> 5.98 us  [on_device(): lax.all_to_all(ortho.reshape(count, rows_local, HD), 'ctx', 0, 0, tiled=T...]
    all_to_all x1, waiting for transfers between devices: 0.65 us -> 0.01 us  [on_device(): lax.all_to_all(ortho.reshape(count, rows_local, HD), 'ctx', 0, 0, tiled=T...]
  transfers between devices with their start and end apart: 11 -> 11, of which waited for: 4 -> 3; matrix products, arithmetic and copies ran while one was open for 0% -> 0% of each run, Pallas kernels for 18% -> 18%
where the time goes in v14:
time: 56.4 us; the launch traced here: 55.8 us
  starting transfers between devices  36.4 us (65%)
  Pallas kernels  12.5 us (22%)
  waiting for transfers between devices  4.42 us (8%)
  between operations  1.46 us (3%)
  local copies, waits for them, and re-layouts  0.93 us (2%)
    all_to_all x1, starting transfers between devices, on_device(): lax.all_to_all(low, 'ctx', 0, 0, tiled=True, axis_index_groups=[listed(nz)])  7.96 us
    ppermute x3, starting transfers between devices, on_device(): partials[d] = lax.ppermute(partials[d], 'ctx', pairs)  7.87 us
    ppermute x3, starting transfers between devices, on_device(): token_slots[d] = lax.ppermute(token_slots[d], 'ctx', pairs)  7.33 us
    all_to_all x1, starting transfers between devices, on_device(): lax.all_to_all(ortho.reshape(count, rows_local, HD), 'ctx', 0, 0, tiled=T...  5.98 us
    ppermute x3, waiting for transfers between devices, on_device(): token_slots[d] = lax.ppermute(token_slots[d], 'ctx', pairs)  3.63 us
    pallas_call x1, Pallas kernels, on_device(): call(functools.partial(ortho_body, heads, nz), sds((hidden, HD), bf16), f...  3.44 us
    all_to_all x1, starting transfers between devices, on_device(): lax.all_to_all(fast_slots, 'ctx', 0, 0, tiled=True, axis_index_groups=[[z...  3.37 us
    ppermute x1, starting transfers between devices, on_device(): kv_back = lax.ppermute(kv_own, 'ctx', ring)  2.38 us
  transfers between devices with their start and end apart: 11, of which 3 were waited for; matrix products, arithmetic and copies ran while one was open for 0% of the time, Pallas kernels for 18%

profile of v14, /device:TPU:0, one launch (start us, length us, event | category | flops | bytes accessed | tf_op | source)
XLA Modules:
  0.0 55.8 jit_solution(1442758473513332891)
XLA Ops:
  0.6 0.0 copy-start.1
  0.6 0.9 %copy-done.1 = f32[3,3,32,128]{3,2,1,0:T(8,128)S(1)} copy-done((f32[3,3,32,128]{3,2,1,0:T(8,128)S(1)}, f32[3,3,32,128]{3,2,1,0:T(8,128)}, u32[]{:S(2)}) %copy-start.1) | copy-done | bytes 147480
  1.5 0.8 %shard_map.86.after = bf16[16,3,32,128]{3,2,1,0:T(8,128)(2,1)} custom-call(f32[3,3,32,128]{3,2,1,0:T(8,128)S(1)} %copy-done.1), custom_call_target="tpu_custom_call" | custom-call | flops 1000000 | bytes 1048576 | tf_op jit(solution)/shard_map/pallas_call | solution.py:337
  2.3 0.0 copy-start
  2.3 0.0 copy-start.3
  2.3 0.0 copy-start.4
  2.3 8.0 %all-to-all-start = ((bf16[16,3,32,128]{3,2,1,0:T(8,128)(2,1)}), bf16[16,3,32,128]{3,2,1,0:T(8,128)(2,1)S(1)}, u32[]{:S(2)}, u32[]{:S(2)}) async-start(bf16[16,3,32,128]{3,2,1,0:T(8,128)(2,1)} %shard_map.86.after), calls=%async_computation | async-start | bytes 786432 | tf_op jit(solution)/shard_map/all_to_all | solution.py:354
  10.3 0.0 copy-start.5
  11.0 0.0 copy-done
  11.0 0.0 copy-done.3
  11.0 0.0 copy-done.4
  11.0 0.0 copy-done.5
  11.0 0.6 %shard_map.87 = (bf16[208,768]{1,0:T(8,128)(2,1)S(1)}, bf16[195,384]{1,0:T(8,128)(2,1)S(1)}, bf16[195,384]{1,0:T(8,128)(2,1)S(1)}, bf16[195,384]{1,0:T(8,128)(2,1)S(1)}, bf16[195,384]{1,0:T(8,128)(2,1)S(1)}) custom-call(bf16[16,3,32,128]{3,2,1,0:T(8,128)(2,1)} %shard_map.86.after, s32[1,1]{1,0:T(1,128)} %bitcast.3.update, f32[3,195]{1,0:T(4,128)S(1)} %bitcast.4, ...), custom_call_target="tpu_custom_call" | custom-call | tf_op jit(solution)/shard_map/pallas_call | solution.py:340
  11.6 1.3 %collective-permute-start.1 = (bf16[195,384]{1,0:T(8,128)(2,1)S(1)}, bf16[195,384]{1,0:T(8,128)(2,1)S(1)}, u32[]{:S(2)}, u32[]{:S(2)}) collective-permute-start(bf16[195,384]{1,0:T(8,128)(2,1)S(1)} %get-tuple-element.25), channel_id=1, source_target_pairs={{2,4},{4,2},{6,0},{10,12},{12,10},{14,8},{18,20},{20,18},{22,16},{... | collective-permute-start | bytes 449288 | tf_op jit(solution)/shard_map/ppermute | solution.py:359
  12.9 4.1 %collective-permute-start.2 = (bf16[195,384]{1,0:T(8,128)(2,1)S(1)}, bf16[195,384]{1,0:T(8,128)(2,1)S(1)}, u32[]{:S(2)}, u32[]{:S(2)}) collective-permute-start(bf16[195,384]{1,0:T(8,128)(2,1)S(1)} %get-tuple-element.26), channel_id=1, source_target_pairs={{0,2},{2,0},{6,4},{8,10},{10,8},{14,12},{16,18},{18,16},{22,20},{2... | collective-permute-start | bytes 449288 | tf_op jit(solution)/shard_map/ppermute | solution.py:359
  17.0 1.9 %collective-permute-start = (bf16[195,384]{1,0:T(8,128)(2,1)S(1)}, bf16[195,384]{1,0:T(8,128)(2,1)S(1)}, u32[]{:S(2)}, u32[]{:S(2)}) collective-permute-start(bf16[195,384]{1,0:T(8,128)(2,1)S(1)} %get-tuple-element.23), channel_id=1, source_target_pairs={{0,4},{4,0},{6,2},{8,12},{12,8},{14,10},{16,20},{20,16},{22,18},{2... | collective-permute-start | bytes 449288 | tf_op jit(solution)/shard_map/ppermute | solution.py:359
  18.9 1.9 %collective-permute-done.1.refs_1_ = bf16[195,384]{1,0:T(8,128)(2,1)S(1)} collective-permute-done((bf16[195,384]{1,0:T(8,128)(2,1)S(1)}, bf16[195,384]{1,0:T(8,128)(2,1)S(1)}, u32[]{:S(2)}, u32[]{:S(2)}) %collective-permute-start.1) | collective-permute-done | bytes 149792 | tf_op jit(solution)/shard_map/ppermute | solution.py:359
  20.8 0.0 collective-permute-done.2.refs_2_
  20.8 0.0 all-to-all-done.refs_3_.w_ref
  20.8 2.2 %shard_map.88 = (f32[3,512,128]{2,1,0:T(8,128)S(1)}, bf16[3,208,128]{2,1,0:T(8,128)(2,1)S(1)}) custom-call(bf16[195,384]{1,0:T(8,128)(2,1)S(1)} %get-tuple-element.24.refs_0_, bf16[195,384]{1,0:T(8,128)(2,1)S(1)} %collective-permute-done.1.refs_1_, bf16[195,384]{1,0:T(8,128)(2,1)S(1)} %collective-permute-done.2.refs_2_, ...), custom_call_target="tpu_custom_call" | custom-call | flops 1000000000 | bytes 1048576 | tf_op jit(solution)/shard_map/pallas_call | solution.py:363
  23.1 1.8 %collective-permute-done.token_ref = bf16[195,384]{1,0:T(8,128)(2,1)S(1)} collective-permute-done((bf16[195,384]{1,0:T(8,128)(2,1)S(1)}, bf16[195,384]{1,0:T(8,128)(2,1)S(1)}, u32[]{:S(2)}, u32[]{:S(2)}) %collective-permute-start) | collective-permute-done | bytes 149792 | tf_op jit(solution)/shard_map/ppermute | solution.py:359
  24.8 0.8 %shard_map.89 = (bf16[512,128]{1,0:T(8,128)(2,1)S(1)}, bf16[512,128]{1,0:T(8,128)(2,1)S(1)}, bf16[512,128]{1,0:T(8,128)(2,1)S(1)}, bf16[512,128]{1,0:T(8,128)(2,1)S(1)}) custom-call(bf16[195,384]{1,0:T(8,128)(2,1)S(1)} %collective-permute-done.token_ref, bf16[16,3,32,128]{3,2,1,0:T(8,128)(2,1)S(1)} %all-to-all-done.refs_3_.w_ref, ...), custom_call_target="tpu_custom_call" | custom-call | flops 500000000 | bytes 1048576 | tf_op jit(solution)/shard_map/pallas_call | solution.py:370
  25.6 1.3 %collective-permute-start.3 = (bf16[512,128]{1,0:T(8,128)(2,1)S(1)}, bf16[512,128]{1,0:T(8,128)(2,1)S(1)}, u32[]{:S(2)}, u32[]{:S(2)}) collective-permute-start(bf16[512,128]{1,0:T(8,128)(2,1)S(1)} %get-tuple-element.33), channel_id=1, source_target_pairs={{2,26},{8,16},{10,18},{12,20},{16,8},{18,10},{20,12},{24,0},{28,4}... | collective-permute-start | bytes 393224 | tf_op jit(solution)/shard_map/ppermute | solution.py:386
  26.9 4.7 %collective-permute-start.4 = (bf16[512,128]{1,0:T(8,128)(2,1)S(1)}, bf16[512,128]{1,0:T(8,128)(2,1)S(1)}, u32[]{:S(2)}, u32[]{:S(2)}) collective-permute-start(bf16[512,128]{1,0:T(8,128)(2,1)S(1)} %get-tuple-element.34), channel_id=1, source_target_pairs={{0,16},{2,18},{4,20},{10,26},{16,0},{20,4},{24,8},{26,10},{28,12},... | collective-permute-start | bytes 393224 | tf_op jit(solution)/shard_map/ppermute | solution.py:386
  31.5 1.9 %collective-permute-start.5 = (bf16[512,128]{1,0:T(8,128)(2,1)S(1)}, bf16[512,128]{1,0:T(8,128)(2,1)S(1)}, u32[]{:S(2)}, u32[]{:S(2)}) collective-permute-start(bf16[512,128]{1,0:T(8,128)(2,1)S(1)} %get-tuple-element.35), channel_id=1, source_target_pairs={{0,8},{2,10},{4,12},{8,0},{12,4},{18,26},{24,16},{26,18},{28,20},{... | collective-permute-start | bytes 393224 | tf_op jit(solution)/shard_map/ppermute | solution.py:386
  33.5 1.1 %shard_map.90 = bf16[4,208,128]{2,1,0:T(8,128)(2,1)} custom-call(bf16[195,384]{1,0:T(8,128)(2,1)S(1)} %collective-permute-done.token_ref, bf16[16,3,32,128]{3,2,1,0:T(8,128)(2,1)S(1)} %all-to-all-done.refs_3_.w_ref, bf16[3,208,128]{2,1,0:T(8,128)(2,1)S(1)} %get-tuple-element.31.early), custom_call_target="tpu_custom_call" | custom-call | flops 1000 | bytes 1024 | tf_op jit(solution)/shard_map/pallas_call | solution.py:388
  34.6 3.4 %all-to-all-start.1 = ((bf16[4,208,128]{2,1,0:T(8,128)(2,1)}), bf16[4,208,128]{2,1,0:T(8,128)(2,1)S(1)}, u32[]{:S(2)}, u32[]{:S(2)}) async-start(bf16[4,208,128]{2,1,0:T(8,128)(2,1)} %shard_map.90), calls=%async_computation.1 | async-start | bytes 425984 | tf_op jit(solution)/shard_map/all_to_all | solution.py:396
  38.0 2.4 %collective-permute-start.6 = (bf16[208,768]{1,0:T(8,128)(2,1)S(1)}, bf16[208,768]{1,0:T(8,128)(2,1)S(1)}, u32[]{:S(2)}, u32[]{:S(2)}) collective-permute-start(bf16[208,768]{1,0:T(8,128)(2,1)S(1)} %get-tuple-element.37.own_ref), channel_id=1, source_target_pairs={{0,2},{2,4},{4,6},{6,8},{8,10},{10,12},{12,14},{14,16},{16,18},{18... | collective-permute-start | bytes 958472 | tf_op jit(solution)/shard_map/ppermute | solution.py:402
  40.4 0.0 collective-permute-done.3.refs_1_
  40.4 0.0 collective-permute-done.4.refs_2_
  40.4 0.0 collective-permute-done.5.refs_3_
  40.4 3.4 %shard_map.91 = bf16[512,128]{1,0:T(8,128)(2,1)} custom-call(bf16[512,128]{1,0:T(8,128)(2,1)S(1)} %get-tuple-element.32.refs_0_, bf16[512,128]{1,0:T(8,128)(2,1)S(1)} %collective-permute-done.3.refs_1_, bf16[512,128]{1,0:T(8,128)(2,1)S(1)} %collective-permute-done.4.refs_2_, bf16[512,128]{1,0:T(8,128)(2,1)S(1)} %collective-permute-done.5.refs_3_), custom_call_target="tpu_custom_call" | custom-call | flops 1000000000 | bytes 1048576 | tf_op jit(solution)/shard_map/pallas_call | solution.py:404
  43.8 0.0 all-to-all-done.1.slots
  43.8 6.0 %all-to-all-start.2 = ((bf16[16,32,128]{2,1,0:T(8,128)(2,1)}), bf16[16,32,128]{2,1,0:T(8,128)(2,1)S(1)}, u32[]{:S(2)}, u32[]{:S(2)}) async-start(bf16[16,32,128]{2,1,0:T(8,128)(2,1)} %bitcast.2), calls=%async_computation.2 | async-start | bytes 262144 | tf_op jit(solution)/shard_map/all_to_all | solution.py:408
  49.8 0.0 copy-start.6
  49.8 0.4 shard_map.93
  50.3 1.6 %collective-permute-start.7 = (f32[8,208]{1,0:T(8,128)S(1)}, f32[8,208]{1,0:T(8,128)S(1)}, u32[]{:S(2)}, u32[]{:S(2)}) collective-permute-start(f32[8,208]{1,0:T(8,128)S(1)} %get-tuple-element.40.refs_0_), channel_id=1, source_target_pairs={{0,1},{1,0},{2,3},{3,2},{4,5},{5,4},{6,7},{7,6},{8,9},{9,8},{10,11... | collective-permute-start | bytes 19976 | tf_op jit(solution)/shard_map/ppermute | solution.py:430
  51.8 0.0 copy-done.6
  51.8 0.0 collective-permute-done.6.back_ref
  51.8 1.3 %shard_map.92.attended_ref = f32[208,384]{1,0:T(8,128)S(1)} custom-call(bf16[195,384]{1,0:T(8,128)(2,1)S(1)} %copy-done, bf16[208,768]{1,0:T(8,128)(2,1)S(1)} %get-tuple-element.37.own_ref, bf16[208,768]{1,0:T(8,128)(2,1)S(1)} %collective-permute-done.6.back_ref), custom_call_target="tpu_custom_call" | custom-call | tf_op jit(solution)/shard_map/pallas_call | solution.py:416
  53.2 0.8 %collective-permute-done.7.refs_1_ = f32[8,208]{1,0:T(8,128)S(1)} collective-permute-done((f32[8,208]{1,0:T(8,128)S(1)}, f32[8,208]{1,0:T(8,128)S(1)}, u32[]{:S(2)}, u32[]{:S(2)}) %collective-permute-start.7) | collective-permute-done | bytes 6688 | tf_op jit(solution)/shard_map/ppermute | solution.py:430
  54.0 0.0 copy-start.2
  54.0 1.0 %shard_map.94 = bf16[195,384]{1,0:T(8,128)(2,1)} custom-call(f32[1,384]{1,0:T(1,128)S(1)} %reshape.13.gain_ref, f32[208,384]{1,0:T(8,128)S(1)} %shard_map.92.attended_ref, bf16[208,384]{1,0:T(8,128)(2,1)S(1)} %get-tuple-element.39.fast_ref, f32[8,208]{1,0:T(8,128)S(1)} %get-tuple-element.40.refs_0_, f32[8,208]{1,0:T(8,128)S(1)} %collective-permute-done.7.refs_1_), custom_call_target="tpu_custom_call" | custom-call | tf_op jit(solution)/shard_map/pallas_call | solution.py:432
  54.9 0.0 all-to-all-done.2.rows_ref
  55.0 0.0 copy-done.2
  55.0 0.8 %shard_map.95 = f32[3,3,32,128]{3,2,1,0:T(8,128)} custom-call(f32[3,3,32,128]{3,2,1,0:T(8,128)S(1)} %copy-done.2, bf16[16,32,128]{2,1,0:T(8,128)(2,1)S(1)} %all-to-all-done.2.rows_ref), custom_call_target="tpu_custom_call" | custom-call | flops 1000000 | bytes 1048576 | tf_op jit(solution)/shard_map/pallas_call | solution.py:412
  (1 shorter events, 0.0 us)
Async XLA Ops:
  0.6 0.9 %copy-start.1 = (f32[3,3,32,128]{3,2,1,0:T(8,128)S(1)}, f32[3,3,32,128]{3,2,1,0:T(8,128)}, u32[]{:S(2)}) copy-start(f32[3,3,32,128]{3,2,1,0:T(8,128)} %w_ref.3) | copy-start | bytes 442372
  2.3 8.6 %copy-start = (bf16[195,384]{1,0:T(8,128)(2,1)S(1)}, bf16[195,384]{1,0:T(8,128)(2,1)}, u32[]{:S(2)}) copy-start(bf16[195,384]{1,0:T(8,128)(2,1)} %q_ref.2) | copy-start | bytes 449284
  2.3 8.6 %copy-start.3 = (bf16[195,384]{1,0:T(8,128)(2,1)S(1)}, bf16[195,384]{1,0:T(8,128)(2,1)}, u32[]{:S(2)}) copy-start(bf16[195,384]{1,0:T(8,128)(2,1)} %k_ref.1) | copy-start | bytes 449284
  2.3 8.7 %copy-start.4 = (bf16[195,384]{1,0:T(8,128)(2,1)S(1)}, bf16[195,384]{1,0:T(8,128)(2,1)}, u32[]{:S(2)}) copy-start(bf16[195,384]{1,0:T(8,128)(2,1)} %v_ref.1) | copy-start | bytes 449284
  2.3 18.5 %all-to-all-start = ((bf16[16,3,32,128]{3,2,1,0:T(8,128)(2,1)}), bf16[16,3,32,128]{3,2,1,0:T(8,128)(2,1)S(1)}, u32[]{:S(2)}, u32[]{:S(2)}) async-start(bf16[16,3,32,128]{3,2,1,0:T(8,128)(2,1)} %shard_map.86.after), calls=%async_computation | async-start | bytes 786432 | tf_op jit(solution)/shard_map/all_to_all | solution.py:354
  10.3 0.7 %copy-start.5 = (f32[195,3]{0,1:T(4,128)S(1)}, f32[195,3]{0,1:T(4,128)}, u32[]{:S(2)}) copy-start(f32[195,3]{0,1:T(4,128)} %param.10) | copy-start | bytes 7024
  11.6 9.2 %collective-permute-start.1 = (bf16[195,384]{1,0:T(8,128)(2,1)S(1)}, bf16[195,384]{1,0:T(8,128)(2,1)S(1)}, u32[]{:S(2)}, u32[]{:S(2)}) collective-permute-start(bf16[195,384]{1,0:T(8,128)(2,1)S(1)} %get-tuple-element.25), channel_id=1, source_target_pairs={{2,4},{4,2},{6,0},{10,12},{12,10},{14,8},{18,20},{20,18},{22,16},{... | collective-permute-start | bytes 449288 | tf_op jit(solution)/shard_map/ppermute | solution.py:359
  12.9 7.9 %collective-permute-start.2 = (bf16[195,384]{1,0:T(8,128)(2,1)S(1)}, bf16[195,384]{1,0:T(8,128)(2,1)S(1)}, u32[]{:S(2)}, u32[]{:S(2)}) collective-permute-start(bf16[195,384]{1,0:T(8,128)(2,1)S(1)} %get-tuple-element.26), channel_id=1, source_target_pairs={{0,2},{2,0},{6,4},{8,10},{10,8},{14,12},{16,18},{18,16},{22,20},{2... | collective-permute-start | bytes 449288 | tf_op jit(solution)/shard_map/ppermute | solution.py:359
  17.0 7.8 %collective-permute-start = (bf16[195,384]{1,0:T(8,128)(2,1)S(1)}, bf16[195,384]{1,0:T(8,128)(2,1)S(1)}, u32[]{:S(2)}, u32[]{:S(2)}) collective-permute-start(bf16[195,384]{1,0:T(8,128)(2,1)S(1)} %get-tuple-element.23), channel_id=1, source_target_pairs={{0,4},{4,0},{6,2},{8,12},{12,8},{14,10},{16,20},{20,16},{22,18},{2... | collective-permute-start | bytes 449288 | tf_op jit(solution)/shard_map/ppermute | solution.py:359
  25.6 14.8 %collective-permute-start.3 = (bf16[512,128]{1,0:T(8,128)(2,1)S(1)}, bf16[512,128]{1,0:T(8,128)(2,1)S(1)}, u32[]{:S(2)}, u32[]{:S(2)}) collective-permute-start(bf16[512,128]{1,0:T(8,128)(2,1)S(1)} %get-tuple-element.33), channel_id=1, source_target_pairs={{2,26},{8,16},{10,18},{12,20},{16,8},{18,10},{20,12},{24,0},{28,4}... | collective-permute-start | bytes 393224 | tf_op jit(solution)/shard_map/ppermute | solution.py:386
  26.9 13.5 %collective-permute-start.4 = (bf16[512,128]{1,0:T(8,128)(2,1)S(1)}, bf16[512,128]{1,0:T(8,128)(2,1)S(1)}, u32[]{:S(2)}, u32[]{:S(2)}) collective-permute-start(bf16[512,128]{1,0:T(8,128)(2,1)S(1)} %get-tuple-element.34), channel_id=1, source_target_pairs={{0,16},{2,18},{4,20},{10,26},{16,0},{20,4},{24,8},{26,10},{28,12},... | collective-permute-start | bytes 393224 | tf_op jit(solution)/shard_map/ppermute | solution.py:386
  31.5 8.8 %collective-permute-start.5 = (bf16[512,128]{1,0:T(8,128)(2,1)S(1)}, bf16[512,128]{1,0:T(8,128)(2,1)S(1)}, u32[]{:S(2)}, u32[]{:S(2)}) collective-permute-start(bf16[512,128]{1,0:T(8,128)(2,1)S(1)} %get-tuple-element.35), channel_id=1, source_target_pairs={{0,8},{2,10},{4,12},{8,0},{12,4},{18,26},{24,16},{26,18},{28,20},{... | collective-permute-start | bytes 393224 | tf_op jit(solution)/shard_map/ppermute | solution.py:386
  34.6 9.2 %all-to-all-start.1 = ((bf16[4,208,128]{2,1,0:T(8,128)(2,1)}), bf16[4,208,128]{2,1,0:T(8,128)(2,1)S(1)}, u32[]{:S(2)}, u32[]{:S(2)}) async-start(bf16[4,208,128]{2,1,0:T(8,128)(2,1)} %shard_map.90), calls=%async_computation.1 | async-start | bytes 425984 | tf_op jit(solution)/shard_map/all_to_all | solution.py:396
  38.0 13.9 %collective-permute-start.6 = (bf16[208,768]{1,0:T(8,128)(2,1)S(1)}, bf16[208,768]{1,0:T(8,128)(2,1)S(1)}, u32[]{:S(2)}, u32[]{:S(2)}) collective-permute-start(bf16[208,768]{1,0:T(8,128)(2,1)S(1)} %get-tuple-element.37.own_ref), channel_id=1, source_target_pairs={{0,2},{2,4},{4,6},{6,8},{8,10},{10,12},{12,14},{14,16},{16,18},{18... | collective-permute-start | bytes 958472 | tf_op jit(solution)/shard_map/ppermute | solution.py:402
  43.8 11.1 %all-to-all-start.2 = ((bf16[16,32,128]{2,1,0:T(8,128)(2,1)}), bf16[16,32,128]{2,1,0:T(8,128)(2,1)S(1)}, u32[]{:S(2)}, u32[]{:S(2)}) async-start(bf16[16,32,128]{2,1,0:T(8,128)(2,1)} %bitcast.2), calls=%async_computation.2 | async-start | bytes 262144 | tf_op jit(solution)/shard_map/all_to_all | solution.py:408
  49.8 2.0 %copy-start.6 = (f32[384]{0:T(512)S(1)}, f32[384]{0:T(512)}, u32[]{:S(2)}) copy-start(f32[384]{0:T(512)} %param.13) | copy-start | bytes 4612
  50.3 3.7 %collective-permute-start.7 = (f32[8,208]{1,0:T(8,128)S(1)}, f32[8,208]{1,0:T(8,128)S(1)}, u32[]{:S(2)}, u32[]{:S(2)}) collective-permute-start(f32[8,208]{1,0:T(8,128)S(1)} %get-tuple-element.40.refs_0_), channel_id=1, source_target_pairs={{0,1},{1,0},{2,3},{3,2},{4,5},{5,4},{6,7},{7,6},{8,9},{9,8},{10,11... | collective-permute-start | bytes 19976 | tf_op jit(solution)/shard_map/ppermute | solution.py:430
  54.0 1.0 %copy-start.2 = (f32[3,3,32,128]{3,2,1,0:T(8,128)S(1)}, f32[3,3,32,128]{3,2,1,0:T(8,128)}, u32[]{:S(2)}) copy-start(f32[3,3,32,128]{3,2,1,0:T(8,128)} %w_ref.3) | copy-start | bytes 442372

commit v15 on v13

--- a/solution.py
+++ b/solution.py
@@ -65,11 +65,11 @@
 
 
 def index_of(z, j, slots):
-    return (slots // 2 - 1 - z) % slots * GROUP + j
+    return (slots // 2 - z) % slots * GROUP + j
 
 
 def listed(slots):
-    return [(slots // 2 - 1 - i) % slots * GROUP + j for i in range(slots) for j in range(GROUP)]
+    return [(slots // 2 - i) % slots * GROUP + j for i in range(slots) for j in range(GROUP)]
 
 
 def sigmoid(x):

time: 56.8 us -> 56.3 us (level)
  waiting for transfers between devices: 5.27 us -> 4.62 us
    all_to_all x1, waiting for transfers between devices: 0.65 us -> 0.01 us  [on_device(): lax.all_to_all(ortho.reshape(count, rows_local, HD), 'ctx', 0, 0, tiled=T...]
  transfers between devices with their start and end apart: 11 -> 11, of which waited for: 5 -> 4; matrix products, arithmetic and copies ran while one was open for 0% -> 0% of each run, Pallas kernels for 18% -> 18%
where the time goes in v15:
time: 56.3 us; the launch traced here: 55.7 us
  starting transfers between devices  36.2 us (64%)
  Pallas kernels  12.6 us (22%)
  waiting for transfers between devices  4.62 us (8%)
  between operations  1.46 us (3%)
  local copies, waits for them, and re-layouts  0.93 us (2%)
    all_to_all x1, starting transfers between devices, on_device(): lax.all_to_all(low, 'ctx', 0, 0, tiled=True, axis_index_groups=[listed(nz)])  7.96 us
    ppermute x3, starting transfers between devices, on_device(): partials[d] = lax.ppermute(partials[d], 'ctx', pairs)  7.87 us
    ppermute x3, starting transfers between devices, on_device(): token_slots[d] = lax.ppermute(token_slots[d], 'ctx', pairs)  7.33 us
    all_to_all x1, starting transfers between devices, on_device(): lax.all_to_all(ortho.reshape(count, rows_local, HD), 'ctx', 0, 0, tiled=T...  5.69 us
    ppermute x3, waiting for transfers between devices, on_device(): token_slots[d] = lax.ppermute(token_slots[d], 'ctx', pairs)  3.63 us
    pallas_call x1, Pallas kernels, on_device(): call(functools.partial(ortho_body, heads), sds((hidden, HD), bf16), flops...  3.41 us
    all_to_all x1, starting transfers between devices, on_device(): lax.all_to_all(fast_slots, 'ctx', 0, 0, tiled=True, axis_index_groups=[[z...  3.37 us
    ppermute x1, starting transfers between devices, on_device(): kv_back = lax.ppermute(kv_own, 'ctx', ring)  2.38 us
  transfers between devices with their start and end apart: 11, of which 4 were waited for; matrix products, arithmetic and copies ran while one was open for 0% of the time, Pallas kernels for 18%

profile of v15, /device:TPU:0, one launch (start us, length us, event | category | flops | bytes accessed | tf_op | source)
XLA Modules:
  0.0 55.7 jit_solution(15534008501384419079)
XLA Ops:
  0.6 0.0 copy-start.1
  0.6 0.9 %copy-done.1 = f32[3,3,32,128]{3,2,1,0:T(8,128)S(1)} copy-done((f32[3,3,32,128]{3,2,1,0:T(8,128)S(1)}, f32[3,3,32,128]{3,2,1,0:T(8,128)}, u32[]{:S(2)}) %copy-start.1) | copy-done | bytes 147480
  1.5 0.8 %shard_map.86.after = bf16[16,3,32,128]{3,2,1,0:T(8,128)(2,1)} custom-call(f32[3,3,32,128]{3,2,1,0:T(8,128)S(1)} %copy-done.1), custom_call_target="tpu_custom_call" | custom-call | flops 1000000 | bytes 1048576 | tf_op jit(solution)/shard_map/pallas_call | solution.py:341
  2.3 0.0 copy-start
  2.3 0.0 copy-start.3
  2.3 0.0 copy-start.4
  2.3 8.0 %all-to-all-start = ((bf16[16,3,32,128]{3,2,1,0:T(8,128)(2,1)}), bf16[16,3,32,128]{3,2,1,0:T(8,128)(2,1)S(1)}, u32[]{:S(2)}, u32[]{:S(2)}) async-start(bf16[16,3,32,128]{3,2,1,0:T(8,128)(2,1)} %shard_map.86.after), calls=%async_computation | async-start | bytes 786432 | tf_op jit(solution)/shard_map/all_to_all | solution.py:358
  10.3 0.0 copy-start.5
  11.0 0.0 copy-done
  11.0 0.0 copy-done.3
  11.0 0.0 copy-done.4
  11.0 0.0 copy-done.5
  11.0 0.6 %shard_map.87 = (bf16[208,768]{1,0:T(8,128)(2,1)S(1)}, bf16[195,384]{1,0:T(8,128)(2,1)S(1)}, bf16[195,384]{1,0:T(8,128)(2,1)S(1)}, bf16[195,384]{1,0:T(8,128)(2,1)S(1)}, bf16[195,384]{1,0:T(8,128)(2,1)S(1)}) custom-call(bf16[16,3,32,128]{3,2,1,0:T(8,128)(2,1)} %shard_map.86.after, s32[1,1]{1,0:T(1,128)} %bitcast.3.update, f32[3,195]{1,0:T(4,128)S(1)} %bitcast.4, ...), custom_call_target="tpu_custom_call" | custom-call | tf_op jit(solution)/shard_map/pallas_call | solution.py:344
  11.6 1.3 %collective-permute-start.1 = (bf16[195,384]{1,0:T(8,128)(2,1)S(1)}, bf16[195,384]{1,0:T(8,128)(2,1)S(1)}, u32[]{:S(2)}, u32[]{:S(2)}) collective-permute-start(bf16[195,384]{1,0:T(8,128)(2,1)S(1)} %get-tuple-element.25), channel_id=1, source_target_pairs={{2,4},{4,2},{6,0},{10,12},{12,10},{14,8},{18,20},{20,18},{22,16},{... | collective-permute-start | bytes 449288 | tf_op jit(solution)/shard_map/ppermute | solution.py:363
  12.9 4.1 %collective-permute-start.2 = (bf16[195,384]{1,0:T(8,128)(2,1)S(1)}, bf16[195,384]{1,0:T(8,128)(2,1)S(1)}, u32[]{:S(2)}, u32[]{:S(2)}) collective-permute-start(bf16[195,384]{1,0:T(8,128)(2,1)S(1)} %get-tuple-element.26), channel_id=1, source_target_pairs={{0,2},{2,0},{6,4},{8,10},{10,8},{14,12},{16,18},{18,16},{22,20},{2... | collective-permute-start | bytes 449288 | tf_op jit(solution)/shard_map/ppermute | solution.py:363
  17.0 1.9 %collective-permute-start = (bf16[195,384]{1,0:T(8,128)(2,1)S(1)}, bf16[195,384]{1,0:T(8,128)(2,1)S(1)}, u32[]{:S(2)}, u32[]{:S(2)}) collective-permute-start(bf16[195,384]{1,0:T(8,128)(2,1)S(1)} %get-tuple-element.23), channel_id=1, source_target_pairs={{0,4},{4,0},{6,2},{8,12},{12,8},{14,10},{16,20},{20,16},{22,18},{2... | collective-permute-start | bytes 449288 | tf_op jit(solution)/shard_map/ppermute | solution.py:363
  18.9 1.9 %collective-permute-done.1.refs_1_ = bf16[195,384]{1,0:T(8,128)(2,1)S(1)} collective-permute-done((bf16[195,384]{1,0:T(8,128)(2,1)S(1)}, bf16[195,384]{1,0:T(8,128)(2,1)S(1)}, u32[]{:S(2)}, u32[]{:S(2)}) %collective-permute-start.1) | collective-permute-done | bytes 149792 | tf_op jit(solution)/shard_map/ppermute | solution.py:363
  20.8 0.0 collective-permute-done.2.refs_2_
  20.8 0.0 all-to-all-done.refs_3_.w_ref
  20.8 2.2 %shard_map.88 = (f32[3,512,128]{2,1,0:T(8,128)S(1)}, bf16[3,208,128]{2,1,0:T(8,128)(2,1)S(1)}) custom-call(bf16[195,384]{1,0:T(8,128)(2,1)S(1)} %get-tuple-element.24.refs_0_, bf16[195,384]{1,0:T(8,128)(2,1)S(1)} %collective-permute-done.1.refs_1_, bf16[195,384]{1,0:T(8,128)(2,1)S(1)} %collective-permute-done.2.refs_2_, ...), custom_call_target="tpu_custom_call" | custom-call | flops 1000000000 | bytes 1048576 | tf_op jit(solution)/shard_map/pallas_call | solution.py:367
  23.1 1.8 %collective-permute-done.token_ref = bf16[195,384]{1,0:T(8,128)(2,1)S(1)} collective-permute-done((bf16[195,384]{1,0:T(8,128)(2,1)S(1)}, bf16[195,384]{1,0:T(8,128)(2,1)S(1)}, u32[]{:S(2)}, u32[]{:S(2)}) %collective-permute-start) | collective-permute-done | bytes 149792 | tf_op jit(solution)/shard_map/ppermute | solution.py:363
  24.8 0.8 %shard_map.89 = (bf16[512,128]{1,0:T(8,128)(2,1)S(1)}, bf16[512,128]{1,0:T(8,128)(2,1)S(1)}, bf16[512,128]{1,0:T(8,128)(2,1)S(1)}, bf16[512,128]{1,0:T(8,128)(2,1)S(1)}) custom-call(bf16[195,384]{1,0:T(8,128)(2,1)S(1)} %collective-permute-done.token_ref, bf16[16,3,32,128]{3,2,1,0:T(8,128)(2,1)S(1)} %all-to-all-done.refs_3_.w_ref, ...), custom_call_target="tpu_custom_call" | custom-call | flops 500000000 | bytes 1048576 | tf_op jit(solution)/shard_map/pallas_call | solution.py:374
  25.6 1.3 %collective-permute-start.3 = (bf16[512,128]{1,0:T(8,128)(2,1)S(1)}, bf16[512,128]{1,0:T(8,128)(2,1)S(1)}, u32[]{:S(2)}, u32[]{:S(2)}) collective-permute-start(bf16[512,128]{1,0:T(8,128)(2,1)S(1)} %get-tuple-element.33), channel_id=1, source_target_pairs={{2,26},{8,16},{10,18},{12,20},{16,8},{20,12},{24,0},{26,2},{28,4},... | collective-permute-start | bytes 393224 | tf_op jit(solution)/shard_map/ppermute | solution.py:390
  26.9 4.7 %collective-permute-start.4 = (bf16[512,128]{1,0:T(8,128)(2,1)S(1)}, bf16[512,128]{1,0:T(8,128)(2,1)S(1)}, u32[]{:S(2)}, u32[]{:S(2)}) collective-permute-start(bf16[512,128]{1,0:T(8,128)(2,1)S(1)} %get-tuple-element.34), channel_id=1, source_target_pairs={{0,16},{2,18},{4,20},{10,26},{16,0},{18,2},{20,4},{24,8},{28,12},{... | collective-permute-start | bytes 393224 | tf_op jit(solution)/shard_map/ppermute | solution.py:390
  31.6 1.9 %collective-permute-start.5 = (bf16[512,128]{1,0:T(8,128)(2,1)S(1)}, bf16[512,128]{1,0:T(8,128)(2,1)S(1)}, u32[]{:S(2)}, u32[]{:S(2)}) collective-permute-start(bf16[512,128]{1,0:T(8,128)(2,1)S(1)} %get-tuple-element.35), channel_id=1, source_target_pairs={{0,8},{4,12},{8,0},{10,2},{12,4},{18,26},{24,16},{26,18},{28,20},{... | collective-permute-start | bytes 393224 | tf_op jit(solution)/shard_map/ppermute | solution.py:390
  33.5 1.1 %shard_map.90 = bf16[4,208,128]{2,1,0:T(8,128)(2,1)} custom-call(bf16[195,384]{1,0:T(8,128)(2,1)S(1)} %collective-permute-done.token_ref, bf16[16,3,32,128]{3,2,1,0:T(8,128)(2,1)S(1)} %all-to-all-done.refs_3_.w_ref, bf16[3,208,128]{2,1,0:T(8,128)(2,1)S(1)} %get-tuple-element.31.early), custom_call_target="tpu_custom_call" | custom-call | flops 1000 | bytes 1024 | tf_op jit(solution)/shard_map/pallas_call | solution.py:392
  34.7 3.4 %all-to-all-start.1 = ((bf16[4,208,128]{2,1,0:T(8,128)(2,1)}), bf16[4,208,128]{2,1,0:T(8,128)(2,1)S(1)}, u32[]{:S(2)}, u32[]{:S(2)}) async-start(bf16[4,208,128]{2,1,0:T(8,128)(2,1)} %shard_map.90), calls=%async_computation.1 | async-start | bytes 425984 | tf_op jit(solution)/shard_map/all_to_all | solution.py:400
  38.0 2.4 %collective-permute-start.6 = (bf16[208,768]{1,0:T(8,128)(2,1)S(1)}, bf16[208,768]{1,0:T(8,128)(2,1)S(1)}, u32[]{:S(2)}, u32[]{:S(2)}) collective-permute-start(bf16[208,768]{1,0:T(8,128)(2,1)S(1)} %get-tuple-element.37.own_ref), channel_id=1, source_target_pairs={{0,2},{2,4},{4,6},{6,8},{8,10},{10,12},{12,14},{14,16},{16,18},{18... | collective-permute-start | bytes 958472 | tf_op jit(solution)/shard_map/ppermute | solution.py:406
  40.4 0.0 collective-permute-done.3.refs_1_
  40.4 0.0 collective-permute-done.4.refs_2_
  40.4 0.2 collective-permute-done.5.refs_3_
  40.7 3.4 %shard_map.91 = bf16[512,128]{1,0:T(8,128)(2,1)} custom-call(bf16[512,128]{1,0:T(8,128)(2,1)S(1)} %get-tuple-element.32.refs_0_, bf16[512,128]{1,0:T(8,128)(2,1)S(1)} %collective-permute-done.3.refs_1_, bf16[512,128]{1,0:T(8,128)(2,1)S(1)} %collective-permute-done.4.refs_2_, bf16[512,128]{1,0:T(8,128)(2,1)S(1)} %collective-permute-done.5.refs_3_), custom_call_target="tpu_custom_call" | custom-call | flops 1000000000 | bytes 1048576 | tf_op jit(solution)/shard_map/pallas_call | solution.py:408
  44.1 0.0 all-to-all-done.1.slots
  44.1 5.7 %all-to-all-start.2 = ((bf16[16,32,128]{2,1,0:T(8,128)(2,1)}), bf16[16,32,128]{2,1,0:T(8,128)(2,1)S(1)}, u32[]{:S(2)}, u32[]{:S(2)}) async-start(bf16[16,32,128]{2,1,0:T(8,128)(2,1)} %bitcast.2), calls=%async_computation.2 | async-start | bytes 262144 | tf_op jit(solution)/shard_map/all_to_all | solution.py:412
  49.8 0.0 copy-start.6
  49.8 0.4 shard_map.93
  50.2 1.6 %collective-permute-start.7 = (f32[8,208]{1,0:T(8,128)S(1)}, f32[8,208]{1,0:T(8,128)S(1)}, u32[]{:S(2)}, u32[]{:S(2)}) collective-permute-start(f32[8,208]{1,0:T(8,128)S(1)} %get-tuple-element.40.refs_0_), channel_id=1, source_target_pairs={{0,1},{1,0},{2,3},{3,2},{4,5},{5,4},{6,7},{7,6},{8,9},{9,8},{10,11... | collective-permute-start | bytes 19976 | tf_op jit(solution)/shard_map/ppermute | solution.py:434
  51.8 0.0 copy-done.6
  51.8 0.0 collective-permute-done.6.back_ref
  51.8 1.3 %shard_map.92.attended_ref = f32[208,384]{1,0:T(8,128)S(1)} custom-call(bf16[195,384]{1,0:T(8,128)(2,1)S(1)} %copy-done, bf16[208,768]{1,0:T(8,128)(2,1)S(1)} %get-tuple-element.37.own_ref, bf16[208,768]{1,0:T(8,128)(2,1)S(1)} %collective-permute-done.6.back_ref), custom_call_target="tpu_custom_call" | custom-call | tf_op jit(solution)/shard_map/pallas_call | solution.py:420
  53.1 0.8 %collective-permute-done.7.refs_1_ = f32[8,208]{1,0:T(8,128)S(1)} collective-permute-done((f32[8,208]{1,0:T(8,128)S(1)}, f32[8,208]{1,0:T(8,128)S(1)}, u32[]{:S(2)}, u32[]{:S(2)}) %collective-permute-start.7) | collective-permute-done | bytes 6688 | tf_op jit(solution)/shard_map/ppermute | solution.py:434
  53.9 0.0 copy-start.2
  53.9 1.0 %shard_map.94 = bf16[195,384]{1,0:T(8,128)(2,1)} custom-call(f32[1,384]{1,0:T(1,128)S(1)} %reshape.13.gain_ref, f32[208,384]{1,0:T(8,128)S(1)} %shard_map.92.attended_ref, bf16[208,384]{1,0:T(8,128)(2,1)S(1)} %get-tuple-element.39.fast_ref, f32[8,208]{1,0:T(8,128)S(1)} %get-tuple-element.40.refs_0_, f32[8,208]{1,0:T(8,128)S(1)} %collective-permute-done.7.refs_1_), custom_call_target="tpu_custom_call" | custom-call | tf_op jit(solution)/shard_map/pallas_call | solution.py:436
  54.9 0.0 all-to-all-done.2.rows_ref
  54.9 0.0 copy-done.2
  54.9 0.8 %shard_map.95 = f32[3,3,32,128]{3,2,1,0:T(8,128)} custom-call(f32[3,3,32,128]{3,2,1,0:T(8,128)S(1)} %copy-done.2, bf16[16,32,128]{2,1,0:T(8,128)(2,1)S(1)} %all-to-all-done.2.rows_ref), custom_call_target="tpu_custom_call" | custom-call | flops 1000000 | bytes 1048576 | tf_op jit(solution)/shard_map/pallas_call | solution.py:416
  (1 shorter events, 0.0 us)
Async XLA Ops:
  0.6 0.9 %copy-start.1 = (f32[3,3,32,128]{3,2,1,0:T(8,128)S(1)}, f32[3,3,32,128]{3,2,1,0:T(8,128)}, u32[]{:S(2)}) copy-start(f32[3,3,32,128]{3,2,1,0:T(8,128)} %w_ref.3) | copy-start | bytes 442372
  2.3 8.6 %copy-start = (bf16[195,384]{1,0:T(8,128)(2,1)S(1)}, bf16[195,384]{1,0:T(8,128)(2,1)}, u32[]{:S(2)}) copy-start(bf16[195,384]{1,0:T(8,128)(2,1)} %q_ref.2) | copy-start | bytes 449284
  2.3 8.6 %copy-start.3 = (bf16[195,384]{1,0:T(8,128)(2,1)S(1)}, bf16[195,384]{1,0:T(8,128)(2,1)}, u32[]{:S(2)}) copy-start(bf16[195,384]{1,0:T(8,128)(2,1)} %k_ref.1) | copy-start | bytes 449284
  2.3 8.7 %copy-start.4 = (bf16[195,384]{1,0:T(8,128)(2,1)S(1)}, bf16[195,384]{1,0:T(8,128)(2,1)}, u32[]{:S(2)}) copy-start(bf16[195,384]{1,0:T(8,128)(2,1)} %v_ref.1) | copy-start | bytes 449284
  2.3 18.5 %all-to-all-start = ((bf16[16,3,32,128]{3,2,1,0:T(8,128)(2,1)}), bf16[16,3,32,128]{3,2,1,0:T(8,128)(2,1)S(1)}, u32[]{:S(2)}, u32[]{:S(2)}) async-start(bf16[16,3,32,128]{3,2,1,0:T(8,128)(2,1)} %shard_map.86.after), calls=%async_computation | async-start | bytes 786432 | tf_op jit(solution)/shard_map/all_to_all | solution.py:358
  10.3 0.7 %copy-start.5 = (f32[195,3]{0,1:T(4,128)S(1)}, f32[195,3]{0,1:T(4,128)}, u32[]{:S(2)}) copy-start(f32[195,3]{0,1:T(4,128)} %param.10) | copy-start | bytes 7024
  11.6 9.2 %collective-permute-start.1 = (bf16[195,384]{1,0:T(8,128)(2,1)S(1)}, bf16[195,384]{1,0:T(8,128)(2,1)S(1)}, u32[]{:S(2)}, u32[]{:S(2)}) collective-permute-start(bf16[195,384]{1,0:T(8,128)(2,1)S(1)} %get-tuple-element.25), channel_id=1, source_target_pairs={{2,4},{4,2},{6,0},{10,12},{12,10},{14,8},{18,20},{20,18},{22,16},{... | collective-permute-start | bytes 449288 | tf_op jit(solution)/shard_map/ppermute | solution.py:363
  12.9 7.9 %collective-permute-start.2 = (bf16[195,384]{1,0:T(8,128)(2,1)S(1)}, bf16[195,384]{1,0:T(8,128)(2,1)S(1)}, u32[]{:S(2)}, u32[]{:S(2)}) collective-permute-start(bf16[195,384]{1,0:T(8,128)(2,1)S(1)} %get-tuple-element.26), channel_id=1, source_target_pairs={{0,2},{2,0},{6,4},{8,10},{10,8},{14,12},{16,18},{18,16},{22,20},{2... | collective-permute-start | bytes 449288 | tf_op jit(solution)/shard_map/ppermute | solution.py:363
  17.0 7.8 %collective-permute-start = (bf16[195,384]{1,0:T(8,128)(2,1)S(1)}, bf16[195,384]{1,0:T(8,128)(2,1)S(1)}, u32[]{:S(2)}, u32[]{:S(2)}) collective-permute-start(bf16[195,384]{1,0:T(8,128)(2,1)S(1)} %get-tuple-element.23), channel_id=1, source_target_pairs={{0,4},{4,0},{6,2},{8,12},{12,8},{14,10},{16,20},{20,16},{22,18},{2... | collective-permute-start | bytes 449288 | tf_op jit(solution)/shard_map/ppermute | solution.py:363
  25.6 14.8 %collective-permute-start.3 = (bf16[512,128]{1,0:T(8,128)(2,1)S(1)}, bf16[512,128]{1,0:T(8,128)(2,1)S(1)}, u32[]{:S(2)}, u32[]{:S(2)}) collective-permute-start(bf16[512,128]{1,0:T(8,128)(2,1)S(1)} %get-tuple-element.33), channel_id=1, source_target_pairs={{2,26},{8,16},{10,18},{12,20},{16,8},{20,12},{24,0},{26,2},{28,4},... | collective-permute-start | bytes 393224 | tf_op jit(solution)/shard_map/ppermute | solution.py:390
  26.9 13.5 %collective-permute-start.4 = (bf16[512,128]{1,0:T(8,128)(2,1)S(1)}, bf16[512,128]{1,0:T(8,128)(2,1)S(1)}, u32[]{:S(2)}, u32[]{:S(2)}) collective-permute-start(bf16[512,128]{1,0:T(8,128)(2,1)S(1)} %get-tuple-element.34), channel_id=1, source_target_pairs={{0,16},{2,18},{4,20},{10,26},{16,0},{18,2},{20,4},{24,8},{28,12},{... | collective-permute-start | bytes 393224 | tf_op jit(solution)/shard_map/ppermute | solution.py:390
  31.6 9.0 %collective-permute-start.5 = (bf16[512,128]{1,0:T(8,128)(2,1)S(1)}, bf16[512,128]{1,0:T(8,128)(2,1)S(1)}, u32[]{:S(2)}, u32[]{:S(2)}) collective-permute-start(bf16[512,128]{1,0:T(8,128)(2,1)S(1)} %get-tuple-element.35), channel_id=1, source_target_pairs={{0,8},{4,12},{8,0},{10,2},{12,4},{18,26},{24,16},{26,18},{28,20},{... | collective-permute-start | bytes 393224 | tf_op jit(solution)/shard_map/ppermute | solution.py:390
  34.7 9.4 %all-to-all-start.1 = ((bf16[4,208,128]{2,1,0:T(8,128)(2,1)}), bf16[4,208,128]{2,1,0:T(8,128)(2,1)S(1)}, u32[]{:S(2)}, u32[]{:S(2)}) async-start(bf16[4,208,128]{2,1,0:T(8,128)(2,1)} %shard_map.90), calls=%async_computation.1 | async-start | bytes 425984 | tf_op jit(solution)/shard_map/all_to_all | solution.py:400
  38.0 13.7 %collective-permute-start.6 = (bf16[208,768]{1,0:T(8,128)(2,1)S(1)}, bf16[208,768]{1,0:T(8,128)(2,1)S(1)}, u32[]{:S(2)}, u32[]{:S(2)}) collective-permute-start(bf16[208,768]{1,0:T(8,128)(2,1)S(1)} %get-tuple-element.37.own_ref), channel_id=1, source_target_pairs={{0,2},{2,4},{4,6},{6,8},{8,10},{10,12},{12,14},{14,16},{16,18},{18... | collective-permute-start | bytes 958472 | tf_op jit(solution)/shard_map/ppermute | solution.py:406
  44.1 10.8 %all-to-all-start.2 = ((bf16[16,32,128]{2,1,0:T(8,128)(2,1)}), bf16[16,32,128]{2,1,0:T(8,128)(2,1)S(1)}, u32[]{:S(2)}, u32[]{:S(2)}) async-start(bf16[16,32,128]{2,1,0:T(8,128)(2,1)} %bitcast.2), calls=%async_computation.2 | async-start | bytes 262144 | tf_op jit(solution)/shard_map/all_to_all | solution.py:412
  49.8 2.0 %copy-start.6 = (f32[384]{0:T(512)S(1)}, f32[384]{0:T(512)}, u32[]{:S(2)}) copy-start(f32[384]{0:T(512)} %param.13) | copy-start | bytes 4612
  50.2 3.7 %collective-permute-start.7 = (f32[8,208]{1,0:T(8,128)S(1)}, f32[8,208]{1,0:T(8,128)S(1)}, u32[]{:S(2)}, u32[]{:S(2)}) collective-permute-start(f32[8,208]{1,0:T(8,128)S(1)} %get-tuple-element.40.refs_0_), channel_id=1, source_target_pairs={{0,1},{1,0},{2,3},{3,2},{4,5},{5,4},{6,7},{7,6},{8,9},{9,8},{10,11... | collective-permute-start | bytes 19976 | tf_op jit(solution)/shard_map/ppermute | solution.py:434
  53.9 1.0 %copy-start.2 = (f32[3,3,32,128]{3,2,1,0:T(8,128)S(1)}, f32[3,3,32,128]{3,2,1,0:T(8,128)}, u32[]{:S(2)}) copy-start(f32[3,3,32,128]{3,2,1,0:T(8,128)} %w_ref.3) | copy-start | bytes 442372

commit v16 on v14

--- a/solution.py
+++ b/solution.py
@@ -60,11 +60,11 @@
 
 
 def index_of(z, j, slots):
-    return (slots // 2 - z) % slots * GROUP + j
+    return (slots // 2 - z) % slots * GROUP + GROUP - 1 - j
 
 
 def listed(slots):
-    return [(slots // 2 - i) % slots * GROUP + j for i in range(slots) for j in range(GROUP)]
+    return [(slots // 2 - i) % slots * GROUP + j for i in range(slots) for j in range(GROUP)[::-1]]
 
 
 def sigmoid(x):

time: 56.4 us -> 56.6 us (level)
    all_to_all x1, starting transfers between devices: 5.98 us -> 6.64 us  [on_device(): lax.all_to_all(ortho.reshape(count, rows_local, HD), 'ctx', 0, 0, tiled=T...]
where the time goes in v16:
time: 56.6 us; the launch traced here: 56 us
  starting transfers between devices  36.7 us (65%)
  Pallas kernels  12.5 us (22%)
  waiting for transfers between devices  4.37 us (8%)
  between operations  1.46 us (3%)
  local copies, waits for them, and re-layouts  0.93 us (2%)
    all_to_all x1, starting transfers between devices, on_device(): lax.all_to_all(low, 'ctx', 0, 0, tiled=True, axis_index_groups=[listed(nz)])  7.97 us
    ppermute x3, starting transfers between devices, on_device(): partials[d] = lax.ppermute(partials[d], 'ctx', pairs)  7.95 us
    ppermute x3, starting transfers between devices, on_device(): token_slots[d] = lax.ppermute(token_slots[d], 'ctx', pairs)  6.82 us
    all_to_all x1, starting transfers between devices, on_device(): lax.all_to_all(ortho.reshape(count, rows_local, HD), 'ctx', 0, 0, tiled=T...  6.64 us
    ppermute x3, waiting for transfers between devices, on_device(): token_slots[d] = lax.ppermute(token_slots[d], 'ctx', pairs)  3.57 us
    pallas_call x1, Pallas kernels, on_device(): call(functools.partial(ortho_body, heads, nz), sds((hidden, HD), bf16), f...  3.44 us
    all_to_all x1, starting transfers between devices, on_device(): lax.all_to_all(fast_slots, 'ctx', 0, 0, tiled=True, axis_index_groups=[[z...  3.37 us
    ppermute x1, starting transfers between devices, on_device(): kv_back = lax.ppermute(kv_own, 'ctx', ring)  2.38 us
  transfers between devices with their start and end apart: 11, of which 3 were waited for; matrix products, arithmetic and copies ran while one was open for 0% of the time, Pallas kernels for 18%

profile of v16, /device:TPU:0, one launch (start us, length us, event | category | flops | bytes accessed | tf_op | source)
XLA Modules:
  0.0 56.0 jit_solution(9797193036918677194)
XLA Ops:
  0.6 0.0 copy-start.1
  0.6 0.9 %copy-done.1 = f32[3,3,32,128]{3,2,1,0:T(8,128)S(1)} copy-done((f32[3,3,32,128]{3,2,1,0:T(8,128)S(1)}, f32[3,3,32,128]{3,2,1,0:T(8,128)}, u32[]{:S(2)}) %copy-start.1) | copy-done | bytes 147480
  1.5 0.8 %shard_map.86.after = bf16[16,3,32,128]{3,2,1,0:T(8,128)(2,1)} custom-call(f32[3,3,32,128]{3,2,1,0:T(8,128)S(1)} %copy-done.1), custom_call_target="tpu_custom_call" | custom-call | flops 1000000 | bytes 1048576 | tf_op jit(solution)/shard_map/pallas_call | solution.py:337
  2.3 0.0 copy-start
  2.3 0.0 copy-start.3
  2.3 0.0 copy-start.4
  2.3 8.0 %all-to-all-start = ((bf16[16,3,32,128]{3,2,1,0:T(8,128)(2,1)}), bf16[16,3,32,128]{3,2,1,0:T(8,128)(2,1)S(1)}, u32[]{:S(2)}, u32[]{:S(2)}) async-start(bf16[16,3,32,128]{3,2,1,0:T(8,128)(2,1)} %shard_map.86.after), calls=%async_computation | async-start | bytes 786432 | tf_op jit(solution)/shard_map/all_to_all | solution.py:354
  10.3 0.0 copy-start.5
  11.0 0.0 copy-done
  11.0 0.0 copy-done.3
  11.0 0.0 copy-done.4
  11.0 0.0 copy-done.5
  11.0 0.6 %shard_map.87 = (bf16[208,768]{1,0:T(8,128)(2,1)S(1)}, bf16[195,384]{1,0:T(8,128)(2,1)S(1)}, bf16[195,384]{1,0:T(8,128)(2,1)S(1)}, bf16[195,384]{1,0:T(8,128)(2,1)S(1)}, bf16[195,384]{1,0:T(8,128)(2,1)S(1)}) custom-call(bf16[16,3,32,128]{3,2,1,0:T(8,128)(2,1)} %shard_map.86.after, s32[1,1]{1,0:T(1,128)} %bitcast.3.update, f32[3,195]{1,0:T(4,128)S(1)} %bitcast.4, ...), custom_call_target="tpu_custom_call" | custom-call | tf_op jit(solution)/shard_map/pallas_call | solution.py:340
  11.6 1.3 %collective-permute-start.1 = (bf16[195,384]{1,0:T(8,128)(2,1)S(1)}, bf16[195,384]{1,0:T(8,128)(2,1)S(1)}, u32[]{:S(2)}, u32[]{:S(2)}) collective-permute-start(bf16[195,384]{1,0:T(8,128)(2,1)S(1)} %get-tuple-element.25), channel_id=1, source_target_pairs={{2,4},{4,2},{6,0},{10,12},{12,10},{14,8},{18,20},{20,18},{22,16},{... | collective-permute-start | bytes 449288 | tf_op jit(solution)/shard_map/ppermute | solution.py:359
  12.9 3.2 %collective-permute-start.2 = (bf16[195,384]{1,0:T(8,128)(2,1)S(1)}, bf16[195,384]{1,0:T(8,128)(2,1)S(1)}, u32[]{:S(2)}, u32[]{:S(2)}) collective-permute-start(bf16[195,384]{1,0:T(8,128)(2,1)S(1)} %get-tuple-element.26), channel_id=1, source_target_pairs={{0,2},{2,0},{6,4},{8,10},{10,8},{14,12},{16,18},{18,16},{22,20},{2... | collective-permute-start | bytes 449288 | tf_op jit(solution)/shard_map/ppermute | solution.py:359
  16.1 2.3 %collective-permute-start = (bf16[195,384]{1,0:T(8,128)(2,1)S(1)}, bf16[195,384]{1,0:T(8,128)(2,1)S(1)}, u32[]{:S(2)}, u32[]{:S(2)}) collective-permute-start(bf16[195,384]{1,0:T(8,128)(2,1)S(1)} %get-tuple-element.23), channel_id=1, source_target_pairs={{0,4},{4,0},{6,2},{8,12},{12,8},{14,10},{16,20},{20,16},{22,18},{2... | collective-permute-start | bytes 449288 | tf_op jit(solution)/shard_map/ppermute | solution.py:359
  18.4 2.4 %collective-permute-done.1.refs_1_ = bf16[195,384]{1,0:T(8,128)(2,1)S(1)} collective-permute-done((bf16[195,384]{1,0:T(8,128)(2,1)S(1)}, bf16[195,384]{1,0:T(8,128)(2,1)S(1)}, u32[]{:S(2)}, u32[]{:S(2)}) %collective-permute-start.1) | collective-permute-done | bytes 149792 | tf_op jit(solution)/shard_map/ppermute | solution.py:359
  20.8 0.0 collective-permute-done.2.refs_2_
  20.8 0.0 all-to-all-done.refs_3_.w_ref
  20.8 2.2 %shard_map.88 = (f32[3,512,128]{2,1,0:T(8,128)S(1)}, bf16[3,208,128]{2,1,0:T(8,128)(2,1)S(1)}) custom-call(bf16[195,384]{1,0:T(8,128)(2,1)S(1)} %get-tuple-element.24.refs_0_, bf16[195,384]{1,0:T(8,128)(2,1)S(1)} %collective-permute-done.1.refs_1_, bf16[195,384]{1,0:T(8,128)(2,1)S(1)} %collective-permute-done.2.refs_2_, ...), custom_call_target="tpu_custom_call" | custom-call | flops 1000000000 | bytes 1048576 | tf_op jit(solution)/shard_map/pallas_call | solution.py:363
  23.1 1.2 %collective-permute-done.token_ref = bf16[195,384]{1,0:T(8,128)(2,1)S(1)} collective-permute-done((bf16[195,384]{1,0:T(8,128)(2,1)S(1)}, bf16[195,384]{1,0:T(8,128)(2,1)S(1)}, u32[]{:S(2)}, u32[]{:S(2)}) %collective-permute-start) | collective-permute-done | bytes 149792 | tf_op jit(solution)/shard_map/ppermute | solution.py:359
  24.3 0.8 %shard_map.89 = (bf16[512,128]{1,0:T(8,128)(2,1)S(1)}, bf16[512,128]{1,0:T(8,128)(2,1)S(1)}, bf16[512,128]{1,0:T(8,128)(2,1)S(1)}, bf16[512,128]{1,0:T(8,128)(2,1)S(1)}) custom-call(bf16[195,384]{1,0:T(8,128)(2,1)S(1)} %collective-permute-done.token_ref, bf16[16,3,32,128]{3,2,1,0:T(8,128)(2,1)S(1)} %all-to-all-done.refs_3_.w_ref, ...), custom_call_target="tpu_custom_call" | custom-call | flops 500000000 | bytes 1048576 | tf_op jit(solution)/shard_map/pallas_call | solution.py:370
  25.0 1.3 %collective-permute-start.3 = (bf16[512,128]{1,0:T(8,128)(2,1)S(1)}, bf16[512,128]{1,0:T(8,128)(2,1)S(1)}, u32[]{:S(2)}, u32[]{:S(2)}) collective-permute-start(bf16[512,128]{1,0:T(8,128)(2,1)S(1)} %get-tuple-element.33), channel_id=1, source_target_pairs={{2,26},{8,16},{10,18},{12,20},{16,8},{18,10},{20,12},{24,0},{28,4}... | collective-permute-start | bytes 393224 | tf_op jit(solution)/shard_map/ppermute | solution.py:386
  26.3 4.7 %collective-permute-start.4 = (bf16[512,128]{1,0:T(8,128)(2,1)S(1)}, bf16[512,128]{1,0:T(8,128)(2,1)S(1)}, u32[]{:S(2)}, u32[]{:S(2)}) collective-permute-start(bf16[512,128]{1,0:T(8,128)(2,1)S(1)} %get-tuple-element.34), channel_id=1, source_target_pairs={{0,16},{2,18},{4,20},{10,26},{16,0},{20,4},{24,8},{26,10},{28,12},... | collective-permute-start | bytes 393224 | tf_op jit(solution)/shard_map/ppermute | solution.py:386
  31.1 1.9 %collective-permute-start.5 = (bf16[512,128]{1,0:T(8,128)(2,1)S(1)}, bf16[512,128]{1,0:T(8,128)(2,1)S(1)}, u32[]{:S(2)}, u32[]{:S(2)}) collective-permute-start(bf16[512,128]{1,0:T(8,128)(2,1)S(1)} %get-tuple-element.35), channel_id=1, source_target_pairs={{0,8},{2,10},{4,12},{8,0},{12,4},{18,26},{24,16},{26,18},{28,20},{... | collective-permute-start | bytes 393224 | tf_op jit(solution)/shard_map/ppermute | solution.py:386
  33.0 1.1 %shard_map.90 = bf16[4,208,128]{2,1,0:T(8,128)(2,1)} custom-call(bf16[195,384]{1,0:T(8,128)(2,1)S(1)} %collective-permute-done.token_ref, bf16[16,3,32,128]{3,2,1,0:T(8,128)(2,1)S(1)} %all-to-all-done.refs_3_.w_ref, bf16[3,208,128]{2,1,0:T(8,128)(2,1)S(1)} %get-tuple-element.31.early), custom_call_target="tpu_custom_call" | custom-call | flops 1000 | bytes 1024 | tf_op jit(solution)/shard_map/pallas_call | solution.py:388
  34.1 3.4 %all-to-all-start.1 = ((bf16[4,208,128]{2,1,0:T(8,128)(2,1)}), bf16[4,208,128]{2,1,0:T(8,128)(2,1)S(1)}, u32[]{:S(2)}, u32[]{:S(2)}) async-start(bf16[4,208,128]{2,1,0:T(8,128)(2,1)} %shard_map.90), calls=%async_computation.1 | async-start | bytes 425984 | tf_op jit(solution)/shard_map/all_to_all | solution.py:396
  37.5 2.4 %collective-permute-start.6 = (bf16[208,768]{1,0:T(8,128)(2,1)S(1)}, bf16[208,768]{1,0:T(8,128)(2,1)S(1)}, u32[]{:S(2)}, u32[]{:S(2)}) collective-permute-start(bf16[208,768]{1,0:T(8,128)(2,1)S(1)} %get-tuple-element.37.own_ref), channel_id=1, source_target_pairs={{0,2},{2,4},{4,6},{6,8},{8,10},{10,12},{12,14},{14,16},{16,18},{18... | collective-permute-start | bytes 958472 | tf_op jit(solution)/shard_map/ppermute | solution.py:402
  39.9 0.0 collective-permute-done.3.refs_1_
  39.9 0.0 collective-permute-done.4.refs_2_
  39.9 0.0 collective-permute-done.5.refs_3_
  39.9 3.4 %shard_map.91 = bf16[512,128]{1,0:T(8,128)(2,1)} custom-call(bf16[512,128]{1,0:T(8,128)(2,1)S(1)} %get-tuple-element.32.refs_0_, bf16[512,128]{1,0:T(8,128)(2,1)S(1)} %collective-permute-done.3.refs_1_, bf16[512,128]{1,0:T(8,128)(2,1)S(1)} %collective-permute-done.4.refs_2_, bf16[512,128]{1,0:T(8,128)(2,1)S(1)} %collective-permute-done.5.refs_3_), custom_call_target="tpu_custom_call" | custom-call | flops 1000000000 | bytes 1048576 | tf_op jit(solution)/shard_map/pallas_call | solution.py:404
  43.4 0.0 all-to-all-done.1.slots
  43.4 6.6 %all-to-all-start.2 = ((bf16[16,32,128]{2,1,0:T(8,128)(2,1)}), bf16[16,32,128]{2,1,0:T(8,128)(2,1)S(1)}, u32[]{:S(2)}, u32[]{:S(2)}) async-start(bf16[16,32,128]{2,1,0:T(8,128)(2,1)} %bitcast.2), calls=%async_computation.2 | async-start | bytes 262144 | tf_op jit(solution)/shard_map/all_to_all | solution.py:408
  50.0 0.0 copy-start.6
  50.0 0.4 shard_map.93
  50.5 1.6 %collective-permute-start.7 = (f32[8,208]{1,0:T(8,128)S(1)}, f32[8,208]{1,0:T(8,128)S(1)}, u32[]{:S(2)}, u32[]{:S(2)}) collective-permute-start(f32[8,208]{1,0:T(8,128)S(1)} %get-tuple-element.40.refs_0_), channel_id=1, source_target_pairs={{0,1},{1,0},{2,3},{3,2},{4,5},{5,4},{6,7},{7,6},{8,9},{9,8},{10,11... | collective-permute-start | bytes 19976 | tf_op jit(solution)/shard_map/ppermute | solution.py:430
  52.0 0.0 copy-done.6
  52.0 0.0 collective-permute-done.6.back_ref
  52.0 1.3 %shard_map.92.attended_ref = f32[208,384]{1,0:T(8,128)S(1)} custom-call(bf16[195,384]{1,0:T(8,128)(2,1)S(1)} %copy-done, bf16[208,768]{1,0:T(8,128)(2,1)S(1)} %get-tuple-element.37.own_ref, bf16[208,768]{1,0:T(8,128)(2,1)S(1)} %collective-permute-done.6.back_ref), custom_call_target="tpu_custom_call" | custom-call | tf_op jit(solution)/shard_map/pallas_call | solution.py:416
  53.4 0.8 %collective-permute-done.7.refs_1_ = f32[8,208]{1,0:T(8,128)S(1)} collective-permute-done((f32[8,208]{1,0:T(8,128)S(1)}, f32[8,208]{1,0:T(8,128)S(1)}, u32[]{:S(2)}, u32[]{:S(2)}) %collective-permute-start.7) | collective-permute-done | bytes 6688 | tf_op jit(solution)/shard_map/ppermute | solution.py:430
  54.1 0.0 copy-start.2
  54.1 1.0 %shard_map.94 = bf16[195,384]{1,0:T(8,128)(2,1)} custom-call(f32[1,384]{1,0:T(1,128)S(1)} %reshape.13.gain_ref, f32[208,384]{1,0:T(8,128)S(1)} %shard_map.92.attended_ref, bf16[208,384]{1,0:T(8,128)(2,1)S(1)} %get-tuple-element.39.fast_ref, f32[8,208]{1,0:T(8,128)S(1)} %get-tuple-element.40.refs_0_, f32[8,208]{1,0:T(8,128)S(1)} %collective-permute-done.7.refs_1_), custom_call_target="tpu_custom_call" | custom-call | tf_op jit(solution)/shard_map/pallas_call | solution.py:432
  55.1 0.0 all-to-all-done.2.rows_ref
  55.1 0.0 copy-done.2
  55.1 0.8 %shard_map.95 = f32[3,3,32,128]{3,2,1,0:T(8,128)} custom-call(f32[3,3,32,128]{3,2,1,0:T(8,128)S(1)} %copy-done.2, bf16[16,32,128]{2,1,0:T(8,128)(2,1)S(1)} %all-to-all-done.2.rows_ref), custom_call_target="tpu_custom_call" | custom-call | flops 1000000 | bytes 1048576 | tf_op jit(solution)/shard_map/pallas_call | solution.py:412
  (1 shorter events, 0.0 us)
Async XLA Ops:
  0.6 0.9 %copy-start.1 = (f32[3,3,32,128]{3,2,1,0:T(8,128)S(1)}, f32[3,3,32,128]{3,2,1,0:T(8,128)}, u32[]{:S(2)}) copy-start(f32[3,3,32,128]{3,2,1,0:T(8,128)} %w_ref.3) | copy-start | bytes 442372
  2.3 8.6 %copy-start = (bf16[195,384]{1,0:T(8,128)(2,1)S(1)}, bf16[195,384]{1,0:T(8,128)(2,1)}, u32[]{:S(2)}) copy-start(bf16[195,384]{1,0:T(8,128)(2,1)} %q_ref.2) | copy-start | bytes 449284
  2.3 8.7 %copy-start.3 = (bf16[195,384]{1,0:T(8,128)(2,1)S(1)}, bf16[195,384]{1,0:T(8,128)(2,1)}, u32[]{:S(2)}) copy-start(bf16[195,384]{1,0:T(8,128)(2,1)} %k_ref.1) | copy-start | bytes 449284
  2.3 8.7 %copy-start.4 = (bf16[195,384]{1,0:T(8,128)(2,1)S(1)}, bf16[195,384]{1,0:T(8,128)(2,1)}, u32[]{:S(2)}) copy-start(bf16[195,384]{1,0:T(8,128)(2,1)} %v_ref.1) | copy-start | bytes 449284
  2.3 18.5 %all-to-all-start = ((bf16[16,3,32,128]{3,2,1,0:T(8,128)(2,1)}), bf16[16,3,32,128]{3,2,1,0:T(8,128)(2,1)S(1)}, u32[]{:S(2)}, u32[]{:S(2)}) async-start(bf16[16,3,32,128]{3,2,1,0:T(8,128)(2,1)} %shard_map.86.after), calls=%async_computation | async-start | bytes 786432 | tf_op jit(solution)/shard_map/all_to_all | solution.py:354
  10.3 0.7 %copy-start.5 = (f32[195,3]{0,1:T(4,128)S(1)}, f32[195,3]{0,1:T(4,128)}, u32[]{:S(2)}) copy-start(f32[195,3]{0,1:T(4,128)} %param.10) | copy-start | bytes 7024
  11.6 9.2 %collective-permute-start.1 = (bf16[195,384]{1,0:T(8,128)(2,1)S(1)}, bf16[195,384]{1,0:T(8,128)(2,1)S(1)}, u32[]{:S(2)}, u32[]{:S(2)}) collective-permute-start(bf16[195,384]{1,0:T(8,128)(2,1)S(1)} %get-tuple-element.25), channel_id=1, source_target_pairs={{2,4},{4,2},{6,0},{10,12},{12,10},{14,8},{18,20},{20,18},{22,16},{... | collective-permute-start | bytes 449288 | tf_op jit(solution)/shard_map/ppermute | solution.py:359
  12.9 7.9 %collective-permute-start.2 = (bf16[195,384]{1,0:T(8,128)(2,1)S(1)}, bf16[195,384]{1,0:T(8,128)(2,1)S(1)}, u32[]{:S(2)}, u32[]{:S(2)}) collective-permute-start(bf16[195,384]{1,0:T(8,128)(2,1)S(1)} %get-tuple-element.26), channel_id=1, source_target_pairs={{0,2},{2,0},{6,4},{8,10},{10,8},{14,12},{16,18},{18,16},{22,20},{2... | collective-permute-start | bytes 449288 | tf_op jit(solution)/shard_map/ppermute | solution.py:359
  16.1 8.2 %collective-permute-start = (bf16[195,384]{1,0:T(8,128)(2,1)S(1)}, bf16[195,384]{1,0:T(8,128)(2,1)S(1)}, u32[]{:S(2)}, u32[]{:S(2)}) collective-permute-start(bf16[195,384]{1,0:T(8,128)(2,1)S(1)} %get-tuple-element.23), channel_id=1, source_target_pairs={{0,4},{4,0},{6,2},{8,12},{12,8},{14,10},{16,20},{20,16},{22,18},{2... | collective-permute-start | bytes 449288 | tf_op jit(solution)/shard_map/ppermute | solution.py:359
  25.0 14.9 %collective-permute-start.3 = (bf16[512,128]{1,0:T(8,128)(2,1)S(1)}, bf16[512,128]{1,0:T(8,128)(2,1)S(1)}, u32[]{:S(2)}, u32[]{:S(2)}) collective-permute-start(bf16[512,128]{1,0:T(8,128)(2,1)S(1)} %get-tuple-element.33), channel_id=1, source_target_pairs={{2,26},{8,16},{10,18},{12,20},{16,8},{18,10},{20,12},{24,0},{28,4}... | collective-permute-start | bytes 393224 | tf_op jit(solution)/shard_map/ppermute | solution.py:386
  26.3 13.6 %collective-permute-start.4 = (bf16[512,128]{1,0:T(8,128)(2,1)S(1)}, bf16[512,128]{1,0:T(8,128)(2,1)S(1)}, u32[]{:S(2)}, u32[]{:S(2)}) collective-permute-start(bf16[512,128]{1,0:T(8,128)(2,1)S(1)} %get-tuple-element.34), channel_id=1, source_target_pairs={{0,16},{2,18},{4,20},{10,26},{16,0},{20,4},{24,8},{26,10},{28,12},... | collective-permute-start | bytes 393224 | tf_op jit(solution)/shard_map/ppermute | solution.py:386
  31.1 8.8 %collective-permute-start.5 = (bf16[512,128]{1,0:T(8,128)(2,1)S(1)}, bf16[512,128]{1,0:T(8,128)(2,1)S(1)}, u32[]{:S(2)}, u32[]{:S(2)}) collective-permute-start(bf16[512,128]{1,0:T(8,128)(2,1)S(1)} %get-tuple-element.35), channel_id=1, source_target_pairs={{0,8},{2,10},{4,12},{8,0},{12,4},{18,26},{24,16},{26,18},{28,20},{... | collective-permute-start | bytes 393224 | tf_op jit(solution)/shard_map/ppermute | solution.py:386
  34.1 9.2 %all-to-all-start.1 = ((bf16[4,208,128]{2,1,0:T(8,128)(2,1)}), bf16[4,208,128]{2,1,0:T(8,128)(2,1)S(1)}, u32[]{:S(2)}, u32[]{:S(2)}) async-start(bf16[4,208,128]{2,1,0:T(8,128)(2,1)} %shard_map.90), calls=%async_computation.1 | async-start | bytes 425984 | tf_op jit(solution)/shard_map/all_to_all | solution.py:396
  37.5 14.5 %collective-permute-start.6 = (bf16[208,768]{1,0:T(8,128)(2,1)S(1)}, bf16[208,768]{1,0:T(8,128)(2,1)S(1)}, u32[]{:S(2)}, u32[]{:S(2)}) collective-permute-start(bf16[208,768]{1,0:T(8,128)(2,1)S(1)} %get-tuple-element.37.own_ref), channel_id=1, source_target_pairs={{0,2},{2,4},{4,6},{6,8},{8,10},{10,12},{12,14},{14,16},{16,18},{18... | collective-permute-start | bytes 958472 | tf_op jit(solution)/shard_map/ppermute | solution.py:402
  43.4 11.8 %all-to-all-start.2 = ((bf16[16,32,128]{2,1,0:T(8,128)(2,1)}), bf16[16,32,128]{2,1,0:T(8,128)(2,1)S(1)}, u32[]{:S(2)}, u32[]{:S(2)}) async-start(bf16[16,32,128]{2,1,0:T(8,128)(2,1)} %bitcast.2), calls=%async_computation.2 | async-start | bytes 262144 | tf_op jit(solution)/shard_map/all_to_all | solution.py:408
  50.0 2.0 %copy-start.6 = (f32[384]{0:T(512)S(1)}, f32[384]{0:T(512)}, u32[]{:S(2)}) copy-start(f32[384]{0:T(512)} %param.13) | copy-start | bytes 4612
  50.5 3.7 %collective-permute-start.7 = (f32[8,208]{1,0:T(8,128)S(1)}, f32[8,208]{1,0:T(8,128)S(1)}, u32[]{:S(2)}, u32[]{:S(2)}) collective-permute-start(f32[8,208]{1,0:T(8,128)S(1)} %get-tuple-element.40.refs_0_), channel_id=1, source_target_pairs={{0,1},{1,0},{2,3},{3,2},{4,5},{5,4},{6,7},{7,6},{8,9},{9,8},{10,11... | collective-permute-start | bytes 19976 | tf_op jit(solution)/shard_map/ppermute | solution.py:430
  54.1 1.0 %copy-start.2 = (f32[3,3,32,128]{3,2,1,0:T(8,128)S(1)}, f32[3,3,32,128]{3,2,1,0:T(8,128)}, u32[]{:S(2)}) copy-start(f32[3,3,32,128]{3,2,1,0:T(8,128)} %w_ref.3) | copy-start | bytes 442372
